TPU v7x, 32 devices: a whole 2x2x4 slice. The times are simulated.
32 devices in a mesh: pre: 8 (over y, x, core), rsp: 4 (over z).
Axes of the slice: x: 2, y: 2, z: 4, core: 2. Of those that a mesh axis runs over, the one named last changes fastest.
Arguments:
- prompt_query: bfloat16 [1024, 2560], P(('pre', 'rsp')), may hold values from -100 to 100
- prompt_k: bfloat16 [1024, 512], P('pre'), may hold values from -5 to 5
- prompt_value: bfloat16 [1024, 512], P('pre'), may hold values from -6 to 6
- prompt_output: bfloat16 [1024, 2560], P(('pre', 'rsp')), may hold values from -6 to 6
- prompt_output_gradient: bfloat16 [1024, 2560], P(('pre', 'rsp')), may hold values from -24 to 24
- reply_query: bfloat16 [4, 2048, 2560], P('rsp', 'pre'), may hold values from -100 to 100
- reply_key: bfloat16 [4, 2048, 512], P('rsp', 'pre'), may hold values from -6 to 6
- reply_value: bfloat16 [4, 2048, 512], P('rsp', 'pre'), may hold values from -6 to 6
- reply_output: bfloat16 [4, 2048, 2560], P('rsp', 'pre'), may hold values from -6 to 6
- reply_output_gradient: bfloat16 [4, 2048, 2560], P('rsp', 'pre'), may hold values from -24 to 24
- reply_len: int32 [8], replicated, may hold values from 1 to 1024, 5120 in all
- reply_slot: int32 [8], replicated, may hold values from 0 to 7, each once
Outputs:
- prompt_dq: bfloat16 [1024, 2560], P(('pre', 'rsp'))
- prompt_dk: bfloat16 [1024, 512], P(('pre', 'rsp'))
- prompt_dv: bfloat16 [1024, 512], P(('pre', 'rsp'))
- reply_dq: bfloat16 [4, 2048, 2560], P('rsp', 'pre')
- reply_dk: bfloat16 [4, 2048, 512], P('rsp', 'pre')
- reply_dv: bfloat16 [4, 2048, 512], P('rsp', 'pre')
Inputs may be any that keep to these rules, and one draw needn't show every extreme that they name: `reply_len`: one response is exactly 1024 long; the lengths sum to 5120, rounded down. `reply_slot`: every slot is taken by exactly one response.
All inputs are finite; a program needn't handle non-finite values.
Results may differ from a plain program's by a relative error of at most 0.012.
Values may be sent and summed in bfloat16 or wider, within the bound.
No kernel may reach another device: no remote copies, remote signals or barrier semaphores. Data moves between devices by JAX's collectives and lax.ppermute only.
A program may use at most 128 MiB of HBM per device.

v0:
```python
import functools
import math

import jax
import jax.numpy as jnp
from jax import lax
from jax.experimental import pallas as pl
from jax.experimental.pallas import tpu as pltpu
from jax.sharding import PartitionSpec as P

QUERY_HEADS = 20
KEY_VALUE_HEADS = 4
GROUP = QUERY_HEADS // KEY_VALUE_HEADS
HEAD_WIDTH = 128
RESP_DEV = 2
CORES = 2
LOCAL_HEADS = KEY_VALUE_HEADS // CORES
GROUP_WIDTH = GROUP * HEAD_WIDTH

SCALE = HEAD_WIDTH ** (-0.5)
SCALE_LOG2 = SCALE * math.log2(math.e)
NEGATIVE_FLOOR = -1e30
DEAD = 1e30
F32 = jnp.float32
BF16 = jnp.bfloat16
VMEM = pl.BlockSpec(memory_space=pltpu.VMEM)
SMEM = pl.BlockSpec(memory_space=pltpu.SMEM)


def params(mib):
    return pltpu.CompilerParams(vmem_limit_bytes=mib * 1024 * 1024)


def dot(a, b, over=(1, 0)):
    return lax.dot_general(
        a, b, (((over[0],), (over[1],)), ((), ())), preferred_element_type=F32
    )


def iota(shape, axis):
    return lax.broadcasted_iota(jnp.int32, shape, axis)


def sorting(rows):
    half = rows // RESP_DEV
    out = iota((rows, rows), 0)
    source = jnp.where(out < half, RESP_DEV * out, RESP_DEV * (out - half) + 1)
    return (iota((rows, rows), 1) == source).astype(BF16)


def unsorting(rows):
    half = rows // RESP_DEV
    out = iota((rows, rows), 1)
    source = jnp.where(out < half, RESP_DEV * out, RESP_DEV * (out - half) + 1)
    return (iota((rows, rows), 0) == source).astype(BF16)


def lanes(index, width):
    return pl.ds(pl.multiple_of(index * width, width), width)


def head_of(core, cross, local):
    owner = (1 - core) if cross else core
    return owner * LOCAL_HEADS + local


def prepare_keys(place, pk, pv, rk, rv, *outs):
    core = place[1]
    prompt = pk.shape[0]
    order = sorting(rk.shape[0])
    for local in range(LOCAL_HEADS):
        for cross in range(CORES):
            out = outs[local * CORES + cross]
            span = lanes(head_of(core, cross, local), HEAD_WIDTH)
            for part, (p, r) in enumerate(((pk, rk), (pv, rv))):
                to = slice(part * HEAD_WIDTH, (part + 1) * HEAD_WIDTH)
                out[:prompt, to] = p[:, span]
                out[prompt:, to] = dot(order, r[:, span]).astype(BF16)


def prepare_rows(place, pq, po, pg, rq, ro, rg, *outs):
    core = place[1]
    reply = rq.shape[0]
    order = sorting(reply)
    pick = (iota((8, GROUP_WIDTH), 1) // HEAD_WIDTH == iota((8, GROUP_WIDTH), 0)).astype(BF16)

    def delta(gradient, output):
        product = gradient.astype(F32) * output.astype(F32)
        high = product.astype(BF16)
        low = (product - high.astype(F32)).astype(BF16)
        return dot(pick, high, (1, 1)) + dot(pick, low, (1, 1))

    for local in range(LOCAL_HEADS):
        for cross in range(CORES):
            rows_out, delta_out = outs[2 * (local * CORES + cross) :][:2]
            span = lanes(head_of(core, cross, local), GROUP_WIDTH)
            rows_out[reply:, :GROUP_WIDTH] = pq[:, span]
            rows_out[reply:, GROUP_WIDTH:] = pg[:, span]
            rows_out[:reply, :GROUP_WIDTH] = dot(order, rq[:, span]).astype(BF16)
            gradient = dot(order, rg[:, span]).astype(BF16)
            rows_out[:reply, GROUP_WIDTH:] = gradient
            output = dot(order, ro[:, span]).astype(BF16)
            delta_out[:, :reply] = delta(gradient, output)
            delta_out[:, reply:] = delta(pg[:, span], po[:, span])


def attend(sizes, place, reply_len, reply_slot, *refs):
    chips, reply_own, prompt_own, prompt_rows, prompt_keys = sizes
    own_positions = reply_own // RESP_DEV
    positions = CORES * own_positions
    chip_prompt = CORES * prompt_keys
    block = positions
    per_chip = chip_prompt // block
    prompt_blocks = chips * per_chip
    rows_in, refs = refs[:2], refs[2:]
    delta_in, refs = refs[:2], refs[2:]
    keys_in, refs = refs[: chips * CORES], refs[chips * CORES :]
    query_out, refs = refs[:2], refs[2:]
    keys_out, refs = refs[: chips * CORES], refs[chips * CORES :]
    keys, keys_t, total, query, gradient, delta, scores, top, mass, prob, score_grad, query_grad = refs
    chip, core, group = place[0], place[1], place[2]

    for index in range(chips * CORES):
        away, other = index // CORES, index % CORES
        source = keys_in[index]
        at = away * chip_prompt + other * prompt_keys
        keys[at : at + prompt_keys] = source[:prompt_keys]
        for slot in range(RESP_DEV):
            at = prompt_blocks * block + (slot * chips + away) * positions + other * own_positions
            begin = prompt_keys + slot * own_positions
            keys[at : at + own_positions] = source[begin : begin + own_positions]
    total[...] = jnp.zeros_like(total)

    def transpose_block(index, carry):
        rows = pl.ds(pl.multiple_of(index * block, block), block)
        keys_t[index] = keys[rows, :HEAD_WIDTH].astype(F32).T.astype(BF16)
        return carry

    lax.fori_loop(0, keys_t.shape[0], transpose_block, 0)

    def score_block(region, place_in, width, chunks, hidden):
        rows = pl.ds(pl.multiple_of(region * block, block), block)
        key_rows = keys[rows, :HEAD_WIDTH]
        for chunk in range(chunks):
            span = slice(chunk * width, (chunk + 1) * width)
            value = dot(key_rows, query[span], (1, 1)) * SCALE_LOG2
            if hidden is not None:
                value = jnp.where(hidden, NEGATIVE_FLOOR, value)
            scores[place_in, :, span] = value
            split = value.reshape(block // 8, 8, width)
            before = top[:, span]
            now = jnp.maximum(before, jnp.max(split, axis=0))
            top[:, span] = now
            mass[:, span] = mass[:, span] * jnp.exp2(before - now) + jnp.sum(
                jnp.exp2(split - now[None]), axis=0
            )

    def grad_block(region, place_in, width, chunks, log_mass):
        rows = pl.ds(pl.multiple_of(region * block, block), block)
        value_rows = keys[rows, HEAD_WIDTH:]
        all_rows = width * chunks
        for chunk in range(chunks):
            span = slice(chunk * width, (chunk + 1) * width)
            p = jnp.exp2(scores[place_in, :, span] - log_mass[chunk])
            dp = dot(value_rows, gradient[span], (1, 1))
            prob[:, span] = p.astype(BF16)
            score_grad[:, span] = (p * (dp - delta[0:1, span])).astype(BF16)
        total[rows, HEAD_WIDTH:] += dot(prob[:, :all_rows], gradient[:all_rows])
        total[rows, :HEAD_WIDTH] += dot(score_grad[:, :all_rows], query[:all_rows])
        query_grad[:, :all_rows] += dot(keys_t[region], score_grad[:, :all_rows])

    def begin(all_rows):
        top[:, :all_rows] = jnp.full((8, all_rows), NEGATIVE_FLOOR, F32)
        mass[:, :all_rows] = jnp.zeros((8, all_rows), F32)
        query_grad[:, :all_rows] = jnp.zeros((HEAD_WIDTH, all_rows), F32)

    def log_masses(width, chunks, live):
        found = []
        for chunk in range(chunks):
            span = slice(chunk * width, (chunk + 1) * width)
            peak = jnp.max(top[:, span], axis=0, keepdims=True)
            summed = jnp.sum(mass[:, span] * jnp.exp2(top[:, span] - peak), axis=0, keepdims=True)
            found.append(jnp.where(live, peak + jnp.log2(summed), DEAD))
        return found

    def absolute(index, half):
        return index + jnp.where(index < half, core * half, -core * half)

    def reply_tile(slot, carry):
        length = jnp.int32(0)
        for response in range(reply_len.shape[0]):
            mine = reply_slot[response] == group * RESP_DEV + slot
            length = length + jnp.where(mine, reply_len[response], 0)
        first = chip * positions
        source = pl.ds(pl.multiple_of(slot * own_positions, own_positions), own_positions)

        @pl.when(length > first)
        def _():
            for head in range(GROUP):
                for other in range(CORES):
                    at = head * positions + other * own_positions
                    to = slice(at, at + own_positions)
                    left = slice(head * HEAD_WIDTH, (head + 1) * HEAD_WIDTH)
                    right = slice(GROUP_WIDTH + head * HEAD_WIDTH, GROUP_WIDTH + (head + 1) * HEAD_WIDTH)
                    query[to] = rows_in[other][source, left]
                    gradient[to] = rows_in[other][source, right]
                    for which in range(RESP_DEV):
                        @pl.when(slot == which)
                        def _():
                            delta[0:1, to] = delta_in[other][
                                head : head + 1, which * own_positions : (which + 1) * own_positions
                            ]
            begin(GROUP * positions)
            base = prompt_blocks + slot * chips
            past = prompt_blocks + chip

            def region_of(index):
                reply = base + ((index - prompt_blocks) ^ chip)
                return jnp.where(index < prompt_blocks, index, reply)

            def stats(index, carry):
                score_block(region_of(index), index, positions, GROUP, None)
                return carry

            lax.fori_loop(0, past, stats, 0)
            row_at = absolute(iota((1, positions), 1), own_positions)
            key_at = absolute(iota((block, 1), 0), own_positions)
            score_block(base, past, positions, GROUP, key_at > row_at)
            live = first + row_at < length
            log_mass = log_masses(positions, GROUP, live)

            def grads(index, carry):
                region = jnp.where(index == past, base, region_of(index))
                grad_block(region, index, positions, GROUP, log_mass)
                return carry

            lax.fori_loop(0, past + 1, grads, 0)
            for head in range(GROUP):
                turned = (query_grad[:, head * positions : (head + 1) * positions].T * SCALE).astype(BF16)
                for other in range(CORES):
                    query_out[other][source, head * HEAD_WIDTH : (head + 1) * HEAD_WIDTH] = turned[
                        other * own_positions : (other + 1) * own_positions
                    ]

        @pl.when(length <= first)
        def _():
            for other in range(CORES):
                query_out[other][source, :] = jnp.zeros((own_positions, GROUP_WIDTH), BF16)

        return carry

    lax.fori_loop(0, RESP_DEV, reply_tile, 0)

    head_rows = CORES * prompt_own
    used = GROUP * head_rows
    all_rows = -(-used // 128) * 128
    if all_rows > used:
        query[used:all_rows] = jnp.zeros((all_rows - used, HEAD_WIDTH), BF16)
        gradient[used:all_rows] = jnp.zeros((all_rows - used, HEAD_WIDTH), BF16)
    delta[0:1, :all_rows] = jnp.zeros((1, all_rows), F32)
    for head in range(GROUP):
        for other in range(CORES):
            at = head * head_rows + other * prompt_own
            to = slice(at, at + prompt_own)
            left = slice(head * HEAD_WIDTH, (head + 1) * HEAD_WIDTH)
            right = slice(GROUP_WIDTH + head * HEAD_WIDTH, GROUP_WIDTH + (head + 1) * HEAD_WIDTH)
            query[to] = rows_in[other][reply_own:, left]
            gradient[to] = rows_in[other][reply_own:, right]
            delta[0:1, to] = delta_in[other][head : head + 1, reply_own:]
    begin(all_rows)
    lane = iota((1, all_rows), 1)
    within = lane
    for head in range(1, GROUP):
        within = within - jnp.where(lane >= head * head_rows, head_rows, 0)
    offset = jnp.where(within < prompt_own, within, within - prompt_own)
    row_core = jnp.where(within < prompt_own, core, 1 - core)
    real = (lane < used) & (offset < prompt_rows)
    row_at = jnp.where(
        real, (chip * CORES + row_core) * prompt_keys + group * prompt_rows + offset, -1
    )
    seen = (chip + 1) * per_chip

    def prompt_region(index):
        return (index // per_chip ^ chip) * per_chip + index % per_chip

    def prompt_stats(index, carry):
        key_row = iota((block, 1), 0) + index % per_chip * block
        key_at = index // per_chip * chip_prompt + absolute(key_row, prompt_keys)
        score_block(prompt_region(index), index, all_rows, 1, key_at > row_at)
        return carry

    lax.fori_loop(0, seen, prompt_stats, 0)
    log_mass = log_masses(all_rows, 1, real)

    def prompt_grads(index, carry):
        grad_block(prompt_region(index), index, all_rows, 1, log_mass)
        return carry

    lax.fori_loop(0, seen, prompt_grads, 0)
    turned = (query_grad[:, :all_rows].T * SCALE).astype(BF16)
    for head in range(GROUP):
        for other in range(CORES):
            at = head * head_rows + other * prompt_own
            query_out[other][reply_own:, head * HEAD_WIDTH : (head + 1) * HEAD_WIDTH] = turned[
                at : at + prompt_own
            ]

    for index in range(chips * CORES):
        away, other = index // CORES, index % CORES
        out = keys_out[index]

        def put(to, at, count):
            out[to : to + count, :HEAD_WIDTH] = (total[at : at + count, :HEAD_WIDTH] * SCALE).astype(BF16)
            out[to : to + count, HEAD_WIDTH:] = total[at : at + count, HEAD_WIDTH:].astype(BF16)

        put(0, away * chip_prompt + other * prompt_keys, prompt_keys)
        for slot in range(RESP_DEV):
            at = prompt_blocks * block + (slot * chips + away) * positions + other * own_positions
            put(prompt_keys + slot * own_positions, at, own_positions)


def spread_prompt(chips, prompt_keys, place, *refs):
    parts, outs, summed = refs[: chips * CORES], refs[chips * CORES : -1], refs[-1]
    groups = len(outs)
    rows = prompt_keys // groups
    for other in range(CORES):
        value = parts[other][:prompt_keys].astype(F32)
        for away in range(1, chips):
            value = value + parts[away * CORES + other][:prompt_keys].astype(F32)
        summed[other] = value
    for shift in range(groups):
        target = lax.rem(place[2] + shift, groups)
        at = pl.ds(pl.multiple_of(target * rows, rows), rows)
        for other in range(CORES):
            outs[shift][other] = summed[other, at].astype(BF16)


def finish(chips, groups, prompt_keys, prompt_own, place, *refs):
    count = chips * CORES
    parts, refs = refs[: LOCAL_HEADS * count], refs[LOCAL_HEADS * count :]
    slices, refs = refs[: LOCAL_HEADS * groups], refs[LOCAL_HEADS * groups :]
    queries, refs = refs[: LOCAL_HEADS * CORES], refs[LOCAL_HEADS * CORES :]
    prompt_dq, prompt_dk, prompt_dv, reply_dq, reply_dk, reply_dv = refs
    core = place[1]
    reply = reply_dq.shape[0]
    order = unsorting(reply)
    for local in range(LOCAL_HEADS):
        for other in range(CORES):
            head = head_of(core, other, local)
            span = lanes(head, HEAD_WIDTH)
            value = slices[local * groups][other].astype(F32)
            for shift in range(1, groups):
                value = value + slices[local * groups + shift][other].astype(F32)
            prompt_dk[:, span] = value[:, :HEAD_WIDTH].astype(BF16)
            prompt_dv[:, span] = value[:, HEAD_WIDTH:].astype(BF16)
            value = parts[local * count + other][prompt_keys:].astype(F32)
            for away in range(1, chips):
                value = value + parts[local * count + away * CORES + other][prompt_keys:].astype(F32)
            value = dot(order, value.astype(BF16)).astype(BF16)
            reply_dk[:, span] = value[:, :HEAD_WIDTH]
            reply_dv[:, span] = value[:, HEAD_WIDTH:]
            span = lanes(head, GROUP_WIDTH)
            source = queries[local * CORES + other]
            reply_dq[:, span] = dot(order, source[:reply]).astype(BF16)
            prompt_dq[:, span] = source[reply:]


def on_device(
    prompt_query,
    prompt_k,
    prompt_value,
    prompt_output,
    prompt_output_gradient,
    reply_query,
    reply_key,
    reply_value,
    reply_output,
    reply_output_gradient,
    reply_len,
    reply_slot,
):
    devices = lax.axis_size("pre")
    groups = lax.axis_size("rsp")
    chips = devices // CORES
    prompt_rows = prompt_query.shape[0]
    prompt_own = -(-prompt_rows // 16) * 16
    prompt_keys = prompt_k.shape[0]
    reply_own = reply_query.shape[1]
    own_positions = reply_own // RESP_DEV
    positions = CORES * own_positions
    chip_prompt = CORES * prompt_keys
    assert chip_prompt % positions == 0 and chips & (chips - 1) == 0
    pre_index = lax.axis_index("pre")
    place = jnp.stack([pre_index // CORES, pre_index % CORES, lax.axis_index("rsp")]).astype(jnp.int32)

    def shape(*dims, dtype=BF16):
        return jax.ShapeDtypeStruct(dims, dtype)

    def move(array, away, cross):
        pairs = [
            (p, (p // CORES ^ away) * CORES + (p % CORES ^ cross)) for p in range(devices)
        ]
        return lax.ppermute(array, "pre", pairs)

    def exchange(same, cross):
        return [
            (same, cross)[other](away) if (away, other) == (0, 0)
            else move((same, cross)[other](away), away, other)
            for away in range(chips)
            for other in range(CORES)
        ]

    key_rows = prompt_keys + reply_own
    key_blocks = pl.pallas_call(
        prepare_keys,
        out_shape=[shape(key_rows, 2 * HEAD_WIDTH)] * KEY_VALUE_HEADS,
        in_specs=[SMEM] + [VMEM] * 4,
        out_specs=[VMEM] * KEY_VALUE_HEADS,
        compiler_params=params(32),
        name="prepare_keys",
    )(place, prompt_k, prompt_value, reply_key[0], reply_value[0])
    gathered = [
        exchange(
            lambda away: key_blocks[local * CORES], lambda away: key_blocks[local * CORES + 1]
        )
        for local in range(LOCAL_HEADS)
    ]
    if prompt_own > prompt_rows:
        room = ((0, prompt_own - prompt_rows), (0, 0))
        prompt_query, prompt_output, prompt_output_gradient = (
            jnp.pad(array, room)
            for array in (prompt_query, prompt_output, prompt_output_gradient)
        )
    own_rows = reply_own + prompt_own
    row_blocks = pl.pallas_call(
        prepare_rows,
        out_shape=[shape(own_rows, 2 * GROUP_WIDTH), shape(8, own_rows, dtype=F32)] * KEY_VALUE_HEADS,
        in_specs=[SMEM] + [VMEM] * 6,
        out_specs=[VMEM] * (2 * KEY_VALUE_HEADS),
        compiler_params=params(48),
        name="prepare_rows",
    )(
        place,
        prompt_query,
        prompt_output,
        prompt_output_gradient,
        reply_query[0],
        reply_output[0],
        reply_output_gradient[0],
    )

    blocks = chips * (chip_prompt // positions) + RESP_DEV * chips
    slots = chips * (chip_prompt // positions) + chips
    all_rows = max(GROUP * positions, -(-GROUP * CORES * prompt_own // 128) * 128)
    sizes = (chips, reply_own, prompt_own, prompt_rows, prompt_keys)
    score_count = GROUP * (positions * RESP_DEV * slots * positions)
    parts, queries, slices = [], [], []
    for local in range(LOCAL_HEADS):
        mine, mine_delta, theirs, theirs_delta = row_blocks[4 * local : 4 * local + 4]
        results = pl.pallas_call(
            functools.partial(attend, sizes),
            out_shape=[shape(own_rows, GROUP_WIDTH)] * CORES
            + [shape(key_rows, 2 * HEAD_WIDTH)] * devices,
            in_specs=[SMEM] * 3 + [VMEM] * (4 + devices),
            out_specs=[VMEM] * (CORES + devices),
            scratch_shapes=[
                pltpu.VMEM((blocks * positions, 2 * HEAD_WIDTH), BF16),
                pltpu.VMEM((blocks, HEAD_WIDTH, positions), BF16),
                pltpu.VMEM((blocks * positions, 2 * HEAD_WIDTH), F32),
                pltpu.VMEM((all_rows, HEAD_WIDTH), BF16),
                pltpu.VMEM((all_rows, HEAD_WIDTH), BF16),
                pltpu.VMEM((8, all_rows), F32),
                pltpu.VMEM((slots, positions, all_rows), F32),
                pltpu.VMEM((8, all_rows), F32),
                pltpu.VMEM((8, all_rows), F32),
                pltpu.VMEM((positions, all_rows), BF16),
                pltpu.VMEM((positions, all_rows), BF16),
                pltpu.VMEM((HEAD_WIDTH, all_rows), F32),
            ],
            compiler_params=params(48),
            cost_estimate=pl.CostEstimate(
                flops=score_count * 10 * HEAD_WIDTH,
                bytes_accessed=8 * 1024 * 1024,
                transcendentals=2 * score_count,
            ),
            name="attend",
        )(
            place,
            reply_len,
            reply_slot,
            mine,
            move(theirs, 0, 1),
            mine_delta,
            move(theirs_delta, 0, 1),
            *gathered[local],
        )
        queries += [results[0], move(results[1], 0, 1)]
        sums = results[CORES:]
        arrived = exchange(lambda away: sums[away * CORES], lambda away: sums[away * CORES + 1])
        parts += arrived
        cut = pl.pallas_call(
            functools.partial(spread_prompt, chips, prompt_keys),
            out_shape=[shape(CORES, prompt_keys // groups, 2 * HEAD_WIDTH)] * groups,
            in_specs=[SMEM] + [VMEM] * devices,
            out_specs=[VMEM] * groups,
            scratch_shapes=[pltpu.VMEM((CORES, prompt_keys, 2 * HEAD_WIDTH), F32)],
            compiler_params=params(32),
            name="spread_prompt",
        )(place, *arrived)
        slices += [cut[0]] + [
            lax.ppermute(cut[shift], "rsp", [(g, (g + shift) % groups) for g in range(groups)])
            for shift in range(1, groups)
        ]

    key_width = KEY_VALUE_HEADS * HEAD_WIDTH
    query_width = QUERY_HEADS * HEAD_WIDTH
    cut_rows = prompt_keys // groups
    prompt_dq, prompt_dk, prompt_dv, reply_dq, reply_dk, reply_dv = pl.pallas_call(
        functools.partial(finish, chips, groups, prompt_keys, prompt_own),
        out_shape=[
            shape(prompt_own, query_width),
            shape(cut_rows, key_width),
            shape(cut_rows, key_width),
            shape(reply_own, query_width),
            shape(reply_own, key_width),
            shape(reply_own, key_width),
        ],
        in_specs=[SMEM] + [VMEM] * (LOCAL_HEADS * (devices + groups + CORES)),
        out_specs=[VMEM] * 6,
        compiler_params=params(48),
        name="finish",
    )(place, *parts, *slices, *queries)
    return (
        prompt_dq[:prompt_rows],
        prompt_dk,
        prompt_dv,
        reply_dq[None],
        reply_dk[None],
        reply_dv[None],
    )


def solution(mesh):
    return jax.shard_map(
        on_device,
        mesh=mesh,
        in_specs=(
            P(("pre", "rsp"), None),
            P("pre", None),
            P("pre", None),
            P(("pre", "rsp"), None),
            P(("pre", "rsp"), None),
            P("rsp", "pre", None),
            P("rsp", "pre", None),
            P("rsp", "pre", None),
            P("rsp", "pre", None),
            P("rsp", "pre", None),
            P(),
            P(),
        ),
        out_specs=(
            P(("pre", "rsp"), None),
            P(("pre", "rsp"), None),
            P(("pre", "rsp"), None),
            P("rsp", "pre", None),
            P("rsp", "pre", None),
            P("rsp", "pre", None),
        ),
        check_vma=False,
    )
```

profile of v0, /device:TPU:0, one launch (start us, length us, event | category | flops | bytes accessed | tf_op | source)
XLA Modules:
  0.0 142.4 jit_solution(10685298268561811763)
XLA Ops:
  0.7 1.3 copy-done
  2.0 1.3 copy-done.1
  6.1 3.9 %prepare_rows.1 = (bf16[288,1280]{1,0:T(8,128)(2,1)S(1)}, f32[8,288]{1,0:T(8,128)S(1)}, bf16[288,1280]{1,0:T(8,128)(2,1)S(1)}, f32[8,288]{1,0:T(8,128)S(1)}, bf1...) custom-call(s32[3]{0:T(128)S(1)} %pad_add_fusion.place, ...), custom_call_target="tpu_custom_call" | custom-call | tf_op jit(solution)/shard_map/prepare_rows/pallas_call | solution.py:435
  10.6 1.0 prepare_keys.1
  11.7 2.9 %collective-permute-start.3 = (bf16[384,256]{1,0:T(8,128)(2,1)S(1)}, bf16[384,256]{1,0:T(8,128)(2,1)S(1)}, u32[]{:S(2)}, u32[]{:S(2)}) collective-permute-start(bf16[384,256]{1,0:T(8,128)(2,1)S(1)} %get-tuple-element.56.refs_4_), channel_id=1, source_target_pairs={{0,8},{4,12},{8,0},{12,4},{16,24},{20,28},{24,16},{28,20},{1,9},{5... | collective-permute-start | bytes 589832 | tf_op jit(solution)/shard_map/ppermute | solution.py:403
  16.0 1.7 %collective-permute-start.5 = (bf16[384,256]{1,0:T(8,128)(2,1)S(1)}, bf16[384,256]{1,0:T(8,128)(2,1)S(1)}, u32[]{:S(2)}, u32[]{:S(2)}) collective-permute-start(bf16[384,256]{1,0:T(8,128)(2,1)S(1)} %get-tuple-element.56.refs_4_), channel_id=1, source_target_pairs={{0,16},{4,20},{8,24},{12,28},{16,0},{20,4},{24,8},{28,12},{1,17},{... | collective-permute-start | bytes 589832 | tf_op jit(solution)/shard_map/ppermute | solution.py:403
  17.7 2.6 %collective-permute-done.3.refs_6_ = bf16[384,256]{1,0:T(8,128)(2,1)S(1)} collective-permute-done((bf16[384,256]{1,0:T(8,128)(2,1)S(1)}, bf16[384,256]{1,0:T(8,128)(2,1)S(1)}, u32[]{:S(2)}, u32[]{:S(2)}) %collective-permute-start.3) | collective-permute-done | bytes 196640 | tf_op jit(solution)/shard_map/ppermute | solution.py:403
  20.3 3.0 %collective-permute-start.7 = (bf16[384,256]{1,0:T(8,128)(2,1)S(1)}, bf16[384,256]{1,0:T(8,128)(2,1)S(1)}, u32[]{:S(2)}, u32[]{:S(2)}) collective-permute-start(bf16[384,256]{1,0:T(8,128)(2,1)S(1)} %get-tuple-element.56.refs_4_), channel_id=1, source_target_pairs={{0,24},{4,28},{8,16},{12,20},{16,8},{20,12},{24,0},{28,4},{1,25},{... | collective-permute-start | bytes 589832 | tf_op jit(solution)/shard_map/ppermute | solution.py:403
  24.1 3.2 %collective-permute-start.8 = (bf16[384,256]{1,0:T(8,128)(2,1)S(1)}, bf16[384,256]{1,0:T(8,128)(2,1)S(1)}, u32[]{:S(2)}, u32[]{:S(2)}) collective-permute-start(bf16[384,256]{1,0:T(8,128)(2,1)S(1)} %get-tuple-element.57), channel_id=1, source_target_pairs={{0,28},{4,24},{8,20},{12,16},{16,12},{20,8},{24,4},{28,0},{1,29},{... | collective-permute-start | bytes 589832 | tf_op jit(solution)/shard_map/ppermute | solution.py:403
  27.3 7.9 %collective-permute-done.6.refs_9_ = bf16[384,256]{1,0:T(8,128)(2,1)S(1)} collective-permute-done((bf16[384,256]{1,0:T(8,128)(2,1)S(1)}, bf16[384,256]{1,0:T(8,128)(2,1)S(1)}, u32[]{:S(2)}, u32[]{:S(2)}) %collective-permute-start.6) | collective-permute-done | bytes 196640 | tf_op jit(solution)/shard_map/ppermute | solution.py:403
  35.2 1.7 %collective-permute-start.19 = (bf16[384,256]{1,0:T(8,128)(2,1)S(1)}, bf16[384,256]{1,0:T(8,128)(2,1)S(1)}, u32[]{:S(2)}, u32[]{:S(2)}) collective-permute-start(bf16[384,256]{1,0:T(8,128)(2,1)S(1)} %get-tuple-element.70.refs_4_), channel_id=1, source_target_pairs={{0,8},{4,12},{8,0},{12,4},{16,24},{20,28},{24,16},{28,20},{1,9},{5... | collective-permute-start | bytes 589832 | tf_op jit(solution)/shard_map/ppermute | solution.py:403
  37.0 1.6 %collective-permute-start.21 = (bf16[384,256]{1,0:T(8,128)(2,1)S(1)}, bf16[384,256]{1,0:T(8,128)(2,1)S(1)}, u32[]{:S(2)}, u32[]{:S(2)}) collective-permute-start(bf16[384,256]{1,0:T(8,128)(2,1)S(1)} %get-tuple-element.70.refs_4_), channel_id=1, source_target_pairs={{0,16},{4,20},{8,24},{12,28},{16,0},{20,4},{24,8},{28,12},{1,17},{... | collective-permute-start | bytes 589832 | tf_op jit(solution)/shard_map/ppermute | solution.py:403
  38.7 4.2 %collective-permute-done.19.refs_6_ = bf16[384,256]{1,0:T(8,128)(2,1)S(1)} collective-permute-done((bf16[384,256]{1,0:T(8,128)(2,1)S(1)}, bf16[384,256]{1,0:T(8,128)(2,1)S(1)}, u32[]{:S(2)}, u32[]{:S(2)}) %collective-permute-start.19) | collective-permute-done | bytes 196640 | tf_op jit(solution)/shard_map/ppermute | solution.py:403
  42.9 2.6 %collective-permute-start.23 = (bf16[384,256]{1,0:T(8,128)(2,1)S(1)}, bf16[384,256]{1,0:T(8,128)(2,1)S(1)}, u32[]{:S(2)}, u32[]{:S(2)}) collective-permute-start(bf16[384,256]{1,0:T(8,128)(2,1)S(1)} %get-tuple-element.70.refs_4_), channel_id=1, source_target_pairs={{0,24},{4,28},{8,16},{12,20},{16,8},{20,12},{24,0},{28,4},{1,25},{... | collective-permute-start | bytes 589832 | tf_op jit(solution)/shard_map/ppermute | solution.py:403
  46.3 3.2 %collective-permute-start.24 = (bf16[384,256]{1,0:T(8,128)(2,1)S(1)}, bf16[384,256]{1,0:T(8,128)(2,1)S(1)}, u32[]{:S(2)}, u32[]{:S(2)}) collective-permute-start(bf16[384,256]{1,0:T(8,128)(2,1)S(1)} %get-tuple-element.71), channel_id=1, source_target_pairs={{0,28},{4,24},{8,20},{12,16},{16,12},{20,8},{24,4},{28,0},{1,29},{... | collective-permute-start | bytes 589832 | tf_op jit(solution)/shard_map/ppermute | solution.py:403
  49.5 17.6 %attend.2 = (bf16[288,640]{1,0:T(8,128)(2,1)S(1)}, bf16[288,640]{1,0:T(8,128)(2,1)S(1)}, bf16[384,256]{1,0:T(8,128)(2,1)S(1)}, bf16[384,256]{1,0:T(8,128)(2,1)S(...) custom-call(s32[3]{0:T(128)S(1)} %pad_add_fusion.place, ...), custom_call_target="tpu_custom_call" | custom-call | flops 6710886400 | bytes 8388608 | tf_op jit(solution)/shard_map/attend/pallas_call | solution.py:460
  67.6 3.9 %collective-permute-start.10 = (bf16[384,256]{1,0:T(8,128)(2,1)S(1)}, bf16[384,256]{1,0:T(8,128)(2,1)S(1)}, u32[]{:S(2)}, u32[]{:S(2)}) collective-permute-start(bf16[384,256]{1,0:T(8,128)(2,1)S(1)} %get-tuple-element.60), channel_id=1, source_target_pairs={{0,8},{4,12},{8,0},{12,4},{16,24},{20,28},{24,16},{28,20},{1,9},{5... | collective-permute-start | bytes 589832 | tf_op jit(solution)/shard_map/ppermute | solution.py:403
  71.6 1.4 %collective-permute-start.13 = (bf16[384,256]{1,0:T(8,128)(2,1)S(1)}, bf16[384,256]{1,0:T(8,128)(2,1)S(1)}, u32[]{:S(2)}, u32[]{:S(2)}) collective-permute-start(bf16[384,256]{1,0:T(8,128)(2,1)S(1)} %get-tuple-element.63), channel_id=1, source_target_pairs={{0,20},{4,16},{8,28},{12,24},{16,4},{20,0},{24,12},{28,8},{1,21},{... | collective-permute-start | bytes 589832 | tf_op jit(solution)/shard_map/ppermute | solution.py:403
  73.1 1.7 %collective-permute-start.14 = (bf16[384,256]{1,0:T(8,128)(2,1)S(1)}, bf16[384,256]{1,0:T(8,128)(2,1)S(1)}, u32[]{:S(2)}, u32[]{:S(2)}) collective-permute-start(bf16[384,256]{1,0:T(8,128)(2,1)S(1)} %get-tuple-element.64), channel_id=1, source_target_pairs={{0,24},{4,28},{8,16},{12,20},{16,8},{20,12},{24,0},{28,4},{1,25},{... | collective-permute-start | bytes 589832 | tf_op jit(solution)/shard_map/ppermute | solution.py:403
  74.8 17.8 %attend.3 = (bf16[288,640]{1,0:T(8,128)(2,1)S(1)}, bf16[288,640]{1,0:T(8,128)(2,1)S(1)}, bf16[384,256]{1,0:T(8,128)(2,1)S(1)}, bf16[384,256]{1,0:T(8,128)(2,1)S(...) custom-call(s32[3]{0:T(128)S(1)} %pad_add_fusion.place, ...), custom_call_target="tpu_custom_call" | custom-call | flops 6710886400 | bytes 8388608 | tf_op jit(solution)/shard_map/attend/pallas_call | solution.py:460
  92.9 3.6 %collective-permute-start.26 = (bf16[384,256]{1,0:T(8,128)(2,1)S(1)}, bf16[384,256]{1,0:T(8,128)(2,1)S(1)}, u32[]{:S(2)}, u32[]{:S(2)}) collective-permute-start(bf16[384,256]{1,0:T(8,128)(2,1)S(1)} %get-tuple-element.74), channel_id=1, source_target_pairs={{0,8},{4,12},{8,0},{12,4},{16,24},{20,28},{24,16},{28,20},{1,9},{5... | collective-permute-start | bytes 589832 | tf_op jit(solution)/shard_map/ppermute | solution.py:403
  96.7 2.7 %collective-permute-start.28 = (bf16[384,256]{1,0:T(8,128)(2,1)S(1)}, bf16[384,256]{1,0:T(8,128)(2,1)S(1)}, u32[]{:S(2)}, u32[]{:S(2)}) collective-permute-start(bf16[384,256]{1,0:T(8,128)(2,1)S(1)} %get-tuple-element.76), channel_id=1, source_target_pairs={{0,16},{4,20},{8,24},{12,28},{16,0},{20,4},{24,8},{28,12},{1,17},{... | collective-permute-start | bytes 589832 | tf_op jit(solution)/shard_map/ppermute | solution.py:403
  99.4 1.4 collective-permute-done.15.refs_7_
  101.3 5.0 %collective-permute-done.26.refs_2_.refs_10_ = bf16[384,256]{1,0:T(8,128)(2,1)S(1)} collective-permute-done((bf16[384,256]{1,0:T(8,128)(2,1)S(1)}, bf16[384,256]{1,0:T(8,128)(2,1)S(1)}, u32[]{:S(2)}, u32[]{:S(2)}) %collective-permute-start.26) | collective-permute-done | bytes 196640 | tf_op jit(solution)/shard_map/ppermute | solution.py:403
  106.4 2.7 %collective-permute-done.27.refs_3_.refs_11_ = bf16[384,256]{1,0:T(8,128)(2,1)S(1)} collective-permute-done((bf16[384,256]{1,0:T(8,128)(2,1)S(1)}, bf16[384,256]{1,0:T(8,128)(2,1)S(1)}, u32[]{:S(2)}, u32[]{:S(2)}) %collective-permute-start.27) | collective-permute-done | bytes 196640 | tf_op jit(solution)/shard_map/ppermute | solution.py:403
  109.1 3.7 %collective-permute-start.30 = (bf16[384,256]{1,0:T(8,128)(2,1)S(1)}, bf16[384,256]{1,0:T(8,128)(2,1)S(1)}, u32[]{:S(2)}, u32[]{:S(2)}) collective-permute-start(bf16[384,256]{1,0:T(8,128)(2,1)S(1)} %get-tuple-element.78), channel_id=1, source_target_pairs={{0,24},{4,28},{8,16},{12,20},{16,8},{20,12},{24,0},{28,4},{1,25},{... | collective-permute-start | bytes 589832 | tf_op jit(solution)/shard_map/ppermute | solution.py:403
  113.4 15.0 %collective-permute-start.32 = (bf16[2,32,256]{2,1,0:T(8,128)(2,1)S(1)}, bf16[2,32,256]{2,1,0:T(8,128)(2,1)S(1)}, u32[]{:S(2)}, u32[]{:S(2)}) collective-permute-start(bf16[2,32,256]{2,1,0:T(8,128)(2,1)S(1)} %get-tuple-element.81), channel_id=1, source_target_pairs={{0,1},{1,2},{2,3},{3,0},{4,5},{5,6},{6,7},{7,4},{8,9},{9,10},{10,1... | collective-permute-start | bytes 98312 | tf_op jit(solution)/shard_map/ppermute | solution.py:511
  128.4 1.1 collective-permute-start.33
  129.5 2.9 %collective-permute-start.34 = (bf16[2,32,256]{2,1,0:T(8,128)(2,1)S(1)}, bf16[2,32,256]{2,1,0:T(8,128)(2,1)S(1)}, u32[]{:S(2)}, u32[]{:S(2)}) collective-permute-start(bf16[2,32,256]{2,1,0:T(8,128)(2,1)S(1)} %get-tuple-element.83), channel_id=1, source_target_pairs={{0,3},{1,0},{2,1},{3,2},{4,7},{5,4},{6,5},{7,6},{8,11},{9,8},{10,9... | collective-permute-start | bytes 98312 | tf_op jit(solution)/shard_map/ppermute | solution.py:511
  133.3 1.7 %collective-permute-start.36 = (bf16[2,32,256]{2,1,0:T(8,128)(2,1)S(1)}, bf16[2,32,256]{2,1,0:T(8,128)(2,1)S(1)}, u32[]{:S(2)}, u32[]{:S(2)}) collective-permute-start(bf16[2,32,256]{2,1,0:T(8,128)(2,1)S(1)} %get-tuple-element.86), channel_id=1, source_target_pairs={{0,2},{1,3},{2,0},{3,1},{4,6},{5,7},{6,4},{7,5},{8,10},{9,11},{10,... | collective-permute-start | bytes 98312 | tf_op jit(solution)/shard_map/ppermute | solution.py:511
  134.9 3.3 %collective-permute-start.37 = (bf16[2,32,256]{2,1,0:T(8,128)(2,1)S(1)}, bf16[2,32,256]{2,1,0:T(8,128)(2,1)S(1)}, u32[]{:S(2)}, u32[]{:S(2)}) collective-permute-start(bf16[2,32,256]{2,1,0:T(8,128)(2,1)S(1)} %get-tuple-element.87), channel_id=1, source_target_pairs={{0,3},{1,0},{2,1},{3,2},{4,7},{5,4},{6,5},{7,6},{8,11},{9,8},{10,9... | collective-permute-start | bytes 98312 | tf_op jit(solution)/shard_map/ppermute | solution.py:511
  139.8 2.6 %finish.1 = (bf16[32,2560]{1,0:T(8,128)(2,1)}, bf16[32,512]{1,0:T(8,128)(2,1)}, bf16[32,512]{1,0:T(8,128)(2,1)}, bf16[256,2560]{1,0:T(8,128)(2,1)}, bf16[256,512]{1,0:T(8,128)(2,1)}, /*index=5*/bf16[256,512]{1,0:T(8,128)(2,1)}) custom-call(s32[3]{0:T(128)S(1)} %pad_add_fusion.place, bf16[384,256]{1,0:T(8,128)(2,1)S(1)} %get-tuple-element.58.refs_0_, ...), custom_call_target="tpu_custom_call" | custom-call | tf_op jit(solution)/shard_map/finish/pallas_call | solution.py:518
  (78 shorter events, 11.4 us)
Async XLA Ops:
  10.1 39.4 %collective-permute-start = (bf16[288,1280]{1,0:T(8,128)(2,1)S(1)}, bf16[288,1280]{1,0:T(8,128)(2,1)S(1)}, u32[]{:S(2)}, u32[]{:S(2)}) collective-permute-start(bf16[288,1280]{1,0:T(8,128)(2,1)S(1)} %get-tuple-element.53), channel_id=1, source_target_pairs={{0,4},{4,0},{8,12},{12,8},{16,20},{20,16},{24,28},{28,24},{1,5},{5... | collective-permute-start | bytes 2211848 | tf_op jit(solution)/shard_map/ppermute | solution.py:403
  11.6 6.1 %collective-permute-start.2 = (bf16[384,256]{1,0:T(8,128)(2,1)S(1)}, bf16[384,256]{1,0:T(8,128)(2,1)S(1)}, u32[]{:S(2)}, u32[]{:S(2)}) collective-permute-start(bf16[384,256]{1,0:T(8,128)(2,1)S(1)} %get-tuple-element.57), channel_id=1, source_target_pairs={{0,4},{4,0},{8,12},{12,8},{16,20},{20,16},{24,28},{28,24},{1,5},{5... | collective-permute-start | bytes 589832 | tf_op jit(solution)/shard_map/ppermute | solution.py:403
  11.7 8.6 %collective-permute-start.3 = (bf16[384,256]{1,0:T(8,128)(2,1)S(1)}, bf16[384,256]{1,0:T(8,128)(2,1)S(1)}, u32[]{:S(2)}, u32[]{:S(2)}) collective-permute-start(bf16[384,256]{1,0:T(8,128)(2,1)S(1)} %get-tuple-element.56.refs_4_), channel_id=1, source_target_pairs={{0,8},{4,12},{8,0},{12,4},{16,24},{20,28},{24,16},{28,20},{1,9},{5... | collective-permute-start | bytes 589832 | tf_op jit(solution)/shard_map/ppermute | solution.py:403
  15.8 8.3 %collective-permute-start.4 = (bf16[384,256]{1,0:T(8,128)(2,1)S(1)}, bf16[384,256]{1,0:T(8,128)(2,1)S(1)}, u32[]{:S(2)}, u32[]{:S(2)}) collective-permute-start(bf16[384,256]{1,0:T(8,128)(2,1)S(1)} %get-tuple-element.57), channel_id=1, source_target_pairs={{0,12},{4,8},{8,4},{12,0},{16,28},{20,24},{24,20},{28,16},{1,13},{... | collective-permute-start | bytes 589832 | tf_op jit(solution)/shard_map/ppermute | solution.py:403
  16.0 11.3 %collective-permute-start.5 = (bf16[384,256]{1,0:T(8,128)(2,1)S(1)}, bf16[384,256]{1,0:T(8,128)(2,1)S(1)}, u32[]{:S(2)}, u32[]{:S(2)}) collective-permute-start(bf16[384,256]{1,0:T(8,128)(2,1)S(1)} %get-tuple-element.56.refs_4_), channel_id=1, source_target_pairs={{0,16},{4,20},{8,24},{12,28},{16,0},{20,4},{24,8},{28,12},{1,17},{... | collective-permute-start | bytes 589832 | tf_op jit(solution)/shard_map/ppermute | solution.py:403
  17.6 17.5 %collective-permute-start.6 = (bf16[384,256]{1,0:T(8,128)(2,1)S(1)}, bf16[384,256]{1,0:T(8,128)(2,1)S(1)}, u32[]{:S(2)}, u32[]{:S(2)}) collective-permute-start(bf16[384,256]{1,0:T(8,128)(2,1)S(1)} %get-tuple-element.57), channel_id=1, source_target_pairs={{0,20},{4,16},{8,28},{12,24},{16,4},{20,0},{24,12},{28,8},{1,21},{... | collective-permute-start | bytes 589832 | tf_op jit(solution)/shard_map/ppermute | solution.py:403
  20.3 16.5 %collective-permute-start.7 = (bf16[384,256]{1,0:T(8,128)(2,1)S(1)}, bf16[384,256]{1,0:T(8,128)(2,1)S(1)}, u32[]{:S(2)}, u32[]{:S(2)}) collective-permute-start(bf16[384,256]{1,0:T(8,128)(2,1)S(1)} %get-tuple-element.56.refs_4_), channel_id=1, source_target_pairs={{0,24},{4,28},{8,16},{12,20},{16,8},{20,12},{24,0},{28,4},{1,25},{... | collective-permute-start | bytes 589832 | tf_op jit(solution)/shard_map/ppermute | solution.py:403
  24.1 12.9 %collective-permute-start.8 = (bf16[384,256]{1,0:T(8,128)(2,1)S(1)}, bf16[384,256]{1,0:T(8,128)(2,1)S(1)}, u32[]{:S(2)}, u32[]{:S(2)}) collective-permute-start(bf16[384,256]{1,0:T(8,128)(2,1)S(1)} %get-tuple-element.57), channel_id=1, source_target_pairs={{0,28},{4,24},{8,20},{12,16},{16,12},{20,8},{24,4},{28,0},{1,29},{... | collective-permute-start | bytes 589832 | tf_op jit(solution)/shard_map/ppermute | solution.py:403
  27.3 11.3 %collective-permute-start.18 = (bf16[384,256]{1,0:T(8,128)(2,1)S(1)}, bf16[384,256]{1,0:T(8,128)(2,1)S(1)}, u32[]{:S(2)}, u32[]{:S(2)}) collective-permute-start(bf16[384,256]{1,0:T(8,128)(2,1)S(1)} %get-tuple-element.71), channel_id=1, source_target_pairs={{0,4},{4,0},{8,12},{12,8},{16,20},{20,16},{24,28},{28,24},{1,5},{5... | collective-permute-start | bytes 589832 | tf_op jit(solution)/shard_map/ppermute | solution.py:403
  35.2 7.7 %collective-permute-start.19 = (bf16[384,256]{1,0:T(8,128)(2,1)S(1)}, bf16[384,256]{1,0:T(8,128)(2,1)S(1)}, u32[]{:S(2)}, u32[]{:S(2)}) collective-permute-start(bf16[384,256]{1,0:T(8,128)(2,1)S(1)} %get-tuple-element.70.refs_4_), channel_id=1, source_target_pairs={{0,8},{4,12},{8,0},{12,4},{16,24},{20,28},{24,16},{28,20},{1,9},{5... | collective-permute-start | bytes 589832 | tf_op jit(solution)/shard_map/ppermute | solution.py:403
  36.8 9.4 %collective-permute-start.20 = (bf16[384,256]{1,0:T(8,128)(2,1)S(1)}, bf16[384,256]{1,0:T(8,128)(2,1)S(1)}, u32[]{:S(2)}, u32[]{:S(2)}) collective-permute-start(bf16[384,256]{1,0:T(8,128)(2,1)S(1)} %get-tuple-element.71), channel_id=1, source_target_pairs={{0,12},{4,8},{8,4},{12,0},{16,28},{20,24},{24,20},{28,16},{1,13},{... | collective-permute-start | bytes 589832 | tf_op jit(solution)/shard_map/ppermute | solution.py:403
  37.0 30.1 %collective-permute-start.21 = (bf16[384,256]{1,0:T(8,128)(2,1)S(1)}, bf16[384,256]{1,0:T(8,128)(2,1)S(1)}, u32[]{:S(2)}, u32[]{:S(2)}) collective-permute-start(bf16[384,256]{1,0:T(8,128)(2,1)S(1)} %get-tuple-element.70.refs_4_), channel_id=1, source_target_pairs={{0,16},{4,20},{8,24},{12,28},{16,0},{20,4},{24,8},{28,12},{1,17},{... | collective-permute-start | bytes 589832 | tf_op jit(solution)/shard_map/ppermute | solution.py:403
  38.6 29.1 %collective-permute-start.22 = (bf16[384,256]{1,0:T(8,128)(2,1)S(1)}, bf16[384,256]{1,0:T(8,128)(2,1)S(1)}, u32[]{:S(2)}, u32[]{:S(2)}) collective-permute-start(bf16[384,256]{1,0:T(8,128)(2,1)S(1)} %get-tuple-element.71), channel_id=1, source_target_pairs={{0,20},{4,16},{8,28},{12,24},{16,4},{20,0},{24,12},{28,8},{1,21},{... | collective-permute-start | bytes 589832 | tf_op jit(solution)/shard_map/ppermute | solution.py:403
  42.9 28.6 %collective-permute-start.23 = (bf16[384,256]{1,0:T(8,128)(2,1)S(1)}, bf16[384,256]{1,0:T(8,128)(2,1)S(1)}, u32[]{:S(2)}, u32[]{:S(2)}) collective-permute-start(bf16[384,256]{1,0:T(8,128)(2,1)S(1)} %get-tuple-element.70.refs_4_), channel_id=1, source_target_pairs={{0,24},{4,28},{8,16},{12,20},{16,8},{20,12},{24,0},{28,4},{1,25},{... | collective-permute-start | bytes 589832 | tf_op jit(solution)/shard_map/ppermute | solution.py:403
  46.3 25.2 %collective-permute-start.24 = (bf16[384,256]{1,0:T(8,128)(2,1)S(1)}, bf16[384,256]{1,0:T(8,128)(2,1)S(1)}, u32[]{:S(2)}, u32[]{:S(2)}) collective-permute-start(bf16[384,256]{1,0:T(8,128)(2,1)S(1)} %get-tuple-element.71), channel_id=1, source_target_pairs={{0,28},{4,24},{8,20},{12,16},{16,12},{20,8},{24,4},{28,0},{1,29},{... | collective-permute-start | bytes 589832 | tf_op jit(solution)/shard_map/ppermute | solution.py:403
  49.5 22.2 %collective-permute-start.16 = (bf16[288,1280]{1,0:T(8,128)(2,1)S(1)}, bf16[288,1280]{1,0:T(8,128)(2,1)S(1)}, u32[]{:S(2)}, u32[]{:S(2)}) collective-permute-start(bf16[288,1280]{1,0:T(8,128)(2,1)S(1)} %get-tuple-element.67), channel_id=1, source_target_pairs={{0,4},{4,0},{8,12},{12,8},{16,20},{20,16},{24,28},{28,24},{1,5},{5... | collective-permute-start | bytes 2211848 | tf_op jit(solution)/shard_map/ppermute | solution.py:403
  67.6 24.9 %collective-permute-start.10 = (bf16[384,256]{1,0:T(8,128)(2,1)S(1)}, bf16[384,256]{1,0:T(8,128)(2,1)S(1)}, u32[]{:S(2)}, u32[]{:S(2)}) collective-permute-start(bf16[384,256]{1,0:T(8,128)(2,1)S(1)} %get-tuple-element.60), channel_id=1, source_target_pairs={{0,8},{4,12},{8,0},{12,4},{16,24},{20,28},{24,16},{28,20},{1,9},{5... | collective-permute-start | bytes 589832 | tf_op jit(solution)/shard_map/ppermute | solution.py:403
  71.5 21.3 %collective-permute-start.11 = (bf16[384,256]{1,0:T(8,128)(2,1)S(1)}, bf16[384,256]{1,0:T(8,128)(2,1)S(1)}, u32[]{:S(2)}, u32[]{:S(2)}) collective-permute-start(bf16[384,256]{1,0:T(8,128)(2,1)S(1)} %get-tuple-element.61), channel_id=1, source_target_pairs={{0,12},{4,8},{8,4},{12,0},{16,28},{20,24},{24,20},{28,16},{1,13},{... | collective-permute-start | bytes 589832 | tf_op jit(solution)/shard_map/ppermute | solution.py:403
  71.5 21.4 %collective-permute-start.12 = (bf16[384,256]{1,0:T(8,128)(2,1)S(1)}, bf16[384,256]{1,0:T(8,128)(2,1)S(1)}, u32[]{:S(2)}, u32[]{:S(2)}) collective-permute-start(bf16[384,256]{1,0:T(8,128)(2,1)S(1)} %get-tuple-element.62), channel_id=1, source_target_pairs={{0,16},{4,20},{8,24},{12,28},{16,0},{20,4},{24,8},{28,12},{1,17},{... | collective-permute-start | bytes 589832 | tf_op jit(solution)/shard_map/ppermute | solution.py:403
  71.6 24.9 %collective-permute-start.13 = (bf16[384,256]{1,0:T(8,128)(2,1)S(1)}, bf16[384,256]{1,0:T(8,128)(2,1)S(1)}, u32[]{:S(2)}, u32[]{:S(2)}) collective-permute-start(bf16[384,256]{1,0:T(8,128)(2,1)S(1)} %get-tuple-element.63), channel_id=1, source_target_pairs={{0,20},{4,16},{8,28},{12,24},{16,4},{20,0},{24,12},{28,8},{1,21},{... | collective-permute-start | bytes 589832 | tf_op jit(solution)/shard_map/ppermute | solution.py:403
  73.1 23.6 %collective-permute-start.14 = (bf16[384,256]{1,0:T(8,128)(2,1)S(1)}, bf16[384,256]{1,0:T(8,128)(2,1)S(1)}, u32[]{:S(2)}, u32[]{:S(2)}) collective-permute-start(bf16[384,256]{1,0:T(8,128)(2,1)S(1)} %get-tuple-element.64), channel_id=1, source_target_pairs={{0,24},{4,28},{8,16},{12,20},{16,8},{20,12},{24,0},{28,4},{1,25},{... | collective-permute-start | bytes 589832 | tf_op jit(solution)/shard_map/ppermute | solution.py:403
  92.6 8.1 %collective-permute-start.15 = (bf16[384,256]{1,0:T(8,128)(2,1)S(1)}, bf16[384,256]{1,0:T(8,128)(2,1)S(1)}, u32[]{:S(2)}, u32[]{:S(2)}) collective-permute-start(bf16[384,256]{1,0:T(8,128)(2,1)S(1)} %get-tuple-element.65), channel_id=1, source_target_pairs={{0,28},{4,24},{8,20},{12,16},{16,12},{20,8},{24,4},{28,0},{1,29},{... | collective-permute-start | bytes 589832 | tf_op jit(solution)/shard_map/ppermute | solution.py:403
  92.8 8.1 %collective-permute-start.25 = (bf16[384,256]{1,0:T(8,128)(2,1)S(1)}, bf16[384,256]{1,0:T(8,128)(2,1)S(1)}, u32[]{:S(2)}, u32[]{:S(2)}) collective-permute-start(bf16[384,256]{1,0:T(8,128)(2,1)S(1)} %get-tuple-element.73), channel_id=1, source_target_pairs={{0,4},{4,0},{8,12},{12,8},{16,20},{20,16},{24,28},{28,24},{1,5},{5... | collective-permute-start | bytes 589832 | tf_op jit(solution)/shard_map/ppermute | solution.py:403
  92.9 13.4 %collective-permute-start.26 = (bf16[384,256]{1,0:T(8,128)(2,1)S(1)}, bf16[384,256]{1,0:T(8,128)(2,1)S(1)}, u32[]{:S(2)}, u32[]{:S(2)}) collective-permute-start(bf16[384,256]{1,0:T(8,128)(2,1)S(1)} %get-tuple-element.74), channel_id=1, source_target_pairs={{0,8},{4,12},{8,0},{12,4},{16,24},{20,28},{24,16},{28,20},{1,9},{5... | collective-permute-start | bytes 589832 | tf_op jit(solution)/shard_map/ppermute | solution.py:403
  96.5 12.6 %collective-permute-start.27 = (bf16[384,256]{1,0:T(8,128)(2,1)S(1)}, bf16[384,256]{1,0:T(8,128)(2,1)S(1)}, u32[]{:S(2)}, u32[]{:S(2)}) collective-permute-start(bf16[384,256]{1,0:T(8,128)(2,1)S(1)} %get-tuple-element.75), channel_id=1, source_target_pairs={{0,12},{4,8},{8,4},{12,0},{16,28},{20,24},{24,20},{28,16},{1,13},{... | collective-permute-start | bytes 589832 | tf_op jit(solution)/shard_map/ppermute | solution.py:403
  96.7 16.1 %collective-permute-start.28 = (bf16[384,256]{1,0:T(8,128)(2,1)S(1)}, bf16[384,256]{1,0:T(8,128)(2,1)S(1)}, u32[]{:S(2)}, u32[]{:S(2)}) collective-permute-start(bf16[384,256]{1,0:T(8,128)(2,1)S(1)} %get-tuple-element.76), channel_id=1, source_target_pairs={{0,16},{4,20},{8,24},{12,28},{16,0},{20,4},{24,8},{28,12},{1,17},{... | collective-permute-start | bytes 589832 | tf_op jit(solution)/shard_map/ppermute | solution.py:403
  100.8 39.0 %collective-permute-start.38 = (bf16[288,640]{1,0:T(8,128)(2,1)S(1)}, bf16[288,640]{1,0:T(8,128)(2,1)S(1)}, u32[]{:S(2)}, u32[]{:S(2)}) collective-permute-start(bf16[288,640]{1,0:T(8,128)(2,1)S(1)} %get-tuple-element.89), channel_id=1, source_target_pairs={{0,4},{4,0},{8,12},{12,8},{16,20},{20,16},{24,28},{28,24},{1,5},{5... | collective-permute-start | bytes 1105928 | tf_op jit(solution)/shard_map/ppermute | solution.py:403
  100.9 38.9 %collective-permute-start.39 = (bf16[288,640]{1,0:T(8,128)(2,1)S(1)}, bf16[288,640]{1,0:T(8,128)(2,1)S(1)}, u32[]{:S(2)}, u32[]{:S(2)}) collective-permute-start(bf16[288,640]{1,0:T(8,128)(2,1)S(1)} %get-tuple-element.91), channel_id=1, source_target_pairs={{0,4},{4,0},{8,12},{12,8},{16,20},{20,16},{24,28},{28,24},{1,5},{5... | collective-permute-start | bytes 1105928 | tf_op jit(solution)/shard_map/ppermute | solution.py:403
  106.3 7.2 %collective-permute-start.29 = (bf16[384,256]{1,0:T(8,128)(2,1)S(1)}, bf16[384,256]{1,0:T(8,128)(2,1)S(1)}, u32[]{:S(2)}, u32[]{:S(2)}) collective-permute-start(bf16[384,256]{1,0:T(8,128)(2,1)S(1)} %get-tuple-element.77), channel_id=1, source_target_pairs={{0,20},{4,16},{8,28},{12,24},{16,4},{20,0},{24,12},{28,8},{1,21},{... | collective-permute-start | bytes 589832 | tf_op jit(solution)/shard_map/ppermute | solution.py:403
  109.1 19.3 %collective-permute-start.30 = (bf16[384,256]{1,0:T(8,128)(2,1)S(1)}, bf16[384,256]{1,0:T(8,128)(2,1)S(1)}, u32[]{:S(2)}, u32[]{:S(2)}) collective-permute-start(bf16[384,256]{1,0:T(8,128)(2,1)S(1)} %get-tuple-element.78), channel_id=1, source_target_pairs={{0,24},{4,28},{8,16},{12,20},{16,8},{20,12},{24,0},{28,4},{1,25},{... | collective-permute-start | bytes 589832 | tf_op jit(solution)/shard_map/ppermute | solution.py:403
  112.8 16.7 %collective-permute-start.31 = (bf16[384,256]{1,0:T(8,128)(2,1)S(1)}, bf16[384,256]{1,0:T(8,128)(2,1)S(1)}, u32[]{:S(2)}, u32[]{:S(2)}) collective-permute-start(bf16[384,256]{1,0:T(8,128)(2,1)S(1)} %get-tuple-element.79), channel_id=1, source_target_pairs={{0,28},{4,24},{8,20},{12,16},{16,12},{20,8},{24,4},{28,0},{1,29},{... | collective-permute-start | bytes 589832 | tf_op jit(solution)/shard_map/ppermute | solution.py:403
  113.4 19.6 %collective-permute-start.32 = (bf16[2,32,256]{2,1,0:T(8,128)(2,1)S(1)}, bf16[2,32,256]{2,1,0:T(8,128)(2,1)S(1)}, u32[]{:S(2)}, u32[]{:S(2)}) collective-permute-start(bf16[2,32,256]{2,1,0:T(8,128)(2,1)S(1)} %get-tuple-element.81), channel_id=1, source_target_pairs={{0,1},{1,2},{2,3},{3,0},{4,5},{5,6},{6,7},{7,4},{8,9},{9,10},{10,1... | collective-permute-start | bytes 98312 | tf_op jit(solution)/shard_map/ppermute | solution.py:511
  (19 other events, 144.8 us)
where the time goes:
time: 145 us; the launch traced here: 142 us
  starting transfers between devices  64 us (44%)
  Pallas kernels  44.1 us (30%)
  waiting for transfers between devices  28 us (19%)
  local copies, waits for them, and re-layouts  5.41 us (4%)
    ppermute x34, starting transfers between devices, move(): return lax.ppermute(array, 'pre', pairs)  40 us
    pallas_call x2, Pallas kernels, on_device(): pl.pallas_call(functools.partial(attend, sizes), out_shape=[shape(own_row...  35.4 us
    ppermute x34, waiting for transfers between devices, move(): return lax.ppermute(array, 'pre', pairs)  26.3 us
    ppermute x6, starting transfers between devices, on_device(): lax.ppermute(cut[shift], 'rsp', [(g, (g + shift) % groups) for g in range...  24 us
    unnamed x22, local copies, waits for them, and re-layouts  5.41 us
    pallas_call x1, Pallas kernels, on_device(): pl.pallas_call(prepare_rows, out_shape=[shape(own_rows, 2 * GROUP_WIDTH),...  3.91 us
  transfers between devices with their start and end apart: 40, of which 13 were waited for; matrix products, arithmetic and copies ran while one was open for 0% of the time, Pallas kernels for 26%

commit v1 on v0

--- a/solution.py
+++ b/solution.py
@@ -27,6 +27,9 @@
 SMEM = pl.BlockSpec(memory_space=pltpu.SMEM)
 
 
+VMEM_MIB = 48
+
+
 def params(mib):
     return pltpu.CompilerParams(vmem_limit_bytes=mib * 1024 * 1024)
 
@@ -65,43 +68,56 @@
 
 
 def prepare_keys(place, pk, pv, rk, rv, *outs):
-    core = place[1]
     prompt = pk.shape[0]
     order = sorting(rk.shape[0])
     for local in range(LOCAL_HEADS):
-        for cross in range(CORES):
-            out = outs[local * CORES + cross]
-            span = lanes(head_of(core, cross, local), HEAD_WIDTH)
+        out = outs[local]
+        for target in range(CORES):
+            head = target * LOCAL_HEADS + local
+            span = slice(head * HEAD_WIDTH, (head + 1) * HEAD_WIDTH)
             for part, (p, r) in enumerate(((pk, rk), (pv, rv))):
                 to = slice(part * HEAD_WIDTH, (part + 1) * HEAD_WIDTH)
-                out[:prompt, to] = p[:, span]
-                out[prompt:, to] = dot(order, r[:, span]).astype(BF16)
-
-
-def prepare_rows(place, pq, po, pg, rq, ro, rg, *outs):
-    core = place[1]
+                reply = dot(order, r[:, span]).astype(BF16)
+                for device in range(target, out.shape[0], CORES):
+                    out[device, :prompt, to] = p[:, span]
+                    out[device, prompt:, to] = reply
+    outs[LOCAL_HEADS][...] = jnp.zeros_like(outs[LOCAL_HEADS])
+
+
+def prepare_rows(place, token, pq, po, pg, rq, ro, rg, own, other):
     reply = rq.shape[0]
     order = sorting(reply)
-    pick = (iota((8, GROUP_WIDTH), 1) // HEAD_WIDTH == iota((8, GROUP_WIDTH), 0)).astype(BF16)
+    column = iota((GROUP_WIDTH, HEAD_WIDTH), 1)
+    pick = (column // 3 == iota((GROUP_WIDTH, HEAD_WIDTH), 0) // HEAD_WIDTH).astype(BF16)
 
     def delta(gradient, output):
         product = gradient.astype(F32) * output.astype(F32)
         high = product.astype(BF16)
         low = (product - high.astype(F32)).astype(BF16)
-        return dot(pick, high, (1, 1)) + dot(pick, low, (1, 1))
-
-    for local in range(LOCAL_HEADS):
-        for cross in range(CORES):
-            rows_out, delta_out = outs[2 * (local * CORES + cross) :][:2]
-            span = lanes(head_of(core, cross, local), GROUP_WIDTH)
-            rows_out[reply:, :GROUP_WIDTH] = pq[:, span]
-            rows_out[reply:, GROUP_WIDTH:] = pg[:, span]
-            rows_out[:reply, :GROUP_WIDTH] = dot(order, rq[:, span]).astype(BF16)
-            gradient = dot(order, rg[:, span]).astype(BF16)
-            rows_out[:reply, GROUP_WIDTH:] = gradient
-            output = dot(order, ro[:, span]).astype(BF16)
-            delta_out[:, :reply] = delta(gradient, output)
-            delta_out[:, reply:] = delta(pg[:, span], po[:, span])
+        value = dot(high, pick) + dot(low, pick)
+        first = value.astype(BF16).astype(F32)
+        second = (value - first).astype(BF16).astype(F32)
+        part = iota(value.shape, 1) % 3
+        return jnp.where(part == 0, first, jnp.where(part == 1, second, value - first - second)).astype(BF16)
+
+    def write(out):
+        out[0, reply:, :GROUP_WIDTH] = pq[...]
+        out[0, reply:, GROUP_WIDTH : 2 * GROUP_WIDTH] = pg[...]
+        out[0, reply:, 2 * GROUP_WIDTH :] = delta(pg[...], po[...])
+        out[0, :reply, :GROUP_WIDTH] = dot(order, rq[...]).astype(BF16)
+        gradient = dot(order, rg[...]).astype(BF16)
+        out[0, :reply, GROUP_WIDTH : 2 * GROUP_WIDTH] = gradient
+        out[0, :reply, 2 * GROUP_WIDTH :] = delta(gradient, dot(order, ro[...]).astype(BF16))
+
+    mine = pl.program_id(0) >= LOCAL_HEADS
+
+    @pl.when(mine)
+    def _():
+        write(own)
+
+    @pl.when(jnp.logical_not(mine))
+    def _():
+        write(other)
 
 
 def attend(sizes, place, reply_len, reply_slot, *refs):
@@ -112,23 +128,26 @@
     block = positions
     per_chip = chip_prompt // block
     prompt_blocks = chips * per_chip
-    rows_in, refs = refs[:2], refs[2:]
-    delta_in, refs = refs[:2], refs[2:]
-    keys_in, refs = refs[: chips * CORES], refs[chips * CORES :]
-    query_out, refs = refs[:2], refs[2:]
-    keys_out, refs = refs[: chips * CORES], refs[chips * CORES :]
-    keys, keys_t, total, query, gradient, delta, scores, top, mass, prob, score_grad, query_grad = refs
+    rows_in, keys_in, query_out, keys_out, refs = refs[:2], refs[2], refs[3:5], refs[5], refs[6:]
+    keys, keys_t, total, query, gradient, deltas, delta, scores, top, mass, prob, score_grad, query_grad = refs
     chip, core, group = place[0], place[1], place[2]
+
+    def device(away, other):
+        return (chip ^ away) * CORES + (core ^ other)
+
+    pick = (iota((8, HEAD_WIDTH), 1) // 3 == iota((8, HEAD_WIDTH), 0)).astype(BF16)
+    for other in range(CORES):
+        deltas[other] = dot(pick, rows_in[other][:, 2 * GROUP_WIDTH :], (1, 1))
 
     for index in range(chips * CORES):
         away, other = index // CORES, index % CORES
-        source = keys_in[index]
+        source = device(away, other)
         at = away * chip_prompt + other * prompt_keys
-        keys[at : at + prompt_keys] = source[:prompt_keys]
+        keys[at : at + prompt_keys] = keys_in[source, :prompt_keys]
         for slot in range(RESP_DEV):
             at = prompt_blocks * block + (slot * chips + away) * positions + other * own_positions
             begin = prompt_keys + slot * own_positions
-            keys[at : at + own_positions] = source[begin : begin + own_positions]
+            keys[at : at + own_positions] = keys_in[source, begin : begin + own_positions]
     total[...] = jnp.zeros_like(total)
 
     def transpose_block(index, carry):
@@ -207,8 +226,8 @@
                     for which in range(RESP_DEV):
                         @pl.when(slot == which)
                         def _():
-                            delta[0:1, to] = delta_in[other][
-                                head : head + 1, which * own_positions : (which + 1) * own_positions
+                            delta[0:1, to] = deltas[
+                                other, head : head + 1, which * own_positions : (which + 1) * own_positions
                             ]
             begin(GROUP * positions)
             base = prompt_blocks + slot * chips
@@ -266,7 +285,7 @@
             right = slice(GROUP_WIDTH + head * HEAD_WIDTH, GROUP_WIDTH + (head + 1) * HEAD_WIDTH)
             query[to] = rows_in[other][reply_own:, left]
             gradient[to] = rows_in[other][reply_own:, right]
-            delta[0:1, to] = delta_in[other][head : head + 1, reply_own:]
+            delta[0:1, to] = deltas[other, head : head + 1, reply_own:]
     begin(all_rows)
     lane = iota((1, all_rows), 1)
     within = lane
@@ -307,11 +326,12 @@
 
     for index in range(chips * CORES):
         away, other = index // CORES, index % CORES
-        out = keys_out[index]
+        out = device(away, other)
 
         def put(to, at, count):
-            out[to : to + count, :HEAD_WIDTH] = (total[at : at + count, :HEAD_WIDTH] * SCALE).astype(BF16)
-            out[to : to + count, HEAD_WIDTH:] = total[at : at + count, HEAD_WIDTH:].astype(BF16)
+            key_sum = (total[at : at + count, :HEAD_WIDTH] * SCALE).astype(BF16)
+            keys_out[out, to : to + count, :HEAD_WIDTH] = key_sum
+            keys_out[out, to : to + count, HEAD_WIDTH:] = total[at : at + count, HEAD_WIDTH:].astype(BF16)
 
         put(0, away * chip_prompt + other * prompt_keys, prompt_keys)
         for slot in range(RESP_DEV):
@@ -319,26 +339,22 @@
             put(prompt_keys + slot * own_positions, at, own_positions)
 
 
-def spread_prompt(chips, prompt_keys, place, *refs):
-    parts, outs, summed = refs[: chips * CORES], refs[chips * CORES : -1], refs[-1]
-    groups = len(outs)
-    rows = prompt_keys // groups
+def spread_prompt(place, parts, outs, summed):
+    groups, rows = outs.shape[0], outs.shape[2]
+    prompt_keys = groups * rows
     for other in range(CORES):
-        value = parts[other][:prompt_keys].astype(F32)
-        for away in range(1, chips):
-            value = value + parts[away * CORES + other][:prompt_keys].astype(F32)
-        summed[other] = value
-    for shift in range(groups):
-        target = lax.rem(place[2] + shift, groups)
-        at = pl.ds(pl.multiple_of(target * rows, rows), rows)
-        for other in range(CORES):
-            outs[shift][other] = summed[other, at].astype(BF16)
-
-
-def finish(chips, groups, prompt_keys, prompt_own, place, *refs):
-    count = chips * CORES
-    parts, refs = refs[: LOCAL_HEADS * count], refs[LOCAL_HEADS * count :]
-    slices, refs = refs[: LOCAL_HEADS * groups], refs[LOCAL_HEADS * groups :]
+        source = place[1] ^ other
+        value = parts[source, :prompt_keys].astype(F32)
+        for chip in range(1, parts.shape[0] // CORES):
+            value = value + parts[chip * CORES + source, :prompt_keys].astype(F32)
+        summed[...] = value
+        for target in range(groups):
+            outs[target, other] = summed[target * rows : (target + 1) * rows].astype(BF16)
+
+
+def finish(prompt_keys, place, *refs):
+    parts, refs = refs[:LOCAL_HEADS], refs[LOCAL_HEADS:]
+    slices, refs = refs[:LOCAL_HEADS], refs[LOCAL_HEADS:]
     queries, refs = refs[: LOCAL_HEADS * CORES], refs[LOCAL_HEADS * CORES :]
     prompt_dq, prompt_dk, prompt_dv, reply_dq, reply_dk, reply_dv = refs
     core = place[1]
@@ -348,21 +364,22 @@
         for other in range(CORES):
             head = head_of(core, other, local)
             span = lanes(head, HEAD_WIDTH)
-            value = slices[local * groups][other].astype(F32)
-            for shift in range(1, groups):
-                value = value + slices[local * groups + shift][other].astype(F32)
+            value = slices[local][0, other].astype(F32)
+            for group in range(1, slices[local].shape[0]):
+                value = value + slices[local][group, other].astype(F32)
             prompt_dk[:, span] = value[:, :HEAD_WIDTH].astype(BF16)
             prompt_dv[:, span] = value[:, HEAD_WIDTH:].astype(BF16)
-            value = parts[local * count + other][prompt_keys:].astype(F32)
-            for away in range(1, chips):
-                value = value + parts[local * count + away * CORES + other][prompt_keys:].astype(F32)
+            source = core ^ other
+            value = parts[local][source, prompt_keys:].astype(F32)
+            for chip in range(1, parts[local].shape[0] // CORES):
+                value = value + parts[local][chip * CORES + source, prompt_keys:].astype(F32)
             value = dot(order, value.astype(BF16)).astype(BF16)
             reply_dk[:, span] = value[:, :HEAD_WIDTH]
             reply_dv[:, span] = value[:, HEAD_WIDTH:]
             span = lanes(head, GROUP_WIDTH)
-            source = queries[local * CORES + other]
-            reply_dq[:, span] = dot(order, source[:reply]).astype(BF16)
-            prompt_dq[:, span] = source[reply:]
+            query = queries[local * CORES + other]
+            reply_dq[:, span] = dot(order, query[:reply]).astype(BF16)
+            prompt_dq[:, span] = query[reply:]
 
 
 def on_device(
@@ -396,35 +413,22 @@
     def shape(*dims, dtype=BF16):
         return jax.ShapeDtypeStruct(dims, dtype)
 
-    def move(array, away, cross):
-        pairs = [
-            (p, (p // CORES ^ away) * CORES + (p % CORES ^ cross)) for p in range(devices)
-        ]
-        return lax.ppermute(array, "pre", pairs)
-
-    def exchange(same, cross):
-        return [
-            (same, cross)[other](away) if (away, other) == (0, 0)
-            else move((same, cross)[other](away), away, other)
-            for away in range(chips)
-            for other in range(CORES)
-        ]
+    def swap(array):
+        return lax.ppermute(array, "pre", [(p, p ^ 1) for p in range(devices)])
+
+    def trade(array, axis):
+        return lax.all_to_all(array, axis, 0, 0, tiled=True)
 
     key_rows = prompt_keys + reply_own
-    key_blocks = pl.pallas_call(
+    *key_blocks, token = pl.pallas_call(
         prepare_keys,
-        out_shape=[shape(key_rows, 2 * HEAD_WIDTH)] * KEY_VALUE_HEADS,
+        out_shape=[shape(devices, key_rows, 2 * HEAD_WIDTH)] * LOCAL_HEADS + [shape(8, 128, dtype=F32)],
         in_specs=[SMEM] + [VMEM] * 4,
-        out_specs=[VMEM] * KEY_VALUE_HEADS,
-        compiler_params=params(32),
+        out_specs=[VMEM] * (LOCAL_HEADS + 1),
+        compiler_params=params(VMEM_MIB),
         name="prepare_keys",
     )(place, prompt_k, prompt_value, reply_key[0], reply_value[0])
-    gathered = [
-        exchange(
-            lambda away: key_blocks[local * CORES], lambda away: key_blocks[local * CORES + 1]
-        )
-        for local in range(LOCAL_HEADS)
-    ]
+    gathered = [trade(block, "pre") for block in key_blocks]
     if prompt_own > prompt_rows:
         room = ((0, prompt_own - prompt_rows), (0, 0))
         prompt_query, prompt_output, prompt_output_gradient = (
@@ -432,15 +436,38 @@
             for array in (prompt_query, prompt_output, prompt_output_gradient)
         )
     own_rows = reply_own + prompt_own
-    row_blocks = pl.pallas_call(
+    row_width = 2 * GROUP_WIDTH + HEAD_WIDTH
+
+    def row_head(step, place):
+        core = place[1]
+        owner = jnp.where(step < LOCAL_HEADS, 1 - core, core)
+        return 0, owner * LOCAL_HEADS + step % LOCAL_HEADS
+
+    mine, theirs = pl.pallas_call(
         prepare_rows,
-        out_shape=[shape(own_rows, 2 * GROUP_WIDTH), shape(8, own_rows, dtype=F32)] * KEY_VALUE_HEADS,
-        in_specs=[SMEM] + [VMEM] * 6,
-        out_specs=[VMEM] * (2 * KEY_VALUE_HEADS),
-        compiler_params=params(48),
+        out_shape=[shape(LOCAL_HEADS, own_rows, row_width)] * CORES,
+        grid_spec=pltpu.PrefetchScalarGridSpec(
+            num_scalar_prefetch=1,
+            grid=(KEY_VALUE_HEADS,),
+            in_specs=[pl.BlockSpec(memory_space=pl.ANY)]
+            + [pl.BlockSpec((prompt_own, GROUP_WIDTH), row_head)] * 3
+            + [pl.BlockSpec((reply_own, GROUP_WIDTH), row_head)] * 3,
+            out_specs=[
+                pl.BlockSpec(
+                    (1, own_rows, row_width),
+                    lambda step, place: (jnp.maximum(step - LOCAL_HEADS, 0), 0, 0),
+                ),
+                pl.BlockSpec(
+                    (1, own_rows, row_width),
+                    lambda step, place: (jnp.minimum(step, LOCAL_HEADS - 1), 0, 0),
+                ),
+            ],
+        ),
+        compiler_params=params(VMEM_MIB),
         name="prepare_rows",
     )(
         place,
+        token,
         prompt_query,
         prompt_output,
         prompt_output_gradient,
@@ -448,6 +475,7 @@
         reply_output[0],
         reply_output_gradient[0],
     )
+    theirs = swap(theirs)
 
     blocks = chips * (chip_prompt // positions) + RESP_DEV * chips
     slots = chips * (chip_prompt // positions) + chips
@@ -456,19 +484,21 @@
     score_count = GROUP * (positions * RESP_DEV * slots * positions)
     parts, queries, slices = [], [], []
     for local in range(LOCAL_HEADS):
-        mine, mine_delta, theirs, theirs_delta = row_blocks[4 * local : 4 * local + 4]
-        results = pl.pallas_call(
+        rows_spec = pl.BlockSpec((pl.squeezed, own_rows, row_width), lambda step, local=local: (local, 0, 0))
+        query_mine, query_theirs, sums = pl.pallas_call(
             functools.partial(attend, sizes),
             out_shape=[shape(own_rows, GROUP_WIDTH)] * CORES
-            + [shape(key_rows, 2 * HEAD_WIDTH)] * devices,
-            in_specs=[SMEM] * 3 + [VMEM] * (4 + devices),
-            out_specs=[VMEM] * (CORES + devices),
+            + [shape(devices, key_rows, 2 * HEAD_WIDTH)],
+            grid=(1,),
+            in_specs=[SMEM] * 3 + [rows_spec] * 2 + [VMEM],
+            out_specs=[VMEM] * 3,
             scratch_shapes=[
                 pltpu.VMEM((blocks * positions, 2 * HEAD_WIDTH), BF16),
                 pltpu.VMEM((blocks, HEAD_WIDTH, positions), BF16),
                 pltpu.VMEM((blocks * positions, 2 * HEAD_WIDTH), F32),
                 pltpu.VMEM((all_rows, HEAD_WIDTH), BF16),
                 pltpu.VMEM((all_rows, HEAD_WIDTH), BF16),
+                pltpu.VMEM((CORES, 8, own_rows), F32),
                 pltpu.VMEM((8, all_rows), F32),
                 pltpu.VMEM((slots, positions, all_rows), F32),
                 pltpu.VMEM((8, all_rows), F32),
@@ -477,46 +507,33 @@
                 pltpu.VMEM((positions, all_rows), BF16),
                 pltpu.VMEM((HEAD_WIDTH, all_rows), F32),
             ],
-            compiler_params=params(48),
+            compiler_params=params(VMEM_MIB),
             cost_estimate=pl.CostEstimate(
                 flops=score_count * 10 * HEAD_WIDTH,
                 bytes_accessed=8 * 1024 * 1024,
                 transcendentals=2 * score_count,
             ),
             name="attend",
-        )(
-            place,
-            reply_len,
-            reply_slot,
-            mine,
-            move(theirs, 0, 1),
-            mine_delta,
-            move(theirs_delta, 0, 1),
-            *gathered[local],
-        )
-        queries += [results[0], move(results[1], 0, 1)]
-        sums = results[CORES:]
-        arrived = exchange(lambda away: sums[away * CORES], lambda away: sums[away * CORES + 1])
-        parts += arrived
+        )(place, reply_len, reply_slot, mine, theirs, gathered[local])
+        queries += [query_mine, swap(query_theirs)]
+        parts.append(trade(sums, "pre"))
+        cut_shape = (groups, CORES, prompt_keys // groups, 2 * HEAD_WIDTH)
         cut = pl.pallas_call(
-            functools.partial(spread_prompt, chips, prompt_keys),
-            out_shape=[shape(CORES, prompt_keys // groups, 2 * HEAD_WIDTH)] * groups,
-            in_specs=[SMEM] + [VMEM] * devices,
-            out_specs=[VMEM] * groups,
-            scratch_shapes=[pltpu.VMEM((CORES, prompt_keys, 2 * HEAD_WIDTH), F32)],
-            compiler_params=params(32),
+            spread_prompt,
+            out_shape=shape(*cut_shape),
+            in_specs=[SMEM, VMEM],
+            out_specs=VMEM,
+            scratch_shapes=[pltpu.VMEM((prompt_keys, 2 * HEAD_WIDTH), F32)],
+            compiler_params=params(VMEM_MIB),
             name="spread_prompt",
-        )(place, *arrived)
-        slices += [cut[0]] + [
-            lax.ppermute(cut[shift], "rsp", [(g, (g + shift) % groups) for g in range(groups)])
-            for shift in range(1, groups)
-        ]
+        )(place, parts[-1])
+        slices.append(trade(cut, "rsp"))
 
     key_width = KEY_VALUE_HEADS * HEAD_WIDTH
     query_width = QUERY_HEADS * HEAD_WIDTH
     cut_rows = prompt_keys // groups
     prompt_dq, prompt_dk, prompt_dv, reply_dq, reply_dk, reply_dv = pl.pallas_call(
-        functools.partial(finish, chips, groups, prompt_keys, prompt_own),
+        functools.partial(finish, prompt_keys),
         out_shape=[
             shape(prompt_own, query_width),
             shape(cut_rows, key_width),
@@ -525,9 +542,9 @@
             shape(reply_own, key_width),
             shape(reply_own, key_width),
         ],
-        in_specs=[SMEM] + [VMEM] * (LOCAL_HEADS * (devices + groups + CORES)),
+        in_specs=[SMEM] + [VMEM] * (LOCAL_HEADS * (2 + CORES)),
         out_specs=[VMEM] * 6,
-        compiler_params=params(48),
+        compiler_params=params(VMEM_MIB),
         name="finish",
     )(place, *parts, *slices, *queries)
     return (

time: 145 us -> 147 us (1.014)
  starting transfers between devices: 64 us -> 35.9 us
  waiting for transfers between devices: 28 us -> 40.7 us
  local copies, waits for them, and re-layouts: 5.41 us -> 17.7 us
  Pallas kernels: 44.1 us -> 49.6 us
    ppermute x40 -> x3, starting transfers between devices: 64 us -> 1.01 us  [swap(): return lax.ppermute(array, 'pre', [(p, p ^ 1) for p in range(devices)])]
    all_to_all x0 -> x6, waiting for transfers between devices: none -> 40.7 us  [trade(): return lax.all_to_all(array, axis, 0, 0, tiled=True)]
    all_to_all x0 -> x6, starting transfers between devices: none -> 34.8 us  [trade(): return lax.all_to_all(array, axis, 0, 0, tiled=True)]
    ppermute x40 -> x3, waiting for transfers between devices: 28 us -> 0.01 us  [swap(): return lax.ppermute(array, 'pre', [(p, p ^ 1) for p in range(devices)])]
    unnamed x22 -> x46, local copies, waits for them, and re-layouts: 5.41 us -> 17.7 us
    pallas_call x5, Pallas kernels: 8.74 us -> 14.2 us  [the longest x1 5.8 us: on_device(): pl.pallas_call(prepare_rows, out_shape=[shape(LOCAL_HEADS, own_rows, row_...]
  transfers between devices with their start and end apart: 40 -> 9, of which waited for: 13 -> 4; matrix products, arithmetic and copies ran while one was open for 0% -> 0% of each run, Pallas kernels for 26% -> 30%
where the time goes in v1:
time: 147 us; the launch traced here: 145 us
  Pallas kernels  49.6 us (34%)
  waiting for transfers between devices  40.7 us (28%)
  starting transfers between devices  35.9 us (24%)
  local copies, waits for them, and re-layouts  17.7 us (12%)
    all_to_all x6, waiting for transfers between devices, trade(): return lax.all_to_all(array, axis, 0, 0, tiled=True)  40.7 us
    pallas_call x2, Pallas kernels, on_device(): pl.pallas_call(functools.partial(attend, sizes), out_shape=[shape(own_row...  35.4 us
    all_to_all x6, starting transfers between devices, trade(): return lax.all_to_all(array, axis, 0, 0, tiled=True)  34.8 us
    unnamed x46, local copies, waits for them, and re-layouts  17.7 us
    pallas_call x1, Pallas kernels, on_device(): pl.pallas_call(prepare_rows, out_shape=[shape(LOCAL_HEADS, own_rows, row_...  5.8 us
    pallas_call x1, Pallas kernels, on_device(): pl.pallas_call(functools.partial(finish, prompt_keys), out_shape=[shape(p...  3.14 us
  transfers between devices with their start and end apart: 9, of which 4 were waited for; matrix products, arithmetic and copies ran while one was open for 0% of the time, Pallas kernels for 30%

profile of v1, /device:TPU:0, one launch (start us, length us, event | category | flops | bytes accessed | tf_op | source)
XLA Modules:
  0.0 144.7 jit_solution(8979765901616895380)
XLA Ops:
  0.7 0.9 copy-done.9
  1.7 0.9 copy-done.10
  2.6 0.9 copy-done.14
  3.5 0.9 copy-done.15
  4.4 2.7 %prepare_keys.1 = (bf16[8,384,256]{2,1,0:T(8,128)(2,1)}, bf16[8,384,256]{2,1,0:T(8,128)(2,1)}, f32[8,128]{1,0:T(8,128)S(1)}) custom-call(s32[3]{0:T(128)S(1)} %pad_add_fusion.place, bf16[128,512]{1,0:T(8,128)(2,1)S(1)} %copy-done.14, bf16[128,512]{1,0:T(8,128)(2,1)S(1)} %copy-done.15, bf16[256,512]{1,0:T(8,128)(2,1)S(1)} %bitcast.14, ...), custom_call_target="tpu_custom_call" | custom-call | tf_op jit(solution)/shard_map/prepare_keys/pallas_call | solution.py:423
  7.2 5.3 %all-to-all-start = ((bf16[8,384,256]{2,1,0:T(8,128)(2,1)}), bf16[8,384,256]{2,1,0:T(8,128)(2,1)S(1)}, u32[]{:S(2)}, u32[]{:S(2)}) async-start(bf16[8,384,256]{2,1,0:T(8,128)(2,1)} %get-tuple-element.26), calls=%async_computation | async-start | bytes 3145728 | tf_op jit(solution)/shard_map/all_to_all | solution.py:420
  12.5 1.3 copy-done.3
  13.8 1.3 copy-done.4
  15.1 5.8 %prepare_rows.1 = (bf16[2,288,1408]{2,1,0:T(8,128)(2,1)S(1)}, bf16[2,288,1408]{2,1,0:T(8,128)(2,1)}) custom-call(s32[3]{0:T(128)S(1)} %pad_add_fusion.place, f32[8,128]{1,0:T(8,128)S(1)} %get-tuple-element.23.token, bf16[32,2560]{1,0:T(8,128)(2,1)S(1)} %copy-done.11, bf16[32,2560]{1,0:T(8,128)(2,1)S(1)} %copy-done.12, bf16[32,2560]{1,0:T(8,128)(2,1)S(1)} %copy-done.13, ...), custom_call_target="tpu_custom_call" | custom-call | tf_op jit(solution)/shard_map/prepare_rows/pallas_call | solution.py:446
  20.9 1.2 copy-done.16
  22.6 10.9 %all-to-all-done.refs_2_ = bf16[8,384,256]{2,1,0:T(8,128)(2,1)S(1)} async-done(((bf16[8,384,256]{2,1,0:T(8,128)(2,1)}), bf16[8,384,256]{2,1,0:T(8,128)(2,1)S(1)}, u32[]{:S(2)}, u32[]{:S(2)}) %all-to-all-start) | async-done | bytes 1572896 | tf_op jit(solution)/shard_map/all_to_all | solution.py:420
  33.5 3.7 %all-to-all-start.2 = ((bf16[8,384,256]{2,1,0:T(8,128)(2,1)}), bf16[8,384,256]{2,1,0:T(8,128)(2,1)S(1)}, u32[]{:S(2)}, u32[]{:S(2)}) async-start(bf16[8,384,256]{2,1,0:T(8,128)(2,1)} %get-tuple-element.28), calls=%async_computation.2 | async-start | bytes 3145728 | tf_op jit(solution)/shard_map/all_to_all | solution.py:420
  37.3 1.4 copy-done.17
  38.7 17.7 %attend.2 = (bf16[288,640]{1,0:T(8,128)(2,1)S(1)}, bf16[288,640]{1,0:T(8,128)(2,1)S(1)}, bf16[8,384,256]{2,1,0:T(8,128)(2,1)S(1)}) custom-call(s32[3]{0:T(128)S(1)} %pad_add_fusion.place, s32[8]{0:T(128)S(1)} %copy-done.21, s32[8]{0:T(128)S(1)} %copy-done.22, bf16[2,288,1408]{2,1,0:T(8,128)(2,1)S(1)} %copy-done.17, ...), custom_call_target="tpu_custom_call" | custom-call | flops 6710886400 | bytes 8388608 | tf_op jit(solution)/shard_map/attend/pallas_call | solution.py:488
  56.4 1.1 copy-done
  59.0 6.4 %all-to-all-start.1 = ((bf16[8,384,256]{2,1,0:T(8,128)(2,1)}), bf16[8,384,256]{2,1,0:T(8,128)(2,1)S(1)}, u32[]{:S(2)}, u32[]{:S(2)}) async-start(bf16[8,384,256]{2,1,0:T(8,128)(2,1)} %copy-done), calls=%async_computation.1 | async-start | bytes 3145728 | tf_op jit(solution)/shard_map/all_to_all | solution.py:420
  65.5 1.4 copy-done.18
  66.9 17.7 %attend.3 = (bf16[288,640]{1,0:T(8,128)(2,1)S(1)}, bf16[288,640]{1,0:T(8,128)(2,1)S(1)}, bf16[8,384,256]{2,1,0:T(8,128)(2,1)S(1)}) custom-call(s32[3]{0:T(128)S(1)} %pad_add_fusion.place, s32[8]{0:T(128)S(1)} %copy-done.21, s32[8]{0:T(128)S(1)} %copy-done.22, bf16[2,288,1408]{2,1,0:T(8,128)(2,1)S(1)} %copy-done.18, ...), custom_call_target="tpu_custom_call" | custom-call | flops 6710886400 | bytes 8388608 | tf_op jit(solution)/shard_map/attend/pallas_call | solution.py:488
  84.6 1.2 copy-done.1
  85.8 0.8 copy-done.7
  86.5 0.8 copy-done.20
  87.3 6.8 %all-to-all-start.3 = ((bf16[8,384,256]{2,1,0:T(8,128)(2,1)}), bf16[8,384,256]{2,1,0:T(8,128)(2,1)S(1)}, u32[]{:S(2)}, u32[]{:S(2)}) async-start(bf16[8,384,256]{2,1,0:T(8,128)(2,1)} %copy-done.1), calls=%async_computation.3 | async-start | bytes 3145728 | tf_op jit(solution)/shard_map/all_to_all | solution.py:420
  94.1 1.3 spread_prompt.2
  95.3 19.8 %all-to-all-done.3.parts.refs_1_ = bf16[8,384,256]{2,1,0:T(8,128)(2,1)S(1)} async-done(((bf16[8,384,256]{2,1,0:T(8,128)(2,1)}), bf16[8,384,256]{2,1,0:T(8,128)(2,1)S(1)}, u32[]{:S(2)}, u32[]{:S(2)}) %all-to-all-start.3) | async-done | bytes 1572896 | tf_op jit(solution)/shard_map/all_to_all | solution.py:420
  115.1 9.3 %all-to-all-start.4 = ((bf16[4,2,32,256]{3,2,1,0:T(8,128)(2,1)}), bf16[4,2,32,256]{3,2,1,0:T(8,128)(2,1)S(1)}, u32[]{:S(2)}, u32[]{:S(2)}) async-start(bf16[4,2,32,256]{3,2,1,0:T(8,128)(2,1)} %spread_prompt.2), calls=%async_computation.4 | async-start | bytes 262144 | tf_op jit(solution)/shard_map/all_to_all | solution.py:420
  124.9 1.3 spread_prompt.3
  126.2 4.1 %all-to-all-done.4.refs_2_ = bf16[4,2,32,256]{3,2,1,0:T(8,128)(2,1)S(1)} async-done(((bf16[4,2,32,256]{3,2,1,0:T(8,128)(2,1)}), bf16[4,2,32,256]{3,2,1,0:T(8,128)(2,1)S(1)}, u32[]{:S(2)}, u32[]{:S(2)}) %all-to-all-start.4) | async-done | bytes 131104 | tf_op jit(solution)/shard_map/all_to_all | solution.py:420
  130.3 3.3 %all-to-all-start.5 = ((bf16[4,2,32,256]{3,2,1,0:T(8,128)(2,1)}), bf16[4,2,32,256]{3,2,1,0:T(8,128)(2,1)S(1)}, u32[]{:S(2)}, u32[]{:S(2)}) async-start(bf16[4,2,32,256]{3,2,1,0:T(8,128)(2,1)} %spread_prompt.3), calls=%async_computation.5 | async-start | bytes 262144 | tf_op jit(solution)/shard_map/all_to_all | solution.py:420
  133.7 5.9 %all-to-all-done.5.refs_3_ = bf16[4,2,32,256]{3,2,1,0:T(8,128)(2,1)S(1)} async-done(((bf16[4,2,32,256]{3,2,1,0:T(8,128)(2,1)}), bf16[4,2,32,256]{3,2,1,0:T(8,128)(2,1)S(1)}, u32[]{:S(2)}, u32[]{:S(2)}) %all-to-all-start.5) | async-done | bytes 131104 | tf_op jit(solution)/shard_map/all_to_all | solution.py:420
  139.5 1.0 copy-done.6
  140.5 1.0 copy-done.8
  141.5 3.1 %finish.1 = (bf16[32,2560]{1,0:T(8,128)(2,1)}, bf16[32,512]{1,0:T(8,128)(2,1)}, bf16[32,512]{1,0:T(8,128)(2,1)}, bf16[256,2560]{1,0:T(8,128)(2,1)}, bf16[256,512]{1,0:T(8,128)(2,1)}, /*index=5*/bf16[256,512]{1,0:T(8,128)(2,1)}) custom-call(s32[3]{0:T(128)S(1)} %pad_add_fusion.place, bf16[8,384,256]{2,1,0:T(8,128)(2,1)S(1)} %all-to-all-done.1.parts.refs_0_, ...), custom_call_target="tpu_custom_call" | custom-call | tf_op jit(solution)/shard_map/finish/pallas_call | solution.py:535
  (40 shorter events, 2.6 us)
Async XLA Ops:
  0.7 1.0 copy-start.9
  1.7 0.9 copy-start.10
  2.6 0.9 copy-start.14
  3.5 0.9 copy-start.15
  7.1 5.3 %copy-start.2 = (bf16[1,256,2560]{2,1,0:T(8,128)(2,1)S(1)}, bf16[1,256,2560]{2,1,0:T(8,128)(2,1)}, u32[]{:S(2)}) copy-start(bf16[1,256,2560]{2,1,0:T(8,128)(2,1)} %param.17) | copy-start | bytes 3932164
  7.1 5.3 %copy-start.11 = (bf16[32,2560]{1,0:T(8,128)(2,1)S(1)}, bf16[32,2560]{1,0:T(8,128)(2,1)}, u32[]{:S(2)}) copy-start(bf16[32,2560]{1,0:T(8,128)(2,1)} %pq.1) | copy-start | bytes 491524
  7.2 5.3 %copy-start.12 = (bf16[32,2560]{1,0:T(8,128)(2,1)S(1)}, bf16[32,2560]{1,0:T(8,128)(2,1)}, u32[]{:S(2)}) copy-start(bf16[32,2560]{1,0:T(8,128)(2,1)} %po.1) | copy-start | bytes 491524
  7.2 5.3 %copy-start.13 = (bf16[32,2560]{1,0:T(8,128)(2,1)S(1)}, bf16[32,2560]{1,0:T(8,128)(2,1)}, u32[]{:S(2)}) copy-start(bf16[32,2560]{1,0:T(8,128)(2,1)} %pg.1) | copy-start | bytes 491524
  7.2 26.3 %all-to-all-start = ((bf16[8,384,256]{2,1,0:T(8,128)(2,1)}), bf16[8,384,256]{2,1,0:T(8,128)(2,1)S(1)}, u32[]{:S(2)}, u32[]{:S(2)}) async-start(bf16[8,384,256]{2,1,0:T(8,128)(2,1)} %get-tuple-element.26), calls=%async_computation | async-start | bytes 3145728 | tf_op jit(solution)/shard_map/all_to_all | solution.py:420
  12.5 1.3 copy-start.3
  13.8 1.3 copy-start.4
  20.9 1.2 copy-start.16
  22.1 15.1 %collective-permute-start = (bf16[2,288,1408]{2,1,0:T(8,128)(2,1)}, bf16[2,288,1408]{2,1,0:T(8,128)(2,1)}, u32[]{:S(2)}, u32[]{:S(2)}) collective-permute-start(bf16[2,288,1408]{2,1,0:T(8,128)(2,1)} %get-tuple-element.25), channel_id=1, source_target_pairs={{0,4},{4,0},{8,12},{12,8},{16,20},{20,16},{24,28},{28,24},{1,5},{5... | collective-permute-start | bytes 4866056 | tf_op jit(solution)/shard_map/ppermute | solution.py:417
  33.5 3.7 %copy-start.21 = (s32[8]{0:T(128)S(1)}, s32[8]{0:T(128)}, u32[]{:S(2)}) copy-start(s32[8]{0:T(128)} %reply_len.3) | copy-start | bytes 100
  33.5 3.7 %copy-start.22 = (s32[8]{0:T(128)S(1)}, s32[8]{0:T(128)}, u32[]{:S(2)}) copy-start(s32[8]{0:T(128)} %reply_slot.3) | copy-start | bytes 100
  33.5 25.5 %all-to-all-start.2 = ((bf16[8,384,256]{2,1,0:T(8,128)(2,1)}), bf16[8,384,256]{2,1,0:T(8,128)(2,1)S(1)}, u32[]{:S(2)}, u32[]{:S(2)}) async-start(bf16[8,384,256]{2,1,0:T(8,128)(2,1)} %get-tuple-element.28), calls=%async_computation.2 | async-start | bytes 3145728 | tf_op jit(solution)/shard_map/all_to_all | solution.py:420
  37.3 1.4 copy-start.17
  56.4 1.2 copy-start
  57.6 0.7 copy-start.5
  58.3 0.7 copy-start.19
  59.0 28.2 %all-to-all-start.1 = ((bf16[8,384,256]{2,1,0:T(8,128)(2,1)}), bf16[8,384,256]{2,1,0:T(8,128)(2,1)S(1)}, u32[]{:S(2)}, u32[]{:S(2)}) async-start(bf16[8,384,256]{2,1,0:T(8,128)(2,1)} %copy-done), calls=%async_computation.1 | async-start | bytes 3145728 | tf_op jit(solution)/shard_map/all_to_all | solution.py:420
  65.5 1.4 copy-start.18
  84.6 1.2 copy-start.1
  85.8 0.8 copy-start.7
  86.5 0.8 copy-start.20
  87.3 27.8 %all-to-all-start.3 = ((bf16[8,384,256]{2,1,0:T(8,128)(2,1)}), bf16[8,384,256]{2,1,0:T(8,128)(2,1)S(1)}, u32[]{:S(2)}, u32[]{:S(2)}) async-start(bf16[8,384,256]{2,1,0:T(8,128)(2,1)} %copy-done.1), calls=%async_computation.3 | async-start | bytes 3145728 | tf_op jit(solution)/shard_map/all_to_all | solution.py:420
  115.1 15.2 %all-to-all-start.4 = ((bf16[4,2,32,256]{3,2,1,0:T(8,128)(2,1)}), bf16[4,2,32,256]{3,2,1,0:T(8,128)(2,1)S(1)}, u32[]{:S(2)}, u32[]{:S(2)}) async-start(bf16[4,2,32,256]{3,2,1,0:T(8,128)(2,1)} %spread_prompt.2), calls=%async_computation.4 | async-start | bytes 262144 | tf_op jit(solution)/shard_map/all_to_all | solution.py:420
  124.4 9.3 %collective-permute-start.2 = (bf16[288,640]{1,0:T(8,128)(2,1)}, bf16[288,640]{1,0:T(8,128)(2,1)}, u32[]{:S(2)}, u32[]{:S(2)}) collective-permute-start(bf16[288,640]{1,0:T(8,128)(2,1)} %copy-done.20), channel_id=1, source_target_pairs={{0,4},{4,0},{8,12},{12,8},{16,20},{20,16},{24,28},{28,24},{1,5},{5... | collective-permute-start | bytes 1105928 | tf_op jit(solution)/shard_map/ppermute | solution.py:417
  124.4 9.3 %collective-permute-start.1 = (bf16[288,640]{1,0:T(8,128)(2,1)}, bf16[288,640]{1,0:T(8,128)(2,1)}, u32[]{:S(2)}, u32[]{:S(2)}) collective-permute-start(bf16[288,640]{1,0:T(8,128)(2,1)} %copy-done.19), channel_id=1, source_target_pairs={{0,4},{4,0},{8,12},{12,8},{16,20},{20,16},{24,28},{28,24},{1,5},{5... | collective-permute-start | bytes 1105928 | tf_op jit(solution)/shard_map/ppermute | solution.py:417
  130.3 9.2 %all-to-all-start.5 = ((bf16[4,2,32,256]{3,2,1,0:T(8,128)(2,1)}), bf16[4,2,32,256]{3,2,1,0:T(8,128)(2,1)S(1)}, u32[]{:S(2)}, u32[]{:S(2)}) async-start(bf16[4,2,32,256]{3,2,1,0:T(8,128)(2,1)} %spread_prompt.3), calls=%async_computation.5 | async-start | bytes 262144 | tf_op jit(solution)/shard_map/all_to_all | solution.py:420
  139.5 1.0 copy-start.6
  140.5 1.0 copy-start.8

commit v2 on v1

--- a/solution.py
+++ b/solution.py
@@ -27,7 +27,8 @@
 SMEM = pl.BlockSpec(memory_space=pltpu.SMEM)
 
 
-VMEM_MIB = 48
+VMEM_MIB = 40
+SMALL_MIB = 24
 
 
 def params(mib):
@@ -67,24 +68,22 @@
     return owner * LOCAL_HEADS + local
 
 
-def prepare_keys(place, pk, pv, rk, rv, *outs):
+def prepare_keys(place, pk, pv, rk, rv, mine0, theirs0, mine1, theirs, token):
+    core = place[1]
     prompt = pk.shape[0]
     order = sorting(rk.shape[0])
-    for local in range(LOCAL_HEADS):
-        out = outs[local]
-        for target in range(CORES):
-            head = target * LOCAL_HEADS + local
-            span = slice(head * HEAD_WIDTH, (head + 1) * HEAD_WIDTH)
+    for local, outs in enumerate(((mine0, theirs.at[0]), (mine1, theirs.at[1]))):
+        for cross, out in enumerate(outs):
+            span = lanes(head_of(core, cross, local), HEAD_WIDTH)
             for part, (p, r) in enumerate(((pk, rk), (pv, rv))):
                 to = slice(part * HEAD_WIDTH, (part + 1) * HEAD_WIDTH)
-                reply = dot(order, r[:, span]).astype(BF16)
-                for device in range(target, out.shape[0], CORES):
-                    out[device, :prompt, to] = p[:, span]
-                    out[device, prompt:, to] = reply
-    outs[LOCAL_HEADS][...] = jnp.zeros_like(outs[LOCAL_HEADS])
-
-
-def prepare_rows(place, token, pq, po, pg, rq, ro, rg, own, other):
+                out[:prompt, to] = p[:, span]
+                out[prompt:, to] = dot(order, r[:, span]).astype(BF16)
+    theirs0[...] = theirs[0]
+    token[...] = jnp.zeros_like(token)
+
+
+def prepare_rows(place, token, pq, po, pg, rq, ro, rg, *outs):
     reply = rq.shape[0]
     order = sorting(reply)
     column = iota((GROUP_WIDTH, HEAD_WIDTH), 1)
@@ -101,26 +100,22 @@
         return jnp.where(part == 0, first, jnp.where(part == 1, second, value - first - second)).astype(BF16)
 
     def write(out):
-        out[0, reply:, :GROUP_WIDTH] = pq[...]
-        out[0, reply:, GROUP_WIDTH : 2 * GROUP_WIDTH] = pg[...]
-        out[0, reply:, 2 * GROUP_WIDTH :] = delta(pg[...], po[...])
-        out[0, :reply, :GROUP_WIDTH] = dot(order, rq[...]).astype(BF16)
+        out[reply:, :GROUP_WIDTH] = pq[...]
+        out[reply:, GROUP_WIDTH : 2 * GROUP_WIDTH] = pg[...]
+        out[reply:, 2 * GROUP_WIDTH :] = delta(pg[...], po[...])
+        out[:reply, :GROUP_WIDTH] = dot(order, rq[...]).astype(BF16)
         gradient = dot(order, rg[...]).astype(BF16)
-        out[0, :reply, GROUP_WIDTH : 2 * GROUP_WIDTH] = gradient
-        out[0, :reply, 2 * GROUP_WIDTH :] = delta(gradient, dot(order, ro[...]).astype(BF16))
-
-    mine = pl.program_id(0) >= LOCAL_HEADS
-
-    @pl.when(mine)
-    def _():
-        write(own)
-
-    @pl.when(jnp.logical_not(mine))
-    def _():
-        write(other)
-
-
-def attend(sizes, place, reply_len, reply_slot, *refs):
+        out[:reply, GROUP_WIDTH : 2 * GROUP_WIDTH] = gradient
+        out[:reply, 2 * GROUP_WIDTH :] = delta(gradient, dot(order, ro[...]).astype(BF16))
+
+    for step, out in enumerate(outs):
+
+        @pl.when(pl.program_id(0) == step)
+        def _():
+            write(out)
+
+
+def attend(sizes, joint_keys, place, reply_len, reply_slot, *refs):
     chips, reply_own, prompt_own, prompt_rows, prompt_keys = sizes
     own_positions = reply_own // RESP_DEV
     positions = CORES * own_positions
@@ -128,12 +123,14 @@
     block = positions
     per_chip = chip_prompt // block
     prompt_blocks = chips * per_chip
-    rows_in, keys_in, query_out, keys_out, refs = refs[:2], refs[2], refs[3:5], refs[5], refs[6:]
+    rows_in, refs = refs[:2], refs[2:]
+    count = chips if joint_keys else chips * CORES
+    keys_in, refs = refs[:count], refs[count:]
+    query_out, refs = refs[:2], refs[2:]
+    count = chips * CORES if joint_keys else chips
+    keys_out, refs = refs[:count], refs[count:]
     keys, keys_t, total, query, gradient, deltas, delta, scores, top, mass, prob, score_grad, query_grad = refs
     chip, core, group = place[0], place[1], place[2]
-
-    def device(away, other):
-        return (chip ^ away) * CORES + (core ^ other)
 
     pick = (iota((8, HEAD_WIDTH), 1) // 3 == iota((8, HEAD_WIDTH), 0)).astype(BF16)
     for other in range(CORES):
@@ -141,13 +138,14 @@
 
     for index in range(chips * CORES):
         away, other = index // CORES, index % CORES
-        source = device(away, other)
+        source = keys_in[away].at[other] if joint_keys else keys_in[index]
+        source = source if len(source.shape) == 2 else source.at[0]
         at = away * chip_prompt + other * prompt_keys
-        keys[at : at + prompt_keys] = keys_in[source, :prompt_keys]
+        keys[at : at + prompt_keys] = source[:prompt_keys]
         for slot in range(RESP_DEV):
             at = prompt_blocks * block + (slot * chips + away) * positions + other * own_positions
             begin = prompt_keys + slot * own_positions
-            keys[at : at + own_positions] = keys_in[source, begin : begin + own_positions]
+            keys[at : at + own_positions] = source[begin : begin + own_positions]
     total[...] = jnp.zeros_like(total)
 
     def transpose_block(index, carry):
@@ -326,12 +324,11 @@
 
     for index in range(chips * CORES):
         away, other = index // CORES, index % CORES
-        out = device(away, other)
+        out = keys_out[index] if joint_keys else keys_out[away].at[other]
 
         def put(to, at, count):
-            key_sum = (total[at : at + count, :HEAD_WIDTH] * SCALE).astype(BF16)
-            keys_out[out, to : to + count, :HEAD_WIDTH] = key_sum
-            keys_out[out, to : to + count, HEAD_WIDTH:] = total[at : at + count, HEAD_WIDTH:].astype(BF16)
+            out[to : to + count, :HEAD_WIDTH] = (total[at : at + count, :HEAD_WIDTH] * SCALE).astype(BF16)
+            out[to : to + count, HEAD_WIDTH:] = total[at : at + count, HEAD_WIDTH:].astype(BF16)
 
         put(0, away * chip_prompt + other * prompt_keys, prompt_keys)
         for slot in range(RESP_DEV):
@@ -339,47 +336,63 @@
             put(prompt_keys + slot * own_positions, at, own_positions)
 
 
-def spread_prompt(place, parts, outs, summed):
-    groups, rows = outs.shape[0], outs.shape[2]
-    prompt_keys = groups * rows
-    for other in range(CORES):
-        source = place[1] ^ other
-        value = parts[source, :prompt_keys].astype(F32)
-        for chip in range(1, parts.shape[0] // CORES):
-            value = value + parts[chip * CORES + source, :prompt_keys].astype(F32)
-        summed[...] = value
-        for target in range(groups):
-            outs[target, other] = summed[target * rows : (target + 1) * rows].astype(BF16)
-
-
-def finish(prompt_keys, place, *refs):
-    parts, refs = refs[:LOCAL_HEADS], refs[LOCAL_HEADS:]
-    slices, refs = refs[:LOCAL_HEADS], refs[LOCAL_HEADS:]
-    queries, refs = refs[: LOCAL_HEADS * CORES], refs[LOCAL_HEADS * CORES :]
-    prompt_dq, prompt_dk, prompt_dv, reply_dq, reply_dk, reply_dv = refs
-    core = place[1]
+def add(first, *rest):
+    value = first.astype(F32)
+    for part in rest:
+        value = value + part.astype(F32)
+    return value
+
+
+def add_pairs(*refs):
+    count = len(refs) // 3
+    for index in range(count):
+        refs[2 * count + index][...] = add(refs[index][...], refs[count + index][...]).astype(BF16)
+
+
+def collect(*refs):
+    parts, mine, theirs = refs[:-2], refs[-2], refs[-1]
+    mine[...] = add(*(part[0] for part in parts))
+    theirs[...] = add(*(part[1] for part in parts)).astype(BF16)
+
+
+def spread_prompt(sizes, place, *refs):
+    refs, outs, summed = refs[: sum(sizes)], refs[sum(sizes) : -1], refs[-1]
+    groups, rows = len(outs), outs[0].shape[1]
+    for index, size in enumerate(sizes):
+        parts, refs = refs[:size], refs[size:]
+        summed[index] = add(*(part[: groups * rows] for part in parts))
+    for shift in range(groups):
+        at = pl.ds(pl.multiple_of(lax.rem(place[2] + shift, groups) * rows, rows), rows)
+        for index in range(len(sizes)):
+            outs[shift][index] = summed[index, at].astype(BF16)
+
+
+def finish_reply(sizes, place, *refs):
+    parts_in, refs = refs[: sum(sizes)], refs[sum(sizes) :]
+    queries, refs = refs[: len(sizes)], refs[len(sizes) :]
+    prompt_dq, reply_dq, reply_dk, reply_dv = refs
     reply = reply_dq.shape[0]
     order = unsorting(reply)
-    for local in range(LOCAL_HEADS):
-        for other in range(CORES):
-            head = head_of(core, other, local)
-            span = lanes(head, HEAD_WIDTH)
-            value = slices[local][0, other].astype(F32)
-            for group in range(1, slices[local].shape[0]):
-                value = value + slices[local][group, other].astype(F32)
-            prompt_dk[:, span] = value[:, :HEAD_WIDTH].astype(BF16)
-            prompt_dv[:, span] = value[:, HEAD_WIDTH:].astype(BF16)
-            source = core ^ other
-            value = parts[local][source, prompt_keys:].astype(F32)
-            for chip in range(1, parts[local].shape[0] // CORES):
-                value = value + parts[local][chip * CORES + source, prompt_keys:].astype(F32)
-            value = dot(order, value.astype(BF16)).astype(BF16)
-            reply_dk[:, span] = value[:, :HEAD_WIDTH]
-            reply_dv[:, span] = value[:, HEAD_WIDTH:]
-            span = lanes(head, GROUP_WIDTH)
-            query = queries[local * CORES + other]
-            reply_dq[:, span] = dot(order, query[:reply]).astype(BF16)
-            prompt_dq[:, span] = query[reply:]
+    for index, size in enumerate(sizes):
+        parts, parts_in = parts_in[:size], parts_in[size:]
+        head = head_of(place[1], index % CORES, index // CORES)
+        span = lanes(head, HEAD_WIDTH)
+        value = add(*(part[part.shape[0] - reply :] for part in parts))
+        value = dot(order, value.astype(BF16)).astype(BF16)
+        reply_dk[:, span] = value[:, :HEAD_WIDTH]
+        reply_dv[:, span] = value[:, HEAD_WIDTH:]
+        span = lanes(head, GROUP_WIDTH)
+        reply_dq[:, span] = dot(order, queries[index][:reply]).astype(BF16)
+        prompt_dq[:, span] = queries[index][reply:]
+
+
+def finish_prompt(place, *refs):
+    parts, prompt_dk, prompt_dv = refs[:-2], refs[-2], refs[-1]
+    for index in range(KEY_VALUE_HEADS):
+        span = lanes(head_of(place[1], index % CORES, index // CORES), HEAD_WIDTH)
+        value = add(*(part[index] for part in parts)).astype(BF16)
+        prompt_dk[:, span] = value[:, :HEAD_WIDTH]
+        prompt_dv[:, span] = value[:, HEAD_WIDTH:]
 
 
 def on_device(
@@ -408,27 +421,42 @@
     chip_prompt = CORES * prompt_keys
     assert chip_prompt % positions == 0 and chips & (chips - 1) == 0
     pre_index = lax.axis_index("pre")
-    place = jnp.stack([pre_index // CORES, pre_index % CORES, lax.axis_index("rsp")]).astype(jnp.int32)
+    place = jnp.stack([lax.div(pre_index, CORES), lax.rem(pre_index, CORES), lax.axis_index("rsp")])
 
     def shape(*dims, dtype=BF16):
         return jax.ShapeDtypeStruct(dims, dtype)
 
+    def move(array, away, cross=0):
+        pairs = [(p, (p // CORES ^ away) * CORES + (p % CORES ^ cross)) for p in range(devices)]
+        return lax.ppermute(array, "pre", pairs)
+
     def swap(array):
-        return lax.ppermute(array, "pre", [(p, p ^ 1) for p in range(devices)])
-
-    def trade(array, axis):
-        return lax.all_to_all(array, axis, 0, 0, tiled=True)
-
-    key_rows = prompt_keys + reply_own
-    *key_blocks, token = pl.pallas_call(
+        return move(array, 0, 1)
+
+    def call(kernel, name, mib, inputs, outs, scalars=1, **more):
+        return pl.pallas_call(
+            kernel,
+            out_shape=outs,
+            in_specs=[SMEM] * scalars + [VMEM] * (len(inputs) - scalars),
+            out_specs=[VMEM] * len(outs),
+            compiler_params=params(mib),
+            name=name,
+            **more,
+        )(*inputs)
+
+    relayed = chips == 4
+    key_shape = (prompt_keys + reply_own, 2 * HEAD_WIDTH)
+    mine0, theirs0, mine1, theirs, token = call(
         prepare_keys,
-        out_shape=[shape(devices, key_rows, 2 * HEAD_WIDTH)] * LOCAL_HEADS + [shape(8, 128, dtype=F32)],
-        in_specs=[SMEM] + [VMEM] * 4,
-        out_specs=[VMEM] * (LOCAL_HEADS + 1),
-        compiler_params=params(VMEM_MIB),
-        name="prepare_keys",
-    )(place, prompt_k, prompt_value, reply_key[0], reply_value[0])
-    gathered = [trade(block, "pre") for block in key_blocks]
+        "prepare_keys",
+        VMEM_MIB,
+        (place, prompt_k, prompt_value, reply_key[0], reply_value[0]),
+        [shape(*key_shape)] * 3 + [shape(LOCAL_HEADS, *key_shape), shape(8, 128, dtype=F32)],
+    )
+    blocks0 = {(0, 0): mine0, (0, 1): swap(theirs)}
+    for away in range(1, 3 if relayed else chips):
+        blocks0[away, 0] = move(mine0, away)
+        blocks0[away, 1] = move(theirs0, away, 1)
     if prompt_own > prompt_rows:
         room = ((0, prompt_own - prompt_rows), (0, 0))
         prompt_query, prompt_output, prompt_output_gradient = (
@@ -438,32 +466,27 @@
     own_rows = reply_own + prompt_own
     row_width = 2 * GROUP_WIDTH + HEAD_WIDTH
 
-    def row_head(step, place):
-        core = place[1]
-        owner = jnp.where(step < LOCAL_HEADS, 1 - core, core)
-        return 0, owner * LOCAL_HEADS + step % LOCAL_HEADS
-
-    mine, theirs = pl.pallas_call(
+    def head_block(step, place):
+        owner = jnp.where(step % CORES == 0, 1 - place[1], place[1])
+        return 0, owner * LOCAL_HEADS + step // CORES
+
+    rows = pl.pallas_call(
         prepare_rows,
-        out_shape=[shape(LOCAL_HEADS, own_rows, row_width)] * CORES,
+        out_shape=[shape(own_rows, row_width)] * KEY_VALUE_HEADS,
         grid_spec=pltpu.PrefetchScalarGridSpec(
             num_scalar_prefetch=1,
             grid=(KEY_VALUE_HEADS,),
             in_specs=[pl.BlockSpec(memory_space=pl.ANY)]
-            + [pl.BlockSpec((prompt_own, GROUP_WIDTH), row_head)] * 3
-            + [pl.BlockSpec((reply_own, GROUP_WIDTH), row_head)] * 3,
-            out_specs=[
-                pl.BlockSpec(
-                    (1, own_rows, row_width),
-                    lambda step, place: (jnp.maximum(step - LOCAL_HEADS, 0), 0, 0),
-                ),
-                pl.BlockSpec(
-                    (1, own_rows, row_width),
-                    lambda step, place: (jnp.minimum(step, LOCAL_HEADS - 1), 0, 0),
-                ),
-            ],
+            + [pl.BlockSpec((prompt_own, GROUP_WIDTH), head_block)] * 3
+            + [pl.BlockSpec((reply_own, GROUP_WIDTH), head_block)] * 3,
+            out_specs=[pl.BlockSpec((own_rows, row_width), lambda step, place: (0, 0))] * KEY_VALUE_HEADS,
         ),
         compiler_params=params(VMEM_MIB),
+        cost_estimate=pl.CostEstimate(
+            flops=6 * reply_own * reply_own * QUERY_HEADS * HEAD_WIDTH,
+            bytes_accessed=20 * reply_own * QUERY_HEADS * HEAD_WIDTH,
+            transcendentals=0,
+        ),
         name="prepare_rows",
     )(
         place,
@@ -475,23 +498,37 @@
         reply_output[0],
         reply_output_gradient[0],
     )
-    theirs = swap(theirs)
+
+    blocks0, rows, mine1 = lax.optimization_barrier((blocks0, rows, mine1))
+    if relayed:
+        blocks0[3, 0] = move(blocks0[1, 0], 2)
+        blocks0[3, 1] = move(blocks0[2, 1], 1)
+    chip1 = jnp.stack([mine1, blocks0[0, 1][1]])
+    blocks1 = [chip1] + [move(chip1, away) for away in range(1, chips)]
 
     blocks = chips * (chip_prompt // positions) + RESP_DEV * chips
     slots = chips * (chip_prompt // positions) + chips
     all_rows = max(GROUP * positions, -(-GROUP * CORES * prompt_own // 128) * 128)
     sizes = (chips, reply_own, prompt_own, prompt_rows, prompt_keys)
     score_count = GROUP * (positions * RESP_DEV * slots * positions)
-    parts, queries, slices = [], [], []
-    for local in range(LOCAL_HEADS):
-        rows_spec = pl.BlockSpec((pl.squeezed, own_rows, row_width), lambda step, local=local: (local, 0, 0))
-        query_mine, query_theirs, sums = pl.pallas_call(
-            functools.partial(attend, sizes),
-            out_shape=[shape(own_rows, GROUP_WIDTH)] * CORES
-            + [shape(devices, key_rows, 2 * HEAD_WIDTH)],
-            grid=(1,),
-            in_specs=[SMEM] * 3 + [rows_spec] * 2 + [VMEM],
-            out_specs=[VMEM] * 3,
+
+    def run_attend(local, key_blocks):
+        joint_keys = local == 1
+        sums = [shape(*key_shape)] * devices if joint_keys else [shape(CORES, *key_shape)] * chips
+        query_mine, query_theirs, *sums = call(
+            functools.partial(attend, sizes, joint_keys),
+            "attend",
+            VMEM_MIB,
+            (
+                place,
+                reply_len,
+                reply_slot,
+                rows[CORES * local + 1],
+                swap(rows[CORES * local]),
+                *key_blocks,
+            ),
+            [shape(own_rows, GROUP_WIDTH)] * CORES + sums,
+            scalars=3,
             scratch_shapes=[
                 pltpu.VMEM((blocks * positions, 2 * HEAD_WIDTH), BF16),
                 pltpu.VMEM((blocks, HEAD_WIDTH, positions), BF16),
@@ -507,46 +544,96 @@
                 pltpu.VMEM((positions, all_rows), BF16),
                 pltpu.VMEM((HEAD_WIDTH, all_rows), F32),
             ],
-            compiler_params=params(VMEM_MIB),
             cost_estimate=pl.CostEstimate(
                 flops=score_count * 10 * HEAD_WIDTH,
                 bytes_accessed=8 * 1024 * 1024,
                 transcendentals=2 * score_count,
             ),
-            name="attend",
-        )(place, reply_len, reply_slot, mine, theirs, gathered[local])
-        queries += [query_mine, swap(query_theirs)]
-        parts.append(trade(sums, "pre"))
-        cut_shape = (groups, CORES, prompt_keys // groups, 2 * HEAD_WIDTH)
-        cut = pl.pallas_call(
-            spread_prompt,
-            out_shape=shape(*cut_shape),
-            in_specs=[SMEM, VMEM],
-            out_specs=VMEM,
-            scratch_shapes=[pltpu.VMEM((prompt_keys, 2 * HEAD_WIDTH), F32)],
-            compiler_params=params(VMEM_MIB),
-            name="spread_prompt",
-        )(place, parts[-1])
-        slices.append(trade(cut, "rsp"))
-
+        )
+        return query_mine, query_theirs, sums
+
+    query_mine0, query_theirs0, sums0 = run_attend(
+        0, [blocks0[away, other] for away in range(chips) for other in range(CORES)]
+    )
+    arrived0 = [sums0[0]] + [move(sums0[away], away) for away in range(1, chips)]
+    query_theirs0 = swap(query_theirs0)
+    query_mine1, query_theirs1, sums1 = run_attend(1, blocks1)
+    arrived0, query_theirs0, query_theirs1, sums1 = lax.optimization_barrier(
+        (arrived0, query_theirs0, query_theirs1, sums1)
+    )
+    sums1 = [sums1[CORES * away : CORES * away + CORES] for away in range(chips)]
+    if relayed:
+        through_y, through_x = move(sums1[3][0], 2), move(sums1[3][1], 1)
+        for_x, for_y = call(
+            add_pairs,
+            "add_pairs",
+            SMALL_MIB,
+            (sums1[1][0], sums1[2][1], through_y, through_x),
+            [shape(*key_shape)] * 2,
+            scalars=0,
+        )
+        near = [sums1[0][0], move(sums1[1][1], 1, 1), move(sums1[2][0], 2)]
+        for_x, for_y, sums1[0][1], query_theirs1 = lax.optimization_barrier(
+            (for_x, for_y, sums1[0][1], query_theirs1)
+        )
+        lists1 = [[near[0], move(for_x, 1), near[2]], [swap(sums1[0][1]), near[1], move(for_y, 2, 1)]]
+    else:
+        lists1 = [
+            [move(pair[other], away, other) if away or other else pair[other] for away, pair in enumerate(sums1)]
+            for other in range(CORES)
+        ]
+    mine0, theirs0 = call(
+        collect,
+        "collect",
+        SMALL_MIB,
+        arrived0,
+        [shape(*key_shape, dtype=F32), shape(*key_shape)],
+        scalars=0,
+    )
+    lists = [[mine0], [swap(theirs0)]] + lists1
+    queries = [query_mine0, query_theirs0, query_mine1, swap(query_theirs1)]
+    counts = [len(parts) for parts in lists]
+    parts = [part for one in lists for part in one]
+    cut_rows = prompt_keys // groups
+    cuts = call(
+        functools.partial(spread_prompt, counts),
+        "spread_prompt",
+        SMALL_MIB,
+        (place, *parts),
+        [shape(KEY_VALUE_HEADS, cut_rows, 2 * HEAD_WIDTH)] * groups,
+        scratch_shapes=[pltpu.VMEM((KEY_VALUE_HEADS, prompt_keys, 2 * HEAD_WIDTH), F32)],
+    )
+    slices = [cuts[0]] + [
+        lax.ppermute(cuts[shift], "rsp", [(g, (g + shift) % groups) for g in range(groups)])
+        for shift in range(1, groups)
+    ]
     key_width = KEY_VALUE_HEADS * HEAD_WIDTH
     query_width = QUERY_HEADS * HEAD_WIDTH
-    cut_rows = prompt_keys // groups
-    prompt_dq, prompt_dk, prompt_dv, reply_dq, reply_dk, reply_dv = pl.pallas_call(
-        functools.partial(finish, prompt_keys),
-        out_shape=[
+    prompt_dq, reply_dq, reply_dk, reply_dv = call(
+        functools.partial(finish_reply, counts),
+        "finish_reply",
+        SMALL_MIB,
+        (place, *parts, *queries),
+        [
             shape(prompt_own, query_width),
-            shape(cut_rows, key_width),
-            shape(cut_rows, key_width),
             shape(reply_own, query_width),
             shape(reply_own, key_width),
             shape(reply_own, key_width),
         ],
-        in_specs=[SMEM] + [VMEM] * (LOCAL_HEADS * (2 + CORES)),
-        out_specs=[VMEM] * 6,
-        compiler_params=params(VMEM_MIB),
-        name="finish",
-    )(place, *parts, *slices, *queries)
+        cost_estimate=pl.CostEstimate(
+            flops=2 * reply_own * reply_own * (query_width + 2 * key_width),
+            bytes_accessed=16 * reply_own * query_width,
+            transcendentals=0,
+        ),
+    )
+    slices, prompt_dq = lax.optimization_barrier((slices, prompt_dq))
+    prompt_dk, prompt_dv = call(
+        finish_prompt,
+        "finish_prompt",
+        SMALL_MIB,
+        (place, *slices),
+        [shape(cut_rows, key_width)] * 2,
+    )
     return (
         prompt_dq[:prompt_rows],
         prompt_dk,

time: 147 us -> 118 us (0.80); the launches traced: 145 us -> 120 us
  waiting for transfers between devices: 40.7 us -> 19.3 us
  starting transfers between devices: 35.9 us -> 44.4 us
  local copies, waits for them, and re-layouts: 17.7 us -> 10.4 us
  Pallas kernels: 49.6 us -> 45 us
    ppermute x3 -> x28, starting transfers between devices: 1.01 us -> 44.4 us  [the longest x25 40.6 us: move(): return lax.ppermute(array, 'pre', pairs)]
    all_to_all x6 -> x0, waiting for transfers between devices: 40.7 us -> none  [trade(): return lax.all_to_all(array, axis, 0, 0, tiled=True)]
    all_to_all x6 -> x0, starting transfers between devices: 34.8 us -> none  [trade(): return lax.all_to_all(array, axis, 0, 0, tiled=True)]
    ppermute x3 -> x28, waiting for transfers between devices: 0.01 us -> 19.3 us  [the longest x25 17.5 us: move(): return lax.ppermute(array, 'pre', pairs)]
    unnamed x46 -> x24, local copies, waits for them, and re-layouts: 17.7 us -> 10.4 us
    pallas_call x7 -> x9, Pallas kernels: 49.6 us -> 45 us  [the longest x8 40 us: call(): pl.pallas_call(kernel, out_shape=outs, in_specs=[SMEM] * scalars + [VMEM]...]
  transfers between devices with their start and end apart: 9 -> 28, of which waited for: 4 -> 7; matrix products, arithmetic and copies ran while one was open for 0% -> 0% of each run, Pallas kernels for 30% -> 36%
where the time goes in v2:
time: 118 us; the launch traced here: 120 us
  Pallas kernels  45 us (38%)
  starting transfers between devices  44.4 us (38%)
  waiting for transfers between devices  19.3 us (16%)
  local copies, waits for them, and re-layouts  10.4 us (9%)
    ppermute x25, starting transfers between devices, move(): return lax.ppermute(array, 'pre', pairs)  40.6 us
    pallas_call x8, Pallas kernels, call(): pl.pallas_call(kernel, out_shape=outs, in_specs=[SMEM] * scalars + [VMEM]...  40 us
    ppermute x25, waiting for transfers between devices, move(): return lax.ppermute(array, 'pre', pairs)  17.5 us
    unnamed x24, local copies, waits for them, and re-layouts  10.4 us
    pallas_call x1, Pallas kernels, on_device(): pl.pallas_call(prepare_rows, out_shape=[shape(own_rows, row_width)] * KEY...  4.95 us
    ppermute x3, starting transfers between devices, on_device(): lax.ppermute(cuts[shift], 'rsp', [(g, (g + shift) % groups) for g in rang...  3.86 us
  transfers between devices with their start and end apart: 28, of which 7 were waited for; matrix products, arithmetic and copies ran while one was open for 0% of the time, Pallas kernels for 36%

profile of v2, /device:TPU:0, one launch (start us, length us, event | category | flops | bytes accessed | tf_op | source)
XLA Modules:
  0.0 120.1 jit_solution(13906702250523075646)
XLA Ops:
  0.7 0.9 copy-done.3
  1.7 0.9 copy-done.4
  4.4 1.0 prepare_keys.1
  6.0 2.6 %collective-permute-start.1 = (bf16[384,256]{1,0:T(8,128)(2,1)S(1)}, bf16[384,256]{1,0:T(8,128)(2,1)S(1)}, u32[]{:S(2)}, u32[]{:S(2)}) collective-permute-start(bf16[384,256]{1,0:T(8,128)(2,1)S(1)} %get-tuple-element.90.refs_2_), channel_id=1, source_target_pairs={{0,8},{4,12},{8,0},{12,4},{16,24},{20,28},{24,16},{28,20},{1,9},{5... | collective-permute-start | bytes 589832 | tf_op jit(solution)/shard_map/ppermute | solution.py:431
  8.6 1.8 %collective-permute-start.3 = (bf16[384,256]{1,0:T(8,128)(2,1)S(1)}, bf16[384,256]{1,0:T(8,128)(2,1)S(1)}, u32[]{:S(2)}, u32[]{:S(2)}) collective-permute-start(bf16[384,256]{1,0:T(8,128)(2,1)S(1)} %get-tuple-element.90.refs_2_), channel_id=1, source_target_pairs={{0,16},{4,20},{8,24},{12,28},{16,0},{20,4},{24,8},{28,12},{1,17},{... | collective-permute-start | bytes 589832 | tf_op jit(solution)/shard_map/ppermute | solution.py:431
  10.4 1.3 %copy-done = bf16[1,256,2560]{2,1,0:T(8,128)(2,1)S(1)} copy-done((bf16[1,256,2560]{2,1,0:T(8,128)(2,1)S(1)}, bf16[1,256,2560]{2,1,0:T(8,128)(2,1)}, u32[]{:S(2)}) %copy-start) | copy-done | bytes 1310744
  11.7 1.3 %copy-done.1 = bf16[1,256,2560]{2,1,0:T(8,128)(2,1)S(1)} copy-done((bf16[1,256,2560]{2,1,0:T(8,128)(2,1)S(1)}, bf16[1,256,2560]{2,1,0:T(8,128)(2,1)}, u32[]{:S(2)}) %copy-start.1) | copy-done | bytes 1310744
  13.0 1.3 %copy-done.2 = bf16[1,256,2560]{2,1,0:T(8,128)(2,1)S(1)} copy-done((bf16[1,256,2560]{2,1,0:T(8,128)(2,1)S(1)}, bf16[1,256,2560]{2,1,0:T(8,128)(2,1)}, u32[]{:S(2)}) %copy-start.2) | copy-done | bytes 1310744
  14.3 0.9 copy-done.5
  15.3 0.9 copy-done.6
  16.2 0.9 copy-done.7
  17.1 5.0 %prepare_rows.1 = (bf16[288,1408]{1,0:T(8,128)(2,1)S(1)}, bf16[288,1408]{1,0:T(8,128)(2,1)S(1)}, bf16[288,1408]{1,0:T(8,128)(2,1)S(1)}, bf16[288,1408]{1,0:T(8,128)(2,1)S(1)}) custom-call(s32[3]{0:T(128)S(1)} %pad_add_fusion.place, f32[8,128]{1,0:T(8,128)S(1)} %get-tuple-element.82.token, bf16[32,2560]{1,0:T(8,128)(2,1)S(1)} %copy-done.5, ...), custom_call_target="tpu_custom_call" | custom-call | flops 1006632960 | bytes 13107200 | tf_op jit(solution)/shard_map/prepare_rows/pallas_call | solution.py:473
  22.5 1.8 %collective-permute-start.6 = (bf16[384,256]{1,0:T(8,128)(2,1)S(1)}, bf16[384,256]{1,0:T(8,128)(2,1)S(1)}, u32[]{:S(2)}, u32[]{:S(2)}) collective-permute-start(bf16[384,256]{1,0:T(8,128)(2,1)S(1)} %collective-permute-done.1.refs_4_), channel_id=1, source_target_pairs={{0,16},{4,20},{8,24},{12,28},{16,0},{20,4},{24,8},{28,12},{1,17},{... | collective-permute-start | bytes 589832 | tf_op jit(solution)/shard_map/ppermute | solution.py:431
  24.3 1.5 %collective-permute-start.7 = (bf16[384,256]{1,0:T(8,128)(2,1)S(1)}, bf16[384,256]{1,0:T(8,128)(2,1)S(1)}, u32[]{:S(2)}, u32[]{:S(2)}) collective-permute-start(bf16[384,256]{1,0:T(8,128)(2,1)S(1)} %collective-permute-done.4.refs_7_), channel_id=1, source_target_pairs={{0,8},{4,12},{8,0},{12,4},{16,24},{20,28},{24,16},{28,20},{1,9},{5... | collective-permute-start | bytes 589832 | tf_op jit(solution)/shard_map/ppermute | solution.py:431
  26.5 3.0 %collective-permute-done.6.refs_8_ = bf16[384,256]{1,0:T(8,128)(2,1)S(1)} collective-permute-done((bf16[384,256]{1,0:T(8,128)(2,1)S(1)}, bf16[384,256]{1,0:T(8,128)(2,1)S(1)}, u32[]{:S(2)}, u32[]{:S(2)}) %collective-permute-start.6) | collective-permute-done | bytes 196640 | tf_op jit(solution)/shard_map/ppermute | solution.py:431
  29.5 1.7 %collective-permute-start.14 = (bf16[2,384,256]{2,1,0:T(8,128)(2,1)S(1)}, bf16[2,384,256]{2,1,0:T(8,128)(2,1)S(1)}, u32[]{:S(2)}, u32[]{:S(2)}) collective-permute-start(bf16[2,384,256]{2,1,0:T(8,128)(2,1)S(1)} %pad_maximum_fusion.refs_2_), channel_id=1, source_target_pairs={{0,16},{4,20},{8,24},{12,28},{16,0},{20,4},{24,8},{28,12},{1,17},{... | collective-permute-start | bytes 1179656 | tf_op jit(solution)/shard_map/ppermute | solution.py:431
  31.2 0.9 collective-permute-done.7.refs_9_
  32.1 1.4 %collective-permute-start.15 = (bf16[2,384,256]{2,1,0:T(8,128)(2,1)S(1)}, bf16[2,384,256]{2,1,0:T(8,128)(2,1)S(1)}, u32[]{:S(2)}, u32[]{:S(2)}) collective-permute-start(bf16[2,384,256]{2,1,0:T(8,128)(2,1)S(1)} %pad_maximum_fusion.refs_2_), channel_id=1, source_target_pairs={{0,24},{4,28},{8,16},{12,20},{16,8},{20,12},{24,0},{28,4},{1,25},{... | collective-permute-start | bytes 1179656 | tf_op jit(solution)/shard_map/ppermute | solution.py:431
  33.5 17.1 %attend.2 = (bf16[288,640]{1,0:T(8,128)(2,1)S(1)}, bf16[288,640]{1,0:T(8,128)(2,1)S(1)}, bf16[2,384,256]{2,1,0:T(8,128)(2,1)S(1)}, bf16[2,384,256]{2,1,0:T(8,128...) custom-call(s32[3]{0:T(128)S(1)} %pad_add_fusion.place, s32[8]{0:T(128)S(1)} %copy-done.10, ...), custom_call_target="tpu_custom_call" | custom-call | flops 6710886400 | bytes 8388608 | tf_op jit(solution)/shard_map/attend/pallas_call | solution.py:437
  50.6 3.6 %collective-permute-start.8 = (bf16[2,384,256]{2,1,0:T(8,128)(2,1)S(1)}, bf16[2,384,256]{2,1,0:T(8,128)(2,1)S(1)}, u32[]{:S(2)}, u32[]{:S(2)}) collective-permute-start(bf16[2,384,256]{2,1,0:T(8,128)(2,1)S(1)} %get-tuple-element.97), channel_id=1, source_target_pairs={{0,8},{4,12},{8,0},{12,4},{16,24},{20,28},{24,16},{28,20},{1,9},{5... | collective-permute-start | bytes 1179656 | tf_op jit(solution)/shard_map/ppermute | solution.py:431
  54.2 8.2 %collective-permute-start.9 = (bf16[2,384,256]{2,1,0:T(8,128)(2,1)S(1)}, bf16[2,384,256]{2,1,0:T(8,128)(2,1)S(1)}, u32[]{:S(2)}, u32[]{:S(2)}) collective-permute-start(bf16[2,384,256]{2,1,0:T(8,128)(2,1)S(1)} %get-tuple-element.98), channel_id=1, source_target_pairs={{0,16},{4,20},{8,24},{12,28},{16,0},{20,4},{24,8},{28,12},{1,17},{... | collective-permute-start | bytes 1179656 | tf_op jit(solution)/shard_map/ppermute | solution.py:431
  62.6 17.3 %attend.3 = (bf16[288,640]{1,0:T(8,128)(2,1)S(1)}, bf16[288,640]{1,0:T(8,128)(2,1)S(1)}, bf16[384,256]{1,0:T(8,128)(2,1)S(1)}, bf16[384,256]{1,0:T(8,128)(2,1)S(...) custom-call(s32[3]{0:T(128)S(1)} %pad_add_fusion.place, ...), custom_call_target="tpu_custom_call" | custom-call | flops 6710886400 | bytes 8388608 | tf_op jit(solution)/shard_map/attend/pallas_call | solution.py:437
  79.9 8.0 %collective-permute-start.17 = (bf16[384,256]{1,0:T(8,128)(2,1)S(1)}, bf16[384,256]{1,0:T(8,128)(2,1)S(1)}, u32[]{:S(2)}, u32[]{:S(2)}) collective-permute-start(bf16[384,256]{1,0:T(8,128)(2,1)S(1)} %get-tuple-element.122), channel_id=1, source_target_pairs={{0,16},{4,20},{8,24},{12,28},{16,0},{20,4},{24,8},{28,12},{1,17},{... | collective-permute-start | bytes 589832 | tf_op jit(solution)/shard_map/ppermute | solution.py:431
  87.9 5.2 %collective-permute-start.18 = (bf16[384,256]{1,0:T(8,128)(2,1)S(1)}, bf16[384,256]{1,0:T(8,128)(2,1)S(1)}, u32[]{:S(2)}, u32[]{:S(2)}) collective-permute-start(bf16[384,256]{1,0:T(8,128)(2,1)S(1)} %get-tuple-element.123), channel_id=1, source_target_pairs={{0,8},{4,12},{8,0},{12,4},{16,24},{20,28},{24,16},{28,20},{1,9},{5... | collective-permute-start | bytes 589832 | tf_op jit(solution)/shard_map/ppermute | solution.py:431
  93.7 4.7 %collective-permute-done.18.refs_3_ = bf16[384,256]{1,0:T(8,128)(2,1)S(1)} collective-permute-done((bf16[384,256]{1,0:T(8,128)(2,1)S(1)}, bf16[384,256]{1,0:T(8,128)(2,1)S(1)}, u32[]{:S(2)}, u32[]{:S(2)}) %collective-permute-start.18) | collective-permute-done | bytes 196640 | tf_op jit(solution)/shard_map/ppermute | solution.py:431
  98.6 1.9 %collective-permute-start.22 = (bf16[384,256]{1,0:T(8,128)(2,1)S(1)}, bf16[384,256]{1,0:T(8,128)(2,1)S(1)}, u32[]{:S(2)}, u32[]{:S(2)}) collective-permute-start(bf16[384,256]{1,0:T(8,128)(2,1)S(1)} %get-tuple-element.131), channel_id=1, source_target_pairs={{0,12},{4,8},{8,4},{12,0},{16,28},{20,24},{24,20},{28,16},{1,13},{... | collective-permute-start | bytes 589832 | tf_op jit(solution)/shard_map/ppermute | solution.py:431
  101.3 4.4 %collective-permute-done.22.refs_6_ = bf16[384,256]{1,0:T(8,128)(2,1)S(1)} collective-permute-done((bf16[384,256]{1,0:T(8,128)(2,1)S(1)}, bf16[384,256]{1,0:T(8,128)(2,1)S(1)}, u32[]{:S(2)}, u32[]{:S(2)}) %collective-permute-start.22) | collective-permute-done | bytes 196640 | tf_op jit(solution)/shard_map/ppermute | solution.py:431
  105.7 4.4 %collective-permute-done.19.refs_3_ = bf16[384,256]{1,0:T(8,128)(2,1)S(1)} collective-permute-done((bf16[384,256]{1,0:T(8,128)(2,1)S(1)}, bf16[384,256]{1,0:T(8,128)(2,1)S(1)}, u32[]{:S(2)}, u32[]{:S(2)}) %collective-permute-start.19) | collective-permute-done | bytes 196640 | tf_op jit(solution)/shard_map/ppermute | solution.py:431
  110.9 3.7 %collective-permute-start.26 = (bf16[4,32,256]{2,1,0:T(8,128)(2,1)S(1)}, bf16[4,32,256]{2,1,0:T(8,128)(2,1)S(1)}, u32[]{:S(2)}, u32[]{:S(2)}) collective-permute-start(bf16[4,32,256]{2,1,0:T(8,128)(2,1)S(1)} %get-tuple-element.136), channel_id=1, source_target_pairs={{0,3},{1,0},{2,1},{3,2},{4,7},{5,4},{6,5},{7,6},{8,11},{9,8},{10,9... | collective-permute-start | bytes 196616 | tf_op jit(solution)/shard_map/ppermute | solution.py:607
  114.6 2.5 %finish_reply.1 = (bf16[32,2560]{1,0:T(8,128)(2,1)}, bf16[256,2560]{1,0:T(8,128)(2,1)}, bf16[256,512]{1,0:T(8,128)(2,1)}, bf16[256,512]{1,0:T(8,128)(2,1)}) custom-call(s32[3]{0:T(128)S(1)} %pad_add_fusion.place, f32[384,256]{1,0:T(8,128)S(1)} %get-tuple-element.117.refs_0_, bf16[384,256]{1,0:T(8,128)(2,1)S(1)} %collective-permute-done.16.refs_1_, ...), custom_call_target="tpu_custom_call" | custom-call | flops 469762048 | bytes 10485760 | tf_op jit(solution)/shard_map/finish_reply/pallas_call | solution.py:437
  117.6 1.3 %collective-permute-done.25.refs_2_ = bf16[4,32,256]{2,1,0:T(8,128)(2,1)S(1)} collective-permute-done((bf16[4,32,256]{2,1,0:T(8,128)(2,1)S(1)}, bf16[4,32,256]{2,1,0:T(8,128)(2,1)S(1)}, u32[]{:S(2)}, u32[]{:S(2)}) %collective-permute-start.25) | collective-permute-done | bytes 65568 | tf_op jit(solution)/shard_map/ppermute | solution.py:607
  118.9 1.2 %finish_prompt.1 = (bf16[32,512]{1,0:T(8,128)(2,1)}, bf16[32,512]{1,0:T(8,128)(2,1)}) custom-call(s32[3]{0:T(128)S(1)} %pad_add_fusion.place, bf16[4,32,256]{2,1,0:T(8,128)(2,1)S(1)} %get-tuple-element.143.refs_0_, bf16[4,32,256]{2,1,0:T(8,128)(2,1)S(1)} %collective-permute-done.24.refs_1_, bf16[4,32,256]{2,1,0:T(8,128)(2,1)S(1)} %collective-permute-done.25.refs_2_, ...), custom_call_target="tpu_custom_call" | custom-call | tf_op jit(solution)/shard_map/finish_prompt/pallas_call | solution.py:437
  (60 shorter events, 6.5 us)
Async XLA Ops:
  5.5 16.6 %collective-permute-start = (bf16[2,384,256]{2,1,0:T(8,128)(2,1)S(1)}, bf16[2,384,256]{2,1,0:T(8,128)(2,1)S(1)}, u32[]{:S(2)}, u32[]{:S(2)}) collective-permute-start(bf16[2,384,256]{2,1,0:T(8,128)(2,1)S(1)} %get-tuple-element.80), channel_id=1, source_target_pairs={{0,4},{4,0},{8,12},{12,8},{16,20},{20,16},{24,28},{28,24},{1,5},{5... | collective-permute-start | bytes 1179656 | tf_op jit(solution)/shard_map/ppermute | solution.py:431
  6.0 16.1 %collective-permute-start.1 = (bf16[384,256]{1,0:T(8,128)(2,1)S(1)}, bf16[384,256]{1,0:T(8,128)(2,1)S(1)}, u32[]{:S(2)}, u32[]{:S(2)}) collective-permute-start(bf16[384,256]{1,0:T(8,128)(2,1)S(1)} %get-tuple-element.90.refs_2_), channel_id=1, source_target_pairs={{0,8},{4,12},{8,0},{12,4},{16,24},{20,28},{24,16},{28,20},{1,9},{5... | collective-permute-start | bytes 589832 | tf_op jit(solution)/shard_map/ppermute | solution.py:431
  8.5 13.5 %collective-permute-start.2 = (bf16[384,256]{1,0:T(8,128)(2,1)S(1)}, bf16[384,256]{1,0:T(8,128)(2,1)S(1)}, u32[]{:S(2)}, u32[]{:S(2)}) collective-permute-start(bf16[384,256]{1,0:T(8,128)(2,1)S(1)} %get-tuple-element.81), channel_id=1, source_target_pairs={{0,12},{4,8},{8,4},{12,0},{16,28},{20,24},{24,20},{28,16},{1,13},{... | collective-permute-start | bytes 589832 | tf_op jit(solution)/shard_map/ppermute | solution.py:431
  8.6 13.5 %collective-permute-start.3 = (bf16[384,256]{1,0:T(8,128)(2,1)S(1)}, bf16[384,256]{1,0:T(8,128)(2,1)S(1)}, u32[]{:S(2)}, u32[]{:S(2)}) collective-permute-start(bf16[384,256]{1,0:T(8,128)(2,1)S(1)} %get-tuple-element.90.refs_2_), channel_id=1, source_target_pairs={{0,16},{4,20},{8,24},{12,28},{16,0},{20,4},{24,8},{28,12},{1,17},{... | collective-permute-start | bytes 589832 | tf_op jit(solution)/shard_map/ppermute | solution.py:431
  10.4 11.7 %collective-permute-start.4 = (bf16[384,256]{1,0:T(8,128)(2,1)S(1)}, bf16[384,256]{1,0:T(8,128)(2,1)S(1)}, u32[]{:S(2)}, u32[]{:S(2)}) collective-permute-start(bf16[384,256]{1,0:T(8,128)(2,1)S(1)} %get-tuple-element.81), channel_id=1, source_target_pairs={{0,20},{4,16},{8,28},{12,24},{16,4},{20,0},{24,12},{28,8},{1,21},{... | collective-permute-start | bytes 589832 | tf_op jit(solution)/shard_map/ppermute | solution.py:431
  10.4 1.3 %copy-start = (bf16[1,256,2560]{2,1,0:T(8,128)(2,1)S(1)}, bf16[1,256,2560]{2,1,0:T(8,128)(2,1)}, u32[]{:S(2)}) copy-start(bf16[1,256,2560]{2,1,0:T(8,128)(2,1)} %param.17) | copy-start | bytes 3932164
  11.7 1.3 %copy-start.1 = (bf16[1,256,2560]{2,1,0:T(8,128)(2,1)S(1)}, bf16[1,256,2560]{2,1,0:T(8,128)(2,1)}, u32[]{:S(2)}) copy-start(bf16[1,256,2560]{2,1,0:T(8,128)(2,1)} %param.20) | copy-start | bytes 3932164
  17.1 16.4 %copy-start.10 = (s32[8]{0:T(128)S(1)}, s32[8]{0:T(128)}, u32[]{:S(2)}) copy-start(s32[8]{0:T(128)} %reply_len.3) | copy-start | bytes 100
  17.1 16.4 %copy-start.11 = (s32[8]{0:T(128)S(1)}, s32[8]{0:T(128)}, u32[]{:S(2)}) copy-start(s32[8]{0:T(128)} %reply_slot.3) | copy-start | bytes 100
  22.1 11.4 %collective-permute-start.5 = (bf16[288,1408]{1,0:T(8,128)(2,1)S(1)}, bf16[288,1408]{1,0:T(8,128)(2,1)S(1)}, u32[]{:S(2)}, u32[]{:S(2)}) collective-permute-start(bf16[288,1408]{1,0:T(8,128)(2,1)S(1)} %get-tuple-element.89), channel_id=1, source_target_pairs={{0,4},{4,0},{8,12},{12,8},{16,20},{20,16},{24,28},{28,24},{1,5},{5... | collective-permute-start | bytes 2433032 | tf_op jit(solution)/shard_map/ppermute | solution.py:431
  22.5 7.0 %collective-permute-start.6 = (bf16[384,256]{1,0:T(8,128)(2,1)S(1)}, bf16[384,256]{1,0:T(8,128)(2,1)S(1)}, u32[]{:S(2)}, u32[]{:S(2)}) collective-permute-start(bf16[384,256]{1,0:T(8,128)(2,1)S(1)} %collective-permute-done.1.refs_4_), channel_id=1, source_target_pairs={{0,16},{4,20},{8,24},{12,28},{16,0},{20,4},{24,8},{28,12},{1,17},{... | collective-permute-start | bytes 589832 | tf_op jit(solution)/shard_map/ppermute | solution.py:431
  24.3 7.8 %collective-permute-start.7 = (bf16[384,256]{1,0:T(8,128)(2,1)S(1)}, bf16[384,256]{1,0:T(8,128)(2,1)S(1)}, u32[]{:S(2)}, u32[]{:S(2)}) collective-permute-start(bf16[384,256]{1,0:T(8,128)(2,1)S(1)} %collective-permute-done.4.refs_7_), channel_id=1, source_target_pairs={{0,8},{4,12},{8,0},{12,4},{16,24},{20,28},{24,16},{28,20},{1,9},{5... | collective-permute-start | bytes 589832 | tf_op jit(solution)/shard_map/ppermute | solution.py:431
  25.8 36.8 %collective-permute-start.12 = (bf16[288,1408]{1,0:T(8,128)(2,1)S(1)}, bf16[288,1408]{1,0:T(8,128)(2,1)S(1)}, u32[]{:S(2)}, u32[]{:S(2)}) collective-permute-start(bf16[288,1408]{1,0:T(8,128)(2,1)S(1)} %get-tuple-element.102), channel_id=1, source_target_pairs={{0,4},{4,0},{8,12},{12,8},{16,20},{20,16},{24,28},{28,24},{1,5},{5... | collective-permute-start | bytes 2433032 | tf_op jit(solution)/shard_map/ppermute | solution.py:431
  25.8 28.4 %collective-permute-start.13 = (bf16[2,384,256]{2,1,0:T(8,128)(2,1)S(1)}, bf16[2,384,256]{2,1,0:T(8,128)(2,1)S(1)}, u32[]{:S(2)}, u32[]{:S(2)}) collective-permute-start(bf16[2,384,256]{2,1,0:T(8,128)(2,1)S(1)} %pad_maximum_fusion.refs_2_), channel_id=1, source_target_pairs={{0,8},{4,12},{8,0},{12,4},{16,24},{20,28},{24,16},{28,20},{1,9},{5... | collective-permute-start | bytes 1179656 | tf_op jit(solution)/shard_map/ppermute | solution.py:431
  29.5 33.0 %collective-permute-start.14 = (bf16[2,384,256]{2,1,0:T(8,128)(2,1)S(1)}, bf16[2,384,256]{2,1,0:T(8,128)(2,1)S(1)}, u32[]{:S(2)}, u32[]{:S(2)}) collective-permute-start(bf16[2,384,256]{2,1,0:T(8,128)(2,1)S(1)} %pad_maximum_fusion.refs_2_), channel_id=1, source_target_pairs={{0,16},{4,20},{8,24},{12,28},{16,0},{20,4},{24,8},{28,12},{1,17},{... | collective-permute-start | bytes 1179656 | tf_op jit(solution)/shard_map/ppermute | solution.py:431
  32.1 30.4 %collective-permute-start.15 = (bf16[2,384,256]{2,1,0:T(8,128)(2,1)S(1)}, bf16[2,384,256]{2,1,0:T(8,128)(2,1)S(1)}, u32[]{:S(2)}, u32[]{:S(2)}) collective-permute-start(bf16[2,384,256]{2,1,0:T(8,128)(2,1)S(1)} %pad_maximum_fusion.refs_2_), channel_id=1, source_target_pairs={{0,24},{4,28},{8,16},{12,20},{16,8},{20,12},{24,0},{28,4},{1,25},{... | collective-permute-start | bytes 1179656 | tf_op jit(solution)/shard_map/ppermute | solution.py:431
  50.6 29.3 %collective-permute-start.8 = (bf16[2,384,256]{2,1,0:T(8,128)(2,1)S(1)}, bf16[2,384,256]{2,1,0:T(8,128)(2,1)S(1)}, u32[]{:S(2)}, u32[]{:S(2)}) collective-permute-start(bf16[2,384,256]{2,1,0:T(8,128)(2,1)S(1)} %get-tuple-element.97), channel_id=1, source_target_pairs={{0,8},{4,12},{8,0},{12,4},{16,24},{20,28},{24,16},{28,20},{1,9},{5... | collective-permute-start | bytes 1179656 | tf_op jit(solution)/shard_map/ppermute | solution.py:431
  54.2 25.7 %collective-permute-start.9 = (bf16[2,384,256]{2,1,0:T(8,128)(2,1)S(1)}, bf16[2,384,256]{2,1,0:T(8,128)(2,1)S(1)}, u32[]{:S(2)}, u32[]{:S(2)}) collective-permute-start(bf16[2,384,256]{2,1,0:T(8,128)(2,1)S(1)} %get-tuple-element.98), channel_id=1, source_target_pairs={{0,16},{4,20},{8,24},{12,28},{16,0},{20,4},{24,8},{28,12},{1,17},{... | collective-permute-start | bytes 1179656 | tf_op jit(solution)/shard_map/ppermute | solution.py:431
  62.5 17.4 %collective-permute-start.10 = (bf16[2,384,256]{2,1,0:T(8,128)(2,1)S(1)}, bf16[2,384,256]{2,1,0:T(8,128)(2,1)S(1)}, u32[]{:S(2)}, u32[]{:S(2)}) collective-permute-start(bf16[2,384,256]{2,1,0:T(8,128)(2,1)S(1)} %get-tuple-element.99), channel_id=1, source_target_pairs={{0,24},{4,28},{8,16},{12,20},{16,8},{20,12},{24,0},{28,4},{1,25},{... | collective-permute-start | bytes 1179656 | tf_op jit(solution)/shard_map/ppermute | solution.py:431
  62.5 17.4 %collective-permute-start.11 = (bf16[288,640]{1,0:T(8,128)(2,1)S(1)}, bf16[288,640]{1,0:T(8,128)(2,1)S(1)}, u32[]{:S(2)}, u32[]{:S(2)}) collective-permute-start(bf16[288,640]{1,0:T(8,128)(2,1)S(1)} %get-tuple-element.100), channel_id=1, source_target_pairs={{0,4},{4,0},{8,12},{12,8},{16,20},{20,16},{24,28},{28,24},{1,5},{5... | collective-permute-start | bytes 1105928 | tf_op jit(solution)/shard_map/ppermute | solution.py:431
  79.9 13.8 %collective-permute-start.17 = (bf16[384,256]{1,0:T(8,128)(2,1)S(1)}, bf16[384,256]{1,0:T(8,128)(2,1)S(1)}, u32[]{:S(2)}, u32[]{:S(2)}) collective-permute-start(bf16[384,256]{1,0:T(8,128)(2,1)S(1)} %get-tuple-element.122), channel_id=1, source_target_pairs={{0,16},{4,20},{8,24},{12,28},{16,0},{20,4},{24,8},{28,12},{1,17},{... | collective-permute-start | bytes 589832 | tf_op jit(solution)/shard_map/ppermute | solution.py:431
  87.9 10.5 %collective-permute-start.18 = (bf16[384,256]{1,0:T(8,128)(2,1)S(1)}, bf16[384,256]{1,0:T(8,128)(2,1)S(1)}, u32[]{:S(2)}, u32[]{:S(2)}) collective-permute-start(bf16[384,256]{1,0:T(8,128)(2,1)S(1)} %get-tuple-element.123), channel_id=1, source_target_pairs={{0,8},{4,12},{8,0},{12,4},{16,24},{20,28},{24,16},{28,20},{1,9},{5... | collective-permute-start | bytes 589832 | tf_op jit(solution)/shard_map/ppermute | solution.py:431
  93.3 7.4 %collective-permute-start.16 = (bf16[384,256]{1,0:T(8,128)(2,1)S(1)}, bf16[384,256]{1,0:T(8,128)(2,1)S(1)}, u32[]{:S(2)}, u32[]{:S(2)}) collective-permute-start(bf16[384,256]{1,0:T(8,128)(2,1)S(1)} %get-tuple-element.118), channel_id=1, source_target_pairs={{0,4},{4,0},{8,12},{12,8},{16,20},{20,16},{24,28},{28,24},{1,5},{5... | collective-permute-start | bytes 589832 | tf_op jit(solution)/shard_map/ppermute | solution.py:431
  93.4 7.4 %collective-permute-start.20 = (bf16[384,256]{1,0:T(8,128)(2,1)S(1)}, bf16[384,256]{1,0:T(8,128)(2,1)S(1)}, u32[]{:S(2)}, u32[]{:S(2)}) collective-permute-start(bf16[384,256]{1,0:T(8,128)(2,1)S(1)} %get-tuple-element.129), channel_id=1, source_target_pairs={{0,16},{4,20},{8,24},{12,28},{16,0},{20,4},{24,8},{28,12},{1,17},{... | collective-permute-start | bytes 589832 | tf_op jit(solution)/shard_map/ppermute | solution.py:431
  98.5 16.1 %collective-permute-start.27 = (bf16[288,640]{1,0:T(8,128)(2,1)S(1)}, bf16[288,640]{1,0:T(8,128)(2,1)S(1)}, u32[]{:S(2)}, u32[]{:S(2)}) collective-permute-start(bf16[288,640]{1,0:T(8,128)(2,1)S(1)} %get-tuple-element.140), channel_id=1, source_target_pairs={{0,4},{4,0},{8,12},{12,8},{16,20},{20,16},{24,28},{28,24},{1,5},{5... | collective-permute-start | bytes 1105928 | tf_op jit(solution)/shard_map/ppermute | solution.py:431
  98.6 7.1 %collective-permute-start.22 = (bf16[384,256]{1,0:T(8,128)(2,1)S(1)}, bf16[384,256]{1,0:T(8,128)(2,1)S(1)}, u32[]{:S(2)}, u32[]{:S(2)}) collective-permute-start(bf16[384,256]{1,0:T(8,128)(2,1)S(1)} %get-tuple-element.131), channel_id=1, source_target_pairs={{0,12},{4,8},{8,4},{12,0},{16,28},{20,24},{24,20},{28,16},{1,13},{... | collective-permute-start | bytes 589832 | tf_op jit(solution)/shard_map/ppermute | solution.py:431
  100.4 9.7 %collective-permute-start.19 = (bf16[384,256]{1,0:T(8,128)(2,1)S(1)}, bf16[384,256]{1,0:T(8,128)(2,1)S(1)}, u32[]{:S(2)}, u32[]{:S(2)}) collective-permute-start(bf16[384,256]{1,0:T(8,128)(2,1)S(1)} %get-tuple-element.128), channel_id=1, source_target_pairs={{0,8},{4,12},{8,0},{12,4},{16,24},{20,28},{24,16},{28,20},{1,9},{5... | collective-permute-start | bytes 589832 | tf_op jit(solution)/shard_map/ppermute | solution.py:431
  100.7 9.4 %collective-permute-start.21 = (bf16[384,256]{1,0:T(8,128)(2,1)S(1)}, bf16[384,256]{1,0:T(8,128)(2,1)S(1)}, u32[]{:S(2)}, u32[]{:S(2)}) collective-permute-start(bf16[384,256]{1,0:T(8,128)(2,1)S(1)} %get-tuple-element.130), channel_id=1, source_target_pairs={{0,4},{4,0},{8,12},{12,8},{16,20},{20,16},{24,28},{28,24},{1,5},{5... | collective-permute-start | bytes 589832 | tf_op jit(solution)/shard_map/ppermute | solution.py:431
  100.7 9.4 %collective-permute-start.23 = (bf16[384,256]{1,0:T(8,128)(2,1)S(1)}, bf16[384,256]{1,0:T(8,128)(2,1)S(1)}, u32[]{:S(2)}, u32[]{:S(2)}) collective-permute-start(bf16[384,256]{1,0:T(8,128)(2,1)S(1)} %get-tuple-element.132), channel_id=1, source_target_pairs={{0,20},{4,16},{8,28},{12,24},{16,4},{20,0},{24,12},{28,8},{1,21},{... | collective-permute-start | bytes 589832 | tf_op jit(solution)/shard_map/ppermute | solution.py:431
  110.8 6.8 %collective-permute-start.24 = (bf16[4,32,256]{2,1,0:T(8,128)(2,1)S(1)}, bf16[4,32,256]{2,1,0:T(8,128)(2,1)S(1)}, u32[]{:S(2)}, u32[]{:S(2)}) collective-permute-start(bf16[4,32,256]{2,1,0:T(8,128)(2,1)S(1)} %get-tuple-element.134), channel_id=1, source_target_pairs={{0,1},{1,2},{2,3},{3,0},{4,5},{5,6},{6,7},{7,4},{8,9},{9,10},{10,1... | collective-permute-start | bytes 196616 | tf_op jit(solution)/shard_map/ppermute | solution.py:607
  110.8 8.1 %collective-permute-start.25 = (bf16[4,32,256]{2,1,0:T(8,128)(2,1)S(1)}, bf16[4,32,256]{2,1,0:T(8,128)(2,1)S(1)}, u32[]{:S(2)}, u32[]{:S(2)}) collective-permute-start(bf16[4,32,256]{2,1,0:T(8,128)(2,1)S(1)} %get-tuple-element.135), channel_id=1, source_target_pairs={{0,2},{1,3},{2,0},{3,1},{4,6},{5,7},{6,4},{7,5},{8,10},{9,11},{10,... | collective-permute-start | bytes 196616 | tf_op jit(solution)/shard_map/ppermute | solution.py:607
  110.9 8.0 %collective-permute-start.26 = (bf16[4,32,256]{2,1,0:T(8,128)(2,1)S(1)}, bf16[4,32,256]{2,1,0:T(8,128)(2,1)S(1)}, u32[]{:S(2)}, u32[]{:S(2)}) collective-permute-start(bf16[4,32,256]{2,1,0:T(8,128)(2,1)S(1)} %get-tuple-element.136), channel_id=1, source_target_pairs={{0,3},{1,0},{2,1},{3,2},{4,7},{5,4},{6,5},{7,6},{8,11},{9,8},{10,9... | collective-permute-start | bytes 196616 | tf_op jit(solution)/shard_map/ppermute | solution.py:607
  (8 other events, 7.8 us)

commit v3 on v2

--- a/solution.py
+++ b/solution.py
@@ -25,10 +25,12 @@
 BF16 = jnp.bfloat16
 VMEM = pl.BlockSpec(memory_space=pltpu.VMEM)
 SMEM = pl.BlockSpec(memory_space=pltpu.SMEM)
+HBM = pl.BlockSpec(memory_space=pltpu.HBM)
 
 
 VMEM_MIB = 40
 SMALL_MIB = 24
+LARGE_MIB = 58
 
 
 def params(mib):
@@ -68,10 +70,22 @@
     return owner * LOCAL_HEADS + local
 
 
-def prepare_keys(place, pk, pv, rk, rv, mine0, theirs0, mine1, theirs, token):
+def fetch(pairs, sems):
+    copies = [pltpu.make_async_copy(src, dst, sems.at[i]) for i, (src, dst) in enumerate(pairs)]
+    for copy in copies:
+        copy.start()
+    return copies
+
+
+def prepare_keys(place, pk, pv, rk, rv, mine0, theirs0, mine1, theirs, token, *scratch):
     core = place[1]
+    bufs, sems = scratch[:-1], scratch[-1]
+    copies = fetch(zip((pk, pv, rk, rv), bufs), sems)
     prompt = pk.shape[0]
     order = sorting(rk.shape[0])
+    for copy in copies:
+        copy.wait()
+    pk, pv, rk, rv = bufs
     for local, outs in enumerate(((mine0, theirs.at[0]), (mine1, theirs.at[1]))):
         for cross, out in enumerate(outs):
             span = lanes(head_of(core, cross, local), HEAD_WIDTH)
@@ -83,8 +97,16 @@
     token[...] = jnp.zeros_like(token)
 
 
-def prepare_rows(place, token, pq, po, pg, rq, ro, rg, *outs):
+def prepare_rows(place, token, pq, po, pg, rq, ro, rg, *refs):
+    outs, bufs, sems = refs[:KEY_VALUE_HEADS], refs[KEY_VALUE_HEADS:-1], refs[-1]
+    core = place[1]
     reply = rq.shape[0]
+    sources = (pq, po, pg, rq, ro, rg)
+    pairs = []
+    for step in range(KEY_VALUE_HEADS):
+        span = lanes(head_of(core, 1 - step % CORES, step // CORES), GROUP_WIDTH)
+        pairs += [(source.at[:, span], buf.at[step]) for source, buf in zip(sources, bufs)]
+    copies = fetch(pairs, sems)
     order = sorting(reply)
     column = iota((GROUP_WIDTH, HEAD_WIDTH), 1)
     pick = (column // 3 == iota((GROUP_WIDTH, HEAD_WIDTH), 0) // HEAD_WIDTH).astype(BF16)
@@ -99,20 +121,17 @@
         part = iota(value.shape, 1) % 3
         return jnp.where(part == 0, first, jnp.where(part == 1, second, value - first - second)).astype(BF16)
 
-    def write(out):
-        out[reply:, :GROUP_WIDTH] = pq[...]
-        out[reply:, GROUP_WIDTH : 2 * GROUP_WIDTH] = pg[...]
-        out[reply:, 2 * GROUP_WIDTH :] = delta(pg[...], po[...])
-        out[:reply, :GROUP_WIDTH] = dot(order, rq[...]).astype(BF16)
-        gradient = dot(order, rg[...]).astype(BF16)
+    for step, out in enumerate(outs):
+        for copy in copies[step * len(sources) : (step + 1) * len(sources)]:
+            copy.wait()
+        pq, po, pg, rq, ro, rg = (buf[step] for buf in bufs)
+        out[reply:, :GROUP_WIDTH] = pq
+        out[reply:, GROUP_WIDTH : 2 * GROUP_WIDTH] = pg
+        out[reply:, 2 * GROUP_WIDTH :] = delta(pg, po)
+        out[:reply, :GROUP_WIDTH] = dot(order, rq).astype(BF16)
+        gradient = dot(order, rg).astype(BF16)
         out[:reply, GROUP_WIDTH : 2 * GROUP_WIDTH] = gradient
-        out[:reply, 2 * GROUP_WIDTH :] = delta(gradient, dot(order, ro[...]).astype(BF16))
-
-    for step, out in enumerate(outs):
-
-        @pl.when(pl.program_id(0) == step)
-        def _():
-            write(out)
+        out[:reply, 2 * GROUP_WIDTH :] = delta(gradient, dot(order, ro).astype(BF16))
 
 
 def attend(sizes, joint_keys, place, reply_len, reply_slot, *refs):
@@ -129,7 +148,7 @@
     query_out, refs = refs[:2], refs[2:]
     count = chips * CORES if joint_keys else chips
     keys_out, refs = refs[:count], refs[count:]
-    keys, keys_t, total, query, gradient, deltas, delta, scores, top, mass, prob, score_grad, query_grad = refs
+    keys, keys_t, total, query, gradient, deltas, delta, scores, top, mass, query_grad = refs
     chip, core, group = place[0], place[1], place[2]
 
     pick = (iota((8, HEAD_WIDTH), 1) // 3 == iota((8, HEAD_WIDTH), 0)).astype(BF16)
@@ -148,9 +167,11 @@
             keys[at : at + own_positions] = source[begin : begin + own_positions]
     total[...] = jnp.zeros_like(total)
 
+    unit = (iota((HEAD_WIDTH, HEAD_WIDTH), 0) == iota((HEAD_WIDTH, HEAD_WIDTH), 1)).astype(BF16)
+
     def transpose_block(index, carry):
         rows = pl.ds(pl.multiple_of(index * block, block), block)
-        keys_t[index] = keys[rows, :HEAD_WIDTH].astype(F32).T.astype(BF16)
+        keys_t[index] = dot(unit, keys[rows, :HEAD_WIDTH], (1, 1)).astype(BF16)
         return carry
 
     lax.fori_loop(0, keys_t.shape[0], transpose_block, 0)
@@ -175,16 +196,20 @@
     def grad_block(region, place_in, width, chunks, log_mass):
         rows = pl.ds(pl.multiple_of(region * block, block), block)
         value_rows = keys[rows, HEAD_WIDTH:]
-        all_rows = width * chunks
+        turned = keys_t[region]
+        value_sum = key_sum = None
         for chunk in range(chunks):
             span = slice(chunk * width, (chunk + 1) * width)
             p = jnp.exp2(scores[place_in, :, span] - log_mass[chunk])
             dp = dot(value_rows, gradient[span], (1, 1))
-            prob[:, span] = p.astype(BF16)
-            score_grad[:, span] = (p * (dp - delta[0:1, span])).astype(BF16)
-        total[rows, HEAD_WIDTH:] += dot(prob[:, :all_rows], gradient[:all_rows])
-        total[rows, :HEAD_WIDTH] += dot(score_grad[:, :all_rows], query[:all_rows])
-        query_grad[:, :all_rows] += dot(keys_t[region], score_grad[:, :all_rows])
+            half = (p * (dp - delta[0:1, span])).astype(BF16)
+            by_value = dot(p.astype(BF16), gradient[span])
+            by_key = dot(half, query[span])
+            value_sum = by_value if chunk == 0 else value_sum + by_value
+            key_sum = by_key if chunk == 0 else key_sum + by_key
+            query_grad[:, span] += dot(turned, half)
+        total[rows, HEAD_WIDTH:] += value_sum
+        total[rows, :HEAD_WIDTH] += key_sum
 
     def begin(all_rows):
         top[:, :all_rows] = jnp.full((8, all_rows), NEGATIVE_FLOOR, F32)
@@ -239,7 +264,12 @@
                 score_block(region_of(index), index, positions, GROUP, None)
                 return carry
 
-            lax.fori_loop(0, past, stats, 0)
+            def two_stats(index, carry):
+                stats(2 * index, carry)
+                return stats(2 * index + 1, carry)
+
+            lax.fori_loop(0, past // 2, two_stats, 0)
+            lax.fori_loop(past // 2 * 2, past, stats, 0)
             row_at = absolute(iota((1, positions), 1), own_positions)
             key_at = absolute(iota((block, 1), 0), own_positions)
             score_block(base, past, positions, GROUP, key_at > row_at)
@@ -251,7 +281,13 @@
                 grad_block(region, index, positions, GROUP, log_mass)
                 return carry
 
-            lax.fori_loop(0, past + 1, grads, 0)
+            def two_grads(index, carry):
+                grads(2 * index, carry)
+                return grads(2 * index + 1, carry)
+
+            every = past + 1
+            lax.fori_loop(0, every // 2, two_grads, 0)
+            lax.fori_loop(every // 2 * 2, every, grads, 0)
             for head in range(GROUP):
                 turned = (query_grad[:, head * positions : (head + 1) * positions].T * SCALE).astype(BF16)
                 for other in range(CORES):
@@ -433,11 +469,11 @@
     def swap(array):
         return move(array, 0, 1)
 
-    def call(kernel, name, mib, inputs, outs, scalars=1, **more):
+    def call(kernel, name, mib, inputs, outs, scalars=1, spec=VMEM, **more):
         return pl.pallas_call(
             kernel,
             out_shape=outs,
-            in_specs=[SMEM] * scalars + [VMEM] * (len(inputs) - scalars),
+            in_specs=[SMEM] * scalars + [spec] * (len(inputs) - scalars),
             out_specs=[VMEM] * len(outs),
             compiler_params=params(mib),
             name=name,
@@ -449,9 +485,15 @@
     mine0, theirs0, mine1, theirs, token = call(
         prepare_keys,
         "prepare_keys",
-        VMEM_MIB,
+        LARGE_MIB,
         (place, prompt_k, prompt_value, reply_key[0], reply_value[0]),
         [shape(*key_shape)] * 3 + [shape(LOCAL_HEADS, *key_shape), shape(8, 128, dtype=F32)],
+        spec=HBM,
+        scratch_shapes=[
+            pltpu.VMEM((rows, KEY_VALUE_HEADS * HEAD_WIDTH), BF16)
+            for rows in (prompt_keys, prompt_keys, reply_own, reply_own)
+        ]
+        + [pltpu.SemaphoreType.DMA((4,))],
     )
     blocks0 = {(0, 0): mine0, (0, 1): swap(theirs)}
     for away in range(1, 3 if relayed else chips):
@@ -466,37 +508,32 @@
     own_rows = reply_own + prompt_own
     row_width = 2 * GROUP_WIDTH + HEAD_WIDTH
 
-    def head_block(step, place):
-        owner = jnp.where(step % CORES == 0, 1 - place[1], place[1])
-        return 0, owner * LOCAL_HEADS + step // CORES
-
-    rows = pl.pallas_call(
+    rows = call(
         prepare_rows,
-        out_shape=[shape(own_rows, row_width)] * KEY_VALUE_HEADS,
-        grid_spec=pltpu.PrefetchScalarGridSpec(
-            num_scalar_prefetch=1,
-            grid=(KEY_VALUE_HEADS,),
-            in_specs=[pl.BlockSpec(memory_space=pl.ANY)]
-            + [pl.BlockSpec((prompt_own, GROUP_WIDTH), head_block)] * 3
-            + [pl.BlockSpec((reply_own, GROUP_WIDTH), head_block)] * 3,
-            out_specs=[pl.BlockSpec((own_rows, row_width), lambda step, place: (0, 0))] * KEY_VALUE_HEADS,
+        "prepare_rows",
+        LARGE_MIB,
+        (
+            place,
+            token,
+            prompt_query,
+            prompt_output,
+            prompt_output_gradient,
+            reply_query[0],
+            reply_output[0],
+            reply_output_gradient[0],
         ),
-        compiler_params=params(VMEM_MIB),
+        [shape(own_rows, row_width)] * KEY_VALUE_HEADS,
+        spec=HBM,
+        scratch_shapes=[
+            pltpu.VMEM((KEY_VALUE_HEADS, rows, GROUP_WIDTH), BF16)
+            for rows in [prompt_own] * 3 + [reply_own] * 3
+        ]
+        + [pltpu.SemaphoreType.DMA((KEY_VALUE_HEADS * 6,))],
         cost_estimate=pl.CostEstimate(
             flops=6 * reply_own * reply_own * QUERY_HEADS * HEAD_WIDTH,
             bytes_accessed=20 * reply_own * QUERY_HEADS * HEAD_WIDTH,
             transcendentals=0,
         ),
-        name="prepare_rows",
-    )(
-        place,
-        token,
-        prompt_query,
-        prompt_output,
-        prompt_output_gradient,
-        reply_query[0],
-        reply_output[0],
-        reply_output_gradient[0],
     )
 
     blocks0, rows, mine1 = lax.optimization_barrier((blocks0, rows, mine1))
@@ -540,8 +577,6 @@
                 pltpu.VMEM((slots, positions, all_rows), F32),
                 pltpu.VMEM((8, all_rows), F32),
                 pltpu.VMEM((8, all_rows), F32),
-                pltpu.VMEM((positions, all_rows), BF16),
-                pltpu.VMEM((positions, all_rows), BF16),
                 pltpu.VMEM((HEAD_WIDTH, all_rows), F32),
             ],
             cost_estimate=pl.CostEstimate(

time: 118 us -> 126 us (1.068); the launches traced: 120 us -> 126 us
  Pallas kernels: 45 us -> 55.3 us
  local copies, waits for them, and re-layouts: 10.4 us -> 1.18 us
  waiting for transfers between devices: 19.3 us -> 22.3 us
    pallas_call x9, Pallas kernels: 45 us -> 55.3 us  [call(): pl.pallas_call(kernel, out_shape=outs, in_specs=[SMEM] * scalars + [spec]...]
    unnamed x24 -> x14, local copies, waits for them, and re-layouts: 10.4 us -> 1.16 us
    ppermute x3, starting transfers between devices: 3.86 us -> 9.72 us  [on_device(): lax.ppermute(cuts[shift], 'rsp', [(g, (g + shift) % groups) for g in rang...]
    ppermute x25, starting transfers between devices: 40.6 us -> 35.9 us  [move(): return lax.ppermute(array, 'pre', pairs)]
    ppermute x25, waiting for transfers between devices: 17.5 us -> 21.1 us  [move(): return lax.ppermute(array, 'pre', pairs)]
  transfers between devices with their start and end apart: 28 -> 28, of which waited for: 7 -> 10; matrix products, arithmetic and copies ran while one was open for 0% -> 0% of each run, Pallas kernels for 36% -> 41%
where the time goes in v3:
time: 126 us
  Pallas kernels  55.3 us (44%)
  starting transfers between devices  45.6 us (36%)
  waiting for transfers between devices  22.3 us (18%)
    pallas_call x9, Pallas kernels, call(): pl.pallas_call(kernel, out_shape=outs, in_specs=[SMEM] * scalars + [spec]...  55.3 us
    ppermute x25, starting transfers between devices, move(): return lax.ppermute(array, 'pre', pairs)  35.9 us
    ppermute x25, waiting for transfers between devices, move(): return lax.ppermute(array, 'pre', pairs)  21.1 us
    ppermute x3, starting transfers between devices, on_device(): lax.ppermute(cuts[shift], 'rsp', [(g, (g + shift) % groups) for g in rang...  9.72 us
  transfers between devices with their start and end apart: 28, of which 10 were waited for; matrix products, arithmetic and copies ran while one was open for 0% of the time, Pallas kernels for 41%

profile of v3, /device:TPU:0, one launch (start us, length us, event | category | flops | bytes accessed | tf_op | source)
XLA Modules:
  0.0 125.8 jit_solution(2326526241173186476)
XLA Ops:
  1.2 3.1 %prepare_keys.1 = (bf16[384,256]{1,0:T(8,128)(2,1)}, bf16[384,256]{1,0:T(8,128)(2,1)}, bf16[384,256]{1,0:T(8,128)(2,1)}, bf16[2,384,256]{2,1,0:T(8,128)(2,1)}, f32[8,128]{1,0:T(8,128)}) custom-call(s32[3]{0:T(128)} %pad_add_fusion.place, bf16[128,512]{1,0:T(8,128)(2,1)} %pk.1, bf16[128,512]{1,0:T(8,128)(2,1)} %pv.1, bf16[256,512]{1,0:T(8,128)(2,1)} %bitcast.15, ...), custom_call_target="tpu_custom_call" | custom-call | tf_op jit(solution)/shard_map/prepare_keys/pallas_call | solution.py:473
  4.8 2.6 %collective-permute-start.1 = (bf16[384,256]{1,0:T(8,128)(2,1)}, bf16[384,256]{1,0:T(8,128)(2,1)S(1)}, u32[]{:S(2)}, u32[]{:S(2)}) collective-permute-start(bf16[384,256]{1,0:T(8,128)(2,1)} %get-tuple-element.90.refs_2_), channel_id=1, source_target_pairs={{0,8},{4,12},{8,0},{12,4},{16,24},{20,28},{24,16},{28,20},{1,9},{5... | collective-permute-start | bytes 589832 | tf_op jit(solution)/shard_map/ppermute | solution.py:467
  7.4 1.8 %collective-permute-start.3 = (bf16[384,256]{1,0:T(8,128)(2,1)}, bf16[384,256]{1,0:T(8,128)(2,1)S(1)}, u32[]{:S(2)}, u32[]{:S(2)}) collective-permute-start(bf16[384,256]{1,0:T(8,128)(2,1)} %get-tuple-element.90.refs_2_), channel_id=1, source_target_pairs={{0,16},{4,20},{8,24},{12,28},{16,0},{20,4},{24,8},{28,12},{1,17},{... | collective-permute-start | bytes 589832 | tf_op jit(solution)/shard_map/ppermute | solution.py:467
  9.3 6.5 %prepare_rows.1 = (bf16[288,1408]{1,0:T(8,128)(2,1)}, bf16[288,1408]{1,0:T(8,128)(2,1)}, bf16[288,1408]{1,0:T(8,128)(2,1)}, bf16[288,1408]{1,0:T(8,128)(2,1)}) custom-call(s32[3]{0:T(128)} %pad_add_fusion.place, f32[8,128]{1,0:T(8,128)} %get-tuple-element.82.token, bf16[32,2560]{1,0:T(8,128)(2,1)} %pq.1, bf16[32,2560]{1,0:T(8,128)(2,1)} %po.1, ...), custom_call_target="tpu_custom_call" | custom-call | flops 1006632960 | bytes 13107200 | tf_op jit(solution)/shard_map/prepare_rows/pallas_call | solution.py:473
  15.7 1.3 %collective-permute-done.2.refs_5_ = bf16[384,256]{1,0:T(8,128)(2,1)S(1)} collective-permute-done((bf16[384,256]{1,0:T(8,128)(2,1)}, bf16[384,256]{1,0:T(8,128)(2,1)S(1)}, u32[]{:S(2)}, u32[]{:S(2)}) %collective-permute-start.2) | collective-permute-done | bytes 196640 | tf_op jit(solution)/shard_map/ppermute | solution.py:467
  17.0 1.5 %collective-permute-done.4.refs_7_ = bf16[384,256]{1,0:T(8,128)(2,1)S(1)} collective-permute-done((bf16[384,256]{1,0:T(8,128)(2,1)}, bf16[384,256]{1,0:T(8,128)(2,1)S(1)}, u32[]{:S(2)}, u32[]{:S(2)}) %collective-permute-start.4) | collective-permute-done | bytes 196640 | tf_op jit(solution)/shard_map/ppermute | solution.py:467
  18.9 1.7 %collective-permute-start.6 = (bf16[384,256]{1,0:T(8,128)(2,1)S(1)}, bf16[384,256]{1,0:T(8,128)(2,1)S(1)}, u32[]{:S(2)}, u32[]{:S(2)}) collective-permute-start(bf16[384,256]{1,0:T(8,128)(2,1)S(1)} %collective-permute-done.1.refs_4_), channel_id=1, source_target_pairs={{0,16},{4,20},{8,24},{12,28},{16,0},{20,4},{24,8},{28,12},{1,17},{... | collective-permute-start | bytes 589832 | tf_op jit(solution)/shard_map/ppermute | solution.py:467
  20.6 1.5 %collective-permute-start.7 = (bf16[384,256]{1,0:T(8,128)(2,1)S(1)}, bf16[384,256]{1,0:T(8,128)(2,1)S(1)}, u32[]{:S(2)}, u32[]{:S(2)}) collective-permute-start(bf16[384,256]{1,0:T(8,128)(2,1)S(1)} %collective-permute-done.4.refs_7_), channel_id=1, source_target_pairs={{0,8},{4,12},{8,0},{12,4},{16,24},{20,28},{24,16},{28,20},{1,9},{5... | collective-permute-start | bytes 589832 | tf_op jit(solution)/shard_map/ppermute | solution.py:467
  22.2 0.6 collective-permute-start.13
  22.8 3.0 %collective-permute-done.6.refs_8_ = bf16[384,256]{1,0:T(8,128)(2,1)S(1)} collective-permute-done((bf16[384,256]{1,0:T(8,128)(2,1)S(1)}, bf16[384,256]{1,0:T(8,128)(2,1)S(1)}, u32[]{:S(2)}, u32[]{:S(2)}) %collective-permute-start.6) | collective-permute-done | bytes 196640 | tf_op jit(solution)/shard_map/ppermute | solution.py:467
  25.8 1.7 %collective-permute-start.14 = (bf16[2,384,256]{2,1,0:T(8,128)(2,1)S(1)}, bf16[2,384,256]{2,1,0:T(8,128)(2,1)S(1)}, u32[]{:S(2)}, u32[]{:S(2)}) collective-permute-start(bf16[2,384,256]{2,1,0:T(8,128)(2,1)S(1)} %pad_maximum_fusion.refs_2_), channel_id=1, source_target_pairs={{0,16},{4,20},{8,24},{12,28},{16,0},{20,4},{24,8},{28,12},{1,17},{... | collective-permute-start | bytes 1179656 | tf_op jit(solution)/shard_map/ppermute | solution.py:467
  27.5 0.9 collective-permute-done.7.refs_9_
  28.4 1.4 %collective-permute-start.15 = (bf16[2,384,256]{2,1,0:T(8,128)(2,1)S(1)}, bf16[2,384,256]{2,1,0:T(8,128)(2,1)S(1)}, u32[]{:S(2)}, u32[]{:S(2)}) collective-permute-start(bf16[2,384,256]{2,1,0:T(8,128)(2,1)S(1)} %pad_maximum_fusion.refs_2_), channel_id=1, source_target_pairs={{0,24},{4,28},{8,16},{12,20},{16,8},{20,12},{24,0},{28,4},{1,25},{... | collective-permute-start | bytes 1179656 | tf_op jit(solution)/shard_map/ppermute | solution.py:467
  29.9 1.1 copy-done.2
  31.0 20.6 %attend.2 = (bf16[288,640]{1,0:T(8,128)(2,1)S(1)}, bf16[288,640]{1,0:T(8,128)(2,1)S(1)}, bf16[2,384,256]{2,1,0:T(8,128)(2,1)S(1)}, bf16[2,384,256]{2,1,0:T(8,128...) custom-call(s32[3]{0:T(128)S(1)} %copy-done, s32[8]{0:T(128)S(1)} %copy-done.4, ...), custom_call_target="tpu_custom_call" | custom-call | flops 6710886400 | bytes 8388608 | tf_op jit(solution)/shard_map/attend/pallas_call | solution.py:473
  51.6 3.8 %collective-permute-start.8 = (bf16[2,384,256]{2,1,0:T(8,128)(2,1)S(1)}, bf16[2,384,256]{2,1,0:T(8,128)(2,1)S(1)}, u32[]{:S(2)}, u32[]{:S(2)}) collective-permute-start(bf16[2,384,256]{2,1,0:T(8,128)(2,1)S(1)} %get-tuple-element.97), channel_id=1, source_target_pairs={{0,8},{4,12},{8,0},{12,4},{16,24},{20,28},{24,16},{28,20},{1,9},{5... | collective-permute-start | bytes 1179656 | tf_op jit(solution)/shard_map/ppermute | solution.py:467
  55.4 5.2 %collective-permute-start.9 = (bf16[2,384,256]{2,1,0:T(8,128)(2,1)S(1)}, bf16[2,384,256]{2,1,0:T(8,128)(2,1)S(1)}, u32[]{:S(2)}, u32[]{:S(2)}) collective-permute-start(bf16[2,384,256]{2,1,0:T(8,128)(2,1)S(1)} %get-tuple-element.98), channel_id=1, source_target_pairs={{0,16},{4,20},{8,24},{12,28},{16,0},{20,4},{24,8},{28,12},{1,17},{... | collective-permute-start | bytes 1179656 | tf_op jit(solution)/shard_map/ppermute | solution.py:467
  60.6 1.4 %collective-permute-start.10 = (bf16[2,384,256]{2,1,0:T(8,128)(2,1)S(1)}, bf16[2,384,256]{2,1,0:T(8,128)(2,1)S(1)}, u32[]{:S(2)}, u32[]{:S(2)}) collective-permute-start(bf16[2,384,256]{2,1,0:T(8,128)(2,1)S(1)} %get-tuple-element.99), channel_id=1, source_target_pairs={{0,24},{4,28},{8,16},{12,20},{16,8},{20,12},{24,0},{28,4},{1,25},{... | collective-permute-start | bytes 1179656 | tf_op jit(solution)/shard_map/ppermute | solution.py:467
  62.1 20.5 %attend.3 = (bf16[288,640]{1,0:T(8,128)(2,1)S(1)}, bf16[288,640]{1,0:T(8,128)(2,1)S(1)}, bf16[384,256]{1,0:T(8,128)(2,1)S(1)}, bf16[384,256]{1,0:T(8,128)(2,1)S(...) custom-call(s32[3]{0:T(128)S(1)} %copy-done, ...), custom_call_target="tpu_custom_call" | custom-call | flops 6710886400 | bytes 8388608 | tf_op jit(solution)/shard_map/attend/pallas_call | solution.py:473
  82.6 9.3 %collective-permute-start.17 = (bf16[384,256]{1,0:T(8,128)(2,1)S(1)}, bf16[384,256]{1,0:T(8,128)(2,1)S(1)}, u32[]{:S(2)}, u32[]{:S(2)}) collective-permute-start(bf16[384,256]{1,0:T(8,128)(2,1)S(1)} %get-tuple-element.122), channel_id=1, source_target_pairs={{0,16},{4,20},{8,24},{12,28},{16,0},{20,4},{24,8},{28,12},{1,17},{... | collective-permute-start | bytes 589832 | tf_op jit(solution)/shard_map/ppermute | solution.py:467
  92.7 4.9 %collective-permute-done.17.refs_2_ = bf16[384,256]{1,0:T(8,128)(2,1)S(1)} collective-permute-done((bf16[384,256]{1,0:T(8,128)(2,1)S(1)}, bf16[384,256]{1,0:T(8,128)(2,1)S(1)}, u32[]{:S(2)}, u32[]{:S(2)}) %collective-permute-start.17) | collective-permute-done | bytes 196640 | tf_op jit(solution)/shard_map/ppermute | solution.py:467
  97.6 1.3 collective-permute-done.18.refs_3_
  99.5 1.7 %collective-permute-start.19 = (bf16[384,256]{1,0:T(8,128)(2,1)S(1)}, bf16[384,256]{1,0:T(8,128)(2,1)S(1)}, u32[]{:S(2)}, u32[]{:S(2)}) collective-permute-start(bf16[384,256]{1,0:T(8,128)(2,1)S(1)} %get-tuple-element.128), channel_id=1, source_target_pairs={{0,8},{4,12},{8,0},{12,4},{16,24},{20,28},{24,16},{28,20},{1,9},{5... | collective-permute-start | bytes 589832 | tf_op jit(solution)/shard_map/ppermute | solution.py:467
  101.6 1.0 collective-permute-start.23
  102.7 3.1 %collective-permute-done.22.refs_6_ = bf16[384,256]{1,0:T(8,128)(2,1)S(1)} collective-permute-done((bf16[384,256]{1,0:T(8,128)(2,1)S(1)}, bf16[384,256]{1,0:T(8,128)(2,1)S(1)}, u32[]{:S(2)}, u32[]{:S(2)}) %collective-permute-start.22) | collective-permute-done | bytes 196640 | tf_op jit(solution)/shard_map/ppermute | solution.py:467
  105.8 4.8 %collective-permute-done.19.refs_3_ = bf16[384,256]{1,0:T(8,128)(2,1)S(1)} collective-permute-done((bf16[384,256]{1,0:T(8,128)(2,1)S(1)}, bf16[384,256]{1,0:T(8,128)(2,1)S(1)}, u32[]{:S(2)}, u32[]{:S(2)}) %collective-permute-start.19) | collective-permute-done | bytes 196640 | tf_op jit(solution)/shard_map/ppermute | solution.py:467
  110.5 0.6 spread_prompt.1
  111.2 7.3 %collective-permute-start.24 = (bf16[4,32,256]{2,1,0:T(8,128)(2,1)S(1)}, bf16[4,32,256]{2,1,0:T(8,128)(2,1)S(1)}, u32[]{:S(2)}, u32[]{:S(2)}) collective-permute-start(bf16[4,32,256]{2,1,0:T(8,128)(2,1)S(1)} %get-tuple-element.134), channel_id=1, source_target_pairs={{0,1},{1,2},{2,3},{3,0},{4,5},{5,6},{6,7},{7,4},{8,9},{9,10},{10,1... | collective-permute-start | bytes 196616 | tf_op jit(solution)/shard_map/ppermute | solution.py:642
  118.5 2.4 %collective-permute-start.26 = (bf16[4,32,256]{2,1,0:T(8,128)(2,1)S(1)}, bf16[4,32,256]{2,1,0:T(8,128)(2,1)S(1)}, u32[]{:S(2)}, u32[]{:S(2)}) collective-permute-start(bf16[4,32,256]{2,1,0:T(8,128)(2,1)S(1)} %get-tuple-element.136), channel_id=1, source_target_pairs={{0,3},{1,0},{2,1},{3,2},{4,7},{5,4},{6,5},{7,6},{8,11},{9,8},{10,9... | collective-permute-start | bytes 196616 | tf_op jit(solution)/shard_map/ppermute | solution.py:642
  120.9 2.5 %finish_reply.1 = (bf16[32,2560]{1,0:T(8,128)(2,1)}, bf16[256,2560]{1,0:T(8,128)(2,1)}, bf16[256,512]{1,0:T(8,128)(2,1)}, bf16[256,512]{1,0:T(8,128)(2,1)}) custom-call(s32[3]{0:T(128)S(1)} %copy-done, f32[384,256]{1,0:T(8,128)S(1)} %get-tuple-element.117.refs_0_, bf16[384,256]{1,0:T(8,128)(2,1)S(1)} %collective-permute-done.16.refs_1_, ...), custom_call_target="tpu_custom_call" | custom-call | flops 469762048 | bytes 10485760 | tf_op jit(solution)/shard_map/finish_reply/pallas_call | solution.py:473
  123.4 1.2 collective-permute-done.25.refs_2_
  124.6 1.2 finish_prompt.1
  (50 shorter events, 3.5 us)
Async XLA Ops:
  4.3 14.2 %collective-permute-start = (bf16[2,384,256]{2,1,0:T(8,128)(2,1)}, bf16[2,384,256]{2,1,0:T(8,128)(2,1)S(1)}, u32[]{:S(2)}, u32[]{:S(2)}) collective-permute-start(bf16[2,384,256]{2,1,0:T(8,128)(2,1)} %get-tuple-element.80), channel_id=1, source_target_pairs={{0,4},{4,0},{8,12},{12,8},{16,20},{20,16},{24,28},{28,24},{1,5},{5... | collective-permute-start | bytes 1179656 | tf_op jit(solution)/shard_map/ppermute | solution.py:467
  4.8 10.9 %collective-permute-start.1 = (bf16[384,256]{1,0:T(8,128)(2,1)}, bf16[384,256]{1,0:T(8,128)(2,1)S(1)}, u32[]{:S(2)}, u32[]{:S(2)}) collective-permute-start(bf16[384,256]{1,0:T(8,128)(2,1)} %get-tuple-element.90.refs_2_), channel_id=1, source_target_pairs={{0,8},{4,12},{8,0},{12,4},{16,24},{20,28},{24,16},{28,20},{1,9},{5... | collective-permute-start | bytes 589832 | tf_op jit(solution)/shard_map/ppermute | solution.py:467
  7.4 9.7 %collective-permute-start.2 = (bf16[384,256]{1,0:T(8,128)(2,1)}, bf16[384,256]{1,0:T(8,128)(2,1)S(1)}, u32[]{:S(2)}, u32[]{:S(2)}) collective-permute-start(bf16[384,256]{1,0:T(8,128)(2,1)} %get-tuple-element.81), channel_id=1, source_target_pairs={{0,12},{4,8},{8,4},{12,0},{16,28},{20,24},{24,20},{28,16},{1,13},{... | collective-permute-start | bytes 589832 | tf_op jit(solution)/shard_map/ppermute | solution.py:467
  7.4 9.6 %collective-permute-start.3 = (bf16[384,256]{1,0:T(8,128)(2,1)}, bf16[384,256]{1,0:T(8,128)(2,1)S(1)}, u32[]{:S(2)}, u32[]{:S(2)}) collective-permute-start(bf16[384,256]{1,0:T(8,128)(2,1)} %get-tuple-element.90.refs_2_), channel_id=1, source_target_pairs={{0,16},{4,20},{8,24},{12,28},{16,0},{20,4},{24,8},{28,12},{1,17},{... | collective-permute-start | bytes 589832 | tf_op jit(solution)/shard_map/ppermute | solution.py:467
  9.2 9.3 %collective-permute-start.4 = (bf16[384,256]{1,0:T(8,128)(2,1)}, bf16[384,256]{1,0:T(8,128)(2,1)S(1)}, u32[]{:S(2)}, u32[]{:S(2)}) collective-permute-start(bf16[384,256]{1,0:T(8,128)(2,1)} %get-tuple-element.81), channel_id=1, source_target_pairs={{0,20},{4,16},{8,28},{12,24},{16,4},{20,0},{24,12},{28,8},{1,21},{... | collective-permute-start | bytes 589832 | tf_op jit(solution)/shard_map/ppermute | solution.py:467
  9.2 20.6 %copy-start = (s32[3]{0:T(128)S(1)}, s32[3]{0:T(128)}, u32[]{:S(2)}) copy-start(s32[3]{0:T(128)} %pad_add_fusion.place) | copy-start | bytes 40
  9.2 20.6 %copy-start.3 = (bf16[384,256]{1,0:T(8,128)(2,1)S(1)}, bf16[384,256]{1,0:T(8,128)(2,1)}, u32[]{:S(2)}) copy-start(bf16[384,256]{1,0:T(8,128)(2,1)} %get-tuple-element.90.refs_2_) | copy-start | bytes 589828
  9.2 20.6 %copy-start.4 = (s32[8]{0:T(128)S(1)}, s32[8]{0:T(128)}, u32[]{:S(2)}) copy-start(s32[8]{0:T(128)} %reply_len.3) | copy-start | bytes 100
  18.5 11.3 %collective-permute-start.5 = (bf16[288,1408]{1,0:T(8,128)(2,1)}, bf16[288,1408]{1,0:T(8,128)(2,1)S(1)}, u32[]{:S(2)}, u32[]{:S(2)}) collective-permute-start(bf16[288,1408]{1,0:T(8,128)(2,1)} %get-tuple-element.89), channel_id=1, source_target_pairs={{0,4},{4,0},{8,12},{12,8},{16,20},{20,16},{24,28},{28,24},{1,5},{5... | collective-permute-start | bytes 2433032 | tf_op jit(solution)/shard_map/ppermute | solution.py:467
  18.9 6.9 %collective-permute-start.6 = (bf16[384,256]{1,0:T(8,128)(2,1)S(1)}, bf16[384,256]{1,0:T(8,128)(2,1)S(1)}, u32[]{:S(2)}, u32[]{:S(2)}) collective-permute-start(bf16[384,256]{1,0:T(8,128)(2,1)S(1)} %collective-permute-done.1.refs_4_), channel_id=1, source_target_pairs={{0,16},{4,20},{8,24},{12,28},{16,0},{20,4},{24,8},{28,12},{1,17},{... | collective-permute-start | bytes 589832 | tf_op jit(solution)/shard_map/ppermute | solution.py:467
  20.6 7.8 %collective-permute-start.7 = (bf16[384,256]{1,0:T(8,128)(2,1)S(1)}, bf16[384,256]{1,0:T(8,128)(2,1)S(1)}, u32[]{:S(2)}, u32[]{:S(2)}) collective-permute-start(bf16[384,256]{1,0:T(8,128)(2,1)S(1)} %collective-permute-done.4.refs_7_), channel_id=1, source_target_pairs={{0,8},{4,12},{8,0},{12,4},{16,24},{20,28},{24,16},{28,20},{1,9},{5... | collective-permute-start | bytes 589832 | tf_op jit(solution)/shard_map/ppermute | solution.py:467
  22.1 40.0 %collective-permute-start.12 = (bf16[288,1408]{1,0:T(8,128)(2,1)}, bf16[288,1408]{1,0:T(8,128)(2,1)S(1)}, u32[]{:S(2)}, u32[]{:S(2)}) collective-permute-start(bf16[288,1408]{1,0:T(8,128)(2,1)} %get-tuple-element.102), channel_id=1, source_target_pairs={{0,4},{4,0},{8,12},{12,8},{16,20},{20,16},{24,28},{28,24},{1,5},{5... | collective-permute-start | bytes 2433032 | tf_op jit(solution)/shard_map/ppermute | solution.py:467
  22.2 39.9 %copy-start.1 = (bf16[288,1408]{1,0:T(8,128)(2,1)S(1)}, bf16[288,1408]{1,0:T(8,128)(2,1)}, u32[]{:S(2)}) copy-start(bf16[288,1408]{1,0:T(8,128)(2,1)} %get-tuple-element.101.refs_0_) | copy-start | bytes 2433028
  22.2 33.3 %collective-permute-start.13 = (bf16[2,384,256]{2,1,0:T(8,128)(2,1)S(1)}, bf16[2,384,256]{2,1,0:T(8,128)(2,1)S(1)}, u32[]{:S(2)}, u32[]{:S(2)}) collective-permute-start(bf16[2,384,256]{2,1,0:T(8,128)(2,1)S(1)} %pad_maximum_fusion.refs_2_), channel_id=1, source_target_pairs={{0,8},{4,12},{8,0},{12,4},{16,24},{20,28},{24,16},{28,20},{1,9},{5... | collective-permute-start | bytes 1179656 | tf_op jit(solution)/shard_map/ppermute | solution.py:467
  25.8 34.8 %collective-permute-start.14 = (bf16[2,384,256]{2,1,0:T(8,128)(2,1)S(1)}, bf16[2,384,256]{2,1,0:T(8,128)(2,1)S(1)}, u32[]{:S(2)}, u32[]{:S(2)}) collective-permute-start(bf16[2,384,256]{2,1,0:T(8,128)(2,1)S(1)} %pad_maximum_fusion.refs_2_), channel_id=1, source_target_pairs={{0,16},{4,20},{8,24},{12,28},{16,0},{20,4},{24,8},{28,12},{1,17},{... | collective-permute-start | bytes 1179656 | tf_op jit(solution)/shard_map/ppermute | solution.py:467
  28.4 33.6 %collective-permute-start.15 = (bf16[2,384,256]{2,1,0:T(8,128)(2,1)S(1)}, bf16[2,384,256]{2,1,0:T(8,128)(2,1)S(1)}, u32[]{:S(2)}, u32[]{:S(2)}) collective-permute-start(bf16[2,384,256]{2,1,0:T(8,128)(2,1)S(1)} %pad_maximum_fusion.refs_2_), channel_id=1, source_target_pairs={{0,24},{4,28},{8,16},{12,20},{16,8},{20,12},{24,0},{28,4},{1,25},{... | collective-permute-start | bytes 1179656 | tf_op jit(solution)/shard_map/ppermute | solution.py:467
  51.6 30.9 %collective-permute-start.8 = (bf16[2,384,256]{2,1,0:T(8,128)(2,1)S(1)}, bf16[2,384,256]{2,1,0:T(8,128)(2,1)S(1)}, u32[]{:S(2)}, u32[]{:S(2)}) collective-permute-start(bf16[2,384,256]{2,1,0:T(8,128)(2,1)S(1)} %get-tuple-element.97), channel_id=1, source_target_pairs={{0,8},{4,12},{8,0},{12,4},{16,24},{20,28},{24,16},{28,20},{1,9},{5... | collective-permute-start | bytes 1179656 | tf_op jit(solution)/shard_map/ppermute | solution.py:467
  55.4 27.1 %collective-permute-start.9 = (bf16[2,384,256]{2,1,0:T(8,128)(2,1)S(1)}, bf16[2,384,256]{2,1,0:T(8,128)(2,1)S(1)}, u32[]{:S(2)}, u32[]{:S(2)}) collective-permute-start(bf16[2,384,256]{2,1,0:T(8,128)(2,1)S(1)} %get-tuple-element.98), channel_id=1, source_target_pairs={{0,16},{4,20},{8,24},{12,28},{16,0},{20,4},{24,8},{28,12},{1,17},{... | collective-permute-start | bytes 1179656 | tf_op jit(solution)/shard_map/ppermute | solution.py:467
  60.6 22.0 %collective-permute-start.10 = (bf16[2,384,256]{2,1,0:T(8,128)(2,1)S(1)}, bf16[2,384,256]{2,1,0:T(8,128)(2,1)S(1)}, u32[]{:S(2)}, u32[]{:S(2)}) collective-permute-start(bf16[2,384,256]{2,1,0:T(8,128)(2,1)S(1)} %get-tuple-element.99), channel_id=1, source_target_pairs={{0,24},{4,28},{8,16},{12,20},{16,8},{20,12},{24,0},{28,4},{1,25},{... | collective-permute-start | bytes 1179656 | tf_op jit(solution)/shard_map/ppermute | solution.py:467
  62.0 20.5 %collective-permute-start.11 = (bf16[288,640]{1,0:T(8,128)(2,1)S(1)}, bf16[288,640]{1,0:T(8,128)(2,1)S(1)}, u32[]{:S(2)}, u32[]{:S(2)}) collective-permute-start(bf16[288,640]{1,0:T(8,128)(2,1)S(1)} %get-tuple-element.100), channel_id=1, source_target_pairs={{0,4},{4,0},{8,12},{12,8},{16,20},{20,16},{24,28},{28,24},{1,5},{5... | collective-permute-start | bytes 1105928 | tf_op jit(solution)/shard_map/ppermute | solution.py:467
  82.6 15.0 %collective-permute-start.17 = (bf16[384,256]{1,0:T(8,128)(2,1)S(1)}, bf16[384,256]{1,0:T(8,128)(2,1)S(1)}, u32[]{:S(2)}, u32[]{:S(2)}) collective-permute-start(bf16[384,256]{1,0:T(8,128)(2,1)S(1)} %get-tuple-element.122), channel_id=1, source_target_pairs={{0,16},{4,20},{8,24},{12,28},{16,0},{20,4},{24,8},{28,12},{1,17},{... | collective-permute-start | bytes 589832 | tf_op jit(solution)/shard_map/ppermute | solution.py:467
  91.9 7.0 %collective-permute-start.18 = (bf16[384,256]{1,0:T(8,128)(2,1)S(1)}, bf16[384,256]{1,0:T(8,128)(2,1)S(1)}, u32[]{:S(2)}, u32[]{:S(2)}) collective-permute-start(bf16[384,256]{1,0:T(8,128)(2,1)S(1)} %get-tuple-element.123), channel_id=1, source_target_pairs={{0,8},{4,12},{8,0},{12,4},{16,24},{20,28},{24,16},{28,20},{1,9},{5... | collective-permute-start | bytes 589832 | tf_op jit(solution)/shard_map/ppermute | solution.py:467
  92.1 9.1 %collective-permute-start.16 = (bf16[384,256]{1,0:T(8,128)(2,1)S(1)}, bf16[384,256]{1,0:T(8,128)(2,1)S(1)}, u32[]{:S(2)}, u32[]{:S(2)}) collective-permute-start(bf16[384,256]{1,0:T(8,128)(2,1)S(1)} %get-tuple-element.118), channel_id=1, source_target_pairs={{0,4},{4,0},{8,12},{12,8},{16,20},{20,16},{24,28},{28,24},{1,5},{5... | collective-permute-start | bytes 589832 | tf_op jit(solution)/shard_map/ppermute | solution.py:467
  92.3 9.3 %collective-permute-start.20 = (bf16[384,256]{1,0:T(8,128)(2,1)S(1)}, bf16[384,256]{1,0:T(8,128)(2,1)S(1)}, u32[]{:S(2)}, u32[]{:S(2)}) collective-permute-start(bf16[384,256]{1,0:T(8,128)(2,1)S(1)} %get-tuple-element.129), channel_id=1, source_target_pairs={{0,16},{4,20},{8,24},{12,28},{16,0},{20,4},{24,8},{28,12},{1,17},{... | collective-permute-start | bytes 589832 | tf_op jit(solution)/shard_map/ppermute | solution.py:467
  99.0 21.9 %collective-permute-start.27 = (bf16[288,640]{1,0:T(8,128)(2,1)S(1)}, bf16[288,640]{1,0:T(8,128)(2,1)S(1)}, u32[]{:S(2)}, u32[]{:S(2)}) collective-permute-start(bf16[288,640]{1,0:T(8,128)(2,1)S(1)} %get-tuple-element.140), channel_id=1, source_target_pairs={{0,4},{4,0},{8,12},{12,8},{16,20},{20,16},{24,28},{28,24},{1,5},{5... | collective-permute-start | bytes 1105928 | tf_op jit(solution)/shard_map/ppermute | solution.py:467
  99.1 6.7 %collective-permute-start.22 = (bf16[384,256]{1,0:T(8,128)(2,1)S(1)}, bf16[384,256]{1,0:T(8,128)(2,1)S(1)}, u32[]{:S(2)}, u32[]{:S(2)}) collective-permute-start(bf16[384,256]{1,0:T(8,128)(2,1)S(1)} %get-tuple-element.131), channel_id=1, source_target_pairs={{0,12},{4,8},{8,4},{12,0},{16,28},{20,24},{24,20},{28,16},{1,13},{... | collective-permute-start | bytes 589832 | tf_op jit(solution)/shard_map/ppermute | solution.py:467
  99.5 11.1 %collective-permute-start.19 = (bf16[384,256]{1,0:T(8,128)(2,1)S(1)}, bf16[384,256]{1,0:T(8,128)(2,1)S(1)}, u32[]{:S(2)}, u32[]{:S(2)}) collective-permute-start(bf16[384,256]{1,0:T(8,128)(2,1)S(1)} %get-tuple-element.128), channel_id=1, source_target_pairs={{0,8},{4,12},{8,0},{12,4},{16,24},{20,28},{24,16},{28,20},{1,9},{5... | collective-permute-start | bytes 589832 | tf_op jit(solution)/shard_map/ppermute | solution.py:467
  101.2 9.3 %collective-permute-start.21 = (bf16[384,256]{1,0:T(8,128)(2,1)S(1)}, bf16[384,256]{1,0:T(8,128)(2,1)S(1)}, u32[]{:S(2)}, u32[]{:S(2)}) collective-permute-start(bf16[384,256]{1,0:T(8,128)(2,1)S(1)} %get-tuple-element.130), channel_id=1, source_target_pairs={{0,4},{4,0},{8,12},{12,8},{16,20},{20,16},{24,28},{28,24},{1,5},{5... | collective-permute-start | bytes 589832 | tf_op jit(solution)/shard_map/ppermute | solution.py:467
  101.6 8.9 %collective-permute-start.23 = (bf16[384,256]{1,0:T(8,128)(2,1)S(1)}, bf16[384,256]{1,0:T(8,128)(2,1)S(1)}, u32[]{:S(2)}, u32[]{:S(2)}) collective-permute-start(bf16[384,256]{1,0:T(8,128)(2,1)S(1)} %get-tuple-element.132), channel_id=1, source_target_pairs={{0,20},{4,16},{8,28},{12,24},{16,4},{20,0},{24,12},{28,8},{1,21},{... | collective-permute-start | bytes 589832 | tf_op jit(solution)/shard_map/ppermute | solution.py:467
  111.2 12.2 %collective-permute-start.24 = (bf16[4,32,256]{2,1,0:T(8,128)(2,1)S(1)}, bf16[4,32,256]{2,1,0:T(8,128)(2,1)S(1)}, u32[]{:S(2)}, u32[]{:S(2)}) collective-permute-start(bf16[4,32,256]{2,1,0:T(8,128)(2,1)S(1)} %get-tuple-element.134), channel_id=1, source_target_pairs={{0,1},{1,2},{2,3},{3,0},{4,5},{5,6},{6,7},{7,4},{8,9},{9,10},{10,1... | collective-permute-start | bytes 196616 | tf_op jit(solution)/shard_map/ppermute | solution.py:642
  118.5 6.1 %collective-permute-start.25 = (bf16[4,32,256]{2,1,0:T(8,128)(2,1)S(1)}, bf16[4,32,256]{2,1,0:T(8,128)(2,1)S(1)}, u32[]{:S(2)}, u32[]{:S(2)}) collective-permute-start(bf16[4,32,256]{2,1,0:T(8,128)(2,1)S(1)} %get-tuple-element.135), channel_id=1, source_target_pairs={{0,2},{1,3},{2,0},{3,1},{4,6},{5,7},{6,4},{7,5},{8,10},{9,11},{10,... | collective-permute-start | bytes 196616 | tf_op jit(solution)/shard_map/ppermute | solution.py:642
  118.5 6.1 %collective-permute-start.26 = (bf16[4,32,256]{2,1,0:T(8,128)(2,1)S(1)}, bf16[4,32,256]{2,1,0:T(8,128)(2,1)S(1)}, u32[]{:S(2)}, u32[]{:S(2)}) collective-permute-start(bf16[4,32,256]{2,1,0:T(8,128)(2,1)S(1)} %get-tuple-element.136), channel_id=1, source_target_pairs={{0,3},{1,0},{2,1},{3,2},{4,7},{5,4},{6,5},{7,6},{8,11},{9,8},{10,9... | collective-permute-start | bytes 196616 | tf_op jit(solution)/shard_map/ppermute | solution.py:642
  (3 other events, 34.6 us)

commit v4 on v3

--- a/solution.py
+++ b/solution.py
@@ -148,7 +148,8 @@
     query_out, refs = refs[:2], refs[2:]
     count = chips * CORES if joint_keys else chips
     keys_out, refs = refs[:count], refs[count:]
-    keys, keys_t, total, query, gradient, deltas, delta, scores, top, mass, query_grad = refs
+    keys, keys_t, total, query, gradient, query_t, gradient_t, deltas, delta, scores, top, mass, *refs = refs
+    query_grad, stages = refs[0], (refs[1:3], refs[3:5])
     chip, core, group = place[0], place[1], place[2]
 
     pick = (iota((8, HEAD_WIDTH), 1) // 3 == iota((8, HEAD_WIDTH), 0)).astype(BF16)
@@ -181,7 +182,7 @@
         key_rows = keys[rows, :HEAD_WIDTH]
         for chunk in range(chunks):
             span = slice(chunk * width, (chunk + 1) * width)
-            value = dot(key_rows, query[span], (1, 1)) * SCALE_LOG2
+            value = dot(key_rows, query_t[:, span]) * SCALE_LOG2
             if hidden is not None:
                 value = jnp.where(hidden, NEGATIVE_FLOOR, value)
             scores[place_in, :, span] = value
@@ -193,23 +194,64 @@
                 jnp.exp2(split - now[None]), axis=0
             )
 
-    def grad_block(region, place_in, width, chunks, log_mass):
+    def weigh(region, place_in, width, chunks, log_mass, stage, earlier=None, earlier_stage=None):
         rows = pl.ds(pl.multiple_of(region * block, block), block)
         value_rows = keys[rows, HEAD_WIDTH:]
-        turned = keys_t[region]
-        value_sum = key_sum = None
         for chunk in range(chunks):
             span = slice(chunk * width, (chunk + 1) * width)
             p = jnp.exp2(scores[place_in, :, span] - log_mass[chunk])
-            dp = dot(value_rows, gradient[span], (1, 1))
-            half = (p * (dp - delta[0:1, span])).astype(BF16)
-            by_value = dot(p.astype(BF16), gradient[span])
-            by_key = dot(half, query[span])
-            value_sum = by_value if chunk == 0 else value_sum + by_value
-            key_sum = by_key if chunk == 0 else key_sum + by_key
-            query_grad[:, span] += dot(turned, half)
-        total[rows, HEAD_WIDTH:] += value_sum
-        total[rows, :HEAD_WIDTH] += key_sum
+            dp = dot(value_rows, gradient_t[:, span])
+            stage[0][:, span] = p.astype(BF16)
+            stage[1][:, span] = (p * (dp - delta[0:1, span])).astype(BF16)
+            if earlier is not None:
+                multiply(earlier, width, chunks, earlier_stage, chunk)
+        if earlier is not None:
+            for chunk in range(chunks, 3):
+                multiply(earlier, width, chunks, earlier_stage, chunk)
+
+    def multiply(region, width, chunks, stage, part):
+        rows = pl.ds(pl.multiple_of(region * block, block), block)
+        used = width * chunks
+        if part == 0:
+            total[rows, HEAD_WIDTH:] += dot(stage[0][:, :used], gradient[:used])
+        elif part == 1:
+            total[rows, :HEAD_WIDTH] += dot(stage[1][:, :used], query[:used])
+        elif part == 2:
+            query_grad[:, :used] += dot(keys_t[region], stage[1][:, :used])
+
+    def grad_blocks(count, region_of, width, chunks, log_mass):
+        first, second = stages
+
+        def later(index, stage, earlier_stage):
+            weigh(
+                region_of(index), index, width, chunks, log_mass, stage, region_of(index - 1), earlier_stage
+            )
+
+        def last(stage):
+            for part in range(3):
+                multiply(region_of(count - 1), width, chunks, stage, part)
+
+        weigh(region_of(0), 0, width, chunks, log_mass, first)
+
+        def two(index, carry):
+            later(2 * index + 1, second, first)
+            later(2 * index + 2, first, second)
+            return carry
+
+        lax.fori_loop(0, (count - 1) // 2, two, 0)
+
+        @pl.when(count % 2 == 0)
+        def _():
+            later(count - 1, second, first)
+            last(second)
+
+        @pl.when(count % 2 == 1)
+        def _():
+            last(first)
+
+    def turn(all_rows):
+        query_t[:, :all_rows] = dot(unit, query[:all_rows], (1, 1)).astype(BF16)
+        gradient_t[:, :all_rows] = dot(unit, gradient[:all_rows], (1, 1)).astype(BF16)
 
     def begin(all_rows):
         top[:, :all_rows] = jnp.full((8, all_rows), NEGATIVE_FLOOR, F32)
@@ -253,6 +295,7 @@
                                 other, head : head + 1, which * own_positions : (which + 1) * own_positions
                             ]
             begin(GROUP * positions)
+            turn(GROUP * positions)
             base = prompt_blocks + slot * chips
             past = prompt_blocks + chip
 
@@ -264,30 +307,20 @@
                 score_block(region_of(index), index, positions, GROUP, None)
                 return carry
 
-            def two_stats(index, carry):
-                stats(2 * index, carry)
-                return stats(2 * index + 1, carry)
-
-            lax.fori_loop(0, past // 2, two_stats, 0)
-            lax.fori_loop(past // 2 * 2, past, stats, 0)
+            lax.fori_loop(0, past, stats, 0)
             row_at = absolute(iota((1, positions), 1), own_positions)
             key_at = absolute(iota((block, 1), 0), own_positions)
             score_block(base, past, positions, GROUP, key_at > row_at)
             live = first + row_at < length
             log_mass = log_masses(positions, GROUP, live)
 
-            def grads(index, carry):
-                region = jnp.where(index == past, base, region_of(index))
-                grad_block(region, index, positions, GROUP, log_mass)
-                return carry
-
-            def two_grads(index, carry):
-                grads(2 * index, carry)
-                return grads(2 * index + 1, carry)
-
-            every = past + 1
-            lax.fori_loop(0, every // 2, two_grads, 0)
-            lax.fori_loop(every // 2 * 2, every, grads, 0)
+            grad_blocks(
+                past + 1,
+                lambda index: jnp.where(index == past, base, region_of(index)),
+                positions,
+                GROUP,
+                log_mass,
+            )
             for head in range(GROUP):
                 turned = (query_grad[:, head * positions : (head + 1) * positions].T * SCALE).astype(BF16)
                 for other in range(CORES):
@@ -321,6 +354,7 @@
             gradient[to] = rows_in[other][reply_own:, right]
             delta[0:1, to] = deltas[other, head : head + 1, reply_own:]
     begin(all_rows)
+    turn(all_rows)
     lane = iota((1, all_rows), 1)
     within = lane
     for head in range(1, GROUP):
@@ -345,11 +379,7 @@
     lax.fori_loop(0, seen, prompt_stats, 0)
     log_mass = log_masses(all_rows, 1, real)
 
-    def prompt_grads(index, carry):
-        grad_block(prompt_region(index), index, all_rows, 1, log_mass)
-        return carry
-
-    lax.fori_loop(0, seen, prompt_grads, 0)
+    grad_blocks(seen, prompt_region, all_rows, 1, log_mass)
     turned = (query_grad[:, :all_rows].T * SCALE).astype(BF16)
     for head in range(GROUP):
         for other in range(CORES):
@@ -572,13 +602,16 @@
                 pltpu.VMEM((blocks * positions, 2 * HEAD_WIDTH), F32),
                 pltpu.VMEM((all_rows, HEAD_WIDTH), BF16),
                 pltpu.VMEM((all_rows, HEAD_WIDTH), BF16),
+                pltpu.VMEM((HEAD_WIDTH, all_rows), BF16),
+                pltpu.VMEM((HEAD_WIDTH, all_rows), BF16),
                 pltpu.VMEM((CORES, 8, own_rows), F32),
                 pltpu.VMEM((8, all_rows), F32),
                 pltpu.VMEM((slots, positions, all_rows), F32),
                 pltpu.VMEM((8, all_rows), F32),
                 pltpu.VMEM((8, all_rows), F32),
                 pltpu.VMEM((HEAD_WIDTH, all_rows), F32),
-            ],
+            ]
+            + [pltpu.VMEM((positions, all_rows), BF16)] * 4,
             cost_estimate=pl.CostEstimate(
                 flops=score_count * 10 * HEAD_WIDTH,
                 bytes_accessed=8 * 1024 * 1024,

time: 126 us -> 117 us (0.929)
  Pallas kernels: 55.3 us -> 50.4 us
  waiting for transfers between devices: 22.3 us -> 17.9 us
    ppermute x3, starting transfers between devices: 9.72 us -> 18.2 us  [on_device(): lax.ppermute(cuts[shift], 'rsp', [(g, (g + shift) % groups) for g in rang...]
    ppermute x25, starting transfers between devices: 35.9 us -> 27.6 us  [move(): return lax.ppermute(array, 'pre', pairs)]
    pallas_call x9, Pallas kernels: 55.3 us -> 50.4 us  [call(): pl.pallas_call(kernel, out_shape=outs, in_specs=[SMEM] * scalars + [spec]...]
    ppermute x25, waiting for transfers between devices: 21.1 us -> 17.9 us  [move(): return lax.ppermute(array, 'pre', pairs)]
  transfers between devices with their start and end apart: 28 -> 28, of which waited for: 10 -> 8; matrix products, arithmetic and copies ran while one was open for 0% -> 0% of each run, Pallas kernels for 41% -> 40%
where the time goes in v4:
time: 117 us
  Pallas kernels  50.4 us (43%)
  starting transfers between devices  45.7 us (39%)
  waiting for transfers between devices  17.9 us (15%)
  local copies, waits for them, and re-layouts  1.18 us (1%)
    pallas_call x9, Pallas kernels, call(): pl.pallas_call(kernel, out_shape=outs, in_specs=[SMEM] * scalars + [spec]...  50.4 us
    ppermute x25, starting transfers between devices, move(): return lax.ppermute(array, 'pre', pairs)  27.6 us
    ppermute x3, starting transfers between devices, on_device(): lax.ppermute(cuts[shift], 'rsp', [(g, (g + shift) % groups) for g in rang...  18.2 us
    ppermute x25, waiting for transfers between devices, move(): return lax.ppermute(array, 'pre', pairs)  17.9 us
  transfers between devices with their start and end apart: 28, of which 8 were waited for; matrix products, arithmetic and copies ran while one was open for 0% of the time, Pallas kernels for 40%

profile of v4, /device:TPU:0, one launch (start us, length us, event | category | flops | bytes accessed | tf_op | source)
XLA Modules:
  0.0 116.7 jit_solution(17326770490493320412)
XLA Ops:
  0.6 0.6 pad_add_fusion.place
  1.2 3.1 %prepare_keys.1 = (bf16[384,256]{1,0:T(8,128)(2,1)}, bf16[384,256]{1,0:T(8,128)(2,1)}, bf16[384,256]{1,0:T(8,128)(2,1)}, bf16[2,384,256]{2,1,0:T(8,128)(2,1)}, f32[8,128]{1,0:T(8,128)}) custom-call(s32[3]{0:T(128)} %pad_add_fusion.place, bf16[128,512]{1,0:T(8,128)(2,1)} %pk.1, bf16[128,512]{1,0:T(8,128)(2,1)} %pv.1, bf16[256,512]{1,0:T(8,128)(2,1)} %bitcast.15, ...), custom_call_target="tpu_custom_call" | custom-call | tf_op jit(solution)/shard_map/prepare_keys/pallas_call | solution.py:503
  4.3 0.5 collective-permute-start
  4.8 2.6 %collective-permute-start.1 = (bf16[384,256]{1,0:T(8,128)(2,1)}, bf16[384,256]{1,0:T(8,128)(2,1)S(1)}, u32[]{:S(2)}, u32[]{:S(2)}) collective-permute-start(bf16[384,256]{1,0:T(8,128)(2,1)} %get-tuple-element.90.refs_2_), channel_id=1, source_target_pairs={{0,8},{4,12},{8,0},{12,4},{16,24},{20,28},{24,16},{28,20},{1,9},{5... | collective-permute-start | bytes 589832 | tf_op jit(solution)/shard_map/ppermute | solution.py:497
  7.4 1.8 %collective-permute-start.3 = (bf16[384,256]{1,0:T(8,128)(2,1)}, bf16[384,256]{1,0:T(8,128)(2,1)S(1)}, u32[]{:S(2)}, u32[]{:S(2)}) collective-permute-start(bf16[384,256]{1,0:T(8,128)(2,1)} %get-tuple-element.90.refs_2_), channel_id=1, source_target_pairs={{0,16},{4,20},{8,24},{12,28},{16,0},{20,4},{24,8},{28,12},{1,17},{... | collective-permute-start | bytes 589832 | tf_op jit(solution)/shard_map/ppermute | solution.py:497
  9.3 6.5 %prepare_rows.1 = (bf16[288,1408]{1,0:T(8,128)(2,1)}, bf16[288,1408]{1,0:T(8,128)(2,1)}, bf16[288,1408]{1,0:T(8,128)(2,1)}, bf16[288,1408]{1,0:T(8,128)(2,1)}) custom-call(s32[3]{0:T(128)} %pad_add_fusion.place, f32[8,128]{1,0:T(8,128)} %get-tuple-element.82.token, bf16[32,2560]{1,0:T(8,128)(2,1)} %pq.1, bf16[32,2560]{1,0:T(8,128)(2,1)} %po.1, ...), custom_call_target="tpu_custom_call" | custom-call | flops 1006632960 | bytes 13107200 | tf_op jit(solution)/shard_map/prepare_rows/pallas_call | solution.py:503
  15.7 1.3 %collective-permute-done.2.refs_5_ = bf16[384,256]{1,0:T(8,128)(2,1)S(1)} collective-permute-done((bf16[384,256]{1,0:T(8,128)(2,1)}, bf16[384,256]{1,0:T(8,128)(2,1)S(1)}, u32[]{:S(2)}, u32[]{:S(2)}) %collective-permute-start.2) | collective-permute-done | bytes 196640 | tf_op jit(solution)/shard_map/ppermute | solution.py:497
  17.0 1.5 %collective-permute-done.4.refs_7_ = bf16[384,256]{1,0:T(8,128)(2,1)S(1)} collective-permute-done((bf16[384,256]{1,0:T(8,128)(2,1)}, bf16[384,256]{1,0:T(8,128)(2,1)S(1)}, u32[]{:S(2)}, u32[]{:S(2)}) %collective-permute-start.4) | collective-permute-done | bytes 196640 | tf_op jit(solution)/shard_map/ppermute | solution.py:497
  18.9 1.7 %collective-permute-start.6 = (bf16[384,256]{1,0:T(8,128)(2,1)S(1)}, bf16[384,256]{1,0:T(8,128)(2,1)S(1)}, u32[]{:S(2)}, u32[]{:S(2)}) collective-permute-start(bf16[384,256]{1,0:T(8,128)(2,1)S(1)} %collective-permute-done.1.refs_4_), channel_id=1, source_target_pairs={{0,16},{4,20},{8,24},{12,28},{16,0},{20,4},{24,8},{28,12},{1,17},{... | collective-permute-start | bytes 589832 | tf_op jit(solution)/shard_map/ppermute | solution.py:497
  20.6 1.5 %collective-permute-start.7 = (bf16[384,256]{1,0:T(8,128)(2,1)S(1)}, bf16[384,256]{1,0:T(8,128)(2,1)S(1)}, u32[]{:S(2)}, u32[]{:S(2)}) collective-permute-start(bf16[384,256]{1,0:T(8,128)(2,1)S(1)} %collective-permute-done.4.refs_7_), channel_id=1, source_target_pairs={{0,8},{4,12},{8,0},{12,4},{16,24},{20,28},{24,16},{28,20},{1,9},{5... | collective-permute-start | bytes 589832 | tf_op jit(solution)/shard_map/ppermute | solution.py:497
  22.2 0.6 collective-permute-start.13
  22.8 3.0 %collective-permute-done.6.refs_8_ = bf16[384,256]{1,0:T(8,128)(2,1)S(1)} collective-permute-done((bf16[384,256]{1,0:T(8,128)(2,1)S(1)}, bf16[384,256]{1,0:T(8,128)(2,1)S(1)}, u32[]{:S(2)}, u32[]{:S(2)}) %collective-permute-start.6) | collective-permute-done | bytes 196640 | tf_op jit(solution)/shard_map/ppermute | solution.py:497
  25.8 1.7 %collective-permute-start.14 = (bf16[2,384,256]{2,1,0:T(8,128)(2,1)S(1)}, bf16[2,384,256]{2,1,0:T(8,128)(2,1)S(1)}, u32[]{:S(2)}, u32[]{:S(2)}) collective-permute-start(bf16[2,384,256]{2,1,0:T(8,128)(2,1)S(1)} %pad_maximum_fusion.refs_2_), channel_id=1, source_target_pairs={{0,16},{4,20},{8,24},{12,28},{16,0},{20,4},{24,8},{28,12},{1,17},{... | collective-permute-start | bytes 1179656 | tf_op jit(solution)/shard_map/ppermute | solution.py:497
  27.5 0.9 collective-permute-done.7.refs_9_
  28.4 1.4 %collective-permute-start.15 = (bf16[2,384,256]{2,1,0:T(8,128)(2,1)S(1)}, bf16[2,384,256]{2,1,0:T(8,128)(2,1)S(1)}, u32[]{:S(2)}, u32[]{:S(2)}) collective-permute-start(bf16[2,384,256]{2,1,0:T(8,128)(2,1)S(1)} %pad_maximum_fusion.refs_2_), channel_id=1, source_target_pairs={{0,24},{4,28},{8,16},{12,20},{16,8},{20,12},{24,0},{28,4},{1,25},{... | collective-permute-start | bytes 1179656 | tf_op jit(solution)/shard_map/ppermute | solution.py:497
  29.9 1.1 copy-done.2
  31.0 18.2 %attend.2 = (bf16[288,640]{1,0:T(8,128)(2,1)S(1)}, bf16[288,640]{1,0:T(8,128)(2,1)S(1)}, bf16[2,384,256]{2,1,0:T(8,128)(2,1)S(1)}, bf16[2,384,256]{2,1,0:T(8,128...) custom-call(s32[3]{0:T(128)S(1)} %copy-done, s32[8]{0:T(128)S(1)} %copy-done.4, ...), custom_call_target="tpu_custom_call" | custom-call | flops 6710886400 | bytes 8388608 | tf_op jit(solution)/shard_map/attend/pallas_call | solution.py:503
  49.2 3.0 %collective-permute-start.8 = (bf16[2,384,256]{2,1,0:T(8,128)(2,1)S(1)}, bf16[2,384,256]{2,1,0:T(8,128)(2,1)S(1)}, u32[]{:S(2)}, u32[]{:S(2)}) collective-permute-start(bf16[2,384,256]{2,1,0:T(8,128)(2,1)S(1)} %get-tuple-element.97), channel_id=1, source_target_pairs={{0,8},{4,12},{8,0},{12,4},{16,24},{20,28},{24,16},{28,20},{1,9},{5... | collective-permute-start | bytes 1179656 | tf_op jit(solution)/shard_map/ppermute | solution.py:497
  52.2 1.5 %collective-permute-start.10 = (bf16[2,384,256]{2,1,0:T(8,128)(2,1)S(1)}, bf16[2,384,256]{2,1,0:T(8,128)(2,1)S(1)}, u32[]{:S(2)}, u32[]{:S(2)}) collective-permute-start(bf16[2,384,256]{2,1,0:T(8,128)(2,1)S(1)} %get-tuple-element.99), channel_id=1, source_target_pairs={{0,24},{4,28},{8,16},{12,20},{16,8},{20,12},{24,0},{28,4},{1,25},{... | collective-permute-start | bytes 1179656 | tf_op jit(solution)/shard_map/ppermute | solution.py:497
  53.8 18.0 %attend.3 = (bf16[288,640]{1,0:T(8,128)(2,1)S(1)}, bf16[288,640]{1,0:T(8,128)(2,1)S(1)}, bf16[384,256]{1,0:T(8,128)(2,1)S(1)}, bf16[384,256]{1,0:T(8,128)(2,1)S(...) custom-call(s32[3]{0:T(128)S(1)} %copy-done, ...), custom_call_target="tpu_custom_call" | custom-call | flops 6710886400 | bytes 8388608 | tf_op jit(solution)/shard_map/attend/pallas_call | solution.py:503
  71.9 4.6 %collective-permute-start.18 = (bf16[384,256]{1,0:T(8,128)(2,1)S(1)}, bf16[384,256]{1,0:T(8,128)(2,1)S(1)}, u32[]{:S(2)}, u32[]{:S(2)}) collective-permute-start(bf16[384,256]{1,0:T(8,128)(2,1)S(1)} %get-tuple-element.123), channel_id=1, source_target_pairs={{0,8},{4,12},{8,0},{12,4},{16,24},{20,28},{24,16},{28,20},{1,9},{5... | collective-permute-start | bytes 589832 | tf_op jit(solution)/shard_map/ppermute | solution.py:497
  77.0 1.8 %collective-permute-start.20 = (bf16[384,256]{1,0:T(8,128)(2,1)S(1)}, bf16[384,256]{1,0:T(8,128)(2,1)S(1)}, u32[]{:S(2)}, u32[]{:S(2)}) collective-permute-start(bf16[384,256]{1,0:T(8,128)(2,1)S(1)} %get-tuple-element.129), channel_id=1, source_target_pairs={{0,16},{4,20},{8,24},{12,28},{16,0},{20,4},{24,8},{28,12},{1,17},{... | collective-permute-start | bytes 589832 | tf_op jit(solution)/shard_map/ppermute | solution.py:497
  79.2 2.9 %collective-permute-done.18.refs_3_ = bf16[384,256]{1,0:T(8,128)(2,1)S(1)} collective-permute-done((bf16[384,256]{1,0:T(8,128)(2,1)S(1)}, bf16[384,256]{1,0:T(8,128)(2,1)S(1)}, u32[]{:S(2)}, u32[]{:S(2)}) %collective-permute-start.18) | collective-permute-done | bytes 196640 | tf_op jit(solution)/shard_map/ppermute | solution.py:497
  82.3 2.2 %collective-permute-start.22 = (bf16[384,256]{1,0:T(8,128)(2,1)S(1)}, bf16[384,256]{1,0:T(8,128)(2,1)S(1)}, u32[]{:S(2)}, u32[]{:S(2)}) collective-permute-start(bf16[384,256]{1,0:T(8,128)(2,1)S(1)} %get-tuple-element.131), channel_id=1, source_target_pairs={{0,12},{4,8},{8,4},{12,0},{16,28},{20,24},{24,20},{28,16},{1,13},{... | collective-permute-start | bytes 589832 | tf_op jit(solution)/shard_map/ppermute | solution.py:497
  84.6 1.6 %collective-permute-start.23 = (bf16[384,256]{1,0:T(8,128)(2,1)S(1)}, bf16[384,256]{1,0:T(8,128)(2,1)S(1)}, u32[]{:S(2)}, u32[]{:S(2)}) collective-permute-start(bf16[384,256]{1,0:T(8,128)(2,1)S(1)} %get-tuple-element.132), channel_id=1, source_target_pairs={{0,20},{4,16},{8,28},{12,24},{16,4},{20,0},{24,12},{28,8},{1,21},{... | collective-permute-start | bytes 589832 | tf_op jit(solution)/shard_map/ppermute | solution.py:497
  86.2 3.5 %collective-permute-done.22.refs_6_ = bf16[384,256]{1,0:T(8,128)(2,1)S(1)} collective-permute-done((bf16[384,256]{1,0:T(8,128)(2,1)S(1)}, bf16[384,256]{1,0:T(8,128)(2,1)S(1)}, u32[]{:S(2)}, u32[]{:S(2)}) %collective-permute-start.22) | collective-permute-done | bytes 196640 | tf_op jit(solution)/shard_map/ppermute | solution.py:497
  89.7 4.4 %collective-permute-done.19.refs_3_ = bf16[384,256]{1,0:T(8,128)(2,1)S(1)} collective-permute-done((bf16[384,256]{1,0:T(8,128)(2,1)S(1)}, bf16[384,256]{1,0:T(8,128)(2,1)S(1)}, u32[]{:S(2)}, u32[]{:S(2)}) %collective-permute-start.19) | collective-permute-done | bytes 196640 | tf_op jit(solution)/shard_map/ppermute | solution.py:497
  94.1 0.6 spread_prompt.1
  94.9 15.3 %collective-permute-start.25 = (bf16[4,32,256]{2,1,0:T(8,128)(2,1)S(1)}, bf16[4,32,256]{2,1,0:T(8,128)(2,1)S(1)}, u32[]{:S(2)}, u32[]{:S(2)}) collective-permute-start(bf16[4,32,256]{2,1,0:T(8,128)(2,1)S(1)} %get-tuple-element.135), channel_id=1, source_target_pairs={{0,2},{1,3},{2,0},{3,1},{4,6},{5,7},{6,4},{7,5},{8,10},{9,11},{10,... | collective-permute-start | bytes 196616 | tf_op jit(solution)/shard_map/ppermute | solution.py:675
  110.1 2.8 %collective-permute-start.26 = (bf16[4,32,256]{2,1,0:T(8,128)(2,1)S(1)}, bf16[4,32,256]{2,1,0:T(8,128)(2,1)S(1)}, u32[]{:S(2)}, u32[]{:S(2)}) collective-permute-start(bf16[4,32,256]{2,1,0:T(8,128)(2,1)S(1)} %get-tuple-element.136), channel_id=1, source_target_pairs={{0,3},{1,0},{2,1},{3,2},{4,7},{5,4},{6,5},{7,6},{8,11},{9,8},{10,9... | collective-permute-start | bytes 196616 | tf_op jit(solution)/shard_map/ppermute | solution.py:675
  113.0 2.5 %finish_reply.1 = (bf16[32,2560]{1,0:T(8,128)(2,1)}, bf16[256,2560]{1,0:T(8,128)(2,1)}, bf16[256,512]{1,0:T(8,128)(2,1)}, bf16[256,512]{1,0:T(8,128)(2,1)}) custom-call(s32[3]{0:T(128)S(1)} %copy-done, f32[384,256]{1,0:T(8,128)S(1)} %get-tuple-element.117.refs_0_, bf16[384,256]{1,0:T(8,128)(2,1)S(1)} %collective-permute-done.16.refs_1_, ...), custom_call_target="tpu_custom_call" | custom-call | flops 469762048 | bytes 10485760 | tf_op jit(solution)/shard_map/finish_reply/pallas_call | solution.py:503
  115.5 1.2 %finish_prompt.1 = (bf16[32,512]{1,0:T(8,128)(2,1)}, bf16[32,512]{1,0:T(8,128)(2,1)}) custom-call(s32[3]{0:T(128)S(1)} %copy-done, bf16[4,32,256]{2,1,0:T(8,128)(2,1)S(1)} %get-tuple-element.143.refs_0_, bf16[4,32,256]{2,1,0:T(8,128)(2,1)S(1)} %collective-permute-done.24.refs_1_, bf16[4,32,256]{2,1,0:T(8,128)(2,1)S(1)} %collective-permute-done.25.refs_2_, ...), custom_call_target="tpu_custom_call" | custom-call | tf_op jit(solution)/shard_map/finish_prompt/pallas_call | solution.py:503
  (50 shorter events, 1.8 us)
Async XLA Ops:
  4.3 14.2 %collective-permute-start = (bf16[2,384,256]{2,1,0:T(8,128)(2,1)}, bf16[2,384,256]{2,1,0:T(8,128)(2,1)S(1)}, u32[]{:S(2)}, u32[]{:S(2)}) collective-permute-start(bf16[2,384,256]{2,1,0:T(8,128)(2,1)} %get-tuple-element.80), channel_id=1, source_target_pairs={{0,4},{4,0},{8,12},{12,8},{16,20},{20,16},{24,28},{28,24},{1,5},{5... | collective-permute-start | bytes 1179656 | tf_op jit(solution)/shard_map/ppermute | solution.py:497
  4.8 10.9 %collective-permute-start.1 = (bf16[384,256]{1,0:T(8,128)(2,1)}, bf16[384,256]{1,0:T(8,128)(2,1)S(1)}, u32[]{:S(2)}, u32[]{:S(2)}) collective-permute-start(bf16[384,256]{1,0:T(8,128)(2,1)} %get-tuple-element.90.refs_2_), channel_id=1, source_target_pairs={{0,8},{4,12},{8,0},{12,4},{16,24},{20,28},{24,16},{28,20},{1,9},{5... | collective-permute-start | bytes 589832 | tf_op jit(solution)/shard_map/ppermute | solution.py:497
  7.4 9.7 %collective-permute-start.2 = (bf16[384,256]{1,0:T(8,128)(2,1)}, bf16[384,256]{1,0:T(8,128)(2,1)S(1)}, u32[]{:S(2)}, u32[]{:S(2)}) collective-permute-start(bf16[384,256]{1,0:T(8,128)(2,1)} %get-tuple-element.81), channel_id=1, source_target_pairs={{0,12},{4,8},{8,4},{12,0},{16,28},{20,24},{24,20},{28,16},{1,13},{... | collective-permute-start | bytes 589832 | tf_op jit(solution)/shard_map/ppermute | solution.py:497
  7.4 9.6 %collective-permute-start.3 = (bf16[384,256]{1,0:T(8,128)(2,1)}, bf16[384,256]{1,0:T(8,128)(2,1)S(1)}, u32[]{:S(2)}, u32[]{:S(2)}) collective-permute-start(bf16[384,256]{1,0:T(8,128)(2,1)} %get-tuple-element.90.refs_2_), channel_id=1, source_target_pairs={{0,16},{4,20},{8,24},{12,28},{16,0},{20,4},{24,8},{28,12},{1,17},{... | collective-permute-start | bytes 589832 | tf_op jit(solution)/shard_map/ppermute | solution.py:497
  9.2 9.3 %collective-permute-start.4 = (bf16[384,256]{1,0:T(8,128)(2,1)}, bf16[384,256]{1,0:T(8,128)(2,1)S(1)}, u32[]{:S(2)}, u32[]{:S(2)}) collective-permute-start(bf16[384,256]{1,0:T(8,128)(2,1)} %get-tuple-element.81), channel_id=1, source_target_pairs={{0,20},{4,16},{8,28},{12,24},{16,4},{20,0},{24,12},{28,8},{1,21},{... | collective-permute-start | bytes 589832 | tf_op jit(solution)/shard_map/ppermute | solution.py:497
  9.2 20.6 %copy-start = (s32[3]{0:T(128)S(1)}, s32[3]{0:T(128)}, u32[]{:S(2)}) copy-start(s32[3]{0:T(128)} %pad_add_fusion.place) | copy-start | bytes 40
  9.2 20.6 %copy-start.3 = (bf16[384,256]{1,0:T(8,128)(2,1)S(1)}, bf16[384,256]{1,0:T(8,128)(2,1)}, u32[]{:S(2)}) copy-start(bf16[384,256]{1,0:T(8,128)(2,1)} %get-tuple-element.90.refs_2_) | copy-start | bytes 589828
  9.2 20.6 %copy-start.4 = (s32[8]{0:T(128)S(1)}, s32[8]{0:T(128)}, u32[]{:S(2)}) copy-start(s32[8]{0:T(128)} %reply_len.3) | copy-start | bytes 100
  18.5 11.3 %collective-permute-start.5 = (bf16[288,1408]{1,0:T(8,128)(2,1)}, bf16[288,1408]{1,0:T(8,128)(2,1)S(1)}, u32[]{:S(2)}, u32[]{:S(2)}) collective-permute-start(bf16[288,1408]{1,0:T(8,128)(2,1)} %get-tuple-element.89), channel_id=1, source_target_pairs={{0,4},{4,0},{8,12},{12,8},{16,20},{20,16},{24,28},{28,24},{1,5},{5... | collective-permute-start | bytes 2433032 | tf_op jit(solution)/shard_map/ppermute | solution.py:497
  18.9 6.9 %collective-permute-start.6 = (bf16[384,256]{1,0:T(8,128)(2,1)S(1)}, bf16[384,256]{1,0:T(8,128)(2,1)S(1)}, u32[]{:S(2)}, u32[]{:S(2)}) collective-permute-start(bf16[384,256]{1,0:T(8,128)(2,1)S(1)} %collective-permute-done.1.refs_4_), channel_id=1, source_target_pairs={{0,16},{4,20},{8,24},{12,28},{16,0},{20,4},{24,8},{28,12},{1,17},{... | collective-permute-start | bytes 589832 | tf_op jit(solution)/shard_map/ppermute | solution.py:497
  20.6 7.8 %collective-permute-start.7 = (bf16[384,256]{1,0:T(8,128)(2,1)S(1)}, bf16[384,256]{1,0:T(8,128)(2,1)S(1)}, u32[]{:S(2)}, u32[]{:S(2)}) collective-permute-start(bf16[384,256]{1,0:T(8,128)(2,1)S(1)} %collective-permute-done.4.refs_7_), channel_id=1, source_target_pairs={{0,8},{4,12},{8,0},{12,4},{16,24},{20,28},{24,16},{28,20},{1,9},{5... | collective-permute-start | bytes 589832 | tf_op jit(solution)/shard_map/ppermute | solution.py:497
  22.1 31.7 %collective-permute-start.12 = (bf16[288,1408]{1,0:T(8,128)(2,1)}, bf16[288,1408]{1,0:T(8,128)(2,1)S(1)}, u32[]{:S(2)}, u32[]{:S(2)}) collective-permute-start(bf16[288,1408]{1,0:T(8,128)(2,1)} %get-tuple-element.102), channel_id=1, source_target_pairs={{0,4},{4,0},{8,12},{12,8},{16,20},{20,16},{24,28},{28,24},{1,5},{5... | collective-permute-start | bytes 2433032 | tf_op jit(solution)/shard_map/ppermute | solution.py:497
  22.2 31.6 %copy-start.1 = (bf16[288,1408]{1,0:T(8,128)(2,1)S(1)}, bf16[288,1408]{1,0:T(8,128)(2,1)}, u32[]{:S(2)}) copy-start(bf16[288,1408]{1,0:T(8,128)(2,1)} %get-tuple-element.101.refs_0_) | copy-start | bytes 2433028
  22.2 30.0 %collective-permute-start.13 = (bf16[2,384,256]{2,1,0:T(8,128)(2,1)S(1)}, bf16[2,384,256]{2,1,0:T(8,128)(2,1)S(1)}, u32[]{:S(2)}, u32[]{:S(2)}) collective-permute-start(bf16[2,384,256]{2,1,0:T(8,128)(2,1)S(1)} %pad_maximum_fusion.refs_2_), channel_id=1, source_target_pairs={{0,8},{4,12},{8,0},{12,4},{16,24},{20,28},{24,16},{28,20},{1,9},{5... | collective-permute-start | bytes 1179656 | tf_op jit(solution)/shard_map/ppermute | solution.py:497
  25.8 26.4 %collective-permute-start.14 = (bf16[2,384,256]{2,1,0:T(8,128)(2,1)S(1)}, bf16[2,384,256]{2,1,0:T(8,128)(2,1)S(1)}, u32[]{:S(2)}, u32[]{:S(2)}) collective-permute-start(bf16[2,384,256]{2,1,0:T(8,128)(2,1)S(1)} %pad_maximum_fusion.refs_2_), channel_id=1, source_target_pairs={{0,16},{4,20},{8,24},{12,28},{16,0},{20,4},{24,8},{28,12},{1,17},{... | collective-permute-start | bytes 1179656 | tf_op jit(solution)/shard_map/ppermute | solution.py:497
  28.4 25.4 %collective-permute-start.15 = (bf16[2,384,256]{2,1,0:T(8,128)(2,1)S(1)}, bf16[2,384,256]{2,1,0:T(8,128)(2,1)S(1)}, u32[]{:S(2)}, u32[]{:S(2)}) collective-permute-start(bf16[2,384,256]{2,1,0:T(8,128)(2,1)S(1)} %pad_maximum_fusion.refs_2_), channel_id=1, source_target_pairs={{0,24},{4,28},{8,16},{12,20},{16,8},{20,12},{24,0},{28,4},{1,25},{... | collective-permute-start | bytes 1179656 | tf_op jit(solution)/shard_map/ppermute | solution.py:497
  49.2 22.6 %collective-permute-start.8 = (bf16[2,384,256]{2,1,0:T(8,128)(2,1)S(1)}, bf16[2,384,256]{2,1,0:T(8,128)(2,1)S(1)}, u32[]{:S(2)}, u32[]{:S(2)}) collective-permute-start(bf16[2,384,256]{2,1,0:T(8,128)(2,1)S(1)} %get-tuple-element.97), channel_id=1, source_target_pairs={{0,8},{4,12},{8,0},{12,4},{16,24},{20,28},{24,16},{28,20},{1,9},{5... | collective-permute-start | bytes 1179656 | tf_op jit(solution)/shard_map/ppermute | solution.py:497
  52.2 19.6 %collective-permute-start.9 = (bf16[2,384,256]{2,1,0:T(8,128)(2,1)S(1)}, bf16[2,384,256]{2,1,0:T(8,128)(2,1)S(1)}, u32[]{:S(2)}, u32[]{:S(2)}) collective-permute-start(bf16[2,384,256]{2,1,0:T(8,128)(2,1)S(1)} %get-tuple-element.98), channel_id=1, source_target_pairs={{0,16},{4,20},{8,24},{12,28},{16,0},{20,4},{24,8},{28,12},{1,17},{... | collective-permute-start | bytes 1179656 | tf_op jit(solution)/shard_map/ppermute | solution.py:497
  52.2 19.6 %collective-permute-start.10 = (bf16[2,384,256]{2,1,0:T(8,128)(2,1)S(1)}, bf16[2,384,256]{2,1,0:T(8,128)(2,1)S(1)}, u32[]{:S(2)}, u32[]{:S(2)}) collective-permute-start(bf16[2,384,256]{2,1,0:T(8,128)(2,1)S(1)} %get-tuple-element.99), channel_id=1, source_target_pairs={{0,24},{4,28},{8,16},{12,20},{16,8},{20,12},{24,0},{28,4},{1,25},{... | collective-permute-start | bytes 1179656 | tf_op jit(solution)/shard_map/ppermute | solution.py:497
  53.8 18.1 %collective-permute-start.11 = (bf16[288,640]{1,0:T(8,128)(2,1)S(1)}, bf16[288,640]{1,0:T(8,128)(2,1)S(1)}, u32[]{:S(2)}, u32[]{:S(2)}) collective-permute-start(bf16[288,640]{1,0:T(8,128)(2,1)S(1)} %get-tuple-element.100), channel_id=1, source_target_pairs={{0,4},{4,0},{8,12},{12,8},{16,20},{20,16},{24,28},{28,24},{1,5},{5... | collective-permute-start | bytes 1105928 | tf_op jit(solution)/shard_map/ppermute | solution.py:497
  71.9 7.4 %collective-permute-start.17 = (bf16[384,256]{1,0:T(8,128)(2,1)S(1)}, bf16[384,256]{1,0:T(8,128)(2,1)S(1)}, u32[]{:S(2)}, u32[]{:S(2)}) collective-permute-start(bf16[384,256]{1,0:T(8,128)(2,1)S(1)} %get-tuple-element.122), channel_id=1, source_target_pairs={{0,16},{4,20},{8,24},{12,28},{16,0},{20,4},{24,8},{28,12},{1,17},{... | collective-permute-start | bytes 589832 | tf_op jit(solution)/shard_map/ppermute | solution.py:497
  71.9 10.2 %collective-permute-start.18 = (bf16[384,256]{1,0:T(8,128)(2,1)S(1)}, bf16[384,256]{1,0:T(8,128)(2,1)S(1)}, u32[]{:S(2)}, u32[]{:S(2)}) collective-permute-start(bf16[384,256]{1,0:T(8,128)(2,1)S(1)} %get-tuple-element.123), channel_id=1, source_target_pairs={{0,8},{4,12},{8,0},{12,4},{16,24},{20,28},{24,16},{28,20},{1,9},{5... | collective-permute-start | bytes 589832 | tf_op jit(solution)/shard_map/ppermute | solution.py:497
  76.8 7.8 %collective-permute-start.16 = (bf16[384,256]{1,0:T(8,128)(2,1)S(1)}, bf16[384,256]{1,0:T(8,128)(2,1)S(1)}, u32[]{:S(2)}, u32[]{:S(2)}) collective-permute-start(bf16[384,256]{1,0:T(8,128)(2,1)S(1)} %get-tuple-element.118), channel_id=1, source_target_pairs={{0,4},{4,0},{8,12},{12,8},{16,20},{20,16},{24,28},{28,24},{1,5},{5... | collective-permute-start | bytes 589832 | tf_op jit(solution)/shard_map/ppermute | solution.py:497
  77.0 7.6 %collective-permute-start.20 = (bf16[384,256]{1,0:T(8,128)(2,1)S(1)}, bf16[384,256]{1,0:T(8,128)(2,1)S(1)}, u32[]{:S(2)}, u32[]{:S(2)}) collective-permute-start(bf16[384,256]{1,0:T(8,128)(2,1)S(1)} %get-tuple-element.129), channel_id=1, source_target_pairs={{0,16},{4,20},{8,24},{12,28},{16,0},{20,4},{24,8},{28,12},{1,17},{... | collective-permute-start | bytes 589832 | tf_op jit(solution)/shard_map/ppermute | solution.py:497
  82.2 30.8 %collective-permute-start.27 = (bf16[288,640]{1,0:T(8,128)(2,1)S(1)}, bf16[288,640]{1,0:T(8,128)(2,1)S(1)}, u32[]{:S(2)}, u32[]{:S(2)}) collective-permute-start(bf16[288,640]{1,0:T(8,128)(2,1)S(1)} %get-tuple-element.140), channel_id=1, source_target_pairs={{0,4},{4,0},{8,12},{12,8},{16,20},{20,16},{24,28},{28,24},{1,5},{5... | collective-permute-start | bytes 1105928 | tf_op jit(solution)/shard_map/ppermute | solution.py:497
  82.3 7.4 %collective-permute-start.22 = (bf16[384,256]{1,0:T(8,128)(2,1)S(1)}, bf16[384,256]{1,0:T(8,128)(2,1)S(1)}, u32[]{:S(2)}, u32[]{:S(2)}) collective-permute-start(bf16[384,256]{1,0:T(8,128)(2,1)S(1)} %get-tuple-element.131), channel_id=1, source_target_pairs={{0,12},{4,8},{8,4},{12,0},{16,28},{20,24},{24,20},{28,16},{1,13},{... | collective-permute-start | bytes 589832 | tf_op jit(solution)/shard_map/ppermute | solution.py:497
  84.5 9.7 %collective-permute-start.19 = (bf16[384,256]{1,0:T(8,128)(2,1)S(1)}, bf16[384,256]{1,0:T(8,128)(2,1)S(1)}, u32[]{:S(2)}, u32[]{:S(2)}) collective-permute-start(bf16[384,256]{1,0:T(8,128)(2,1)S(1)} %get-tuple-element.128), channel_id=1, source_target_pairs={{0,8},{4,12},{8,0},{12,4},{16,24},{20,28},{24,16},{28,20},{1,9},{5... | collective-permute-start | bytes 589832 | tf_op jit(solution)/shard_map/ppermute | solution.py:497
  84.5 9.6 %collective-permute-start.21 = (bf16[384,256]{1,0:T(8,128)(2,1)S(1)}, bf16[384,256]{1,0:T(8,128)(2,1)S(1)}, u32[]{:S(2)}, u32[]{:S(2)}) collective-permute-start(bf16[384,256]{1,0:T(8,128)(2,1)S(1)} %get-tuple-element.130), channel_id=1, source_target_pairs={{0,4},{4,0},{8,12},{12,8},{16,20},{20,16},{24,28},{28,24},{1,5},{5... | collective-permute-start | bytes 589832 | tf_op jit(solution)/shard_map/ppermute | solution.py:497
  84.6 9.5 %collective-permute-start.23 = (bf16[384,256]{1,0:T(8,128)(2,1)S(1)}, bf16[384,256]{1,0:T(8,128)(2,1)S(1)}, u32[]{:S(2)}, u32[]{:S(2)}) collective-permute-start(bf16[384,256]{1,0:T(8,128)(2,1)S(1)} %get-tuple-element.132), channel_id=1, source_target_pairs={{0,20},{4,16},{8,28},{12,24},{16,4},{20,0},{24,12},{28,8},{1,21},{... | collective-permute-start | bytes 589832 | tf_op jit(solution)/shard_map/ppermute | solution.py:497
  94.8 20.7 %collective-permute-start.24 = (bf16[4,32,256]{2,1,0:T(8,128)(2,1)S(1)}, bf16[4,32,256]{2,1,0:T(8,128)(2,1)S(1)}, u32[]{:S(2)}, u32[]{:S(2)}) collective-permute-start(bf16[4,32,256]{2,1,0:T(8,128)(2,1)S(1)} %get-tuple-element.134), channel_id=1, source_target_pairs={{0,1},{1,2},{2,3},{3,0},{4,5},{5,6},{6,7},{7,4},{8,9},{9,10},{10,1... | collective-permute-start | bytes 196616 | tf_op jit(solution)/shard_map/ppermute | solution.py:675
  94.9 20.6 %collective-permute-start.25 = (bf16[4,32,256]{2,1,0:T(8,128)(2,1)S(1)}, bf16[4,32,256]{2,1,0:T(8,128)(2,1)S(1)}, u32[]{:S(2)}, u32[]{:S(2)}) collective-permute-start(bf16[4,32,256]{2,1,0:T(8,128)(2,1)S(1)} %get-tuple-element.135), channel_id=1, source_target_pairs={{0,2},{1,3},{2,0},{3,1},{4,6},{5,7},{6,4},{7,5},{8,10},{9,11},{10,... | collective-permute-start | bytes 196616 | tf_op jit(solution)/shard_map/ppermute | solution.py:675
  110.1 5.4 %collective-permute-start.26 = (bf16[4,32,256]{2,1,0:T(8,128)(2,1)S(1)}, bf16[4,32,256]{2,1,0:T(8,128)(2,1)S(1)}, u32[]{:S(2)}, u32[]{:S(2)}) collective-permute-start(bf16[4,32,256]{2,1,0:T(8,128)(2,1)S(1)} %get-tuple-element.136), channel_id=1, source_target_pairs={{0,3},{1,0},{2,1},{3,2},{4,7},{5,4},{6,5},{7,6},{8,11},{9,8},{10,9... | collective-permute-start | bytes 196616 | tf_op jit(solution)/shard_map/ppermute | solution.py:675
  (3 other events, 34.6 us)

commit v5 on v4

--- a/solution.py
+++ b/solution.py
@@ -139,9 +139,8 @@
     own_positions = reply_own // RESP_DEV
     positions = CORES * own_positions
     chip_prompt = CORES * prompt_keys
-    block = positions
-    per_chip = chip_prompt // block
-    prompt_blocks = chips * per_chip
+    block = 2 * positions
+    prompt_blocks = chips * chip_prompt // block
     rows_in, refs = refs[:2], refs[2:]
     count = chips if joint_keys else chips * CORES
     keys_in, refs = refs[:count], refs[count:]
@@ -163,7 +162,7 @@
         at = away * chip_prompt + other * prompt_keys
         keys[at : at + prompt_keys] = source[:prompt_keys]
         for slot in range(RESP_DEV):
-            at = prompt_blocks * block + (slot * chips + away) * positions + other * own_positions
+            at = chips * chip_prompt + (slot * chips + away) * positions + other * own_positions
             begin = prompt_keys + slot * own_positions
             keys[at : at + own_positions] = source[begin : begin + own_positions]
     total[...] = jnp.zeros_like(total)
@@ -296,12 +295,12 @@
                             ]
             begin(GROUP * positions)
             turn(GROUP * positions)
-            base = prompt_blocks + slot * chips
-            past = prompt_blocks + chip
+            base = prompt_blocks + slot * (chips // 2)
+            past = prompt_blocks + chip // 2
 
             def region_of(index):
-                reply = base + ((index - prompt_blocks) ^ chip)
-                return jnp.where(index < prompt_blocks, index, reply)
+                reply = base + ((index - prompt_blocks) ^ (chip // 2))
+                return jnp.where(index < prompt_blocks, index, jnp.where(index == past, base, reply))
 
             def stats(index, carry):
                 score_block(region_of(index), index, positions, GROUP, None)
@@ -309,18 +308,13 @@
 
             lax.fori_loop(0, past, stats, 0)
             row_at = absolute(iota((1, positions), 1), own_positions)
-            key_at = absolute(iota((block, 1), 0), own_positions)
+            key = iota((block, 1), 0)
+            key_at = jnp.where(key < positions, absolute(key, own_positions), lax.rem(chip + 1, 2) * block - 1)
             score_block(base, past, positions, GROUP, key_at > row_at)
             live = first + row_at < length
             log_mass = log_masses(positions, GROUP, live)
 
-            grad_blocks(
-                past + 1,
-                lambda index: jnp.where(index == past, base, region_of(index)),
-                positions,
-                GROUP,
-                log_mass,
-            )
+            grad_blocks(past + 1, region_of, positions, GROUP, log_mass)
             for head in range(GROUP):
                 turned = (query_grad[:, head * positions : (head + 1) * positions].T * SCALE).astype(BF16)
                 for other in range(CORES):
@@ -365,14 +359,18 @@
     row_at = jnp.where(
         real, (chip * CORES + row_core) * prompt_keys + group * prompt_rows + offset, -1
     )
-    seen = (chip + 1) * per_chip
+    per_block = max(block // chip_prompt, 1)
+    block_parts = max(chip_prompt // block, 1)
+    pair = chip // per_block
+    seen = (pair + 1) * block_parts
 
     def prompt_region(index):
-        return (index // per_chip ^ chip) * per_chip + index % per_chip
+        return (index // block_parts ^ pair) * block_parts + index % block_parts
 
     def prompt_stats(index, carry):
-        key_row = iota((block, 1), 0) + index % per_chip * block
-        key_at = index // per_chip * chip_prompt + absolute(key_row, prompt_keys)
+        key = iota((block, 1), 0) + index % block_parts * block
+        key_chip = ((index // block_parts ^ pair) * per_block + key // chip_prompt) ^ chip
+        key_at = key_chip * chip_prompt + absolute(key % chip_prompt, prompt_keys)
         score_block(prompt_region(index), index, all_rows, 1, key_at > row_at)
         return carry
 
@@ -398,7 +396,7 @@
 
         put(0, away * chip_prompt + other * prompt_keys, prompt_keys)
         for slot in range(RESP_DEV):
-            at = prompt_blocks * block + (slot * chips + away) * positions + other * own_positions
+            at = chips * chip_prompt + (slot * chips + away) * positions + other * own_positions
             put(prompt_keys + slot * own_positions, at, own_positions)
 
 
@@ -485,7 +483,8 @@
     own_positions = reply_own // RESP_DEV
     positions = CORES * own_positions
     chip_prompt = CORES * prompt_keys
-    assert chip_prompt % positions == 0 and chips & (chips - 1) == 0
+    block = 2 * positions
+    assert (chip_prompt % block == 0 or block % chip_prompt == 0) and chips > 1 and chips & (chips - 1) == 0
     pre_index = lax.axis_index("pre")
     place = jnp.stack([lax.div(pre_index, CORES), lax.rem(pre_index, CORES), lax.axis_index("rsp")])
 
@@ -573,11 +572,11 @@
     chip1 = jnp.stack([mine1, blocks0[0, 1][1]])
     blocks1 = [chip1] + [move(chip1, away) for away in range(1, chips)]
 
-    blocks = chips * (chip_prompt // positions) + RESP_DEV * chips
-    slots = chips * (chip_prompt // positions) + chips
+    blocks = (chips * chip_prompt + RESP_DEV * chips * positions) // block
+    slots = (chips * chip_prompt + chips * positions) // block
     all_rows = max(GROUP * positions, -(-GROUP * CORES * prompt_own // 128) * 128)
     sizes = (chips, reply_own, prompt_own, prompt_rows, prompt_keys)
-    score_count = GROUP * (positions * RESP_DEV * slots * positions)
+    score_count = GROUP * (positions * RESP_DEV * slots * block)
 
     def run_attend(local, key_blocks):
         joint_keys = local == 1
@@ -597,21 +596,21 @@
             [shape(own_rows, GROUP_WIDTH)] * CORES + sums,
             scalars=3,
             scratch_shapes=[
-                pltpu.VMEM((blocks * positions, 2 * HEAD_WIDTH), BF16),
-                pltpu.VMEM((blocks, HEAD_WIDTH, positions), BF16),
-                pltpu.VMEM((blocks * positions, 2 * HEAD_WIDTH), F32),
+                pltpu.VMEM((blocks * block, 2 * HEAD_WIDTH), BF16),
+                pltpu.VMEM((blocks, HEAD_WIDTH, block), BF16),
+                pltpu.VMEM((blocks * block, 2 * HEAD_WIDTH), F32),
                 pltpu.VMEM((all_rows, HEAD_WIDTH), BF16),
                 pltpu.VMEM((all_rows, HEAD_WIDTH), BF16),
                 pltpu.VMEM((HEAD_WIDTH, all_rows), BF16),
                 pltpu.VMEM((HEAD_WIDTH, all_rows), BF16),
                 pltpu.VMEM((CORES, 8, own_rows), F32),
                 pltpu.VMEM((8, all_rows), F32),
-                pltpu.VMEM((slots, positions, all_rows), F32),
+                pltpu.VMEM((slots, block, all_rows), F32),
                 pltpu.VMEM((8, all_rows), F32),
                 pltpu.VMEM((8, all_rows), F32),
                 pltpu.VMEM((HEAD_WIDTH, all_rows), F32),
             ]
-            + [pltpu.VMEM((positions, all_rows), BF16)] * 4,
+            + [pltpu.VMEM((block, all_rows), BF16)] * 4,
             cost_estimate=pl.CostEstimate(
                 flops=score_count * 10 * HEAD_WIDTH,
                 bytes_accessed=8 * 1024 * 1024,

time: 117 us -> 113 us (0.966)
  starting transfers between devices: 45.7 us -> 36.5 us
  waiting for transfers between devices: 17.9 us -> 22 us
  Pallas kernels: 50.4 us -> 52.2 us
    ppermute x25, starting transfers between devices: 27.6 us -> 20.3 us  [move(): return lax.ppermute(array, 'pre', pairs)]
    ppermute x25, waiting for transfers between devices: 17.9 us -> 21.2 us  [move(): return lax.ppermute(array, 'pre', pairs)]
    ppermute x3, starting transfers between devices: 18.2 us -> 16.1 us  [on_device(): lax.ppermute(cuts[shift], 'rsp', [(g, (g + shift) % groups) for g in rang...]
    pallas_call x9, Pallas kernels: 50.4 us -> 52.2 us  [call(): pl.pallas_call(kernel, out_shape=outs, in_specs=[SMEM] * scalars + [spec]...]
  transfers between devices with their start and end apart: 28 -> 28, of which waited for: 8 -> 9; matrix products, arithmetic and copies ran while one was open for 0% -> 0% of each run, Pallas kernels for 40% -> 42%
where the time goes in v5:
time: 113 us
  Pallas kernels  52.2 us (46%)
  starting transfers between devices  36.5 us (32%)
  waiting for transfers between devices  22 us (19%)
  local copies, waits for them, and re-layouts  1.18 us (1%)
    pallas_call x9, Pallas kernels, call(): pl.pallas_call(kernel, out_shape=outs, in_specs=[SMEM] * scalars + [spec]...  52.2 us
    ppermute x25, waiting for transfers between devices, move(): return lax.ppermute(array, 'pre', pairs)  21.2 us
    ppermute x25, starting transfers between devices, move(): return lax.ppermute(array, 'pre', pairs)  20.3 us
    ppermute x3, starting transfers between devices, on_device(): lax.ppermute(cuts[shift], 'rsp', [(g, (g + shift) % groups) for g in rang...  16.1 us
  transfers between devices with their start and end apart: 28, of which 9 were waited for; matrix products, arithmetic and copies ran while one was open for 0% of the time, Pallas kernels for 42%

profile of v5, /device:TPU:0, one launch (start us, length us, event | category | flops | bytes accessed | tf_op | source)
XLA Modules:
  0.0 113.3 jit_solution(14427638798905748430)
XLA Ops:
  0.6 0.6 pad_add_fusion.place
  1.2 3.1 %prepare_keys.1 = (bf16[384,256]{1,0:T(8,128)(2,1)}, bf16[384,256]{1,0:T(8,128)(2,1)}, bf16[384,256]{1,0:T(8,128)(2,1)}, bf16[2,384,256]{2,1,0:T(8,128)(2,1)}, f32[8,128]{1,0:T(8,128)}) custom-call(s32[3]{0:T(128)} %pad_add_fusion.place, bf16[128,512]{1,0:T(8,128)(2,1)} %pk.1, bf16[128,512]{1,0:T(8,128)(2,1)} %pv.1, bf16[256,512]{1,0:T(8,128)(2,1)} %bitcast.15, ...), custom_call_target="tpu_custom_call" | custom-call | tf_op jit(solution)/shard_map/prepare_keys/pallas_call | solution.py:502
  4.8 2.6 %collective-permute-start.1 = (bf16[384,256]{1,0:T(8,128)(2,1)}, bf16[384,256]{1,0:T(8,128)(2,1)S(1)}, u32[]{:S(2)}, u32[]{:S(2)}) collective-permute-start(bf16[384,256]{1,0:T(8,128)(2,1)} %get-tuple-element.90.refs_2_), channel_id=1, source_target_pairs={{0,8},{4,12},{8,0},{12,4},{16,24},{20,28},{24,16},{28,20},{1,9},{5... | collective-permute-start | bytes 589832 | tf_op jit(solution)/shard_map/ppermute | solution.py:496
  7.4 1.8 %collective-permute-start.3 = (bf16[384,256]{1,0:T(8,128)(2,1)}, bf16[384,256]{1,0:T(8,128)(2,1)S(1)}, u32[]{:S(2)}, u32[]{:S(2)}) collective-permute-start(bf16[384,256]{1,0:T(8,128)(2,1)} %get-tuple-element.90.refs_2_), channel_id=1, source_target_pairs={{0,16},{4,20},{8,24},{12,28},{16,0},{20,4},{24,8},{28,12},{1,17},{... | collective-permute-start | bytes 589832 | tf_op jit(solution)/shard_map/ppermute | solution.py:496
  9.3 6.5 %prepare_rows.1 = (bf16[288,1408]{1,0:T(8,128)(2,1)}, bf16[288,1408]{1,0:T(8,128)(2,1)}, bf16[288,1408]{1,0:T(8,128)(2,1)}, bf16[288,1408]{1,0:T(8,128)(2,1)}) custom-call(s32[3]{0:T(128)} %pad_add_fusion.place, f32[8,128]{1,0:T(8,128)} %get-tuple-element.82.token, bf16[32,2560]{1,0:T(8,128)(2,1)} %pq.1, bf16[32,2560]{1,0:T(8,128)(2,1)} %po.1, ...), custom_call_target="tpu_custom_call" | custom-call | flops 1006632960 | bytes 13107200 | tf_op jit(solution)/shard_map/prepare_rows/pallas_call | solution.py:502
  15.7 1.3 %collective-permute-done.2.refs_5_ = bf16[384,256]{1,0:T(8,128)(2,1)S(1)} collective-permute-done((bf16[384,256]{1,0:T(8,128)(2,1)}, bf16[384,256]{1,0:T(8,128)(2,1)S(1)}, u32[]{:S(2)}, u32[]{:S(2)}) %collective-permute-start.2) | collective-permute-done | bytes 196640 | tf_op jit(solution)/shard_map/ppermute | solution.py:496
  17.0 1.5 %collective-permute-done.4.refs_7_ = bf16[384,256]{1,0:T(8,128)(2,1)S(1)} collective-permute-done((bf16[384,256]{1,0:T(8,128)(2,1)}, bf16[384,256]{1,0:T(8,128)(2,1)S(1)}, u32[]{:S(2)}, u32[]{:S(2)}) %collective-permute-start.4) | collective-permute-done | bytes 196640 | tf_op jit(solution)/shard_map/ppermute | solution.py:496
  18.9 1.7 %collective-permute-start.6 = (bf16[384,256]{1,0:T(8,128)(2,1)S(1)}, bf16[384,256]{1,0:T(8,128)(2,1)S(1)}, u32[]{:S(2)}, u32[]{:S(2)}) collective-permute-start(bf16[384,256]{1,0:T(8,128)(2,1)S(1)} %collective-permute-done.1.refs_4_), channel_id=1, source_target_pairs={{0,16},{4,20},{8,24},{12,28},{16,0},{20,4},{24,8},{28,12},{1,17},{... | collective-permute-start | bytes 589832 | tf_op jit(solution)/shard_map/ppermute | solution.py:496
  20.6 1.5 %collective-permute-start.7 = (bf16[384,256]{1,0:T(8,128)(2,1)S(1)}, bf16[384,256]{1,0:T(8,128)(2,1)S(1)}, u32[]{:S(2)}, u32[]{:S(2)}) collective-permute-start(bf16[384,256]{1,0:T(8,128)(2,1)S(1)} %collective-permute-done.4.refs_7_), channel_id=1, source_target_pairs={{0,8},{4,12},{8,0},{12,4},{16,24},{20,28},{24,16},{28,20},{1,9},{5... | collective-permute-start | bytes 589832 | tf_op jit(solution)/shard_map/ppermute | solution.py:496
  22.2 0.6 collective-permute-start.13
  22.8 3.0 %collective-permute-done.6.refs_8_ = bf16[384,256]{1,0:T(8,128)(2,1)S(1)} collective-permute-done((bf16[384,256]{1,0:T(8,128)(2,1)S(1)}, bf16[384,256]{1,0:T(8,128)(2,1)S(1)}, u32[]{:S(2)}, u32[]{:S(2)}) %collective-permute-start.6) | collective-permute-done | bytes 196640 | tf_op jit(solution)/shard_map/ppermute | solution.py:496
  25.8 1.7 %collective-permute-start.14 = (bf16[2,384,256]{2,1,0:T(8,128)(2,1)S(1)}, bf16[2,384,256]{2,1,0:T(8,128)(2,1)S(1)}, u32[]{:S(2)}, u32[]{:S(2)}) collective-permute-start(bf16[2,384,256]{2,1,0:T(8,128)(2,1)S(1)} %pad_maximum_fusion.refs_2_), channel_id=1, source_target_pairs={{0,16},{4,20},{8,24},{12,28},{16,0},{20,4},{24,8},{28,12},{1,17},{... | collective-permute-start | bytes 1179656 | tf_op jit(solution)/shard_map/ppermute | solution.py:496
  27.5 0.9 collective-permute-done.7.refs_9_
  28.4 1.4 %collective-permute-start.15 = (bf16[2,384,256]{2,1,0:T(8,128)(2,1)S(1)}, bf16[2,384,256]{2,1,0:T(8,128)(2,1)S(1)}, u32[]{:S(2)}, u32[]{:S(2)}) collective-permute-start(bf16[2,384,256]{2,1,0:T(8,128)(2,1)S(1)} %pad_maximum_fusion.refs_2_), channel_id=1, source_target_pairs={{0,24},{4,28},{8,16},{12,20},{16,8},{20,12},{24,0},{28,4},{1,25},{... | collective-permute-start | bytes 1179656 | tf_op jit(solution)/shard_map/ppermute | solution.py:496
  29.9 1.1 copy-done.2
  31.0 19.1 %attend.2 = (bf16[288,640]{1,0:T(8,128)(2,1)S(1)}, bf16[288,640]{1,0:T(8,128)(2,1)S(1)}, bf16[2,384,256]{2,1,0:T(8,128)(2,1)S(1)}, bf16[2,384,256]{2,1,0:T(8,128...) custom-call(s32[3]{0:T(128)S(1)} %copy-done, s32[8]{0:T(128)S(1)} %copy-done.4, ...), custom_call_target="tpu_custom_call" | custom-call | flops 6710886400 | bytes 8388608 | tf_op jit(solution)/shard_map/attend/pallas_call | solution.py:502
  50.2 3.4 %collective-permute-start.10 = (bf16[2,384,256]{2,1,0:T(8,128)(2,1)S(1)}, bf16[2,384,256]{2,1,0:T(8,128)(2,1)S(1)}, u32[]{:S(2)}, u32[]{:S(2)}) collective-permute-start(bf16[2,384,256]{2,1,0:T(8,128)(2,1)S(1)} %get-tuple-element.99), channel_id=1, source_target_pairs={{0,24},{4,28},{8,16},{12,20},{16,8},{20,12},{24,0},{28,4},{1,25},{... | collective-permute-start | bytes 1179656 | tf_op jit(solution)/shard_map/ppermute | solution.py:496
  53.6 19.0 %attend.3 = (bf16[288,640]{1,0:T(8,128)(2,1)S(1)}, bf16[288,640]{1,0:T(8,128)(2,1)S(1)}, bf16[384,256]{1,0:T(8,128)(2,1)S(1)}, bf16[384,256]{1,0:T(8,128)(2,1)S(...) custom-call(s32[3]{0:T(128)S(1)} %copy-done, ...), custom_call_target="tpu_custom_call" | custom-call | flops 6710886400 | bytes 8388608 | tf_op jit(solution)/shard_map/attend/pallas_call | solution.py:502
  73.0 0.6 collective-permute-start.16
  73.6 1.7 %collective-permute-start.20 = (bf16[384,256]{1,0:T(8,128)(2,1)S(1)}, bf16[384,256]{1,0:T(8,128)(2,1)S(1)}, u32[]{:S(2)}, u32[]{:S(2)}) collective-permute-start(bf16[384,256]{1,0:T(8,128)(2,1)S(1)} %get-tuple-element.129), channel_id=1, source_target_pairs={{0,16},{4,20},{8,24},{12,28},{16,0},{20,4},{24,8},{28,12},{1,17},{... | collective-permute-start | bytes 589832 | tf_op jit(solution)/shard_map/ppermute | solution.py:496
  75.2 5.2 %collective-permute-done.17.refs_2_ = bf16[384,256]{1,0:T(8,128)(2,1)S(1)} collective-permute-done((bf16[384,256]{1,0:T(8,128)(2,1)S(1)}, bf16[384,256]{1,0:T(8,128)(2,1)S(1)}, u32[]{:S(2)}, u32[]{:S(2)}) %collective-permute-start.17) | collective-permute-done | bytes 196640 | tf_op jit(solution)/shard_map/ppermute | solution.py:496
  80.7 2.1 %collective-permute-start.19 = (bf16[384,256]{1,0:T(8,128)(2,1)S(1)}, bf16[384,256]{1,0:T(8,128)(2,1)S(1)}, u32[]{:S(2)}, u32[]{:S(2)}) collective-permute-start(bf16[384,256]{1,0:T(8,128)(2,1)S(1)} %get-tuple-element.128), channel_id=1, source_target_pairs={{0,8},{4,12},{8,0},{12,4},{16,24},{20,28},{24,16},{28,20},{1,9},{5... | collective-permute-start | bytes 589832 | tf_op jit(solution)/shard_map/ppermute | solution.py:496
  82.7 1.5 %collective-permute-done.20.refs_4_ = bf16[384,256]{1,0:T(8,128)(2,1)S(1)} collective-permute-done((bf16[384,256]{1,0:T(8,128)(2,1)S(1)}, bf16[384,256]{1,0:T(8,128)(2,1)S(1)}, u32[]{:S(2)}, u32[]{:S(2)}) %collective-permute-start.20) | collective-permute-done | bytes 196640 | tf_op jit(solution)/shard_map/ppermute | solution.py:496
  84.2 3.1 %collective-permute-done.22.refs_6_ = bf16[384,256]{1,0:T(8,128)(2,1)S(1)} collective-permute-done((bf16[384,256]{1,0:T(8,128)(2,1)S(1)}, bf16[384,256]{1,0:T(8,128)(2,1)S(1)}, u32[]{:S(2)}, u32[]{:S(2)}) %collective-permute-start.22) | collective-permute-done | bytes 196640 | tf_op jit(solution)/shard_map/ppermute | solution.py:496
  87.3 4.8 %collective-permute-done.19.refs_3_ = bf16[384,256]{1,0:T(8,128)(2,1)S(1)} collective-permute-done((bf16[384,256]{1,0:T(8,128)(2,1)S(1)}, bf16[384,256]{1,0:T(8,128)(2,1)S(1)}, u32[]{:S(2)}, u32[]{:S(2)}) %collective-permute-start.19) | collective-permute-done | bytes 196640 | tf_op jit(solution)/shard_map/ppermute | solution.py:496
  92.1 0.6 spread_prompt.1
  92.7 1.6 %collective-permute-start.24 = (bf16[4,32,256]{2,1,0:T(8,128)(2,1)S(1)}, bf16[4,32,256]{2,1,0:T(8,128)(2,1)S(1)}, u32[]{:S(2)}, u32[]{:S(2)}) collective-permute-start(bf16[4,32,256]{2,1,0:T(8,128)(2,1)S(1)} %get-tuple-element.134), channel_id=1, source_target_pairs={{0,1},{1,2},{2,3},{3,0},{4,5},{5,6},{6,7},{7,4},{8,9},{9,10},{10,1... | collective-permute-start | bytes 196616 | tf_op jit(solution)/shard_map/ppermute | solution.py:674
  94.4 13.2 %collective-permute-start.25 = (bf16[4,32,256]{2,1,0:T(8,128)(2,1)S(1)}, bf16[4,32,256]{2,1,0:T(8,128)(2,1)S(1)}, u32[]{:S(2)}, u32[]{:S(2)}) collective-permute-start(bf16[4,32,256]{2,1,0:T(8,128)(2,1)S(1)} %get-tuple-element.135), channel_id=1, source_target_pairs={{0,2},{1,3},{2,0},{3,1},{4,6},{5,7},{6,4},{7,5},{8,10},{9,11},{10,... | collective-permute-start | bytes 196616 | tf_op jit(solution)/shard_map/ppermute | solution.py:674
  107.5 1.3 %collective-permute-start.26 = (bf16[4,32,256]{2,1,0:T(8,128)(2,1)S(1)}, bf16[4,32,256]{2,1,0:T(8,128)(2,1)S(1)}, u32[]{:S(2)}, u32[]{:S(2)}) collective-permute-start(bf16[4,32,256]{2,1,0:T(8,128)(2,1)S(1)} %get-tuple-element.136), channel_id=1, source_target_pairs={{0,3},{1,0},{2,1},{3,2},{4,7},{5,4},{6,5},{7,6},{8,11},{9,8},{10,9... | collective-permute-start | bytes 196616 | tf_op jit(solution)/shard_map/ppermute | solution.py:674
  108.9 2.5 %finish_reply.1 = (bf16[32,2560]{1,0:T(8,128)(2,1)}, bf16[256,2560]{1,0:T(8,128)(2,1)}, bf16[256,512]{1,0:T(8,128)(2,1)}, bf16[256,512]{1,0:T(8,128)(2,1)}) custom-call(s32[3]{0:T(128)S(1)} %copy-done, f32[384,256]{1,0:T(8,128)S(1)} %get-tuple-element.117.refs_0_, bf16[384,256]{1,0:T(8,128)(2,1)S(1)} %collective-permute-done.16.refs_1_, ...), custom_call_target="tpu_custom_call" | custom-call | flops 469762048 | bytes 10485760 | tf_op jit(solution)/shard_map/finish_reply/pallas_call | solution.py:502
  111.4 0.7 collective-permute-done.25.refs_2_
  112.1 1.2 %finish_prompt.1 = (bf16[32,512]{1,0:T(8,128)(2,1)}, bf16[32,512]{1,0:T(8,128)(2,1)}) custom-call(s32[3]{0:T(128)S(1)} %copy-done, bf16[4,32,256]{2,1,0:T(8,128)(2,1)S(1)} %get-tuple-element.143.refs_0_, bf16[4,32,256]{2,1,0:T(8,128)(2,1)S(1)} %collective-permute-done.24.refs_1_, bf16[4,32,256]{2,1,0:T(8,128)(2,1)S(1)} %collective-permute-done.25.refs_2_, ...), custom_call_target="tpu_custom_call" | custom-call | tf_op jit(solution)/shard_map/finish_prompt/pallas_call | solution.py:502
  (50 shorter events, 1.9 us)
Async XLA Ops:
  4.3 14.2 %collective-permute-start = (bf16[2,384,256]{2,1,0:T(8,128)(2,1)}, bf16[2,384,256]{2,1,0:T(8,128)(2,1)S(1)}, u32[]{:S(2)}, u32[]{:S(2)}) collective-permute-start(bf16[2,384,256]{2,1,0:T(8,128)(2,1)} %get-tuple-element.80), channel_id=1, source_target_pairs={{0,4},{4,0},{8,12},{12,8},{16,20},{20,16},{24,28},{28,24},{1,5},{5... | collective-permute-start | bytes 1179656 | tf_op jit(solution)/shard_map/ppermute | solution.py:496
  4.8 10.9 %collective-permute-start.1 = (bf16[384,256]{1,0:T(8,128)(2,1)}, bf16[384,256]{1,0:T(8,128)(2,1)S(1)}, u32[]{:S(2)}, u32[]{:S(2)}) collective-permute-start(bf16[384,256]{1,0:T(8,128)(2,1)} %get-tuple-element.90.refs_2_), channel_id=1, source_target_pairs={{0,8},{4,12},{8,0},{12,4},{16,24},{20,28},{24,16},{28,20},{1,9},{5... | collective-permute-start | bytes 589832 | tf_op jit(solution)/shard_map/ppermute | solution.py:496
  7.4 9.7 %collective-permute-start.2 = (bf16[384,256]{1,0:T(8,128)(2,1)}, bf16[384,256]{1,0:T(8,128)(2,1)S(1)}, u32[]{:S(2)}, u32[]{:S(2)}) collective-permute-start(bf16[384,256]{1,0:T(8,128)(2,1)} %get-tuple-element.81), channel_id=1, source_target_pairs={{0,12},{4,8},{8,4},{12,0},{16,28},{20,24},{24,20},{28,16},{1,13},{... | collective-permute-start | bytes 589832 | tf_op jit(solution)/shard_map/ppermute | solution.py:496
  7.4 9.6 %collective-permute-start.3 = (bf16[384,256]{1,0:T(8,128)(2,1)}, bf16[384,256]{1,0:T(8,128)(2,1)S(1)}, u32[]{:S(2)}, u32[]{:S(2)}) collective-permute-start(bf16[384,256]{1,0:T(8,128)(2,1)} %get-tuple-element.90.refs_2_), channel_id=1, source_target_pairs={{0,16},{4,20},{8,24},{12,28},{16,0},{20,4},{24,8},{28,12},{1,17},{... | collective-permute-start | bytes 589832 | tf_op jit(solution)/shard_map/ppermute | solution.py:496
  9.2 9.3 %collective-permute-start.4 = (bf16[384,256]{1,0:T(8,128)(2,1)}, bf16[384,256]{1,0:T(8,128)(2,1)S(1)}, u32[]{:S(2)}, u32[]{:S(2)}) collective-permute-start(bf16[384,256]{1,0:T(8,128)(2,1)} %get-tuple-element.81), channel_id=1, source_target_pairs={{0,20},{4,16},{8,28},{12,24},{16,4},{20,0},{24,12},{28,8},{1,21},{... | collective-permute-start | bytes 589832 | tf_op jit(solution)/shard_map/ppermute | solution.py:496
  9.2 20.6 %copy-start = (s32[3]{0:T(128)S(1)}, s32[3]{0:T(128)}, u32[]{:S(2)}) copy-start(s32[3]{0:T(128)} %pad_add_fusion.place) | copy-start | bytes 40
  9.2 20.6 %copy-start.3 = (bf16[384,256]{1,0:T(8,128)(2,1)S(1)}, bf16[384,256]{1,0:T(8,128)(2,1)}, u32[]{:S(2)}) copy-start(bf16[384,256]{1,0:T(8,128)(2,1)} %get-tuple-element.90.refs_2_) | copy-start | bytes 589828
  9.2 20.6 %copy-start.4 = (s32[8]{0:T(128)S(1)}, s32[8]{0:T(128)}, u32[]{:S(2)}) copy-start(s32[8]{0:T(128)} %reply_len.3) | copy-start | bytes 100
  18.5 11.3 %collective-permute-start.5 = (bf16[288,1408]{1,0:T(8,128)(2,1)}, bf16[288,1408]{1,0:T(8,128)(2,1)S(1)}, u32[]{:S(2)}, u32[]{:S(2)}) collective-permute-start(bf16[288,1408]{1,0:T(8,128)(2,1)} %get-tuple-element.89), channel_id=1, source_target_pairs={{0,4},{4,0},{8,12},{12,8},{16,20},{20,16},{24,28},{28,24},{1,5},{5... | collective-permute-start | bytes 2433032 | tf_op jit(solution)/shard_map/ppermute | solution.py:496
  18.9 6.9 %collective-permute-start.6 = (bf16[384,256]{1,0:T(8,128)(2,1)S(1)}, bf16[384,256]{1,0:T(8,128)(2,1)S(1)}, u32[]{:S(2)}, u32[]{:S(2)}) collective-permute-start(bf16[384,256]{1,0:T(8,128)(2,1)S(1)} %collective-permute-done.1.refs_4_), channel_id=1, source_target_pairs={{0,16},{4,20},{8,24},{12,28},{16,0},{20,4},{24,8},{28,12},{1,17},{... | collective-permute-start | bytes 589832 | tf_op jit(solution)/shard_map/ppermute | solution.py:496
  20.6 7.8 %collective-permute-start.7 = (bf16[384,256]{1,0:T(8,128)(2,1)S(1)}, bf16[384,256]{1,0:T(8,128)(2,1)S(1)}, u32[]{:S(2)}, u32[]{:S(2)}) collective-permute-start(bf16[384,256]{1,0:T(8,128)(2,1)S(1)} %collective-permute-done.4.refs_7_), channel_id=1, source_target_pairs={{0,8},{4,12},{8,0},{12,4},{16,24},{20,28},{24,16},{28,20},{1,9},{5... | collective-permute-start | bytes 589832 | tf_op jit(solution)/shard_map/ppermute | solution.py:496
  22.1 31.5 %collective-permute-start.12 = (bf16[288,1408]{1,0:T(8,128)(2,1)}, bf16[288,1408]{1,0:T(8,128)(2,1)S(1)}, u32[]{:S(2)}, u32[]{:S(2)}) collective-permute-start(bf16[288,1408]{1,0:T(8,128)(2,1)} %get-tuple-element.102), channel_id=1, source_target_pairs={{0,4},{4,0},{8,12},{12,8},{16,20},{20,16},{24,28},{28,24},{1,5},{5... | collective-permute-start | bytes 2433032 | tf_op jit(solution)/shard_map/ppermute | solution.py:496
  22.2 31.5 %copy-start.1 = (bf16[288,1408]{1,0:T(8,128)(2,1)S(1)}, bf16[288,1408]{1,0:T(8,128)(2,1)}, u32[]{:S(2)}) copy-start(bf16[288,1408]{1,0:T(8,128)(2,1)} %get-tuple-element.101.refs_0_) | copy-start | bytes 2433028
  22.2 28.0 %collective-permute-start.13 = (bf16[2,384,256]{2,1,0:T(8,128)(2,1)S(1)}, bf16[2,384,256]{2,1,0:T(8,128)(2,1)S(1)}, u32[]{:S(2)}, u32[]{:S(2)}) collective-permute-start(bf16[2,384,256]{2,1,0:T(8,128)(2,1)S(1)} %pad_maximum_fusion.refs_2_), channel_id=1, source_target_pairs={{0,8},{4,12},{8,0},{12,4},{16,24},{20,28},{24,16},{28,20},{1,9},{5... | collective-permute-start | bytes 1179656 | tf_op jit(solution)/shard_map/ppermute | solution.py:496
  25.8 24.4 %collective-permute-start.14 = (bf16[2,384,256]{2,1,0:T(8,128)(2,1)S(1)}, bf16[2,384,256]{2,1,0:T(8,128)(2,1)S(1)}, u32[]{:S(2)}, u32[]{:S(2)}) collective-permute-start(bf16[2,384,256]{2,1,0:T(8,128)(2,1)S(1)} %pad_maximum_fusion.refs_2_), channel_id=1, source_target_pairs={{0,16},{4,20},{8,24},{12,28},{16,0},{20,4},{24,8},{28,12},{1,17},{... | collective-permute-start | bytes 1179656 | tf_op jit(solution)/shard_map/ppermute | solution.py:496
  28.4 25.2 %collective-permute-start.15 = (bf16[2,384,256]{2,1,0:T(8,128)(2,1)S(1)}, bf16[2,384,256]{2,1,0:T(8,128)(2,1)S(1)}, u32[]{:S(2)}, u32[]{:S(2)}) collective-permute-start(bf16[2,384,256]{2,1,0:T(8,128)(2,1)S(1)} %pad_maximum_fusion.refs_2_), channel_id=1, source_target_pairs={{0,24},{4,28},{8,16},{12,20},{16,8},{20,12},{24,0},{28,4},{1,25},{... | collective-permute-start | bytes 1179656 | tf_op jit(solution)/shard_map/ppermute | solution.py:496
  50.1 22.6 %collective-permute-start.8 = (bf16[2,384,256]{2,1,0:T(8,128)(2,1)S(1)}, bf16[2,384,256]{2,1,0:T(8,128)(2,1)S(1)}, u32[]{:S(2)}, u32[]{:S(2)}) collective-permute-start(bf16[2,384,256]{2,1,0:T(8,128)(2,1)S(1)} %get-tuple-element.97), channel_id=1, source_target_pairs={{0,8},{4,12},{8,0},{12,4},{16,24},{20,28},{24,16},{28,20},{1,9},{5... | collective-permute-start | bytes 1179656 | tf_op jit(solution)/shard_map/ppermute | solution.py:496
  50.1 22.5 %collective-permute-start.9 = (bf16[2,384,256]{2,1,0:T(8,128)(2,1)S(1)}, bf16[2,384,256]{2,1,0:T(8,128)(2,1)S(1)}, u32[]{:S(2)}, u32[]{:S(2)}) collective-permute-start(bf16[2,384,256]{2,1,0:T(8,128)(2,1)S(1)} %get-tuple-element.98), channel_id=1, source_target_pairs={{0,16},{4,20},{8,24},{12,28},{16,0},{20,4},{24,8},{28,12},{1,17},{... | collective-permute-start | bytes 1179656 | tf_op jit(solution)/shard_map/ppermute | solution.py:496
  50.2 22.4 %collective-permute-start.10 = (bf16[2,384,256]{2,1,0:T(8,128)(2,1)S(1)}, bf16[2,384,256]{2,1,0:T(8,128)(2,1)S(1)}, u32[]{:S(2)}, u32[]{:S(2)}) collective-permute-start(bf16[2,384,256]{2,1,0:T(8,128)(2,1)S(1)} %get-tuple-element.99), channel_id=1, source_target_pairs={{0,24},{4,28},{8,16},{12,20},{16,8},{20,12},{24,0},{28,4},{1,25},{... | collective-permute-start | bytes 1179656 | tf_op jit(solution)/shard_map/ppermute | solution.py:496
  53.6 19.0 %collective-permute-start.11 = (bf16[288,640]{1,0:T(8,128)(2,1)S(1)}, bf16[288,640]{1,0:T(8,128)(2,1)S(1)}, u32[]{:S(2)}, u32[]{:S(2)}) collective-permute-start(bf16[288,640]{1,0:T(8,128)(2,1)S(1)} %get-tuple-element.100), channel_id=1, source_target_pairs={{0,4},{4,0},{8,12},{12,8},{16,20},{20,16},{24,28},{28,24},{1,5},{5... | collective-permute-start | bytes 1105928 | tf_op jit(solution)/shard_map/ppermute | solution.py:496
  72.7 7.8 %collective-permute-start.17 = (bf16[384,256]{1,0:T(8,128)(2,1)S(1)}, bf16[384,256]{1,0:T(8,128)(2,1)S(1)}, u32[]{:S(2)}, u32[]{:S(2)}) collective-permute-start(bf16[384,256]{1,0:T(8,128)(2,1)S(1)} %get-tuple-element.122), channel_id=1, source_target_pairs={{0,16},{4,20},{8,24},{12,28},{16,0},{20,4},{24,8},{28,12},{1,17},{... | collective-permute-start | bytes 589832 | tf_op jit(solution)/shard_map/ppermute | solution.py:496
  72.7 7.7 %collective-permute-start.18 = (bf16[384,256]{1,0:T(8,128)(2,1)S(1)}, bf16[384,256]{1,0:T(8,128)(2,1)S(1)}, u32[]{:S(2)}, u32[]{:S(2)}) collective-permute-start(bf16[384,256]{1,0:T(8,128)(2,1)S(1)} %get-tuple-element.123), channel_id=1, source_target_pairs={{0,8},{4,12},{8,0},{12,4},{16,24},{20,28},{24,16},{28,20},{1,9},{5... | collective-permute-start | bytes 589832 | tf_op jit(solution)/shard_map/ppermute | solution.py:496
  73.0 9.7 %collective-permute-start.16 = (bf16[384,256]{1,0:T(8,128)(2,1)S(1)}, bf16[384,256]{1,0:T(8,128)(2,1)S(1)}, u32[]{:S(2)}, u32[]{:S(2)}) collective-permute-start(bf16[384,256]{1,0:T(8,128)(2,1)S(1)} %get-tuple-element.118), channel_id=1, source_target_pairs={{0,4},{4,0},{8,12},{12,8},{16,20},{20,16},{24,28},{28,24},{1,5},{5... | collective-permute-start | bytes 589832 | tf_op jit(solution)/shard_map/ppermute | solution.py:496
  73.6 10.7 %collective-permute-start.20 = (bf16[384,256]{1,0:T(8,128)(2,1)S(1)}, bf16[384,256]{1,0:T(8,128)(2,1)S(1)}, u32[]{:S(2)}, u32[]{:S(2)}) collective-permute-start(bf16[384,256]{1,0:T(8,128)(2,1)S(1)} %get-tuple-element.129), channel_id=1, source_target_pairs={{0,16},{4,20},{8,24},{12,28},{16,0},{20,4},{24,8},{28,12},{1,17},{... | collective-permute-start | bytes 589832 | tf_op jit(solution)/shard_map/ppermute | solution.py:496
  80.5 28.4 %collective-permute-start.27 = (bf16[288,640]{1,0:T(8,128)(2,1)S(1)}, bf16[288,640]{1,0:T(8,128)(2,1)S(1)}, u32[]{:S(2)}, u32[]{:S(2)}) collective-permute-start(bf16[288,640]{1,0:T(8,128)(2,1)S(1)} %get-tuple-element.140), channel_id=1, source_target_pairs={{0,4},{4,0},{8,12},{12,8},{16,20},{20,16},{24,28},{28,24},{1,5},{5... | collective-permute-start | bytes 1105928 | tf_op jit(solution)/shard_map/ppermute | solution.py:496
  80.6 6.7 %collective-permute-start.22 = (bf16[384,256]{1,0:T(8,128)(2,1)S(1)}, bf16[384,256]{1,0:T(8,128)(2,1)S(1)}, u32[]{:S(2)}, u32[]{:S(2)}) collective-permute-start(bf16[384,256]{1,0:T(8,128)(2,1)S(1)} %get-tuple-element.131), channel_id=1, source_target_pairs={{0,12},{4,8},{8,4},{12,0},{16,28},{20,24},{24,20},{28,16},{1,13},{... | collective-permute-start | bytes 589832 | tf_op jit(solution)/shard_map/ppermute | solution.py:496
  80.7 11.4 %collective-permute-start.19 = (bf16[384,256]{1,0:T(8,128)(2,1)S(1)}, bf16[384,256]{1,0:T(8,128)(2,1)S(1)}, u32[]{:S(2)}, u32[]{:S(2)}) collective-permute-start(bf16[384,256]{1,0:T(8,128)(2,1)S(1)} %get-tuple-element.128), channel_id=1, source_target_pairs={{0,8},{4,12},{8,0},{12,4},{16,24},{20,28},{24,16},{28,20},{1,9},{5... | collective-permute-start | bytes 589832 | tf_op jit(solution)/shard_map/ppermute | solution.py:496
  82.7 9.3 %collective-permute-start.21 = (bf16[384,256]{1,0:T(8,128)(2,1)S(1)}, bf16[384,256]{1,0:T(8,128)(2,1)S(1)}, u32[]{:S(2)}, u32[]{:S(2)}) collective-permute-start(bf16[384,256]{1,0:T(8,128)(2,1)S(1)} %get-tuple-element.130), channel_id=1, source_target_pairs={{0,4},{4,0},{8,12},{12,8},{16,20},{20,16},{24,28},{28,24},{1,5},{5... | collective-permute-start | bytes 589832 | tf_op jit(solution)/shard_map/ppermute | solution.py:496
  84.2 7.9 %collective-permute-start.23 = (bf16[384,256]{1,0:T(8,128)(2,1)S(1)}, bf16[384,256]{1,0:T(8,128)(2,1)S(1)}, u32[]{:S(2)}, u32[]{:S(2)}) collective-permute-start(bf16[384,256]{1,0:T(8,128)(2,1)S(1)} %get-tuple-element.132), channel_id=1, source_target_pairs={{0,20},{4,16},{8,28},{12,24},{16,4},{20,0},{24,12},{28,8},{1,21},{... | collective-permute-start | bytes 589832 | tf_op jit(solution)/shard_map/ppermute | solution.py:496
  92.7 18.6 %collective-permute-start.24 = (bf16[4,32,256]{2,1,0:T(8,128)(2,1)S(1)}, bf16[4,32,256]{2,1,0:T(8,128)(2,1)S(1)}, u32[]{:S(2)}, u32[]{:S(2)}) collective-permute-start(bf16[4,32,256]{2,1,0:T(8,128)(2,1)S(1)} %get-tuple-element.134), channel_id=1, source_target_pairs={{0,1},{1,2},{2,3},{3,0},{4,5},{5,6},{6,7},{7,4},{8,9},{9,10},{10,1... | collective-permute-start | bytes 196616 | tf_op jit(solution)/shard_map/ppermute | solution.py:674
  94.4 17.7 %collective-permute-start.25 = (bf16[4,32,256]{2,1,0:T(8,128)(2,1)S(1)}, bf16[4,32,256]{2,1,0:T(8,128)(2,1)S(1)}, u32[]{:S(2)}, u32[]{:S(2)}) collective-permute-start(bf16[4,32,256]{2,1,0:T(8,128)(2,1)S(1)} %get-tuple-element.135), channel_id=1, source_target_pairs={{0,2},{1,3},{2,0},{3,1},{4,6},{5,7},{6,4},{7,5},{8,10},{9,11},{10,... | collective-permute-start | bytes 196616 | tf_op jit(solution)/shard_map/ppermute | solution.py:674
  107.5 4.6 %collective-permute-start.26 = (bf16[4,32,256]{2,1,0:T(8,128)(2,1)S(1)}, bf16[4,32,256]{2,1,0:T(8,128)(2,1)S(1)}, u32[]{:S(2)}, u32[]{:S(2)}) collective-permute-start(bf16[4,32,256]{2,1,0:T(8,128)(2,1)S(1)} %get-tuple-element.136), channel_id=1, source_target_pairs={{0,3},{1,0},{2,1},{3,2},{4,7},{5,4},{6,5},{7,6},{8,11},{9,8},{10,9... | collective-permute-start | bytes 196616 | tf_op jit(solution)/shard_map/ppermute | solution.py:674
  (3 other events, 34.6 us)

commit v6 on v5

--- a/solution.py
+++ b/solution.py
@@ -19,6 +19,7 @@
 
 SCALE = HEAD_WIDTH ** (-0.5)
 SCALE_LOG2 = SCALE * math.log2(math.e)
+PART = 128
 NEGATIVE_FLOOR = -1e30
 DEAD = 1e30
 F32 = jnp.float32
@@ -98,7 +99,8 @@
 
 
 def prepare_rows(place, token, pq, po, pg, rq, ro, rg, *refs):
-    outs, bufs, sems = refs[:KEY_VALUE_HEADS], refs[KEY_VALUE_HEADS:-1], refs[-1]
+    (theirs, *mine), bufs, sems = refs[: 1 + LOCAL_HEADS], refs[1 + LOCAL_HEADS : -1], refs[-1]
+    outs = [out for local in range(LOCAL_HEADS) for out in (theirs.at[local], mine[local])]
     core = place[1]
     reply = rq.shape[0]
     sources = (pq, po, pg, rq, ro, rg)
@@ -141,13 +143,13 @@
     chip_prompt = CORES * prompt_keys
     block = 2 * positions
     prompt_blocks = chips * chip_prompt // block
-    rows_in, refs = refs[:2], refs[2:]
+    rows_in, refs = (refs[0], refs[1].at[int(joint_keys)]), refs[2:]
     count = chips if joint_keys else chips * CORES
     keys_in, refs = refs[:count], refs[count:]
     query_out, refs = refs[:2], refs[2:]
     count = chips * CORES if joint_keys else chips
     keys_out, refs = refs[:count], refs[count:]
-    keys, keys_t, total, query, gradient, query_t, gradient_t, deltas, delta, scores, top, mass, *refs = refs
+    keys, keys_t, total, query, gradient, query_t, gradient_t, deltas, delta, scores, peaks, top, mass, *refs = refs
     query_grad, stages = refs[0], (refs[1:3], refs[3:5])
     chip, core, group = place[0], place[1], place[2]
 
@@ -184,24 +186,31 @@
             value = dot(key_rows, query_t[:, span]) * SCALE_LOG2
             if hidden is not None:
                 value = jnp.where(hidden, NEGATIVE_FLOOR, value)
-            scores[place_in, :, span] = value
             split = value.reshape(block // 8, 8, width)
-            before = top[:, span]
-            now = jnp.maximum(before, jnp.max(split, axis=0))
-            top[:, span] = now
-            mass[:, span] = mass[:, span] * jnp.exp2(before - now) + jnp.sum(
-                jnp.exp2(split - now[None]), axis=0
-            )
+            peak, summed = top[:, span], mass[:, span]
+            for part in range(block // PART):
+                piece = split[part * PART // 8 : (part + 1) * PART // 8]
+                now = jnp.maximum(peak, jnp.max(piece, axis=0))
+                shifted = jnp.exp2(piece - now[None])
+                scores[place_in, part * PART : (part + 1) * PART, span] = shifted.reshape(PART, width)
+                peaks[place_in, part, :, span] = now
+                summed = summed * jnp.exp2(peak - now) + jnp.sum(shifted, axis=0)
+                peak = now
+            top[:, span], mass[:, span] = peak, summed
 
     def weigh(region, place_in, width, chunks, log_mass, stage, earlier=None, earlier_stage=None):
         rows = pl.ds(pl.multiple_of(region * block, block), block)
         value_rows = keys[rows, HEAD_WIDTH:]
         for chunk in range(chunks):
             span = slice(chunk * width, (chunk + 1) * width)
-            p = jnp.exp2(scores[place_in, :, span] - log_mass[chunk])
             dp = dot(value_rows, gradient_t[:, span])
-            stage[0][:, span] = p.astype(BF16)
-            stage[1][:, span] = (p * (dp - delta[0:1, span])).astype(BF16)
+            for part in range(block // PART):
+                at = slice(part * PART, (part + 1) * PART)
+                factor = jnp.exp2(peaks[place_in, part, :, span] - log_mass[chunk])
+                p = scores[place_in, at, span].reshape(PART // 8, 8, width) * factor[None]
+                p = p.reshape(PART, width)
+                stage[0][at, span] = p.astype(BF16)
+                stage[1][at, span] = (p * (dp[at] - delta[0:1, span])).astype(BF16)
             if earlier is not None:
                 multiply(earlier, width, chunks, earlier_stage, chunk)
         if earlier is not None:
@@ -551,7 +560,7 @@
             reply_output[0],
             reply_output_gradient[0],
         ),
-        [shape(own_rows, row_width)] * KEY_VALUE_HEADS,
+        [shape(LOCAL_HEADS, own_rows, row_width)] + [shape(own_rows, row_width)] * LOCAL_HEADS,
         spec=HBM,
         scratch_shapes=[
             pltpu.VMEM((KEY_VALUE_HEADS, rows, GROUP_WIDTH), BF16)
@@ -578,6 +587,9 @@
     sizes = (chips, reply_own, prompt_own, prompt_rows, prompt_keys)
     score_count = GROUP * (positions * RESP_DEV * slots * block)
 
+    rows_theirs, *rows_mine = rows
+    rows_theirs = swap(rows_theirs)
+
     def run_attend(local, key_blocks):
         joint_keys = local == 1
         sums = [shape(*key_shape)] * devices if joint_keys else [shape(CORES, *key_shape)] * chips
@@ -589,8 +601,8 @@
                 place,
                 reply_len,
                 reply_slot,
-                rows[CORES * local + 1],
-                swap(rows[CORES * local]),
+                rows_mine[local],
+                rows_theirs,
                 *key_blocks,
             ),
             [shape(own_rows, GROUP_WIDTH)] * CORES + sums,
@@ -606,6 +618,7 @@
                 pltpu.VMEM((CORES, 8, own_rows), F32),
                 pltpu.VMEM((8, all_rows), F32),
                 pltpu.VMEM((slots, block, all_rows), F32),
+                pltpu.VMEM((slots, block // PART, 8, all_rows), F32),
                 pltpu.VMEM((8, all_rows), F32),
                 pltpu.VMEM((8, all_rows), F32),
                 pltpu.VMEM((HEAD_WIDTH, all_rows), F32),
@@ -629,6 +642,14 @@
         (arrived0, query_theirs0, query_theirs1, sums1)
     )
     sums1 = [sums1[CORES * away : CORES * away + CORES] for away in range(chips)]
+    mine0, theirs0 = call(
+        collect,
+        "collect",
+        SMALL_MIB,
+        arrived0,
+        [shape(*key_shape, dtype=F32), shape(*key_shape)],
+        scalars=0,
+    )
     if relayed:
         through_y, through_x = move(sums1[3][0], 2), move(sums1[3][1], 1)
         for_x, for_y = call(
@@ -640,8 +661,8 @@
             scalars=0,
         )
         near = [sums1[0][0], move(sums1[1][1], 1, 1), move(sums1[2][0], 2)]
-        for_x, for_y, sums1[0][1], query_theirs1 = lax.optimization_barrier(
-            (for_x, for_y, sums1[0][1], query_theirs1)
+        for_x, for_y, near, sums1[0][1], query_theirs1, theirs0 = lax.optimization_barrier(
+            (for_x, for_y, near, sums1[0][1], query_theirs1, theirs0)
         )
         lists1 = [[near[0], move(for_x, 1), near[2]], [swap(sums1[0][1]), near[1], move(for_y, 2, 1)]]
     else:
@@ -649,14 +670,6 @@
             [move(pair[other], away, other) if away or other else pair[other] for away, pair in enumerate(sums1)]
             for other in range(CORES)
         ]
-    mine0, theirs0 = call(
-        collect,
-        "collect",
-        SMALL_MIB,
-        arrived0,
-        [shape(*key_shape, dtype=F32), shape(*key_shape)],
-        scalars=0,
-    )
     lists = [[mine0], [swap(theirs0)]] + lists1
     queries = [query_mine0, query_theirs0, query_mine1, swap(query_theirs1)]
     counts = [len(parts) for parts in lists]

time: 113 us -> 111 us (0.982)
  starting transfers between devices: 36.5 us -> 35 us
    ppermute x3, starting transfers between devices: 16.1 us -> 13.4 us  [on_device(): lax.ppermute(cuts[shift], 'rsp', [(g, (g + shift) % groups) for g in rang...]
    ppermute x3, waiting for transfers between devices: 0.75 us -> 2.88 us  [on_device(): lax.ppermute(cuts[shift], 'rsp', [(g, (g + shift) % groups) for g in rang...]
    ppermute x25 -> x24, waiting for transfers between devices: 21.2 us -> 19.3 us  [move(): return lax.ppermute(array, 'pre', pairs)]
    ppermute x25 -> x24, starting transfers between devices: 20.3 us -> 21.6 us  [move(): return lax.ppermute(array, 'pre', pairs)]
  transfers between devices with their start and end apart: 28 -> 27, of which waited for: 9 -> 11; matrix products, arithmetic and copies ran while one was open for 0% -> 0% of each run, Pallas kernels for 42% -> 42%
where the time goes in v6:
time: 111 us; the launch traced here: 112 us
  Pallas kernels  51.6 us (46%)
  starting transfers between devices  35 us (32%)
  waiting for transfers between devices  22.2 us (20%)
  local copies, waits for them, and re-layouts  1.18 us (1%)
    pallas_call x9, Pallas kernels, call(): pl.pallas_call(kernel, out_shape=outs, in_specs=[SMEM] * scalars + [spec]...  51.6 us
    ppermute x24, starting transfers between devices, move(): return lax.ppermute(array, 'pre', pairs)  21.6 us
    ppermute x24, waiting for transfers between devices, move(): return lax.ppermute(array, 'pre', pairs)  19.3 us
    ppermute x3, starting transfers between devices, on_device(): lax.ppermute(cuts[shift], 'rsp', [(g, (g + shift) % groups) for g in rang...  13.4 us
    ppermute x3, waiting for transfers between devices, on_device(): lax.ppermute(cuts[shift], 'rsp', [(g, (g + shift) % groups) for g in rang...  2.88 us
  transfers between devices with their start and end apart: 27, of which 11 were waited for; matrix products, arithmetic and copies ran while one was open for 0% of the time, Pallas kernels for 42%

profile of v6, /device:TPU:0, one launch (start us, length us, event | category | flops | bytes accessed | tf_op | source)
XLA Modules:
  0.0 111.5 jit_solution(721284129799895878)
XLA Ops:
  0.6 0.7 pad_add_fusion.place
  1.3 3.1 %prepare_keys.1 = (bf16[384,256]{1,0:T(8,128)(2,1)}, bf16[384,256]{1,0:T(8,128)(2,1)}, bf16[384,256]{1,0:T(8,128)(2,1)}, bf16[2,384,256]{2,1,0:T(8,128)(2,1)}, f32[8,128]{1,0:T(8,128)}) custom-call(s32[3]{0:T(128)} %pad_add_fusion.place, bf16[128,512]{1,0:T(8,128)(2,1)} %pk.1, bf16[128,512]{1,0:T(8,128)(2,1)} %pv.1, bf16[256,512]{1,0:T(8,128)(2,1)} %bitcast.15, ...), custom_call_target="tpu_custom_call" | custom-call | tf_op jit(solution)/shard_map/prepare_keys/pallas_call | solution.py:511
  4.4 0.5 collective-permute-start
  4.9 2.6 %collective-permute-start.1 = (bf16[384,256]{1,0:T(8,128)(2,1)}, bf16[384,256]{1,0:T(8,128)(2,1)S(1)}, u32[]{:S(2)}, u32[]{:S(2)}) collective-permute-start(bf16[384,256]{1,0:T(8,128)(2,1)} %get-tuple-element.91.refs_2_), channel_id=1, source_target_pairs={{0,8},{4,12},{8,0},{12,4},{16,24},{20,28},{24,16},{28,20},{1,9},{5... | collective-permute-start | bytes 589832 | tf_op jit(solution)/shard_map/ppermute | solution.py:505
  7.5 1.8 %collective-permute-start.3 = (bf16[384,256]{1,0:T(8,128)(2,1)}, bf16[384,256]{1,0:T(8,128)(2,1)S(1)}, u32[]{:S(2)}, u32[]{:S(2)}) collective-permute-start(bf16[384,256]{1,0:T(8,128)(2,1)} %get-tuple-element.91.refs_2_), channel_id=1, source_target_pairs={{0,16},{4,20},{8,24},{12,28},{16,0},{20,4},{24,8},{28,12},{1,17},{... | collective-permute-start | bytes 589832 | tf_op jit(solution)/shard_map/ppermute | solution.py:505
  9.3 6.5 %prepare_rows.1 = (bf16[2,288,1408]{2,1,0:T(8,128)(2,1)}, bf16[288,1408]{1,0:T(8,128)(2,1)}, bf16[288,1408]{1,0:T(8,128)(2,1)}) custom-call(s32[3]{0:T(128)} %pad_add_fusion.place, f32[8,128]{1,0:T(8,128)} %get-tuple-element.84.token, bf16[32,2560]{1,0:T(8,128)(2,1)} %pq.1, bf16[32,2560]{1,0:T(8,128)(2,1)} %po.1, bf16[32,2560]{1,0:T(8,128)(2,1)} %pg.1, ...), custom_call_target="tpu_custom_call" | custom-call | flops 1006632960 | bytes 13107200 | tf_op jit(solution)/shard_map/prepare_rows/pallas_call | solution.py:511
  15.8 1.3 %collective-permute-done.2.refs_5_ = bf16[384,256]{1,0:T(8,128)(2,1)S(1)} collective-permute-done((bf16[384,256]{1,0:T(8,128)(2,1)}, bf16[384,256]{1,0:T(8,128)(2,1)S(1)}, u32[]{:S(2)}, u32[]{:S(2)}) %collective-permute-start.2) | collective-permute-done | bytes 196640 | tf_op jit(solution)/shard_map/ppermute | solution.py:505
  17.1 1.4 %collective-permute-done.4.refs_7_ = bf16[384,256]{1,0:T(8,128)(2,1)S(1)} collective-permute-done((bf16[384,256]{1,0:T(8,128)(2,1)}, bf16[384,256]{1,0:T(8,128)(2,1)S(1)}, u32[]{:S(2)}, u32[]{:S(2)}) %collective-permute-start.4) | collective-permute-done | bytes 196640 | tf_op jit(solution)/shard_map/ppermute | solution.py:505
  19.0 1.7 %collective-permute-start.6 = (bf16[384,256]{1,0:T(8,128)(2,1)S(1)}, bf16[384,256]{1,0:T(8,128)(2,1)S(1)}, u32[]{:S(2)}, u32[]{:S(2)}) collective-permute-start(bf16[384,256]{1,0:T(8,128)(2,1)S(1)} %collective-permute-done.1.refs_4_), channel_id=1, source_target_pairs={{0,16},{4,20},{8,24},{12,28},{16,0},{20,4},{24,8},{28,12},{1,17},{... | collective-permute-start | bytes 589832 | tf_op jit(solution)/shard_map/ppermute | solution.py:505
  20.7 1.5 %collective-permute-start.7 = (bf16[384,256]{1,0:T(8,128)(2,1)S(1)}, bf16[384,256]{1,0:T(8,128)(2,1)S(1)}, u32[]{:S(2)}, u32[]{:S(2)}) collective-permute-start(bf16[384,256]{1,0:T(8,128)(2,1)S(1)} %collective-permute-done.4.refs_7_), channel_id=1, source_target_pairs={{0,8},{4,12},{8,0},{12,4},{16,24},{20,28},{24,16},{28,20},{1,9},{5... | collective-permute-start | bytes 589832 | tf_op jit(solution)/shard_map/ppermute | solution.py:505
  22.3 0.6 collective-permute-start.12
  23.2 3.6 %collective-permute-done.6.refs_8_ = bf16[384,256]{1,0:T(8,128)(2,1)S(1)} collective-permute-done((bf16[384,256]{1,0:T(8,128)(2,1)S(1)}, bf16[384,256]{1,0:T(8,128)(2,1)S(1)}, u32[]{:S(2)}, u32[]{:S(2)}) %collective-permute-start.6) | collective-permute-done | bytes 196640 | tf_op jit(solution)/shard_map/ppermute | solution.py:505
  26.7 2.7 %collective-permute-start.14 = (bf16[2,384,256]{2,1,0:T(8,128)(2,1)S(1)}, bf16[2,384,256]{2,1,0:T(8,128)(2,1)S(1)}, u32[]{:S(2)}, u32[]{:S(2)}) collective-permute-start(bf16[2,384,256]{2,1,0:T(8,128)(2,1)S(1)} %pad_maximum_fusion.refs_2_), channel_id=1, source_target_pairs={{0,24},{4,28},{8,16},{12,20},{16,8},{20,12},{24,0},{28,4},{1,25},{... | collective-permute-start | bytes 1179656 | tf_op jit(solution)/shard_map/ppermute | solution.py:505
  29.4 1.1 %copy-done.2 = bf16[288,1408]{1,0:T(8,128)(2,1)S(1)} copy-done((bf16[288,1408]{1,0:T(8,128)(2,1)S(1)}, bf16[288,1408]{1,0:T(8,128)(2,1)}, u32[]{:S(2)}) %copy-start.2) | copy-done | bytes 811032
  30.6 18.8 %attend.2 = (bf16[288,640]{1,0:T(8,128)(2,1)S(1)}, bf16[288,640]{1,0:T(8,128)(2,1)S(1)}, bf16[2,384,256]{2,1,0:T(8,128)(2,1)S(1)}, bf16[2,384,256]{2,1,0:T(8,128...) custom-call(s32[3]{0:T(128)S(1)} %copy-done, s32[8]{0:T(128)S(1)} %copy-done.4, ...), custom_call_target="tpu_custom_call" | custom-call | flops 6710886400 | bytes 8388608 | tf_op jit(solution)/shard_map/attend/pallas_call | solution.py:511
  49.3 0.7 collective-permute-start.8
  50.0 2.9 %collective-permute-start.10 = (bf16[2,384,256]{2,1,0:T(8,128)(2,1)S(1)}, bf16[2,384,256]{2,1,0:T(8,128)(2,1)S(1)}, u32[]{:S(2)}, u32[]{:S(2)}) collective-permute-start(bf16[2,384,256]{2,1,0:T(8,128)(2,1)S(1)} %get-tuple-element.100), channel_id=1, source_target_pairs={{0,24},{4,28},{8,16},{12,20},{16,8},{20,12},{24,0},{28,4},{1,25},{... | collective-permute-start | bytes 1179656 | tf_op jit(solution)/shard_map/ppermute | solution.py:505
  52.9 18.7 %attend.3 = (bf16[288,640]{1,0:T(8,128)(2,1)S(1)}, bf16[288,640]{1,0:T(8,128)(2,1)S(1)}, bf16[384,256]{1,0:T(8,128)(2,1)S(1)}, bf16[384,256]{1,0:T(8,128)(2,1)S(...) custom-call(s32[3]{0:T(128)S(1)} %copy-done, ...), custom_call_target="tpu_custom_call" | custom-call | flops 6710886400 | bytes 8388608 | tf_op jit(solution)/shard_map/attend/pallas_call | solution.py:511
  71.7 0.7 collective-permute-start.16
  72.4 1.2 %collective-permute-start.17 = (bf16[384,256]{1,0:T(8,128)(2,1)S(1)}, bf16[384,256]{1,0:T(8,128)(2,1)S(1)}, u32[]{:S(2)}, u32[]{:S(2)}) collective-permute-start(bf16[384,256]{1,0:T(8,128)(2,1)S(1)} %get-tuple-element.125), channel_id=1, source_target_pairs={{0,12},{4,8},{8,4},{12,0},{16,28},{20,24},{24,20},{28,16},{1,13},{... | collective-permute-start | bytes 589832 | tf_op jit(solution)/shard_map/ppermute | solution.py:505
  73.6 1.7 %collective-permute-start.18 = (bf16[384,256]{1,0:T(8,128)(2,1)S(1)}, bf16[384,256]{1,0:T(8,128)(2,1)S(1)}, u32[]{:S(2)}, u32[]{:S(2)}) collective-permute-start(bf16[384,256]{1,0:T(8,128)(2,1)S(1)} %get-tuple-element.126), channel_id=1, source_target_pairs={{0,16},{4,20},{8,24},{12,28},{16,0},{20,4},{24,8},{28,12},{1,17},{... | collective-permute-start | bytes 589832 | tf_op jit(solution)/shard_map/ppermute | solution.py:505
  75.5 3.9 %collective-permute-done.15.refs_2_ = bf16[384,256]{1,0:T(8,128)(2,1)S(1)} collective-permute-done((bf16[384,256]{1,0:T(8,128)(2,1)S(1)}, bf16[384,256]{1,0:T(8,128)(2,1)S(1)}, u32[]{:S(2)}, u32[]{:S(2)}) %collective-permute-start.15) | collective-permute-done | bytes 196640 | tf_op jit(solution)/shard_map/ppermute | solution.py:505
  79.6 3.3 %collective-permute-done.17.refs_6_ = bf16[384,256]{1,0:T(8,128)(2,1)S(1)} collective-permute-done((bf16[384,256]{1,0:T(8,128)(2,1)S(1)}, bf16[384,256]{1,0:T(8,128)(2,1)S(1)}, u32[]{:S(2)}, u32[]{:S(2)}) %collective-permute-start.17) | collective-permute-done | bytes 196640 | tf_op jit(solution)/shard_map/ppermute | solution.py:505
  83.7 0.6 collective-permute-start.20
  84.3 1.2 %collective-permute-start.22 = (bf16[384,256]{1,0:T(8,128)(2,1)S(1)}, bf16[384,256]{1,0:T(8,128)(2,1)S(1)}, u32[]{:S(2)}, u32[]{:S(2)}) collective-permute-start(bf16[384,256]{1,0:T(8,128)(2,1)S(1)} %get-tuple-element.136), channel_id=1, source_target_pairs={{0,20},{4,16},{8,28},{12,24},{16,4},{20,0},{24,12},{28,8},{1,21},{... | collective-permute-start | bytes 589832 | tf_op jit(solution)/shard_map/ppermute | solution.py:505
  85.5 5.1 %collective-permute-done.20.refs_3_ = bf16[384,256]{1,0:T(8,128)(2,1)S(1)} collective-permute-done((bf16[384,256]{1,0:T(8,128)(2,1)S(1)}, bf16[384,256]{1,0:T(8,128)(2,1)S(1)}, u32[]{:S(2)}, u32[]{:S(2)}) %collective-permute-start.20) | collective-permute-done | bytes 196640 | tf_op jit(solution)/shard_map/ppermute | solution.py:505
  90.9 0.6 spread_prompt.1
  91.5 1.6 %collective-permute-start.23 = (bf16[4,32,256]{2,1,0:T(8,128)(2,1)S(1)}, bf16[4,32,256]{2,1,0:T(8,128)(2,1)S(1)}, u32[]{:S(2)}, u32[]{:S(2)}) collective-permute-start(bf16[4,32,256]{2,1,0:T(8,128)(2,1)S(1)} %get-tuple-element.138), channel_id=1, source_target_pairs={{0,1},{1,2},{2,3},{3,0},{4,5},{5,6},{6,7},{7,4},{8,9},{9,10},{10,1... | collective-permute-start | bytes 196616 | tf_op jit(solution)/shard_map/ppermute | solution.py:687
  93.2 11.8 %collective-permute-start.24 = (bf16[4,32,256]{2,1,0:T(8,128)(2,1)S(1)}, bf16[4,32,256]{2,1,0:T(8,128)(2,1)S(1)}, u32[]{:S(2)}, u32[]{:S(2)}) collective-permute-start(bf16[4,32,256]{2,1,0:T(8,128)(2,1)S(1)} %get-tuple-element.139), channel_id=1, source_target_pairs={{0,2},{1,3},{2,0},{3,1},{4,6},{5,7},{6,4},{7,5},{8,10},{9,11},{10,... | collective-permute-start | bytes 196616 | tf_op jit(solution)/shard_map/ppermute | solution.py:687
  105.0 2.5 %finish_reply.1 = (bf16[32,2560]{1,0:T(8,128)(2,1)}, bf16[256,2560]{1,0:T(8,128)(2,1)}, bf16[256,512]{1,0:T(8,128)(2,1)}, bf16[256,512]{1,0:T(8,128)(2,1)}) custom-call(s32[3]{0:T(128)S(1)} %copy-done, f32[384,256]{1,0:T(8,128)S(1)} %get-tuple-element.117.refs_0_, bf16[384,256]{1,0:T(8,128)(2,1)S(1)} %collective-permute-done.19.refs_1_, ...), custom_call_target="tpu_custom_call" | custom-call | flops 469762048 | bytes 10485760 | tf_op jit(solution)/shard_map/finish_reply/pallas_call | solution.py:511
  107.5 2.4 %collective-permute-done.24.refs_2_ = bf16[4,32,256]{2,1,0:T(8,128)(2,1)S(1)} collective-permute-done((bf16[4,32,256]{2,1,0:T(8,128)(2,1)S(1)}, bf16[4,32,256]{2,1,0:T(8,128)(2,1)S(1)}, u32[]{:S(2)}, u32[]{:S(2)}) %collective-permute-start.24) | collective-permute-done | bytes 65568 | tf_op jit(solution)/shard_map/ppermute | solution.py:687
  110.3 1.2 %finish_prompt.1 = (bf16[32,512]{1,0:T(8,128)(2,1)}, bf16[32,512]{1,0:T(8,128)(2,1)}) custom-call(s32[3]{0:T(128)S(1)} %copy-done, bf16[4,32,256]{2,1,0:T(8,128)(2,1)S(1)} %get-tuple-element.147.refs_0_, bf16[4,32,256]{2,1,0:T(8,128)(2,1)S(1)} %collective-permute-done.23.refs_1_, bf16[4,32,256]{2,1,0:T(8,128)(2,1)S(1)} %collective-permute-done.24.refs_2_, ...), custom_call_target="tpu_custom_call" | custom-call | tf_op jit(solution)/shard_map/finish_prompt/pallas_call | solution.py:511
  (48 shorter events, 2.9 us)
Async XLA Ops:
  4.4 14.2 %collective-permute-start = (bf16[2,384,256]{2,1,0:T(8,128)(2,1)}, bf16[2,384,256]{2,1,0:T(8,128)(2,1)S(1)}, u32[]{:S(2)}, u32[]{:S(2)}) collective-permute-start(bf16[2,384,256]{2,1,0:T(8,128)(2,1)} %get-tuple-element.82), channel_id=1, source_target_pairs={{0,4},{4,0},{8,12},{12,8},{16,20},{20,16},{24,28},{28,24},{1,5},{5... | collective-permute-start | bytes 1179656 | tf_op jit(solution)/shard_map/ppermute | solution.py:505
  4.9 10.9 %collective-permute-start.1 = (bf16[384,256]{1,0:T(8,128)(2,1)}, bf16[384,256]{1,0:T(8,128)(2,1)S(1)}, u32[]{:S(2)}, u32[]{:S(2)}) collective-permute-start(bf16[384,256]{1,0:T(8,128)(2,1)} %get-tuple-element.91.refs_2_), channel_id=1, source_target_pairs={{0,8},{4,12},{8,0},{12,4},{16,24},{20,28},{24,16},{28,20},{1,9},{5... | collective-permute-start | bytes 589832 | tf_op jit(solution)/shard_map/ppermute | solution.py:505
  7.5 9.7 %collective-permute-start.2 = (bf16[384,256]{1,0:T(8,128)(2,1)}, bf16[384,256]{1,0:T(8,128)(2,1)S(1)}, u32[]{:S(2)}, u32[]{:S(2)}) collective-permute-start(bf16[384,256]{1,0:T(8,128)(2,1)} %get-tuple-element.83), channel_id=1, source_target_pairs={{0,12},{4,8},{8,4},{12,0},{16,28},{20,24},{24,20},{28,16},{1,13},{... | collective-permute-start | bytes 589832 | tf_op jit(solution)/shard_map/ppermute | solution.py:505
  7.5 9.6 %collective-permute-start.3 = (bf16[384,256]{1,0:T(8,128)(2,1)}, bf16[384,256]{1,0:T(8,128)(2,1)S(1)}, u32[]{:S(2)}, u32[]{:S(2)}) collective-permute-start(bf16[384,256]{1,0:T(8,128)(2,1)} %get-tuple-element.91.refs_2_), channel_id=1, source_target_pairs={{0,16},{4,20},{8,24},{12,28},{16,0},{20,4},{24,8},{28,12},{1,17},{... | collective-permute-start | bytes 589832 | tf_op jit(solution)/shard_map/ppermute | solution.py:505
  9.3 9.3 %collective-permute-start.4 = (bf16[384,256]{1,0:T(8,128)(2,1)}, bf16[384,256]{1,0:T(8,128)(2,1)S(1)}, u32[]{:S(2)}, u32[]{:S(2)}) collective-permute-start(bf16[384,256]{1,0:T(8,128)(2,1)} %get-tuple-element.83), channel_id=1, source_target_pairs={{0,20},{4,16},{8,28},{12,24},{16,4},{20,0},{24,12},{28,8},{1,21},{... | collective-permute-start | bytes 589832 | tf_op jit(solution)/shard_map/ppermute | solution.py:505
  9.3 20.1 %copy-start = (s32[3]{0:T(128)S(1)}, s32[3]{0:T(128)}, u32[]{:S(2)}) copy-start(s32[3]{0:T(128)} %pad_add_fusion.place) | copy-start | bytes 40
  9.3 20.1 %copy-start.3 = (bf16[384,256]{1,0:T(8,128)(2,1)S(1)}, bf16[384,256]{1,0:T(8,128)(2,1)}, u32[]{:S(2)}) copy-start(bf16[384,256]{1,0:T(8,128)(2,1)} %get-tuple-element.91.refs_2_) | copy-start | bytes 589828
  9.3 20.1 %copy-start.4 = (s32[8]{0:T(128)S(1)}, s32[8]{0:T(128)}, u32[]{:S(2)}) copy-start(s32[8]{0:T(128)} %reply_len.3) | copy-start | bytes 100
  9.3 20.1 %copy-start.5 = (s32[8]{0:T(128)S(1)}, s32[8]{0:T(128)}, u32[]{:S(2)}) copy-start(s32[8]{0:T(128)} %reply_slot.3) | copy-start | bytes 100
  18.6 10.8 %collective-permute-start.5 = (bf16[2,288,1408]{2,1,0:T(8,128)(2,1)}, bf16[2,288,1408]{2,1,0:T(8,128)(2,1)S(1)}, u32[]{:S(2)}, u32[]{:S(2)}) collective-permute-start(bf16[2,288,1408]{2,1,0:T(8,128)(2,1)} %get-tuple-element.90), channel_id=1, source_target_pairs={{0,4},{4,0},{8,12},{12,8},{16,20},{20,16},{24,28},{28,24},{1,5},{5... | collective-permute-start | bytes 4866056 | tf_op jit(solution)/shard_map/ppermute | solution.py:505
  19.0 7.8 %collective-permute-start.6 = (bf16[384,256]{1,0:T(8,128)(2,1)S(1)}, bf16[384,256]{1,0:T(8,128)(2,1)S(1)}, u32[]{:S(2)}, u32[]{:S(2)}) collective-permute-start(bf16[384,256]{1,0:T(8,128)(2,1)S(1)} %collective-permute-done.1.refs_4_), channel_id=1, source_target_pairs={{0,16},{4,20},{8,24},{12,28},{16,0},{20,4},{24,8},{28,12},{1,17},{... | collective-permute-start | bytes 589832 | tf_op jit(solution)/shard_map/ppermute | solution.py:505
  20.7 8.7 %collective-permute-start.7 = (bf16[384,256]{1,0:T(8,128)(2,1)S(1)}, bf16[384,256]{1,0:T(8,128)(2,1)S(1)}, u32[]{:S(2)}, u32[]{:S(2)}) collective-permute-start(bf16[384,256]{1,0:T(8,128)(2,1)S(1)} %collective-permute-done.4.refs_7_), channel_id=1, source_target_pairs={{0,8},{4,12},{8,0},{12,4},{16,24},{20,28},{24,16},{28,20},{1,9},{5... | collective-permute-start | bytes 589832 | tf_op jit(solution)/shard_map/ppermute | solution.py:505
  22.3 30.6 %copy-start.1 = (bf16[288,1408]{1,0:T(8,128)(2,1)S(1)}, bf16[288,1408]{1,0:T(8,128)(2,1)}, u32[]{:S(2)}) copy-start(bf16[288,1408]{1,0:T(8,128)(2,1)} %get-tuple-element.102.refs_0_) | copy-start | bytes 2433028
  22.3 27.7 %collective-permute-start.12 = (bf16[2,384,256]{2,1,0:T(8,128)(2,1)S(1)}, bf16[2,384,256]{2,1,0:T(8,128)(2,1)S(1)}, u32[]{:S(2)}, u32[]{:S(2)}) collective-permute-start(bf16[2,384,256]{2,1,0:T(8,128)(2,1)S(1)} %pad_maximum_fusion.refs_2_), channel_id=1, source_target_pairs={{0,8},{4,12},{8,0},{12,4},{16,24},{20,28},{24,16},{28,20},{1,9},{5... | collective-permute-start | bytes 1179656 | tf_op jit(solution)/shard_map/ppermute | solution.py:505
  22.9 30.0 %collective-permute-start.13 = (bf16[2,384,256]{2,1,0:T(8,128)(2,1)S(1)}, bf16[2,384,256]{2,1,0:T(8,128)(2,1)S(1)}, u32[]{:S(2)}, u32[]{:S(2)}) collective-permute-start(bf16[2,384,256]{2,1,0:T(8,128)(2,1)S(1)} %pad_maximum_fusion.refs_2_), channel_id=1, source_target_pairs={{0,16},{4,20},{8,24},{12,28},{16,0},{20,4},{24,8},{28,12},{1,17},{... | collective-permute-start | bytes 1179656 | tf_op jit(solution)/shard_map/ppermute | solution.py:505
  26.7 26.2 %collective-permute-start.14 = (bf16[2,384,256]{2,1,0:T(8,128)(2,1)S(1)}, bf16[2,384,256]{2,1,0:T(8,128)(2,1)S(1)}, u32[]{:S(2)}, u32[]{:S(2)}) collective-permute-start(bf16[2,384,256]{2,1,0:T(8,128)(2,1)S(1)} %pad_maximum_fusion.refs_2_), channel_id=1, source_target_pairs={{0,24},{4,28},{8,16},{12,20},{16,8},{20,12},{24,0},{28,4},{1,25},{... | collective-permute-start | bytes 1179656 | tf_op jit(solution)/shard_map/ppermute | solution.py:505
  49.3 22.3 %collective-permute-start.8 = (bf16[2,384,256]{2,1,0:T(8,128)(2,1)S(1)}, bf16[2,384,256]{2,1,0:T(8,128)(2,1)S(1)}, u32[]{:S(2)}, u32[]{:S(2)}) collective-permute-start(bf16[2,384,256]{2,1,0:T(8,128)(2,1)S(1)} %get-tuple-element.98), channel_id=1, source_target_pairs={{0,8},{4,12},{8,0},{12,4},{16,24},{20,28},{24,16},{28,20},{1,9},{5... | collective-permute-start | bytes 1179656 | tf_op jit(solution)/shard_map/ppermute | solution.py:505
  50.0 21.6 %collective-permute-start.9 = (bf16[2,384,256]{2,1,0:T(8,128)(2,1)S(1)}, bf16[2,384,256]{2,1,0:T(8,128)(2,1)S(1)}, u32[]{:S(2)}, u32[]{:S(2)}) collective-permute-start(bf16[2,384,256]{2,1,0:T(8,128)(2,1)S(1)} %get-tuple-element.99), channel_id=1, source_target_pairs={{0,16},{4,20},{8,24},{12,28},{16,0},{20,4},{24,8},{28,12},{1,17},{... | collective-permute-start | bytes 1179656 | tf_op jit(solution)/shard_map/ppermute | solution.py:505
  50.0 21.6 %collective-permute-start.10 = (bf16[2,384,256]{2,1,0:T(8,128)(2,1)S(1)}, bf16[2,384,256]{2,1,0:T(8,128)(2,1)S(1)}, u32[]{:S(2)}, u32[]{:S(2)}) collective-permute-start(bf16[2,384,256]{2,1,0:T(8,128)(2,1)S(1)} %get-tuple-element.100), channel_id=1, source_target_pairs={{0,24},{4,28},{8,16},{12,20},{16,8},{20,12},{24,0},{28,4},{1,25},{... | collective-permute-start | bytes 1179656 | tf_op jit(solution)/shard_map/ppermute | solution.py:505
  52.9 18.7 %collective-permute-start.11 = (bf16[288,640]{1,0:T(8,128)(2,1)S(1)}, bf16[288,640]{1,0:T(8,128)(2,1)S(1)}, u32[]{:S(2)}, u32[]{:S(2)}) collective-permute-start(bf16[288,640]{1,0:T(8,128)(2,1)S(1)} %get-tuple-element.101), channel_id=1, source_target_pairs={{0,4},{4,0},{8,12},{12,8},{16,20},{20,16},{24,28},{28,24},{1,5},{5... | collective-permute-start | bytes 1105928 | tf_op jit(solution)/shard_map/ppermute | solution.py:505
  71.6 7.8 %collective-permute-start.15 = (bf16[384,256]{1,0:T(8,128)(2,1)S(1)}, bf16[384,256]{1,0:T(8,128)(2,1)S(1)}, u32[]{:S(2)}, u32[]{:S(2)}) collective-permute-start(bf16[384,256]{1,0:T(8,128)(2,1)S(1)} %get-tuple-element.120), channel_id=1, source_target_pairs={{0,16},{4,20},{8,24},{12,28},{16,0},{20,4},{24,8},{28,12},{1,17},{... | collective-permute-start | bytes 589832 | tf_op jit(solution)/shard_map/ppermute | solution.py:505
  71.7 7.8 %collective-permute-start.16 = (bf16[384,256]{1,0:T(8,128)(2,1)S(1)}, bf16[384,256]{1,0:T(8,128)(2,1)S(1)}, u32[]{:S(2)}, u32[]{:S(2)}) collective-permute-start(bf16[384,256]{1,0:T(8,128)(2,1)S(1)} %get-tuple-element.121), channel_id=1, source_target_pairs={{0,8},{4,12},{8,0},{12,4},{16,24},{20,28},{24,16},{28,20},{1,9},{5... | collective-permute-start | bytes 589832 | tf_op jit(solution)/shard_map/ppermute | solution.py:505
  72.4 10.5 %collective-permute-start.17 = (bf16[384,256]{1,0:T(8,128)(2,1)S(1)}, bf16[384,256]{1,0:T(8,128)(2,1)S(1)}, u32[]{:S(2)}, u32[]{:S(2)}) collective-permute-start(bf16[384,256]{1,0:T(8,128)(2,1)S(1)} %get-tuple-element.125), channel_id=1, source_target_pairs={{0,12},{4,8},{8,4},{12,0},{16,28},{20,24},{24,20},{28,16},{1,13},{... | collective-permute-start | bytes 589832 | tf_op jit(solution)/shard_map/ppermute | solution.py:505
  73.6 9.6 %collective-permute-start.18 = (bf16[384,256]{1,0:T(8,128)(2,1)S(1)}, bf16[384,256]{1,0:T(8,128)(2,1)S(1)}, u32[]{:S(2)}, u32[]{:S(2)}) collective-permute-start(bf16[384,256]{1,0:T(8,128)(2,1)S(1)} %get-tuple-element.126), channel_id=1, source_target_pairs={{0,16},{4,20},{8,24},{12,28},{16,0},{20,4},{24,8},{28,12},{1,17},{... | collective-permute-start | bytes 589832 | tf_op jit(solution)/shard_map/ppermute | solution.py:505
  83.2 21.8 %collective-permute-start.26 = (bf16[288,640]{1,0:T(8,128)(2,1)S(1)}, bf16[288,640]{1,0:T(8,128)(2,1)S(1)}, u32[]{:S(2)}, u32[]{:S(2)}) collective-permute-start(bf16[288,640]{1,0:T(8,128)(2,1)S(1)} %get-tuple-element.144), channel_id=1, source_target_pairs={{0,4},{4,0},{8,12},{12,8},{16,20},{20,16},{24,28},{28,24},{1,5},{5... | collective-permute-start | bytes 1105928 | tf_op jit(solution)/shard_map/ppermute | solution.py:505
  83.3 2.2 %collective-permute-start.19 = (bf16[384,256]{1,0:T(8,128)(2,1)S(1)}, bf16[384,256]{1,0:T(8,128)(2,1)S(1)}, u32[]{:S(2)}, u32[]{:S(2)}) collective-permute-start(bf16[384,256]{1,0:T(8,128)(2,1)S(1)} %get-tuple-element.130), channel_id=1, source_target_pairs={{0,4},{4,0},{8,12},{12,8},{16,20},{20,16},{24,28},{28,24},{1,5},{5... | collective-permute-start | bytes 589832 | tf_op jit(solution)/shard_map/ppermute | solution.py:505
  83.7 6.9 %collective-permute-start.20 = (bf16[384,256]{1,0:T(8,128)(2,1)S(1)}, bf16[384,256]{1,0:T(8,128)(2,1)S(1)}, u32[]{:S(2)}, u32[]{:S(2)}) collective-permute-start(bf16[384,256]{1,0:T(8,128)(2,1)S(1)} %get-tuple-element.132), channel_id=1, source_target_pairs={{0,8},{4,12},{8,0},{12,4},{16,24},{20,28},{24,16},{28,20},{1,9},{5... | collective-permute-start | bytes 589832 | tf_op jit(solution)/shard_map/ppermute | solution.py:505
  84.3 6.3 %collective-permute-start.21 = (bf16[384,256]{1,0:T(8,128)(2,1)S(1)}, bf16[384,256]{1,0:T(8,128)(2,1)S(1)}, u32[]{:S(2)}, u32[]{:S(2)}) collective-permute-start(bf16[384,256]{1,0:T(8,128)(2,1)S(1)} %get-tuple-element.134), channel_id=1, source_target_pairs={{0,4},{4,0},{8,12},{12,8},{16,20},{20,16},{24,28},{28,24},{1,5},{5... | collective-permute-start | bytes 589832 | tf_op jit(solution)/shard_map/ppermute | solution.py:505
  84.3 6.6 %collective-permute-start.22 = (bf16[384,256]{1,0:T(8,128)(2,1)S(1)}, bf16[384,256]{1,0:T(8,128)(2,1)S(1)}, u32[]{:S(2)}, u32[]{:S(2)}) collective-permute-start(bf16[384,256]{1,0:T(8,128)(2,1)S(1)} %get-tuple-element.136), channel_id=1, source_target_pairs={{0,20},{4,16},{8,28},{12,24},{16,4},{20,0},{24,12},{28,8},{1,21},{... | collective-permute-start | bytes 589832 | tf_op jit(solution)/shard_map/ppermute | solution.py:505
  91.5 15.9 %collective-permute-start.23 = (bf16[4,32,256]{2,1,0:T(8,128)(2,1)S(1)}, bf16[4,32,256]{2,1,0:T(8,128)(2,1)S(1)}, u32[]{:S(2)}, u32[]{:S(2)}) collective-permute-start(bf16[4,32,256]{2,1,0:T(8,128)(2,1)S(1)} %get-tuple-element.138), channel_id=1, source_target_pairs={{0,1},{1,2},{2,3},{3,0},{4,5},{5,6},{6,7},{7,4},{8,9},{9,10},{10,1... | collective-permute-start | bytes 196616 | tf_op jit(solution)/shard_map/ppermute | solution.py:687
  93.2 16.7 %collective-permute-start.24 = (bf16[4,32,256]{2,1,0:T(8,128)(2,1)S(1)}, bf16[4,32,256]{2,1,0:T(8,128)(2,1)S(1)}, u32[]{:S(2)}, u32[]{:S(2)}) collective-permute-start(bf16[4,32,256]{2,1,0:T(8,128)(2,1)S(1)} %get-tuple-element.139), channel_id=1, source_target_pairs={{0,2},{1,3},{2,0},{3,1},{4,6},{5,7},{6,4},{7,5},{8,10},{9,11},{10,... | collective-permute-start | bytes 196616 | tf_op jit(solution)/shard_map/ppermute | solution.py:687
  105.0 5.4 %collective-permute-start.25 = (bf16[4,32,256]{2,1,0:T(8,128)(2,1)S(1)}, bf16[4,32,256]{2,1,0:T(8,128)(2,1)S(1)}, u32[]{:S(2)}, u32[]{:S(2)}) collective-permute-start(bf16[4,32,256]{2,1,0:T(8,128)(2,1)S(1)} %get-tuple-element.140), channel_id=1, source_target_pairs={{0,3},{1,0},{2,1},{3,2},{4,7},{5,4},{6,5},{7,6},{8,11},{9,8},{10,9... | collective-permute-start | bytes 196616 | tf_op jit(solution)/shard_map/ppermute | solution.py:687
  (2 other events, 14.0 us)

commit v7 on v6

--- a/solution.py
+++ b/solution.py
@@ -147,8 +147,9 @@
     count = chips if joint_keys else chips * CORES
     keys_in, refs = refs[:count], refs[count:]
     query_out, refs = refs[:2], refs[2:]
-    count = chips * CORES if joint_keys else chips
-    keys_out, refs = refs[:count], refs[count:]
+    keys_out, refs = refs[:chips], refs[chips:]
+    groups = prompt_keys // prompt_rows
+    cuts_out, refs = (refs[:groups], refs[groups:]) if joint_keys else ((), refs)
     keys, keys_t, total, query, gradient, query_t, gradient_t, deltas, delta, scores, peaks, top, mass, *refs = refs
     query_grad, stages = refs[0], (refs[1:3], refs[3:5])
     chip, core, group = place[0], place[1], place[2]
@@ -395,18 +396,23 @@
                 at : at + prompt_own
             ]
 
+    def put(out, at, count):
+        out[:, :HEAD_WIDTH] = (total[pl.ds(at, count), :HEAD_WIDTH] * SCALE).astype(BF16)
+        out[:, HEAD_WIDTH:] = total[pl.ds(at, count), HEAD_WIDTH:].astype(BF16)
+
     for index in range(chips * CORES):
         away, other = index // CORES, index % CORES
-        out = keys_out[index] if joint_keys else keys_out[away].at[other]
-
-        def put(to, at, count):
-            out[to : to + count, :HEAD_WIDTH] = (total[at : at + count, :HEAD_WIDTH] * SCALE).astype(BF16)
-            out[to : to + count, HEAD_WIDTH:] = total[at : at + count, HEAD_WIDTH:].astype(BF16)
-
-        put(0, away * chip_prompt + other * prompt_keys, prompt_keys)
+        out = keys_out[away].at[other]
+        prompt_at = away * chip_prompt + other * prompt_keys
+        if not joint_keys:
+            put(out.at[:prompt_keys], prompt_at, prompt_keys)
+        for shift, cut in enumerate(cuts_out):
+            part = lax.rem(group + shift, groups) * prompt_rows
+            put(cut.at[index], pl.multiple_of(prompt_at + part, prompt_rows), prompt_rows)
         for slot in range(RESP_DEV):
             at = chips * chip_prompt + (slot * chips + away) * positions + other * own_positions
-            put(prompt_keys + slot * own_positions, at, own_positions)
+            to = slot * own_positions + (0 if joint_keys else prompt_keys)
+            put(out.at[to : to + own_positions], at, own_positions)
 
 
 def add(first, *rest):
@@ -416,56 +422,75 @@
     return value
 
 
-def add_pairs(*refs):
-    count = len(refs) // 3
-    for index in range(count):
-        refs[2 * count + index][...] = add(refs[index][...], refs[count + index][...]).astype(BF16)
-
-
-def collect(*refs):
-    parts, mine, theirs = refs[:-2], refs[-2], refs[-1]
-    mine[...] = add(*(part[0] for part in parts))
-    theirs[...] = add(*(part[1] for part in parts)).astype(BF16)
-
-
-def spread_prompt(sizes, place, *refs):
-    refs, outs, summed = refs[: sum(sizes)], refs[sum(sizes) : -1], refs[-1]
-    groups, rows = len(outs), outs[0].shape[1]
-    for index, size in enumerate(sizes):
-        parts, refs = refs[:size], refs[size:]
-        summed[index] = add(*(part[: groups * rows] for part in parts))
+def collect_first(chips, prompt_keys, place, *refs):
+    parts, refs = refs[:chips], refs[chips:]
+    groups = (len(refs) - 3) // 2
+    cuts, mine, theirs, outs, summed = refs[:groups], refs[groups], refs[groups + 1], refs[groups + 2 : -1], refs[-1]
+    rows = prompt_keys // groups
+    for other in range(CORES):
+        value = add(*(part[other, prompt_keys:] for part in parts))
+        if other == 0:
+            mine[...] = value
+        else:
+            theirs[...] = value.astype(BF16)
+        summed[other] = add(*(part[other, :prompt_keys] for part in parts))
     for shift in range(groups):
         at = pl.ds(pl.multiple_of(lax.rem(place[2] + shift, groups) * rows, rows), rows)
-        for index in range(len(sizes)):
-            outs[shift][index] = summed[index, at].astype(BF16)
-
-
-def finish_reply(sizes, place, *refs):
-    parts_in, refs = refs[: sum(sizes)], refs[sum(sizes) :]
-    queries, refs = refs[: len(sizes)], refs[len(sizes) :]
-    prompt_dq, reply_dq, reply_dk, reply_dv = refs
+        for other in range(CORES):
+            outs[shift][other] = summed[other, at].astype(BF16)
+        outs[shift][CORES:] = cuts[shift][...]
+
+
+def add_groups(groups, *refs):
+    parts, first, outs = refs[:groups], refs[groups], refs[groups + 1 :]
+    value = add(*(part[...] for part in parts)).astype(BF16)
+    first[...] = value[:CORES]
+    for away, out in enumerate(outs):
+        out[...] = value[CORES * (away + 1) : CORES * (away + 2)]
+
+
+def collect_second(chips, *refs):
+    reply_parts, refs = refs[:chips], refs[chips:]
+    prompt_parts, refs = refs[:chips], refs[chips:]
+    prompt0, theirs0, reply1, prompt1, theirs = refs
+    reply, rows = theirs0.shape[0], prompt0.shape[1]
+    step = max(rows, 16)
+    reply1[...] = add(*(part[0] for part in reply_parts))
+    prompt1[...] = add(*(part[0] for part in prompt_parts))
+    theirs[:reply] = theirs0[...]
+    theirs[reply : 2 * reply] = add(*(part[1] for part in reply_parts)).astype(BF16)
+    theirs[2 * reply : 2 * reply + rows] = prompt0[1]
+    theirs[2 * reply + step : 2 * reply + step + rows] = add(*(part[1] for part in prompt_parts)).astype(BF16)
+
+
+def finish_queries(place, *refs):
+    queries, prompt_dq, reply_dq = refs[:-2], refs[-2], refs[-1]
     reply = reply_dq.shape[0]
     order = unsorting(reply)
-    for index, size in enumerate(sizes):
-        parts, parts_in = parts_in[:size], parts_in[size:]
-        head = head_of(place[1], index % CORES, index // CORES)
-        span = lanes(head, HEAD_WIDTH)
-        value = add(*(part[part.shape[0] - reply :] for part in parts))
-        value = dot(order, value.astype(BF16)).astype(BF16)
-        reply_dk[:, span] = value[:, :HEAD_WIDTH]
-        reply_dv[:, span] = value[:, HEAD_WIDTH:]
-        span = lanes(head, GROUP_WIDTH)
-        reply_dq[:, span] = dot(order, queries[index][:reply]).astype(BF16)
-        prompt_dq[:, span] = queries[index][reply:]
-
-
-def finish_prompt(place, *refs):
-    parts, prompt_dk, prompt_dv = refs[:-2], refs[-2], refs[-1]
-    for index in range(KEY_VALUE_HEADS):
-        span = lanes(head_of(place[1], index % CORES, index // CORES), HEAD_WIDTH)
-        value = add(*(part[index] for part in parts)).astype(BF16)
-        prompt_dk[:, span] = value[:, :HEAD_WIDTH]
-        prompt_dv[:, span] = value[:, HEAD_WIDTH:]
+    for index, query in enumerate(queries):
+        span = lanes(head_of(place[1], index % CORES, index // CORES), GROUP_WIDTH)
+        reply_dq[:, span] = dot(order, query[:reply]).astype(BF16)
+        prompt_dq[:, span] = query[reply:]
+
+
+def finish_keys(place, reply0, reply1, prompt0, prompt1, theirs, prompt_dk, prompt_dv, reply_dk, reply_dv):
+    reply, rows = reply_dk.shape[0], prompt_dk.shape[0]
+    step = max(rows, 16)
+    order = unsorting(reply)
+    for local in range(LOCAL_HEADS):
+        for other in range(CORES):
+            span = lanes(head_of(place[1], other, local), HEAD_WIDTH)
+            if other:
+                value = theirs[local * reply : (local + 1) * reply]
+                prompt = theirs[2 * reply + local * step : 2 * reply + local * step + rows]
+            else:
+                value = (reply1 if local else reply0)[...].astype(BF16)
+                prompt = prompt1[...].astype(BF16) if local else prompt0[0]
+            value = dot(order, value).astype(BF16)
+            reply_dk[:, span] = value[:, :HEAD_WIDTH]
+            reply_dv[:, span] = value[:, HEAD_WIDTH:]
+            prompt_dk[:, span] = prompt[:, :HEAD_WIDTH]
+            prompt_dv[:, span] = prompt[:, HEAD_WIDTH:]
 
 
 def on_device(
@@ -587,12 +612,14 @@
     sizes = (chips, reply_own, prompt_own, prompt_rows, prompt_keys)
     score_count = GROUP * (positions * RESP_DEV * slots * block)
 
+    cut_rows = prompt_keys // groups
     rows_theirs, *rows_mine = rows
     rows_theirs = swap(rows_theirs)
 
     def run_attend(local, key_blocks):
         joint_keys = local == 1
-        sums = [shape(*key_shape)] * devices if joint_keys else [shape(CORES, *key_shape)] * chips
+        cut = [shape(devices, cut_rows, 2 * HEAD_WIDTH)] * groups
+        sums = [shape(CORES, reply_own, 2 * HEAD_WIDTH)] * chips + cut if joint_keys else [shape(CORES, *key_shape)] * chips
         query_mine, query_theirs, *sums = call(
             functools.partial(attend, sizes, joint_keys),
             "attend",
@@ -641,78 +668,66 @@
     arrived0, query_theirs0, query_theirs1, sums1 = lax.optimization_barrier(
         (arrived0, query_theirs0, query_theirs1, sums1)
     )
-    sums1 = [sums1[CORES * away : CORES * away + CORES] for away in range(chips)]
-    mine0, theirs0 = call(
-        collect,
-        "collect",
+    sums1, cuts1 = sums1[:chips], sums1[chips:]
+    key_width = KEY_VALUE_HEADS * HEAD_WIDTH
+    query_width = QUERY_HEADS * HEAD_WIDTH
+    reply0, theirs0, *cuts = call(
+        functools.partial(collect_first, chips, prompt_keys),
+        "collect_first",
         SMALL_MIB,
-        arrived0,
-        [shape(*key_shape, dtype=F32), shape(*key_shape)],
-        scalars=0,
-    )
-    if relayed:
-        through_y, through_x = move(sums1[3][0], 2), move(sums1[3][1], 1)
-        for_x, for_y = call(
-            add_pairs,
-            "add_pairs",
-            SMALL_MIB,
-            (sums1[1][0], sums1[2][1], through_y, through_x),
-            [shape(*key_shape)] * 2,
-            scalars=0,
-        )
-        near = [sums1[0][0], move(sums1[1][1], 1, 1), move(sums1[2][0], 2)]
-        for_x, for_y, near, sums1[0][1], query_theirs1, theirs0 = lax.optimization_barrier(
-            (for_x, for_y, near, sums1[0][1], query_theirs1, theirs0)
-        )
-        lists1 = [[near[0], move(for_x, 1), near[2]], [swap(sums1[0][1]), near[1], move(for_y, 2, 1)]]
-    else:
-        lists1 = [
-            [move(pair[other], away, other) if away or other else pair[other] for away, pair in enumerate(sums1)]
-            for other in range(CORES)
-        ]
-    lists = [[mine0], [swap(theirs0)]] + lists1
-    queries = [query_mine0, query_theirs0, query_mine1, swap(query_theirs1)]
-    counts = [len(parts) for parts in lists]
-    parts = [part for one in lists for part in one]
-    cut_rows = prompt_keys // groups
-    cuts = call(
-        functools.partial(spread_prompt, counts),
-        "spread_prompt",
-        SMALL_MIB,
-        (place, *parts),
-        [shape(KEY_VALUE_HEADS, cut_rows, 2 * HEAD_WIDTH)] * groups,
-        scratch_shapes=[pltpu.VMEM((KEY_VALUE_HEADS, prompt_keys, 2 * HEAD_WIDTH), F32)],
+        (place, *arrived0, *cuts1),
+        [shape(reply_own, 2 * HEAD_WIDTH, dtype=F32), shape(reply_own, 2 * HEAD_WIDTH)]
+        + [shape(CORES + devices, cut_rows, 2 * HEAD_WIDTH)] * groups,
+        scratch_shapes=[pltpu.VMEM((CORES, prompt_keys, 2 * HEAD_WIDTH), F32)],
     )
     slices = [cuts[0]] + [
         lax.ppermute(cuts[shift], "rsp", [(g, (g + shift) % groups) for g in range(groups)])
         for shift in range(1, groups)
     ]
-    key_width = KEY_VALUE_HEADS * HEAD_WIDTH
-    query_width = QUERY_HEADS * HEAD_WIDTH
-    prompt_dq, reply_dq, reply_dk, reply_dv = call(
-        functools.partial(finish_reply, counts),
-        "finish_reply",
+    slices[1], sums1[chips - 1], query_theirs1 = lax.optimization_barrier(
+        (slices[1], sums1[chips - 1], query_theirs1)
+    )
+    arrived1 = [sums1[0]] + [move(sums1[away], away) for away in range(1, chips)]
+    prompt_dq, reply_dq = call(
+        finish_queries,
+        "finish_queries",
         SMALL_MIB,
-        (place, *parts, *queries),
-        [
-            shape(prompt_own, query_width),
-            shape(reply_own, query_width),
-            shape(reply_own, key_width),
-            shape(reply_own, key_width),
-        ],
+        (place, query_mine0, query_theirs0, query_mine1, swap(query_theirs1)),
+        [shape(prompt_own, query_width), shape(reply_own, query_width)],
         cost_estimate=pl.CostEstimate(
-            flops=2 * reply_own * reply_own * (query_width + 2 * key_width),
-            bytes_accessed=16 * reply_own * query_width,
+            flops=2 * reply_own * reply_own * query_width,
+            bytes_accessed=8 * reply_own * query_width,
             transcendentals=0,
         ),
     )
-    slices, prompt_dq = lax.optimization_barrier((slices, prompt_dq))
-    prompt_dk, prompt_dv = call(
-        finish_prompt,
-        "finish_prompt",
+    slices, prompt_dq, reply_dq = lax.optimization_barrier((slices, prompt_dq, reply_dq))
+    prompt0, *prompt_parts = call(
+        functools.partial(add_groups, groups),
+        "add_groups",
         SMALL_MIB,
-        (place, *slices),
-        [shape(cut_rows, key_width)] * 2,
+        slices,
+        [shape(CORES, cut_rows, 2 * HEAD_WIDTH)] * (1 + chips),
+        scalars=0,
+    )
+    prompt_parts = [prompt_parts[0]] + [move(prompt_parts[away], away) for away in range(1, chips)]
+    reply1, prompt1, theirs = call(
+        functools.partial(collect_second, chips),
+        "collect_second",
+        SMALL_MIB,
+        (*arrived1, *prompt_parts, prompt0, theirs0),
+        [
+            shape(reply_own, 2 * HEAD_WIDTH, dtype=F32),
+            shape(cut_rows, 2 * HEAD_WIDTH, dtype=F32),
+            shape(2 * reply_own + 2 * max(cut_rows, 16), 2 * HEAD_WIDTH),
+        ],
+        scalars=0,
+    )
+    prompt_dk, prompt_dv, reply_dk, reply_dv = call(
+        finish_keys,
+        "finish_keys",
+        SMALL_MIB,
+        (place, reply0, reply1, prompt0, prompt1, swap(theirs)),
+        [shape(cut_rows, key_width)] * 2 + [shape(reply_own, key_width)] * 2,
     )
     return (
         prompt_dq[:prompt_rows],

time: 111 us -> 113 us (1.018); the launches traced: 112 us -> 112 us
  waiting for transfers between devices: 22.2 us -> 19.9 us
  starting transfers between devices: 35 us -> 37.3 us
    ppermute x24 -> x23, waiting for transfers between devices: 19.3 us -> 11.3 us  [move(): return lax.ppermute(array, 'pre', pairs)]
    ppermute x24 -> x23, starting transfers between devices: 21.6 us -> 27.6 us  [move(): return lax.ppermute(array, 'pre', pairs)]
    ppermute x3, waiting for transfers between devices: 2.88 us -> 8.56 us  [on_device(): lax.ppermute(cuts[shift], 'rsp', [(g, (g + shift) % groups) for g in rang...]
    ppermute x3, starting transfers between devices: 13.4 us -> 9.72 us  [on_device(): lax.ppermute(cuts[shift], 'rsp', [(g, (g + shift) % groups) for g in rang...]
  transfers between devices with their start and end apart: 27 -> 26, of which waited for: 11 -> 9; matrix products, arithmetic and copies ran while one was open for 0% -> 0% of each run, Pallas kernels for 42% -> 41%
where the time goes in v7:
time: 113 us; the launch traced here: 112 us
  Pallas kernels  51.9 us (46%)
  starting transfers between devices  37.3 us (33%)
  waiting for transfers between devices  19.9 us (18%)
  local copies, waits for them, and re-layouts  1.18 us (1%)
    pallas_call x9, Pallas kernels, call(): pl.pallas_call(kernel, out_shape=outs, in_specs=[SMEM] * scalars + [spec]...  51.9 us
    ppermute x23, starting transfers between devices, move(): return lax.ppermute(array, 'pre', pairs)  27.6 us
    ppermute x23, waiting for transfers between devices, move(): return lax.ppermute(array, 'pre', pairs)  11.3 us
    ppermute x3, starting transfers between devices, on_device(): lax.ppermute(cuts[shift], 'rsp', [(g, (g + shift) % groups) for g in rang...  9.72 us
    ppermute x3, waiting for transfers between devices, on_device(): lax.ppermute(cuts[shift], 'rsp', [(g, (g + shift) % groups) for g in rang...  8.56 us
  transfers between devices with their start and end apart: 26, of which 9 were waited for; matrix products, arithmetic and copies ran while one was open for 0% of the time, Pallas kernels for 41%

profile of v7, /device:TPU:0, one launch (start us, length us, event | category | flops | bytes accessed | tf_op | source)
XLA Modules:
  0.0 111.7 jit_solution(10236880045215979656)
XLA Ops:
  1.2 3.1 %prepare_keys.1 = (bf16[384,256]{1,0:T(8,128)(2,1)}, bf16[384,256]{1,0:T(8,128)(2,1)}, bf16[384,256]{1,0:T(8,128)(2,1)}, bf16[2,384,256]{2,1,0:T(8,128)(2,1)}, f32[8,128]{1,0:T(8,128)}) custom-call(s32[3]{0:T(128)} %pad_add_fusion.place, bf16[128,512]{1,0:T(8,128)(2,1)} %pk.1, bf16[128,512]{1,0:T(8,128)(2,1)} %pv.1, bf16[256,512]{1,0:T(8,128)(2,1)} %bitcast.15, ...), custom_call_target="tpu_custom_call" | custom-call | tf_op jit(solution)/shard_map/prepare_keys/pallas_call | solution.py:536
  4.8 2.6 %collective-permute-start.1 = (bf16[384,256]{1,0:T(8,128)(2,1)}, bf16[384,256]{1,0:T(8,128)(2,1)S(1)}, u32[]{:S(2)}, u32[]{:S(2)}) collective-permute-start(bf16[384,256]{1,0:T(8,128)(2,1)} %get-tuple-element.93.refs_2_), channel_id=1, source_target_pairs={{0,8},{4,12},{8,0},{12,4},{16,24},{20,28},{24,16},{28,20},{1,9},{5... | collective-permute-start | bytes 589832 | tf_op jit(solution)/shard_map/ppermute | solution.py:530
  7.5 1.8 %collective-permute-start.3 = (bf16[384,256]{1,0:T(8,128)(2,1)}, bf16[384,256]{1,0:T(8,128)(2,1)S(1)}, u32[]{:S(2)}, u32[]{:S(2)}) collective-permute-start(bf16[384,256]{1,0:T(8,128)(2,1)} %get-tuple-element.93.refs_2_), channel_id=1, source_target_pairs={{0,16},{4,20},{8,24},{12,28},{16,0},{20,4},{24,8},{28,12},{1,17},{... | collective-permute-start | bytes 589832 | tf_op jit(solution)/shard_map/ppermute | solution.py:530
  9.3 6.5 %prepare_rows.1 = (bf16[2,288,1408]{2,1,0:T(8,128)(2,1)}, bf16[288,1408]{1,0:T(8,128)(2,1)}, bf16[288,1408]{1,0:T(8,128)(2,1)}) custom-call(s32[3]{0:T(128)} %pad_add_fusion.place, f32[8,128]{1,0:T(8,128)} %get-tuple-element.86.token, bf16[32,2560]{1,0:T(8,128)(2,1)} %pq.1, bf16[32,2560]{1,0:T(8,128)(2,1)} %po.1, bf16[32,2560]{1,0:T(8,128)(2,1)} %pg.1, ...), custom_call_target="tpu_custom_call" | custom-call | flops 1006632960 | bytes 13107200 | tf_op jit(solution)/shard_map/prepare_rows/pallas_call | solution.py:536
  15.8 1.3 %collective-permute-done.2.refs_5_ = bf16[384,256]{1,0:T(8,128)(2,1)S(1)} collective-permute-done((bf16[384,256]{1,0:T(8,128)(2,1)}, bf16[384,256]{1,0:T(8,128)(2,1)S(1)}, u32[]{:S(2)}, u32[]{:S(2)}) %collective-permute-start.2) | collective-permute-done | bytes 196640 | tf_op jit(solution)/shard_map/ppermute | solution.py:530
  17.1 1.4 %collective-permute-done.4.refs_7_ = bf16[384,256]{1,0:T(8,128)(2,1)S(1)} collective-permute-done((bf16[384,256]{1,0:T(8,128)(2,1)}, bf16[384,256]{1,0:T(8,128)(2,1)S(1)}, u32[]{:S(2)}, u32[]{:S(2)}) %collective-permute-start.4) | collective-permute-done | bytes 196640 | tf_op jit(solution)/shard_map/ppermute | solution.py:530
  18.9 1.7 %collective-permute-start.6 = (bf16[384,256]{1,0:T(8,128)(2,1)S(1)}, bf16[384,256]{1,0:T(8,128)(2,1)S(1)}, u32[]{:S(2)}, u32[]{:S(2)}) collective-permute-start(bf16[384,256]{1,0:T(8,128)(2,1)S(1)} %collective-permute-done.1.refs_4_), channel_id=1, source_target_pairs={{0,16},{4,20},{8,24},{12,28},{16,0},{20,4},{24,8},{28,12},{1,17},{... | collective-permute-start | bytes 589832 | tf_op jit(solution)/shard_map/ppermute | solution.py:530
  20.6 1.5 %collective-permute-start.7 = (bf16[384,256]{1,0:T(8,128)(2,1)S(1)}, bf16[384,256]{1,0:T(8,128)(2,1)S(1)}, u32[]{:S(2)}, u32[]{:S(2)}) collective-permute-start(bf16[384,256]{1,0:T(8,128)(2,1)S(1)} %collective-permute-done.4.refs_7_), channel_id=1, source_target_pairs={{0,8},{4,12},{8,0},{12,4},{16,24},{20,28},{24,16},{28,20},{1,9},{5... | collective-permute-start | bytes 589832 | tf_op jit(solution)/shard_map/ppermute | solution.py:530
  22.2 0.6 collective-permute-start.12
  23.1 3.6 %collective-permute-done.6.refs_8_ = bf16[384,256]{1,0:T(8,128)(2,1)S(1)} collective-permute-done((bf16[384,256]{1,0:T(8,128)(2,1)S(1)}, bf16[384,256]{1,0:T(8,128)(2,1)S(1)}, u32[]{:S(2)}, u32[]{:S(2)}) %collective-permute-start.6) | collective-permute-done | bytes 196640 | tf_op jit(solution)/shard_map/ppermute | solution.py:530
  26.7 2.7 %collective-permute-start.14 = (bf16[2,384,256]{2,1,0:T(8,128)(2,1)S(1)}, bf16[2,384,256]{2,1,0:T(8,128)(2,1)S(1)}, u32[]{:S(2)}, u32[]{:S(2)}) collective-permute-start(bf16[2,384,256]{2,1,0:T(8,128)(2,1)S(1)} %pad_maximum_fusion.refs_2_), channel_id=1, source_target_pairs={{0,24},{4,28},{8,16},{12,20},{16,8},{20,12},{24,0},{28,4},{1,25},{... | collective-permute-start | bytes 1179656 | tf_op jit(solution)/shard_map/ppermute | solution.py:530
  29.4 1.1 %copy-done.2 = bf16[288,1408]{1,0:T(8,128)(2,1)S(1)} copy-done((bf16[288,1408]{1,0:T(8,128)(2,1)S(1)}, bf16[288,1408]{1,0:T(8,128)(2,1)}, u32[]{:S(2)}) %copy-start.2) | copy-done | bytes 811032
  30.5 18.8 %attend.2 = (bf16[288,640]{1,0:T(8,128)(2,1)S(1)}, bf16[288,640]{1,0:T(8,128)(2,1)S(1)}, bf16[2,384,256]{2,1,0:T(8,128)(2,1)S(1)}, bf16[2,384,256]{2,1,0:T(8,128...) custom-call(s32[3]{0:T(128)S(1)} %copy-done, s32[8]{0:T(128)S(1)} %copy-done.4, ...), custom_call_target="tpu_custom_call" | custom-call | flops 6710886400 | bytes 8388608 | tf_op jit(solution)/shard_map/attend/pallas_call | solution.py:536
  49.3 0.7 collective-permute-start.8
  49.9 2.9 %collective-permute-start.10 = (bf16[2,384,256]{2,1,0:T(8,128)(2,1)S(1)}, bf16[2,384,256]{2,1,0:T(8,128)(2,1)S(1)}, u32[]{:S(2)}, u32[]{:S(2)}) collective-permute-start(bf16[2,384,256]{2,1,0:T(8,128)(2,1)S(1)} %get-tuple-element.102), channel_id=1, source_target_pairs={{0,24},{4,28},{8,16},{12,20},{16,8},{20,12},{24,0},{28,4},{1,25},{... | collective-permute-start | bytes 1179656 | tf_op jit(solution)/shard_map/ppermute | solution.py:530
  52.9 18.7 %attend.3 = (bf16[288,640]{1,0:T(8,128)(2,1)S(1)}, bf16[288,640]{1,0:T(8,128)(2,1)S(1)}, bf16[2,256,256]{2,1,0:T(8,128)(2,1)S(1)}, bf16[2,256,256]{2,1,0:T(8,128...) custom-call(s32[3]{0:T(128)S(1)} %copy-done, ...), custom_call_target="tpu_custom_call" | custom-call | flops 6710886400 | bytes 8388608 | tf_op jit(solution)/shard_map/attend/pallas_call | solution.py:536
  71.6 0.8 collect_first.1
  72.4 4.9 %collective-permute-start.15 = (bf16[10,32,256]{2,1,0:T(8,128)(2,1)S(1)}, bf16[10,32,256]{2,1,0:T(8,128)(2,1)S(1)}, u32[]{:S(2)}, u32[]{:S(2)}) collective-permute-start(bf16[10,32,256]{2,1,0:T(8,128)(2,1)S(1)} %get-tuple-element.124), channel_id=1, source_target_pairs={{0,1},{1,2},{2,3},{3,0},{4,5},{5,6},{6,7},{7,4},{8,9},{9,10},{10,1... | collective-permute-start | bytes 491528 | tf_op jit(solution)/shard_map/ppermute | solution.py:684
  77.3 4.1 %collective-permute-done.15.refs_1_ = bf16[10,32,256]{2,1,0:T(8,128)(2,1)S(1)} collective-permute-done((bf16[10,32,256]{2,1,0:T(8,128)(2,1)S(1)}, bf16[10,32,256]{2,1,0:T(8,128)(2,1)S(1)}, u32[]{:S(2)}, u32[]{:S(2)}) %collective-permute-start.15) | collective-permute-done | bytes 163872 | tf_op jit(solution)/shard_map/ppermute | solution.py:684
  81.4 0.6 collective-permute-start.19
  82.0 6.2 %collective-permute-start.20 = (bf16[2,256,256]{2,1,0:T(8,128)(2,1)S(1)}, bf16[2,256,256]{2,1,0:T(8,128)(2,1)S(1)}, u32[]{:S(2)}, u32[]{:S(2)}) collective-permute-start(bf16[2,256,256]{2,1,0:T(8,128)(2,1)S(1)} %get-tuple-element.140), channel_id=1, source_target_pairs={{0,16},{4,20},{8,24},{12,28},{16,0},{20,4},{24,8},{28,12},{1,17},{... | collective-permute-start | bytes 786440 | tf_op jit(solution)/shard_map/ppermute | solution.py:530
  88.2 1.5 %collective-permute-start.21 = (bf16[2,256,256]{2,1,0:T(8,128)(2,1)S(1)}, bf16[2,256,256]{2,1,0:T(8,128)(2,1)S(1)}, u32[]{:S(2)}, u32[]{:S(2)}) collective-permute-start(bf16[2,256,256]{2,1,0:T(8,128)(2,1)S(1)} %get-tuple-element.141), channel_id=1, source_target_pairs={{0,24},{4,28},{8,16},{12,20},{16,8},{20,12},{24,0},{28,4},{1,25},{... | collective-permute-start | bytes 786440 | tf_op jit(solution)/shard_map/ppermute | solution.py:530
  89.7 2.2 %collective-permute-start.16 = (bf16[10,32,256]{2,1,0:T(8,128)(2,1)S(1)}, bf16[10,32,256]{2,1,0:T(8,128)(2,1)S(1)}, u32[]{:S(2)}, u32[]{:S(2)}) collective-permute-start(bf16[10,32,256]{2,1,0:T(8,128)(2,1)S(1)} %get-tuple-element.128), channel_id=1, source_target_pairs={{0,2},{1,3},{2,0},{3,1},{4,6},{5,7},{6,4},{7,5},{8,10},{9,11},{10,... | collective-permute-start | bytes 491528 | tf_op jit(solution)/shard_map/ppermute | solution.py:684
  91.9 2.6 %collective-permute-start.17 = (bf16[10,32,256]{2,1,0:T(8,128)(2,1)S(1)}, bf16[10,32,256]{2,1,0:T(8,128)(2,1)S(1)}, u32[]{:S(2)}, u32[]{:S(2)}) collective-permute-start(bf16[10,32,256]{2,1,0:T(8,128)(2,1)S(1)} %get-tuple-element.129), channel_id=1, source_target_pairs={{0,3},{1,0},{2,1},{3,2},{4,7},{5,4},{6,5},{7,6},{8,11},{9,8},{10,9... | collective-permute-start | bytes 491528 | tf_op jit(solution)/shard_map/ppermute | solution.py:684
  94.5 2.2 %finish_queries.1 = (bf16[32,2560]{1,0:T(8,128)(2,1)}, bf16[256,2560]{1,0:T(8,128)(2,1)}) custom-call(s32[3]{0:T(128)S(1)} %copy-done, bf16[288,640]{1,0:T(8,128)(2,1)S(1)} %get-tuple-element.130.refs_0_, bf16[288,640]{1,0:T(8,128)(2,1)S(1)} %collective-permute-done.11.refs_1_, bf16[288,640]{1,0:T(8,128)(2,1)S(1)} %get-tuple-element.132.refs_2_, ...), custom_call_target="tpu_custom_call" | custom-call | flops 335544320 | bytes 5242880 | tf_op jit(solution)/shard_map/finish_queries/pallas_call | solution.py:536
  96.7 4.5 %collective-permute-done.16.refs_2_ = bf16[10,32,256]{2,1,0:T(8,128)(2,1)S(1)} collective-permute-done((bf16[10,32,256]{2,1,0:T(8,128)(2,1)S(1)}, bf16[10,32,256]{2,1,0:T(8,128)(2,1)S(1)}, u32[]{:S(2)}, u32[]{:S(2)}) %collective-permute-start.16) | collective-permute-done | bytes 163872 | tf_op jit(solution)/shard_map/ppermute | solution.py:684
  101.2 0.6 collective-permute-start.22
  101.9 1.6 %collective-permute-start.23 = (bf16[2,32,256]{2,1,0:T(8,128)(2,1)S(1)}, bf16[2,32,256]{2,1,0:T(8,128)(2,1)S(1)}, u32[]{:S(2)}, u32[]{:S(2)}) collective-permute-start(bf16[2,32,256]{2,1,0:T(8,128)(2,1)S(1)} %get-tuple-element.148), channel_id=1, source_target_pairs={{0,16},{4,20},{8,24},{12,28},{16,0},{20,4},{24,8},{28,12},{1,17},{... | collective-permute-start | bytes 98312 | tf_op jit(solution)/shard_map/ppermute | solution.py:530
  103.4 1.4 %collective-permute-start.24 = (bf16[2,32,256]{2,1,0:T(8,128)(2,1)S(1)}, bf16[2,32,256]{2,1,0:T(8,128)(2,1)S(1)}, u32[]{:S(2)}, u32[]{:S(2)}) collective-permute-start(bf16[2,32,256]{2,1,0:T(8,128)(2,1)S(1)} %get-tuple-element.149), channel_id=1, source_target_pairs={{0,24},{4,28},{8,16},{12,20},{16,8},{20,12},{24,0},{28,4},{1,25},{... | collective-permute-start | bytes 98312 | tf_op jit(solution)/shard_map/ppermute | solution.py:530
  105.8 2.5 %collective-permute-done.24.refs_7_ = bf16[2,32,256]{2,1,0:T(8,128)(2,1)S(1)} collective-permute-done((bf16[2,32,256]{2,1,0:T(8,128)(2,1)S(1)}, bf16[2,32,256]{2,1,0:T(8,128)(2,1)S(1)}, u32[]{:S(2)}, u32[]{:S(2)}) %collective-permute-start.24) | collective-permute-done | bytes 32800 | tf_op jit(solution)/shard_map/ppermute | solution.py:530
  108.5 1.6 %collective-permute-done.25.theirs = bf16[576,256]{1,0:T(8,128)(2,1)S(1)} collective-permute-done((bf16[576,256]{1,0:T(8,128)(2,1)S(1)}, bf16[576,256]{1,0:T(8,128)(2,1)S(1)}, u32[]{:S(2)}, u32[]{:S(2)}) %collective-permute-start.25) | collective-permute-done | bytes 294944 | tf_op jit(solution)/shard_map/ppermute | solution.py:530
  110.1 1.7 %finish_keys.1 = (bf16[32,512]{1,0:T(8,128)(2,1)}, bf16[32,512]{1,0:T(8,128)(2,1)}, bf16[256,512]{1,0:T(8,128)(2,1)}, bf16[256,512]{1,0:T(8,128)(2,1)}) custom-call(s32[3]{0:T(128)S(1)} %copy-done, f32[256,256]{1,0:T(8,128)S(1)} %get-tuple-element.137.reply0, f32[256,256]{1,0:T(8,128)S(1)} %get-tuple-element.152.reply1, ...), custom_call_target="tpu_custom_call" | custom-call | tf_op jit(solution)/shard_map/finish_keys/pallas_call | solution.py:536
  (46 shorter events, 3.2 us)
Async XLA Ops:
  4.3 14.2 %collective-permute-start = (bf16[2,384,256]{2,1,0:T(8,128)(2,1)}, bf16[2,384,256]{2,1,0:T(8,128)(2,1)S(1)}, u32[]{:S(2)}, u32[]{:S(2)}) collective-permute-start(bf16[2,384,256]{2,1,0:T(8,128)(2,1)} %get-tuple-element.84), channel_id=1, source_target_pairs={{0,4},{4,0},{8,12},{12,8},{16,20},{20,16},{24,28},{28,24},{1,5},{5... | collective-permute-start | bytes 1179656 | tf_op jit(solution)/shard_map/ppermute | solution.py:530
  4.8 10.9 %collective-permute-start.1 = (bf16[384,256]{1,0:T(8,128)(2,1)}, bf16[384,256]{1,0:T(8,128)(2,1)S(1)}, u32[]{:S(2)}, u32[]{:S(2)}) collective-permute-start(bf16[384,256]{1,0:T(8,128)(2,1)} %get-tuple-element.93.refs_2_), channel_id=1, source_target_pairs={{0,8},{4,12},{8,0},{12,4},{16,24},{20,28},{24,16},{28,20},{1,9},{5... | collective-permute-start | bytes 589832 | tf_op jit(solution)/shard_map/ppermute | solution.py:530
  7.4 9.7 %collective-permute-start.2 = (bf16[384,256]{1,0:T(8,128)(2,1)}, bf16[384,256]{1,0:T(8,128)(2,1)S(1)}, u32[]{:S(2)}, u32[]{:S(2)}) collective-permute-start(bf16[384,256]{1,0:T(8,128)(2,1)} %get-tuple-element.85), channel_id=1, source_target_pairs={{0,12},{4,8},{8,4},{12,0},{16,28},{20,24},{24,20},{28,16},{1,13},{... | collective-permute-start | bytes 589832 | tf_op jit(solution)/shard_map/ppermute | solution.py:530
  7.5 9.6 %collective-permute-start.3 = (bf16[384,256]{1,0:T(8,128)(2,1)}, bf16[384,256]{1,0:T(8,128)(2,1)S(1)}, u32[]{:S(2)}, u32[]{:S(2)}) collective-permute-start(bf16[384,256]{1,0:T(8,128)(2,1)} %get-tuple-element.93.refs_2_), channel_id=1, source_target_pairs={{0,16},{4,20},{8,24},{12,28},{16,0},{20,4},{24,8},{28,12},{1,17},{... | collective-permute-start | bytes 589832 | tf_op jit(solution)/shard_map/ppermute | solution.py:530
  9.3 9.3 %collective-permute-start.4 = (bf16[384,256]{1,0:T(8,128)(2,1)}, bf16[384,256]{1,0:T(8,128)(2,1)S(1)}, u32[]{:S(2)}, u32[]{:S(2)}) collective-permute-start(bf16[384,256]{1,0:T(8,128)(2,1)} %get-tuple-element.85), channel_id=1, source_target_pairs={{0,20},{4,16},{8,28},{12,24},{16,4},{20,0},{24,12},{28,8},{1,21},{... | collective-permute-start | bytes 589832 | tf_op jit(solution)/shard_map/ppermute | solution.py:530
  9.3 12.9 %copy-start.6 = (bf16[384,256]{1,0:T(8,128)(2,1)S(1)}, bf16[384,256]{1,0:T(8,128)(2,1)}, u32[]{:S(2)}) copy-start(bf16[384,256]{1,0:T(8,128)(2,1)} %get-tuple-element.105) | copy-start | bytes 589828
  9.3 20.1 %copy-start = (s32[3]{0:T(128)S(1)}, s32[3]{0:T(128)}, u32[]{:S(2)}) copy-start(s32[3]{0:T(128)} %pad_add_fusion.place) | copy-start | bytes 40
  9.3 20.1 %copy-start.3 = (bf16[384,256]{1,0:T(8,128)(2,1)S(1)}, bf16[384,256]{1,0:T(8,128)(2,1)}, u32[]{:S(2)}) copy-start(bf16[384,256]{1,0:T(8,128)(2,1)} %get-tuple-element.93.refs_2_) | copy-start | bytes 589828
  9.3 20.1 %copy-start.4 = (s32[8]{0:T(128)S(1)}, s32[8]{0:T(128)}, u32[]{:S(2)}) copy-start(s32[8]{0:T(128)} %reply_len.3) | copy-start | bytes 100
  9.3 20.1 %copy-start.5 = (s32[8]{0:T(128)S(1)}, s32[8]{0:T(128)}, u32[]{:S(2)}) copy-start(s32[8]{0:T(128)} %reply_slot.3) | copy-start | bytes 100
  18.5 10.8 %collective-permute-start.5 = (bf16[2,288,1408]{2,1,0:T(8,128)(2,1)}, bf16[2,288,1408]{2,1,0:T(8,128)(2,1)S(1)}, u32[]{:S(2)}, u32[]{:S(2)}) collective-permute-start(bf16[2,288,1408]{2,1,0:T(8,128)(2,1)} %get-tuple-element.92), channel_id=1, source_target_pairs={{0,4},{4,0},{8,12},{12,8},{16,20},{20,16},{24,28},{28,24},{1,5},{5... | collective-permute-start | bytes 4866056 | tf_op jit(solution)/shard_map/ppermute | solution.py:530
  18.9 7.8 %collective-permute-start.6 = (bf16[384,256]{1,0:T(8,128)(2,1)S(1)}, bf16[384,256]{1,0:T(8,128)(2,1)S(1)}, u32[]{:S(2)}, u32[]{:S(2)}) collective-permute-start(bf16[384,256]{1,0:T(8,128)(2,1)S(1)} %collective-permute-done.1.refs_4_), channel_id=1, source_target_pairs={{0,16},{4,20},{8,24},{12,28},{16,0},{20,4},{24,8},{28,12},{1,17},{... | collective-permute-start | bytes 589832 | tf_op jit(solution)/shard_map/ppermute | solution.py:530
  20.6 8.7 %collective-permute-start.7 = (bf16[384,256]{1,0:T(8,128)(2,1)S(1)}, bf16[384,256]{1,0:T(8,128)(2,1)S(1)}, u32[]{:S(2)}, u32[]{:S(2)}) collective-permute-start(bf16[384,256]{1,0:T(8,128)(2,1)S(1)} %collective-permute-done.4.refs_7_), channel_id=1, source_target_pairs={{0,8},{4,12},{8,0},{12,4},{16,24},{20,28},{24,16},{28,20},{1,9},{5... | collective-permute-start | bytes 589832 | tf_op jit(solution)/shard_map/ppermute | solution.py:530
  22.2 30.6 %copy-start.1 = (bf16[288,1408]{1,0:T(8,128)(2,1)S(1)}, bf16[288,1408]{1,0:T(8,128)(2,1)}, u32[]{:S(2)}) copy-start(bf16[288,1408]{1,0:T(8,128)(2,1)} %get-tuple-element.104.refs_0_) | copy-start | bytes 2433028
  22.2 27.7 %collective-permute-start.12 = (bf16[2,384,256]{2,1,0:T(8,128)(2,1)S(1)}, bf16[2,384,256]{2,1,0:T(8,128)(2,1)S(1)}, u32[]{:S(2)}, u32[]{:S(2)}) collective-permute-start(bf16[2,384,256]{2,1,0:T(8,128)(2,1)S(1)} %pad_maximum_fusion.refs_2_), channel_id=1, source_target_pairs={{0,8},{4,12},{8,0},{12,4},{16,24},{20,28},{24,16},{28,20},{1,9},{5... | collective-permute-start | bytes 1179656 | tf_op jit(solution)/shard_map/ppermute | solution.py:530
  22.8 30.0 %collective-permute-start.13 = (bf16[2,384,256]{2,1,0:T(8,128)(2,1)S(1)}, bf16[2,384,256]{2,1,0:T(8,128)(2,1)S(1)}, u32[]{:S(2)}, u32[]{:S(2)}) collective-permute-start(bf16[2,384,256]{2,1,0:T(8,128)(2,1)S(1)} %pad_maximum_fusion.refs_2_), channel_id=1, source_target_pairs={{0,16},{4,20},{8,24},{12,28},{16,0},{20,4},{24,8},{28,12},{1,17},{... | collective-permute-start | bytes 1179656 | tf_op jit(solution)/shard_map/ppermute | solution.py:530
  26.7 26.2 %collective-permute-start.14 = (bf16[2,384,256]{2,1,0:T(8,128)(2,1)S(1)}, bf16[2,384,256]{2,1,0:T(8,128)(2,1)S(1)}, u32[]{:S(2)}, u32[]{:S(2)}) collective-permute-start(bf16[2,384,256]{2,1,0:T(8,128)(2,1)S(1)} %pad_maximum_fusion.refs_2_), channel_id=1, source_target_pairs={{0,24},{4,28},{8,16},{12,20},{16,8},{20,12},{24,0},{28,4},{1,25},{... | collective-permute-start | bytes 1179656 | tf_op jit(solution)/shard_map/ppermute | solution.py:530
  49.3 22.3 %collective-permute-start.8 = (bf16[2,384,256]{2,1,0:T(8,128)(2,1)S(1)}, bf16[2,384,256]{2,1,0:T(8,128)(2,1)S(1)}, u32[]{:S(2)}, u32[]{:S(2)}) collective-permute-start(bf16[2,384,256]{2,1,0:T(8,128)(2,1)S(1)} %get-tuple-element.100), channel_id=1, source_target_pairs={{0,8},{4,12},{8,0},{12,4},{16,24},{20,28},{24,16},{28,20},{1,9},{5... | collective-permute-start | bytes 1179656 | tf_op jit(solution)/shard_map/ppermute | solution.py:530
  49.9 21.6 %collective-permute-start.9 = (bf16[2,384,256]{2,1,0:T(8,128)(2,1)S(1)}, bf16[2,384,256]{2,1,0:T(8,128)(2,1)S(1)}, u32[]{:S(2)}, u32[]{:S(2)}) collective-permute-start(bf16[2,384,256]{2,1,0:T(8,128)(2,1)S(1)} %get-tuple-element.101), channel_id=1, source_target_pairs={{0,16},{4,20},{8,24},{12,28},{16,0},{20,4},{24,8},{28,12},{1,17},{... | collective-permute-start | bytes 1179656 | tf_op jit(solution)/shard_map/ppermute | solution.py:530
  49.9 21.6 %collective-permute-start.10 = (bf16[2,384,256]{2,1,0:T(8,128)(2,1)S(1)}, bf16[2,384,256]{2,1,0:T(8,128)(2,1)S(1)}, u32[]{:S(2)}, u32[]{:S(2)}) collective-permute-start(bf16[2,384,256]{2,1,0:T(8,128)(2,1)S(1)} %get-tuple-element.102), channel_id=1, source_target_pairs={{0,24},{4,28},{8,16},{12,20},{16,8},{20,12},{24,0},{28,4},{1,25},{... | collective-permute-start | bytes 1179656 | tf_op jit(solution)/shard_map/ppermute | solution.py:530
  52.8 18.7 %collective-permute-start.11 = (bf16[288,640]{1,0:T(8,128)(2,1)S(1)}, bf16[288,640]{1,0:T(8,128)(2,1)S(1)}, u32[]{:S(2)}, u32[]{:S(2)}) collective-permute-start(bf16[288,640]{1,0:T(8,128)(2,1)S(1)} %get-tuple-element.103), channel_id=1, source_target_pairs={{0,4},{4,0},{8,12},{12,8},{16,20},{20,16},{24,28},{28,24},{1,5},{5... | collective-permute-start | bytes 1105928 | tf_op jit(solution)/shard_map/ppermute | solution.py:530
  72.4 9.0 %collective-permute-start.15 = (bf16[10,32,256]{2,1,0:T(8,128)(2,1)S(1)}, bf16[10,32,256]{2,1,0:T(8,128)(2,1)S(1)}, u32[]{:S(2)}, u32[]{:S(2)}) collective-permute-start(bf16[10,32,256]{2,1,0:T(8,128)(2,1)S(1)} %get-tuple-element.124), channel_id=1, source_target_pairs={{0,1},{1,2},{2,3},{3,0},{4,5},{5,6},{6,7},{7,4},{8,9},{9,10},{10,1... | collective-permute-start | bytes 491528 | tf_op jit(solution)/shard_map/ppermute | solution.py:684
  81.4 10.5 %collective-permute-start.18 = (bf16[288,640]{1,0:T(8,128)(2,1)S(1)}, bf16[288,640]{1,0:T(8,128)(2,1)S(1)}, u32[]{:S(2)}, u32[]{:S(2)}) collective-permute-start(bf16[288,640]{1,0:T(8,128)(2,1)S(1)} %get-tuple-element.133), channel_id=1, source_target_pairs={{0,4},{4,0},{8,12},{12,8},{16,20},{20,16},{24,28},{28,24},{1,5},{5... | collective-permute-start | bytes 1105928 | tf_op jit(solution)/shard_map/ppermute | solution.py:530
  81.4 22.0 %collective-permute-start.19 = (bf16[2,256,256]{2,1,0:T(8,128)(2,1)S(1)}, bf16[2,256,256]{2,1,0:T(8,128)(2,1)S(1)}, u32[]{:S(2)}, u32[]{:S(2)}) collective-permute-start(bf16[2,256,256]{2,1,0:T(8,128)(2,1)S(1)} %get-tuple-element.139), channel_id=1, source_target_pairs={{0,8},{4,12},{8,0},{12,4},{16,24},{20,28},{24,16},{28,20},{1,9},{5... | collective-permute-start | bytes 786440 | tf_op jit(solution)/shard_map/ppermute | solution.py:530
  82.0 22.8 %collective-permute-start.20 = (bf16[2,256,256]{2,1,0:T(8,128)(2,1)S(1)}, bf16[2,256,256]{2,1,0:T(8,128)(2,1)S(1)}, u32[]{:S(2)}, u32[]{:S(2)}) collective-permute-start(bf16[2,256,256]{2,1,0:T(8,128)(2,1)S(1)} %get-tuple-element.140), channel_id=1, source_target_pairs={{0,16},{4,20},{8,24},{12,28},{16,0},{20,4},{24,8},{28,12},{1,17},{... | collective-permute-start | bytes 786440 | tf_op jit(solution)/shard_map/ppermute | solution.py:530
  88.2 16.6 %collective-permute-start.21 = (bf16[2,256,256]{2,1,0:T(8,128)(2,1)S(1)}, bf16[2,256,256]{2,1,0:T(8,128)(2,1)S(1)}, u32[]{:S(2)}, u32[]{:S(2)}) collective-permute-start(bf16[2,256,256]{2,1,0:T(8,128)(2,1)S(1)} %get-tuple-element.141), channel_id=1, source_target_pairs={{0,24},{4,28},{8,16},{12,20},{16,8},{20,12},{24,0},{28,4},{1,25},{... | collective-permute-start | bytes 786440 | tf_op jit(solution)/shard_map/ppermute | solution.py:530
  89.7 11.5 %collective-permute-start.16 = (bf16[10,32,256]{2,1,0:T(8,128)(2,1)S(1)}, bf16[10,32,256]{2,1,0:T(8,128)(2,1)S(1)}, u32[]{:S(2)}, u32[]{:S(2)}) collective-permute-start(bf16[10,32,256]{2,1,0:T(8,128)(2,1)S(1)} %get-tuple-element.128), channel_id=1, source_target_pairs={{0,2},{1,3},{2,0},{3,1},{4,6},{5,7},{6,4},{7,5},{8,10},{9,11},{10,... | collective-permute-start | bytes 491528 | tf_op jit(solution)/shard_map/ppermute | solution.py:684
  91.9 9.3 %collective-permute-start.17 = (bf16[10,32,256]{2,1,0:T(8,128)(2,1)S(1)}, bf16[10,32,256]{2,1,0:T(8,128)(2,1)S(1)}, u32[]{:S(2)}, u32[]{:S(2)}) collective-permute-start(bf16[10,32,256]{2,1,0:T(8,128)(2,1)S(1)} %get-tuple-element.129), channel_id=1, source_target_pairs={{0,3},{1,0},{2,1},{3,2},{4,7},{5,4},{6,5},{7,6},{8,11},{9,8},{10,9... | collective-permute-start | bytes 491528 | tf_op jit(solution)/shard_map/ppermute | solution.py:684
  101.2 4.0 %collective-permute-start.22 = (bf16[2,32,256]{2,1,0:T(8,128)(2,1)S(1)}, bf16[2,32,256]{2,1,0:T(8,128)(2,1)S(1)}, u32[]{:S(2)}, u32[]{:S(2)}) collective-permute-start(bf16[2,32,256]{2,1,0:T(8,128)(2,1)S(1)} %get-tuple-element.147), channel_id=1, source_target_pairs={{0,8},{4,12},{8,0},{12,4},{16,24},{20,28},{24,16},{28,20},{1,9},{5... | collective-permute-start | bytes 98312 | tf_op jit(solution)/shard_map/ppermute | solution.py:530
  101.9 3.9 %collective-permute-start.23 = (bf16[2,32,256]{2,1,0:T(8,128)(2,1)S(1)}, bf16[2,32,256]{2,1,0:T(8,128)(2,1)S(1)}, u32[]{:S(2)}, u32[]{:S(2)}) collective-permute-start(bf16[2,32,256]{2,1,0:T(8,128)(2,1)S(1)} %get-tuple-element.148), channel_id=1, source_target_pairs={{0,16},{4,20},{8,24},{12,28},{16,0},{20,4},{24,8},{28,12},{1,17},{... | collective-permute-start | bytes 98312 | tf_op jit(solution)/shard_map/ppermute | solution.py:530
  103.4 4.8 %collective-permute-start.24 = (bf16[2,32,256]{2,1,0:T(8,128)(2,1)S(1)}, bf16[2,32,256]{2,1,0:T(8,128)(2,1)S(1)}, u32[]{:S(2)}, u32[]{:S(2)}) collective-permute-start(bf16[2,32,256]{2,1,0:T(8,128)(2,1)S(1)} %get-tuple-element.149), channel_id=1, source_target_pairs={{0,24},{4,28},{8,16},{12,20},{16,8},{20,12},{24,0},{28,4},{1,25},{... | collective-permute-start | bytes 98312 | tf_op jit(solution)/shard_map/ppermute | solution.py:530
  108.4 1.6 %collective-permute-start.25 = (bf16[576,256]{1,0:T(8,128)(2,1)S(1)}, bf16[576,256]{1,0:T(8,128)(2,1)S(1)}, u32[]{:S(2)}, u32[]{:S(2)}) collective-permute-start(bf16[576,256]{1,0:T(8,128)(2,1)S(1)} %get-tuple-element.154), channel_id=1, source_target_pairs={{0,4},{4,0},{8,12},{12,8},{16,20},{20,16},{24,28},{28,24},{1,5},{5... | collective-permute-start | bytes 884744 | tf_op jit(solution)/shard_map/ppermute | solution.py:530
  (1 other events, 1.1 us)

commit v8 on v7

--- a/solution.py
+++ b/solution.py
@@ -148,8 +148,7 @@
     keys_in, refs = refs[:count], refs[count:]
     query_out, refs = refs[:2], refs[2:]
     keys_out, refs = refs[:chips], refs[chips:]
-    groups = prompt_keys // prompt_rows
-    cuts_out, refs = (refs[:groups], refs[groups:]) if joint_keys else ((), refs)
+    prompt_out, refs = (refs[:chips], refs[chips:]) if joint_keys else (keys_out, refs)
     keys, keys_t, total, query, gradient, query_t, gradient_t, deltas, delta, scores, peaks, top, mass, *refs = refs
     query_grad, stages = refs[0], (refs[1:3], refs[3:5])
     chip, core, group = place[0], place[1], place[2]
@@ -397,22 +396,16 @@
             ]
 
     def put(out, at, count):
-        out[:, :HEAD_WIDTH] = (total[pl.ds(at, count), :HEAD_WIDTH] * SCALE).astype(BF16)
-        out[:, HEAD_WIDTH:] = total[pl.ds(at, count), HEAD_WIDTH:].astype(BF16)
+        out[:, :HEAD_WIDTH] = (total[at : at + count, :HEAD_WIDTH] * SCALE).astype(BF16)
+        out[:, HEAD_WIDTH:] = total[at : at + count, HEAD_WIDTH:].astype(BF16)
 
     for index in range(chips * CORES):
         away, other = index // CORES, index % CORES
-        out = keys_out[away].at[other]
-        prompt_at = away * chip_prompt + other * prompt_keys
-        if not joint_keys:
-            put(out.at[:prompt_keys], prompt_at, prompt_keys)
-        for shift, cut in enumerate(cuts_out):
-            part = lax.rem(group + shift, groups) * prompt_rows
-            put(cut.at[index], pl.multiple_of(prompt_at + part, prompt_rows), prompt_rows)
+        put(prompt_out[away].at[other, :prompt_keys], away * chip_prompt + other * prompt_keys, prompt_keys)
         for slot in range(RESP_DEV):
             at = chips * chip_prompt + (slot * chips + away) * positions + other * own_positions
             to = slot * own_positions + (0 if joint_keys else prompt_keys)
-            put(out.at[to : to + own_positions], at, own_positions)
+            put(keys_out[away].at[other, to : to + own_positions], at, own_positions)
 
 
 def add(first, *rest):
@@ -422,45 +415,33 @@
     return value
 
 
-def collect_first(chips, prompt_keys, place, *refs):
-    parts, refs = refs[:chips], refs[chips:]
-    groups = (len(refs) - 3) // 2
-    cuts, mine, theirs, outs, summed = refs[:groups], refs[groups], refs[groups + 1], refs[groups + 2 : -1], refs[-1]
-    rows = prompt_keys // groups
+def collect_first(chips, place, *refs):
+    parts, prompt_parts, refs = refs[:chips], refs[chips : 2 * chips], refs[2 * chips :]
+    mine, theirs, outs, summed = refs[0], refs[1], refs[2:-1], refs[-1]
+    groups, rows = len(outs), outs[0].shape[1]
+    prompt_keys = groups * rows
+    mine[...] = add(*(part[0, prompt_keys:] for part in parts))
+    theirs[...] = add(*(part[1, prompt_keys:] for part in parts)).astype(BF16)
     for other in range(CORES):
-        value = add(*(part[other, prompt_keys:] for part in parts))
-        if other == 0:
-            mine[...] = value
-        else:
-            theirs[...] = value.astype(BF16)
         summed[other] = add(*(part[other, :prompt_keys] for part in parts))
+        summed[CORES + other] = add(*(part[other] for part in prompt_parts))
     for shift in range(groups):
         at = pl.ds(pl.multiple_of(lax.rem(place[2] + shift, groups) * rows, rows), rows)
-        for other in range(CORES):
-            outs[shift][other] = summed[other, at].astype(BF16)
-        outs[shift][CORES:] = cuts[shift][...]
-
-
-def add_groups(groups, *refs):
-    parts, first, outs = refs[:groups], refs[groups], refs[groups + 1 :]
-    value = add(*(part[...] for part in parts)).astype(BF16)
-    first[...] = value[:CORES]
-    for away, out in enumerate(outs):
-        out[...] = value[CORES * (away + 1) : CORES * (away + 2)]
+        for index in range(summed.shape[0]):
+            outs[shift][index] = summed[index, at].astype(BF16)
 
 
 def collect_second(chips, *refs):
-    reply_parts, refs = refs[:chips], refs[chips:]
-    prompt_parts, refs = refs[:chips], refs[chips:]
-    prompt0, theirs0, reply1, prompt1, theirs = refs
-    reply, rows = theirs0.shape[0], prompt0.shape[1]
+    parts, slices, (theirs0, mine, prompt, theirs) = refs[:chips], refs[chips:-4], refs[-4:]
+    reply, rows = theirs0.shape[0], prompt.shape[1]
     step = max(rows, 16)
-    reply1[...] = add(*(part[0] for part in reply_parts))
-    prompt1[...] = add(*(part[0] for part in prompt_parts))
+    mine[...] = add(*(part[0] for part in parts))
     theirs[:reply] = theirs0[...]
-    theirs[reply : 2 * reply] = add(*(part[1] for part in reply_parts)).astype(BF16)
-    theirs[2 * reply : 2 * reply + rows] = prompt0[1]
-    theirs[2 * reply + step : 2 * reply + step + rows] = add(*(part[1] for part in prompt_parts)).astype(BF16)
+    theirs[reply : 2 * reply] = add(*(part[1] for part in parts)).astype(BF16)
+    for local in range(LOCAL_HEADS):
+        prompt[local] = add(*(part[CORES * local] for part in slices))
+        at = 2 * reply + local * step
+        theirs[at : at + rows] = add(*(part[CORES * local + 1] for part in slices)).astype(BF16)
 
 
 def finish_queries(place, *refs):
@@ -473,7 +454,7 @@
         prompt_dq[:, span] = query[reply:]
 
 
-def finish_keys(place, reply0, reply1, prompt0, prompt1, theirs, prompt_dk, prompt_dv, reply_dk, reply_dv):
+def finish_keys(place, reply0, reply1, prompts, theirs, prompt_dk, prompt_dv, reply_dk, reply_dv):
     reply, rows = reply_dk.shape[0], prompt_dk.shape[0]
     step = max(rows, 16)
     order = unsorting(reply)
@@ -485,7 +466,7 @@
                 prompt = theirs[2 * reply + local * step : 2 * reply + local * step + rows]
             else:
                 value = (reply1 if local else reply0)[...].astype(BF16)
-                prompt = prompt1[...].astype(BF16) if local else prompt0[0]
+                prompt = prompts[local].astype(BF16)
             value = dot(order, value).astype(BF16)
             reply_dk[:, span] = value[:, :HEAD_WIDTH]
             reply_dv[:, span] = value[:, HEAD_WIDTH:]
@@ -618,8 +599,9 @@
 
     def run_attend(local, key_blocks):
         joint_keys = local == 1
-        cut = [shape(devices, cut_rows, 2 * HEAD_WIDTH)] * groups
-        sums = [shape(CORES, reply_own, 2 * HEAD_WIDTH)] * chips + cut if joint_keys else [shape(CORES, *key_shape)] * chips
+        sums = [shape(CORES, *key_shape)] * chips
+        if joint_keys:
+            sums = [shape(CORES, n, 2 * HEAD_WIDTH) for n in [reply_own] * chips + [prompt_keys] * chips]
         query_mine, query_theirs, *sums = call(
             functools.partial(attend, sizes, joint_keys),
             "attend",
@@ -668,26 +650,23 @@
     arrived0, query_theirs0, query_theirs1, sums1 = lax.optimization_barrier(
         (arrived0, query_theirs0, query_theirs1, sums1)
     )
-    sums1, cuts1 = sums1[:chips], sums1[chips:]
+    prompt1 = [sums1[chips]] + [move(sums1[chips + away], away) for away in range(1, chips)]
+    arrived1 = [sums1[0]] + [move(sums1[away], away) for away in range(1, chips)]
     key_width = KEY_VALUE_HEADS * HEAD_WIDTH
     query_width = QUERY_HEADS * HEAD_WIDTH
     reply0, theirs0, *cuts = call(
-        functools.partial(collect_first, chips, prompt_keys),
+        functools.partial(collect_first, chips),
         "collect_first",
         SMALL_MIB,
-        (place, *arrived0, *cuts1),
+        (place, *arrived0, *prompt1),
         [shape(reply_own, 2 * HEAD_WIDTH, dtype=F32), shape(reply_own, 2 * HEAD_WIDTH)]
-        + [shape(CORES + devices, cut_rows, 2 * HEAD_WIDTH)] * groups,
-        scratch_shapes=[pltpu.VMEM((CORES, prompt_keys, 2 * HEAD_WIDTH), F32)],
+        + [shape(KEY_VALUE_HEADS, cut_rows, 2 * HEAD_WIDTH)] * groups,
+        scratch_shapes=[pltpu.VMEM((KEY_VALUE_HEADS, prompt_keys, 2 * HEAD_WIDTH), F32)],
     )
     slices = [cuts[0]] + [
         lax.ppermute(cuts[shift], "rsp", [(g, (g + shift) % groups) for g in range(groups)])
         for shift in range(1, groups)
     ]
-    slices[1], sums1[chips - 1], query_theirs1 = lax.optimization_barrier(
-        (slices[1], sums1[chips - 1], query_theirs1)
-    )
-    arrived1 = [sums1[0]] + [move(sums1[away], away) for away in range(1, chips)]
     prompt_dq, reply_dq = call(
         finish_queries,
         "finish_queries",
@@ -701,23 +680,14 @@
         ),
     )
     slices, prompt_dq, reply_dq = lax.optimization_barrier((slices, prompt_dq, reply_dq))
-    prompt0, *prompt_parts = call(
-        functools.partial(add_groups, groups),
-        "add_groups",
-        SMALL_MIB,
-        slices,
-        [shape(CORES, cut_rows, 2 * HEAD_WIDTH)] * (1 + chips),
-        scalars=0,
-    )
-    prompt_parts = [prompt_parts[0]] + [move(prompt_parts[away], away) for away in range(1, chips)]
-    reply1, prompt1, theirs = call(
+    reply1, prompts, theirs = call(
         functools.partial(collect_second, chips),
         "collect_second",
         SMALL_MIB,
-        (*arrived1, *prompt_parts, prompt0, theirs0),
+        (*arrived1, *slices, theirs0),
         [
             shape(reply_own, 2 * HEAD_WIDTH, dtype=F32),
-            shape(cut_rows, 2 * HEAD_WIDTH, dtype=F32),
+            shape(LOCAL_HEADS, cut_rows, 2 * HEAD_WIDTH, dtype=F32),
             shape(2 * reply_own + 2 * max(cut_rows, 16), 2 * HEAD_WIDTH),
         ],
         scalars=0,
@@ -726,7 +696,7 @@
         finish_keys,
         "finish_keys",
         SMALL_MIB,
-        (place, reply0, reply1, prompt0, prompt1, swap(theirs)),
+        (place, reply0, reply1, prompts, swap(theirs)),
         [shape(cut_rows, key_width)] * 2 + [shape(reply_own, key_width)] * 2,
     )
     return (

time: 113 us -> 109 us (0.965)
  waiting for transfers between devices: 19.9 us -> 16 us
    ppermute x3, starting transfers between devices: 9.72 us -> 16.8 us  [on_device(): lax.ppermute(cuts[shift], 'rsp', [(g, (g + shift) % groups) for g in rang...]
    ppermute x23, starting transfers between devices: 27.6 us -> 20.9 us  [move(): return lax.ppermute(array, 'pre', pairs)]
    ppermute x3, waiting for transfers between devices: 8.56 us -> 2.69 us  [on_device(): lax.ppermute(cuts[shift], 'rsp', [(g, (g + shift) % groups) for g in rang...]
    ppermute x23, waiting for transfers between devices: 11.3 us -> 13.3 us  [move(): return lax.ppermute(array, 'pre', pairs)]
    pallas_call x9 -> x8, Pallas kernels: 51.9 us -> 51.9 us  [call(): pl.pallas_call(kernel, out_shape=outs, in_specs=[SMEM] * scalars + [spec]...]
  transfers between devices with their start and end apart: 26 -> 26, of which waited for: 9 -> 8; matrix products, arithmetic and copies ran while one was open for 0% -> 0% of each run, Pallas kernels for 41% -> 43%
where the time goes in v8:
time: 109 us; the launch traced here: 108 us
  Pallas kernels  51.9 us (48%)
  starting transfers between devices  37.7 us (35%)
  waiting for transfers between devices  16 us (15%)
  local copies, waits for them, and re-layouts  1.18 us (1%)
    pallas_call x8, Pallas kernels, call(): pl.pallas_call(kernel, out_shape=outs, in_specs=[SMEM] * scalars + [spec]...  51.9 us
    ppermute x23, starting transfers between devices, move(): return lax.ppermute(array, 'pre', pairs)  20.9 us
    ppermute x3, starting transfers between devices, on_device(): lax.ppermute(cuts[shift], 'rsp', [(g, (g + shift) % groups) for g in rang...  16.8 us
    ppermute x23, waiting for transfers between devices, move(): return lax.ppermute(array, 'pre', pairs)  13.3 us
    ppermute x3, waiting for transfers between devices, on_device(): lax.ppermute(cuts[shift], 'rsp', [(g, (g + shift) % groups) for g in rang...  2.69 us
  transfers between devices with their start and end apart: 26, of which 8 were waited for; matrix products, arithmetic and copies ran while one was open for 0% of the time, Pallas kernels for 43%

profile of v8, /device:TPU:0, one launch (start us, length us, event | category | flops | bytes accessed | tf_op | source)
XLA Modules:
  0.0 108.3 jit_solution(179356851198656186)
XLA Ops:
  0.6 0.7 pad_add_fusion.place
  1.3 3.1 %prepare_keys.1 = (bf16[384,256]{1,0:T(8,128)(2,1)}, bf16[384,256]{1,0:T(8,128)(2,1)}, bf16[384,256]{1,0:T(8,128)(2,1)}, bf16[2,384,256]{2,1,0:T(8,128)(2,1)}, f32[8,128]{1,0:T(8,128)}) custom-call(s32[3]{0:T(128)} %pad_add_fusion.place, bf16[128,512]{1,0:T(8,128)(2,1)} %pk.1, bf16[128,512]{1,0:T(8,128)(2,1)} %pv.1, bf16[256,512]{1,0:T(8,128)(2,1)} %bitcast.15, ...), custom_call_target="tpu_custom_call" | custom-call | tf_op jit(solution)/shard_map/prepare_keys/pallas_call | solution.py:517
  4.9 2.6 %collective-permute-start.1 = (bf16[384,256]{1,0:T(8,128)(2,1)}, bf16[384,256]{1,0:T(8,128)(2,1)S(1)}, u32[]{:S(2)}, u32[]{:S(2)}) collective-permute-start(bf16[384,256]{1,0:T(8,128)(2,1)} %get-tuple-element.85.refs_2_), channel_id=1, source_target_pairs={{0,8},{4,12},{8,0},{12,4},{16,24},{20,28},{24,16},{28,20},{1,9},{5... | collective-permute-start | bytes 589832 | tf_op jit(solution)/shard_map/ppermute | solution.py:511
  7.5 1.8 %collective-permute-start.3 = (bf16[384,256]{1,0:T(8,128)(2,1)}, bf16[384,256]{1,0:T(8,128)(2,1)S(1)}, u32[]{:S(2)}, u32[]{:S(2)}) collective-permute-start(bf16[384,256]{1,0:T(8,128)(2,1)} %get-tuple-element.85.refs_2_), channel_id=1, source_target_pairs={{0,16},{4,20},{8,24},{12,28},{16,0},{20,4},{24,8},{28,12},{1,17},{... | collective-permute-start | bytes 589832 | tf_op jit(solution)/shard_map/ppermute | solution.py:511
  9.4 6.5 %prepare_rows.1 = (bf16[2,288,1408]{2,1,0:T(8,128)(2,1)}, bf16[288,1408]{1,0:T(8,128)(2,1)}, bf16[288,1408]{1,0:T(8,128)(2,1)}) custom-call(s32[3]{0:T(128)} %pad_add_fusion.place, f32[8,128]{1,0:T(8,128)} %get-tuple-element.78.token, bf16[32,2560]{1,0:T(8,128)(2,1)} %pq.1, bf16[32,2560]{1,0:T(8,128)(2,1)} %po.1, bf16[32,2560]{1,0:T(8,128)(2,1)} %pg.1, ...), custom_call_target="tpu_custom_call" | custom-call | flops 1006632960 | bytes 13107200 | tf_op jit(solution)/shard_map/prepare_rows/pallas_call | solution.py:517
  15.8 1.3 %collective-permute-done.2.refs_5_ = bf16[384,256]{1,0:T(8,128)(2,1)S(1)} collective-permute-done((bf16[384,256]{1,0:T(8,128)(2,1)}, bf16[384,256]{1,0:T(8,128)(2,1)S(1)}, u32[]{:S(2)}, u32[]{:S(2)}) %collective-permute-start.2) | collective-permute-done | bytes 196640 | tf_op jit(solution)/shard_map/ppermute | solution.py:511
  17.1 1.4 %collective-permute-done.4.refs_7_ = bf16[384,256]{1,0:T(8,128)(2,1)S(1)} collective-permute-done((bf16[384,256]{1,0:T(8,128)(2,1)}, bf16[384,256]{1,0:T(8,128)(2,1)S(1)}, u32[]{:S(2)}, u32[]{:S(2)}) %collective-permute-start.4) | collective-permute-done | bytes 196640 | tf_op jit(solution)/shard_map/ppermute | solution.py:511
  19.0 1.7 %collective-permute-start.6 = (bf16[384,256]{1,0:T(8,128)(2,1)S(1)}, bf16[384,256]{1,0:T(8,128)(2,1)S(1)}, u32[]{:S(2)}, u32[]{:S(2)}) collective-permute-start(bf16[384,256]{1,0:T(8,128)(2,1)S(1)} %collective-permute-done.1.refs_4_), channel_id=1, source_target_pairs={{0,16},{4,20},{8,24},{12,28},{16,0},{20,4},{24,8},{28,12},{1,17},{... | collective-permute-start | bytes 589832 | tf_op jit(solution)/shard_map/ppermute | solution.py:511
  20.7 1.5 %collective-permute-start.7 = (bf16[384,256]{1,0:T(8,128)(2,1)S(1)}, bf16[384,256]{1,0:T(8,128)(2,1)S(1)}, u32[]{:S(2)}, u32[]{:S(2)}) collective-permute-start(bf16[384,256]{1,0:T(8,128)(2,1)S(1)} %collective-permute-done.4.refs_7_), channel_id=1, source_target_pairs={{0,8},{4,12},{8,0},{12,4},{16,24},{20,28},{24,16},{28,20},{1,9},{5... | collective-permute-start | bytes 589832 | tf_op jit(solution)/shard_map/ppermute | solution.py:511
  22.3 0.6 collective-permute-start.12
  23.2 3.6 %collective-permute-done.6.refs_8_ = bf16[384,256]{1,0:T(8,128)(2,1)S(1)} collective-permute-done((bf16[384,256]{1,0:T(8,128)(2,1)S(1)}, bf16[384,256]{1,0:T(8,128)(2,1)S(1)}, u32[]{:S(2)}, u32[]{:S(2)}) %collective-permute-start.6) | collective-permute-done | bytes 196640 | tf_op jit(solution)/shard_map/ppermute | solution.py:511
  26.7 2.7 %collective-permute-start.14 = (bf16[2,384,256]{2,1,0:T(8,128)(2,1)S(1)}, bf16[2,384,256]{2,1,0:T(8,128)(2,1)S(1)}, u32[]{:S(2)}, u32[]{:S(2)}) collective-permute-start(bf16[2,384,256]{2,1,0:T(8,128)(2,1)S(1)} %pad_maximum_fusion.refs_2_), channel_id=1, source_target_pairs={{0,24},{4,28},{8,16},{12,20},{16,8},{20,12},{24,0},{28,4},{1,25},{... | collective-permute-start | bytes 1179656 | tf_op jit(solution)/shard_map/ppermute | solution.py:511
  29.4 1.1 %copy-done.2 = bf16[288,1408]{1,0:T(8,128)(2,1)S(1)} copy-done((bf16[288,1408]{1,0:T(8,128)(2,1)S(1)}, bf16[288,1408]{1,0:T(8,128)(2,1)}, u32[]{:S(2)}) %copy-start.2) | copy-done | bytes 811032
  30.6 18.8 %attend.2 = (bf16[288,640]{1,0:T(8,128)(2,1)S(1)}, bf16[288,640]{1,0:T(8,128)(2,1)S(1)}, bf16[2,384,256]{2,1,0:T(8,128)(2,1)S(1)}, bf16[2,384,256]{2,1,0:T(8,128...) custom-call(s32[3]{0:T(128)S(1)} %copy-done, s32[8]{0:T(128)S(1)} %copy-done.4, ...), custom_call_target="tpu_custom_call" | custom-call | flops 6710886400 | bytes 8388608 | tf_op jit(solution)/shard_map/attend/pallas_call | solution.py:517
  49.3 0.7 collective-permute-start.8
  50.0 2.9 %collective-permute-start.10 = (bf16[2,384,256]{2,1,0:T(8,128)(2,1)S(1)}, bf16[2,384,256]{2,1,0:T(8,128)(2,1)S(1)}, u32[]{:S(2)}, u32[]{:S(2)}) collective-permute-start(bf16[2,384,256]{2,1,0:T(8,128)(2,1)S(1)} %get-tuple-element.94), channel_id=1, source_target_pairs={{0,24},{4,28},{8,16},{12,20},{16,8},{20,12},{24,0},{28,4},{1,25},{... | collective-permute-start | bytes 1179656 | tf_op jit(solution)/shard_map/ppermute | solution.py:511
  52.9 18.7 %attend.3 = (bf16[288,640]{1,0:T(8,128)(2,1)S(1)}, bf16[288,640]{1,0:T(8,128)(2,1)S(1)}, bf16[2,256,256]{2,1,0:T(8,128)(2,1)S(1)}, bf16[2,256,256]{2,1,0:T(8,128...) custom-call(s32[3]{0:T(128)S(1)} %copy-done, ...), custom_call_target="tpu_custom_call" | custom-call | flops 6710886400 | bytes 8388608 | tf_op jit(solution)/shard_map/attend/pallas_call | solution.py:517
  71.7 0.6 collective-permute-start.21
  72.2 0.6 collective-permute-start.15
  72.8 2.9 %collective-permute-start.17 = (bf16[2,128,256]{2,1,0:T(8,128)(2,1)S(1)}, bf16[2,128,256]{2,1,0:T(8,128)(2,1)S(1)}, u32[]{:S(2)}, u32[]{:S(2)}) collective-permute-start(bf16[2,128,256]{2,1,0:T(8,128)(2,1)S(1)} %get-tuple-element.114), channel_id=1, source_target_pairs={{0,24},{4,28},{8,16},{12,20},{16,8},{20,12},{24,0},{28,4},{1,25},{... | collective-permute-start | bytes 393224 | tf_op jit(solution)/shard_map/ppermute | solution.py:511
  75.7 0.6 collective-permute-start.22
  76.3 2.3 %collective-permute-done.15.refs_5_ = bf16[2,128,256]{2,1,0:T(8,128)(2,1)S(1)} collective-permute-done((bf16[2,128,256]{2,1,0:T(8,128)(2,1)S(1)}, bf16[2,128,256]{2,1,0:T(8,128)(2,1)S(1)}, u32[]{:S(2)}, u32[]{:S(2)}) %collective-permute-start.15) | collective-permute-done | bytes 131104 | tf_op jit(solution)/shard_map/ppermute | solution.py:511
  78.6 3.2 %collective-permute-done.16.refs_6_ = bf16[2,128,256]{2,1,0:T(8,128)(2,1)S(1)} collective-permute-done((bf16[2,128,256]{2,1,0:T(8,128)(2,1)S(1)}, bf16[2,128,256]{2,1,0:T(8,128)(2,1)S(1)}, u32[]{:S(2)}, u32[]{:S(2)}) %collective-permute-start.16) | collective-permute-done | bytes 131104 | tf_op jit(solution)/shard_map/ppermute | solution.py:511
  82.2 0.9 collect_first.1
  83.1 12.1 %collective-permute-start.18 = (bf16[4,32,256]{2,1,0:T(8,128)(2,1)S(1)}, bf16[4,32,256]{2,1,0:T(8,128)(2,1)S(1)}, u32[]{:S(2)}, u32[]{:S(2)}) collective-permute-start(bf16[4,32,256]{2,1,0:T(8,128)(2,1)S(1)} %get-tuple-element.116), channel_id=1, source_target_pairs={{0,1},{1,2},{2,3},{3,0},{4,5},{5,6},{6,7},{7,4},{8,9},{9,10},{10,1... | collective-permute-start | bytes 196616 | tf_op jit(solution)/shard_map/ppermute | solution.py:667
  95.2 1.9 %collective-permute-done.18.refs_5_ = bf16[4,32,256]{2,1,0:T(8,128)(2,1)S(1)} collective-permute-done((bf16[4,32,256]{2,1,0:T(8,128)(2,1)S(1)}, bf16[4,32,256]{2,1,0:T(8,128)(2,1)S(1)}, u32[]{:S(2)}, u32[]{:S(2)}) %collective-permute-start.18) | collective-permute-done | bytes 65568 | tf_op jit(solution)/shard_map/ppermute | solution.py:667
  97.1 3.4 %collective-permute-start.19 = (bf16[4,32,256]{2,1,0:T(8,128)(2,1)S(1)}, bf16[4,32,256]{2,1,0:T(8,128)(2,1)S(1)}, u32[]{:S(2)}, u32[]{:S(2)}) collective-permute-start(bf16[4,32,256]{2,1,0:T(8,128)(2,1)S(1)} %get-tuple-element.117), channel_id=1, source_target_pairs={{0,2},{1,3},{2,0},{3,1},{4,6},{5,7},{6,4},{7,5},{8,10},{9,11},{10,... | collective-permute-start | bytes 196616 | tf_op jit(solution)/shard_map/ppermute | solution.py:667
  100.6 1.3 %collective-permute-start.20 = (bf16[4,32,256]{2,1,0:T(8,128)(2,1)S(1)}, bf16[4,32,256]{2,1,0:T(8,128)(2,1)S(1)}, u32[]{:S(2)}, u32[]{:S(2)}) collective-permute-start(bf16[4,32,256]{2,1,0:T(8,128)(2,1)S(1)} %get-tuple-element.118), channel_id=1, source_target_pairs={{0,3},{1,0},{2,1},{3,2},{4,7},{5,4},{6,5},{7,6},{8,11},{9,8},{10,9... | collective-permute-start | bytes 196616 | tf_op jit(solution)/shard_map/ppermute | solution.py:667
  101.9 2.2 %finish_queries.1 = (bf16[32,2560]{1,0:T(8,128)(2,1)}, bf16[256,2560]{1,0:T(8,128)(2,1)}) custom-call(s32[3]{0:T(128)S(1)} %copy-done, bf16[288,640]{1,0:T(8,128)(2,1)S(1)} %get-tuple-element.119.refs_0_, bf16[288,640]{1,0:T(8,128)(2,1)S(1)} %collective-permute-done.11.refs_1_, bf16[288,640]{1,0:T(8,128)(2,1)S(1)} %get-tuple-element.121.refs_2_, ...), custom_call_target="tpu_custom_call" | custom-call | flops 335544320 | bytes 5242880 | tf_op jit(solution)/shard_map/finish_queries/pallas_call | solution.py:517
  104.1 0.8 collective-permute-done.20.refs_7_
  105.1 1.6 %collective-permute-done.25.theirs = bf16[576,256]{1,0:T(8,128)(2,1)S(1)} collective-permute-done((bf16[576,256]{1,0:T(8,128)(2,1)S(1)}, bf16[576,256]{1,0:T(8,128)(2,1)S(1)}, u32[]{:S(2)}, u32[]{:S(2)}) %collective-permute-start.25) | collective-permute-done | bytes 294944 | tf_op jit(solution)/shard_map/ppermute | solution.py:511
  106.7 1.7 %finish_keys.1 = (bf16[32,512]{1,0:T(8,128)(2,1)}, bf16[32,512]{1,0:T(8,128)(2,1)}, bf16[256,512]{1,0:T(8,128)(2,1)}, bf16[256,512]{1,0:T(8,128)(2,1)}) custom-call(s32[3]{0:T(128)S(1)} %copy-done, f32[256,256]{1,0:T(8,128)S(1)} %get-tuple-element.126.reply0, f32[256,256]{1,0:T(8,128)S(1)} %get-tuple-element.136.reply1, ...), custom_call_target="tpu_custom_call" | custom-call | tf_op jit(solution)/shard_map/finish_keys/pallas_call | solution.py:517
  (45 shorter events, 2.1 us)
Async XLA Ops:
  4.4 14.2 %collective-permute-start = (bf16[2,384,256]{2,1,0:T(8,128)(2,1)}, bf16[2,384,256]{2,1,0:T(8,128)(2,1)S(1)}, u32[]{:S(2)}, u32[]{:S(2)}) collective-permute-start(bf16[2,384,256]{2,1,0:T(8,128)(2,1)} %get-tuple-element.76), channel_id=1, source_target_pairs={{0,4},{4,0},{8,12},{12,8},{16,20},{20,16},{24,28},{28,24},{1,5},{5... | collective-permute-start | bytes 1179656 | tf_op jit(solution)/shard_map/ppermute | solution.py:511
  4.9 10.9 %collective-permute-start.1 = (bf16[384,256]{1,0:T(8,128)(2,1)}, bf16[384,256]{1,0:T(8,128)(2,1)S(1)}, u32[]{:S(2)}, u32[]{:S(2)}) collective-permute-start(bf16[384,256]{1,0:T(8,128)(2,1)} %get-tuple-element.85.refs_2_), channel_id=1, source_target_pairs={{0,8},{4,12},{8,0},{12,4},{16,24},{20,28},{24,16},{28,20},{1,9},{5... | collective-permute-start | bytes 589832 | tf_op jit(solution)/shard_map/ppermute | solution.py:511
  7.5 9.7 %collective-permute-start.2 = (bf16[384,256]{1,0:T(8,128)(2,1)}, bf16[384,256]{1,0:T(8,128)(2,1)S(1)}, u32[]{:S(2)}, u32[]{:S(2)}) collective-permute-start(bf16[384,256]{1,0:T(8,128)(2,1)} %get-tuple-element.77), channel_id=1, source_target_pairs={{0,12},{4,8},{8,4},{12,0},{16,28},{20,24},{24,20},{28,16},{1,13},{... | collective-permute-start | bytes 589832 | tf_op jit(solution)/shard_map/ppermute | solution.py:511
  7.5 9.6 %collective-permute-start.3 = (bf16[384,256]{1,0:T(8,128)(2,1)}, bf16[384,256]{1,0:T(8,128)(2,1)S(1)}, u32[]{:S(2)}, u32[]{:S(2)}) collective-permute-start(bf16[384,256]{1,0:T(8,128)(2,1)} %get-tuple-element.85.refs_2_), channel_id=1, source_target_pairs={{0,16},{4,20},{8,24},{12,28},{16,0},{20,4},{24,8},{28,12},{1,17},{... | collective-permute-start | bytes 589832 | tf_op jit(solution)/shard_map/ppermute | solution.py:511
  9.3 9.3 %collective-permute-start.4 = (bf16[384,256]{1,0:T(8,128)(2,1)}, bf16[384,256]{1,0:T(8,128)(2,1)S(1)}, u32[]{:S(2)}, u32[]{:S(2)}) collective-permute-start(bf16[384,256]{1,0:T(8,128)(2,1)} %get-tuple-element.77), channel_id=1, source_target_pairs={{0,20},{4,16},{8,28},{12,24},{16,4},{20,0},{24,12},{28,8},{1,21},{... | collective-permute-start | bytes 589832 | tf_op jit(solution)/shard_map/ppermute | solution.py:511
  9.3 12.9 %copy-start.6 = (bf16[384,256]{1,0:T(8,128)(2,1)S(1)}, bf16[384,256]{1,0:T(8,128)(2,1)}, u32[]{:S(2)}) copy-start(bf16[384,256]{1,0:T(8,128)(2,1)} %get-tuple-element.97) | copy-start | bytes 589828
  9.3 20.1 %copy-start = (s32[3]{0:T(128)S(1)}, s32[3]{0:T(128)}, u32[]{:S(2)}) copy-start(s32[3]{0:T(128)} %pad_add_fusion.place) | copy-start | bytes 40
  9.3 20.1 %copy-start.3 = (bf16[384,256]{1,0:T(8,128)(2,1)S(1)}, bf16[384,256]{1,0:T(8,128)(2,1)}, u32[]{:S(2)}) copy-start(bf16[384,256]{1,0:T(8,128)(2,1)} %get-tuple-element.85.refs_2_) | copy-start | bytes 589828
  9.3 20.1 %copy-start.4 = (s32[8]{0:T(128)S(1)}, s32[8]{0:T(128)}, u32[]{:S(2)}) copy-start(s32[8]{0:T(128)} %reply_len.3) | copy-start | bytes 100
  9.3 20.1 %copy-start.5 = (s32[8]{0:T(128)S(1)}, s32[8]{0:T(128)}, u32[]{:S(2)}) copy-start(s32[8]{0:T(128)} %reply_slot.3) | copy-start | bytes 100
  18.6 10.8 %collective-permute-start.5 = (bf16[2,288,1408]{2,1,0:T(8,128)(2,1)}, bf16[2,288,1408]{2,1,0:T(8,128)(2,1)S(1)}, u32[]{:S(2)}, u32[]{:S(2)}) collective-permute-start(bf16[2,288,1408]{2,1,0:T(8,128)(2,1)} %get-tuple-element.84), channel_id=1, source_target_pairs={{0,4},{4,0},{8,12},{12,8},{16,20},{20,16},{24,28},{28,24},{1,5},{5... | collective-permute-start | bytes 4866056 | tf_op jit(solution)/shard_map/ppermute | solution.py:511
  19.0 7.8 %collective-permute-start.6 = (bf16[384,256]{1,0:T(8,128)(2,1)S(1)}, bf16[384,256]{1,0:T(8,128)(2,1)S(1)}, u32[]{:S(2)}, u32[]{:S(2)}) collective-permute-start(bf16[384,256]{1,0:T(8,128)(2,1)S(1)} %collective-permute-done.1.refs_4_), channel_id=1, source_target_pairs={{0,16},{4,20},{8,24},{12,28},{16,0},{20,4},{24,8},{28,12},{1,17},{... | collective-permute-start | bytes 589832 | tf_op jit(solution)/shard_map/ppermute | solution.py:511
  20.7 8.7 %collective-permute-start.7 = (bf16[384,256]{1,0:T(8,128)(2,1)S(1)}, bf16[384,256]{1,0:T(8,128)(2,1)S(1)}, u32[]{:S(2)}, u32[]{:S(2)}) collective-permute-start(bf16[384,256]{1,0:T(8,128)(2,1)S(1)} %collective-permute-done.4.refs_7_), channel_id=1, source_target_pairs={{0,8},{4,12},{8,0},{12,4},{16,24},{20,28},{24,16},{28,20},{1,9},{5... | collective-permute-start | bytes 589832 | tf_op jit(solution)/shard_map/ppermute | solution.py:511
  22.3 30.7 %copy-start.1 = (bf16[288,1408]{1,0:T(8,128)(2,1)S(1)}, bf16[288,1408]{1,0:T(8,128)(2,1)}, u32[]{:S(2)}) copy-start(bf16[288,1408]{1,0:T(8,128)(2,1)} %get-tuple-element.96.refs_0_) | copy-start | bytes 2433028
  22.3 27.7 %collective-permute-start.12 = (bf16[2,384,256]{2,1,0:T(8,128)(2,1)S(1)}, bf16[2,384,256]{2,1,0:T(8,128)(2,1)S(1)}, u32[]{:S(2)}, u32[]{:S(2)}) collective-permute-start(bf16[2,384,256]{2,1,0:T(8,128)(2,1)S(1)} %pad_maximum_fusion.refs_2_), channel_id=1, source_target_pairs={{0,8},{4,12},{8,0},{12,4},{16,24},{20,28},{24,16},{28,20},{1,9},{5... | collective-permute-start | bytes 1179656 | tf_op jit(solution)/shard_map/ppermute | solution.py:511
  22.9 30.0 %collective-permute-start.13 = (bf16[2,384,256]{2,1,0:T(8,128)(2,1)S(1)}, bf16[2,384,256]{2,1,0:T(8,128)(2,1)S(1)}, u32[]{:S(2)}, u32[]{:S(2)}) collective-permute-start(bf16[2,384,256]{2,1,0:T(8,128)(2,1)S(1)} %pad_maximum_fusion.refs_2_), channel_id=1, source_target_pairs={{0,16},{4,20},{8,24},{12,28},{16,0},{20,4},{24,8},{28,12},{1,17},{... | collective-permute-start | bytes 1179656 | tf_op jit(solution)/shard_map/ppermute | solution.py:511
  26.7 26.2 %collective-permute-start.14 = (bf16[2,384,256]{2,1,0:T(8,128)(2,1)S(1)}, bf16[2,384,256]{2,1,0:T(8,128)(2,1)S(1)}, u32[]{:S(2)}, u32[]{:S(2)}) collective-permute-start(bf16[2,384,256]{2,1,0:T(8,128)(2,1)S(1)} %pad_maximum_fusion.refs_2_), channel_id=1, source_target_pairs={{0,24},{4,28},{8,16},{12,20},{16,8},{20,12},{24,0},{28,4},{1,25},{... | collective-permute-start | bytes 1179656 | tf_op jit(solution)/shard_map/ppermute | solution.py:511
  49.3 22.3 %collective-permute-start.8 = (bf16[2,384,256]{2,1,0:T(8,128)(2,1)S(1)}, bf16[2,384,256]{2,1,0:T(8,128)(2,1)S(1)}, u32[]{:S(2)}, u32[]{:S(2)}) collective-permute-start(bf16[2,384,256]{2,1,0:T(8,128)(2,1)S(1)} %get-tuple-element.92), channel_id=1, source_target_pairs={{0,8},{4,12},{8,0},{12,4},{16,24},{20,28},{24,16},{28,20},{1,9},{5... | collective-permute-start | bytes 1179656 | tf_op jit(solution)/shard_map/ppermute | solution.py:511
  50.0 21.6 %collective-permute-start.9 = (bf16[2,384,256]{2,1,0:T(8,128)(2,1)S(1)}, bf16[2,384,256]{2,1,0:T(8,128)(2,1)S(1)}, u32[]{:S(2)}, u32[]{:S(2)}) collective-permute-start(bf16[2,384,256]{2,1,0:T(8,128)(2,1)S(1)} %get-tuple-element.93), channel_id=1, source_target_pairs={{0,16},{4,20},{8,24},{12,28},{16,0},{20,4},{24,8},{28,12},{1,17},{... | collective-permute-start | bytes 1179656 | tf_op jit(solution)/shard_map/ppermute | solution.py:511
  50.0 21.6 %collective-permute-start.10 = (bf16[2,384,256]{2,1,0:T(8,128)(2,1)S(1)}, bf16[2,384,256]{2,1,0:T(8,128)(2,1)S(1)}, u32[]{:S(2)}, u32[]{:S(2)}) collective-permute-start(bf16[2,384,256]{2,1,0:T(8,128)(2,1)S(1)} %get-tuple-element.94), channel_id=1, source_target_pairs={{0,24},{4,28},{8,16},{12,20},{16,8},{20,12},{24,0},{28,4},{1,25},{... | collective-permute-start | bytes 1179656 | tf_op jit(solution)/shard_map/ppermute | solution.py:511
  52.9 18.7 %collective-permute-start.11 = (bf16[288,640]{1,0:T(8,128)(2,1)S(1)}, bf16[288,640]{1,0:T(8,128)(2,1)S(1)}, u32[]{:S(2)}, u32[]{:S(2)}) collective-permute-start(bf16[288,640]{1,0:T(8,128)(2,1)S(1)} %get-tuple-element.95), channel_id=1, source_target_pairs={{0,4},{4,0},{8,12},{12,8},{16,20},{20,16},{24,28},{28,24},{1,5},{5... | collective-permute-start | bytes 1105928 | tf_op jit(solution)/shard_map/ppermute | solution.py:511
  71.7 28.9 %collective-permute-start.21 = (bf16[288,640]{1,0:T(8,128)(2,1)S(1)}, bf16[288,640]{1,0:T(8,128)(2,1)S(1)}, u32[]{:S(2)}, u32[]{:S(2)}) collective-permute-start(bf16[288,640]{1,0:T(8,128)(2,1)S(1)} %get-tuple-element.122), channel_id=1, source_target_pairs={{0,4},{4,0},{8,12},{12,8},{16,20},{20,16},{24,28},{28,24},{1,5},{5... | collective-permute-start | bytes 1105928 | tf_op jit(solution)/shard_map/ppermute | solution.py:511
  72.2 6.4 %collective-permute-start.15 = (bf16[2,128,256]{2,1,0:T(8,128)(2,1)S(1)}, bf16[2,128,256]{2,1,0:T(8,128)(2,1)S(1)}, u32[]{:S(2)}, u32[]{:S(2)}) collective-permute-start(bf16[2,128,256]{2,1,0:T(8,128)(2,1)S(1)} %get-tuple-element.112), channel_id=1, source_target_pairs={{0,8},{4,12},{8,0},{12,4},{16,24},{20,28},{24,16},{28,20},{1,9},{5... | collective-permute-start | bytes 393224 | tf_op jit(solution)/shard_map/ppermute | solution.py:511
  72.8 8.9 %collective-permute-start.16 = (bf16[2,128,256]{2,1,0:T(8,128)(2,1)S(1)}, bf16[2,128,256]{2,1,0:T(8,128)(2,1)S(1)}, u32[]{:S(2)}, u32[]{:S(2)}) collective-permute-start(bf16[2,128,256]{2,1,0:T(8,128)(2,1)S(1)} %get-tuple-element.113), channel_id=1, source_target_pairs={{0,16},{4,20},{8,24},{12,28},{16,0},{20,4},{24,8},{28,12},{1,17},{... | collective-permute-start | bytes 393224 | tf_op jit(solution)/shard_map/ppermute | solution.py:511
  72.8 9.4 %collective-permute-start.17 = (bf16[2,128,256]{2,1,0:T(8,128)(2,1)S(1)}, bf16[2,128,256]{2,1,0:T(8,128)(2,1)S(1)}, u32[]{:S(2)}, u32[]{:S(2)}) collective-permute-start(bf16[2,128,256]{2,1,0:T(8,128)(2,1)S(1)} %get-tuple-element.114), channel_id=1, source_target_pairs={{0,24},{4,28},{8,16},{12,20},{16,8},{20,12},{24,0},{28,4},{1,25},{... | collective-permute-start | bytes 393224 | tf_op jit(solution)/shard_map/ppermute | solution.py:511
  75.7 29.1 %collective-permute-start.22 = (bf16[2,256,256]{2,1,0:T(8,128)(2,1)S(1)}, bf16[2,256,256]{2,1,0:T(8,128)(2,1)S(1)}, u32[]{:S(2)}, u32[]{:S(2)}) collective-permute-start(bf16[2,256,256]{2,1,0:T(8,128)(2,1)S(1)} %get-tuple-element.128), channel_id=1, source_target_pairs={{0,8},{4,12},{8,0},{12,4},{16,24},{20,28},{24,16},{28,20},{1,9},{5... | collective-permute-start | bytes 786440 | tf_op jit(solution)/shard_map/ppermute | solution.py:511
  78.6 26.3 %collective-permute-start.23 = (bf16[2,256,256]{2,1,0:T(8,128)(2,1)S(1)}, bf16[2,256,256]{2,1,0:T(8,128)(2,1)S(1)}, u32[]{:S(2)}, u32[]{:S(2)}) collective-permute-start(bf16[2,256,256]{2,1,0:T(8,128)(2,1)S(1)} %get-tuple-element.129), channel_id=1, source_target_pairs={{0,16},{4,20},{8,24},{12,28},{16,0},{20,4},{24,8},{28,12},{1,17},{... | collective-permute-start | bytes 786440 | tf_op jit(solution)/shard_map/ppermute | solution.py:511
  81.7 23.1 %collective-permute-start.24 = (bf16[2,256,256]{2,1,0:T(8,128)(2,1)S(1)}, bf16[2,256,256]{2,1,0:T(8,128)(2,1)S(1)}, u32[]{:S(2)}, u32[]{:S(2)}) collective-permute-start(bf16[2,256,256]{2,1,0:T(8,128)(2,1)S(1)} %get-tuple-element.130), channel_id=1, source_target_pairs={{0,24},{4,28},{8,16},{12,20},{16,8},{20,12},{24,0},{28,4},{1,25},{... | collective-permute-start | bytes 786440 | tf_op jit(solution)/shard_map/ppermute | solution.py:511
  83.1 14.0 %collective-permute-start.18 = (bf16[4,32,256]{2,1,0:T(8,128)(2,1)S(1)}, bf16[4,32,256]{2,1,0:T(8,128)(2,1)S(1)}, u32[]{:S(2)}, u32[]{:S(2)}) collective-permute-start(bf16[4,32,256]{2,1,0:T(8,128)(2,1)S(1)} %get-tuple-element.116), channel_id=1, source_target_pairs={{0,1},{1,2},{2,3},{3,0},{4,5},{5,6},{6,7},{7,4},{8,9},{9,10},{10,1... | collective-permute-start | bytes 196616 | tf_op jit(solution)/shard_map/ppermute | solution.py:667
  97.1 6.9 %collective-permute-start.19 = (bf16[4,32,256]{2,1,0:T(8,128)(2,1)S(1)}, bf16[4,32,256]{2,1,0:T(8,128)(2,1)S(1)}, u32[]{:S(2)}, u32[]{:S(2)}) collective-permute-start(bf16[4,32,256]{2,1,0:T(8,128)(2,1)S(1)} %get-tuple-element.117), channel_id=1, source_target_pairs={{0,2},{1,3},{2,0},{3,1},{4,6},{5,7},{6,4},{7,5},{8,10},{9,11},{10,... | collective-permute-start | bytes 196616 | tf_op jit(solution)/shard_map/ppermute | solution.py:667
  100.6 4.3 %collective-permute-start.20 = (bf16[4,32,256]{2,1,0:T(8,128)(2,1)S(1)}, bf16[4,32,256]{2,1,0:T(8,128)(2,1)S(1)}, u32[]{:S(2)}, u32[]{:S(2)}) collective-permute-start(bf16[4,32,256]{2,1,0:T(8,128)(2,1)S(1)} %get-tuple-element.118), channel_id=1, source_target_pairs={{0,3},{1,0},{2,1},{3,2},{4,7},{5,4},{6,5},{7,6},{8,11},{9,8},{10,9... | collective-permute-start | bytes 196616 | tf_op jit(solution)/shard_map/ppermute | solution.py:667
  105.0 1.6 %collective-permute-start.25 = (bf16[576,256]{1,0:T(8,128)(2,1)S(1)}, bf16[576,256]{1,0:T(8,128)(2,1)S(1)}, u32[]{:S(2)}, u32[]{:S(2)}) collective-permute-start(bf16[576,256]{1,0:T(8,128)(2,1)S(1)} %get-tuple-element.138), channel_id=1, source_target_pairs={{0,4},{4,0},{8,12},{12,8},{16,20},{20,16},{24,28},{28,24},{1,5},{5... | collective-permute-start | bytes 884744 | tf_op jit(solution)/shard_map/ppermute | solution.py:511
  (1 other events, 1.1 us)
